TPU v7x, 128 devices: a whole 4x4x4 slice. The times are simulated.
128 devices in a mesh: img: 16 (over y, z_lo, core), txt: 8 (over x, z_hi).
Axes of the slice: x: 4, y: 4, z: 4 (z_hi: 2, z_lo: 2; z = z_hi * 2 + z_lo), core: 2. Of those that a mesh axis runs over, the one named last changes fastest.
Arguments:
- image_embed: float32 [16384, 1152], P(('img', 'txt')), may hold values from -0.18 to 0.18
- text_embed: float32 [16384, 1152], P(('txt', 'img')), may hold values from -0.18 to 0.18
- log_scale: float32 [], replicated, may hold values from 1.5 to 2.5
- logit_bias: float32 [], replicated, may hold values from -4 to -2
Outputs:
- loss_mean: float32 [], replicated
- image_grad: float32 [16384, 1152], P(('img', 'txt'))
- text_grad: float32 [16384, 1152], P(('txt', 'img'))
- scale_grad: float32 [], replicated
- bias_grad: float32 [], replicated
All inputs are finite; a program needn't handle non-finite values.
Results may differ from a plain program's by a relative error of at most 0.001.
The roundings to bfloat16 on the way count: a program that leaves them out, or rounds other values in their place, can miss the bound.
Values may be sent and summed in bfloat16 or wider, within the bound.
No kernel may reach another device: no remote copies, remote signals or barrier semaphores. Data moves between devices by JAX's collectives and lax.ppermute only.
A program may use at most 128 MiB of HBM per device.

v0:
```python
import jax
import jax.numpy as jnp
from jax import lax
from jax.sharding import PartitionSpec as P


def normalize(embed):
    norm = jnp.sqrt(jnp.sum(embed * embed, axis=1, keepdims=True) + 1e-06)
    return (embed / norm, norm)


def unnormalize(hat, norm, pull):
    return (pull - hat * jnp.sum(hat * pull, axis=1, keepdims=True)) / norm


def local(image_embed, text_embed, log_scale, logit_bias):
    image_hat, image_norm = normalize(image_embed)
    text_hat, text_norm = normalize(text_embed)
    image_block = lax.all_gather(image_hat.astype(jnp.bfloat16), "txt", axis=0, tiled=True)
    text_block = lax.all_gather(text_hat.astype(jnp.bfloat16), "img", axis=0, tiled=True)
    img_rows = image_block.shape[0]
    txt_rows = text_block.shape[0]
    width = image_block.shape[1]
    image_start = lax.axis_index("img") * img_rows
    text_start = lax.axis_index("txt") * txt_rows
    scale = jnp.exp(log_scale)
    block = min(512, img_rows)
    count = img_rows // block
    columns = text_start + jnp.arange(txt_rows, dtype=jnp.int32)

    def score(index):
        start = index * block
        rows = lax.dynamic_slice_in_dim(image_block, start, block, 0)
        similar = jnp.dot(rows, text_block.T, preferred_element_type=jnp.float32)
        logit = scale * similar + logit_bias
        row_ids = image_start + start + jnp.arange(block, dtype=jnp.int32)
        sign = jnp.where(row_ids[:, None] == columns[None, :], 1.0, -1.0).astype(jnp.float32)
        total = jnp.sum(jax.nn.softplus(-sign * logit))
        slope = -sign * jax.nn.sigmoid(-sign * logit)
        weight = (scale * slope).astype(jnp.bfloat16)
        image_pull = jnp.dot(weight, text_block, preferred_element_type=jnp.float32)
        return (weight, image_pull, total, jnp.sum(slope * scale * similar), jnp.sum(slope))

    weights, image_pulls, totals, scale_parts, bias_parts = lax.map(
        score, jnp.arange(count, dtype=jnp.int32)
    )
    weight_all = weights.reshape(img_rows, txt_rows)
    image_terms = image_pulls.reshape(img_rows, width)
    total, scale_sum, bias_sum = lax.psum(
        (jnp.sum(totals), jnp.sum(scale_parts), jnp.sum(bias_parts)), ("img", "txt")
    )
    image_pull = lax.psum_scatter(image_terms, "txt", scatter_dimension=0, tiled=True)
    terms = lax.dot_general(
        weight_all, image_block, (((0,), (0,)), ((), ())), preferred_element_type=jnp.float32
    )
    text_pull = lax.psum_scatter(terms, "img", scatter_dimension=0, tiled=True)
    pairs = jnp.float32(img_rows * lax.axis_size("img")) * jnp.float32(
        txt_rows * lax.axis_size("txt")
    )
    image_grad = unnormalize(image_hat, image_norm, image_pull)
    text_grad = unnormalize(text_hat, text_norm, text_pull)
    return (total / pairs, image_grad, text_grad, scale_sum / pairs, bias_sum / pairs)


def solution(mesh):
    placed = (P(("img", "txt"), None), P(("txt", "img"), None), P(), P())
    return jax.shard_map(
        local,
        mesh=mesh,
        in_specs=placed,
        out_specs=(P(), P(("img", "txt"), None), P(("txt", "img"), None), P(), P()),
        check_vma=False,
    )
```

profile of v0, /device:TPU:0, one launch (start us, length us, event | category | flops | bytes accessed | tf_op | source)
XLA Modules:
  0.0 371.9 jit_solution(99555204664185254)
XLA Ops:
  7.2 0.0 all-gather.3.cloned.1.call-start
  7.2 1.2 multiply_reduce_fusion.4
  8.4 1.9 fusion.7
  10.3 0.0 all-gather.3.cloned.1.call-update
  10.3 0.0 all-gather.5.cloned.1.call-start
  10.4 1.2 multiply_reduce_fusion.3
  11.6 1.9 fusion.8
  13.5 0.0 all-gather.5.cloned.1.call-update
  13.5 0.0 reduce-scatter.3.cloned.1.call-start
  14.3 56.0 %all-gather.3.cloned.1.call-done = bf16[1024,1152]{1,0:T(8,128)(2,1)} async-done(((bf16[128,1152]{1,0:T(8,128)(2,1)}), bf16[1024,1152]{1,0:T(8,128)(2,1)}) %all-gather.3.cloned.1.call-update) | async-done | bytes 2359312 | tf_op jit(solution)/shard_map/all_gather | solution.py:19
  70.2 39.4 %all-gather.5.cloned.1.call-done = bf16[2048,1152]{1,0:T(8,128)(2,1)} async-done(((bf16[128,1152]{1,0:T(8,128)(2,1)}), bf16[2048,1152]{1,0:T(8,128)(2,1)}) %all-gather.5.cloned.1.call-update) | async-done | bytes 4718608 | tf_op jit(solution)/shard_map/all_gather | solution.py:20
  109.6 54.0 %while.19 = (s32[]{:T(128)}, bf16[2,512,2048]{2,1,0:T(8,128)(2,1)}, f32[2,512,1152]{2,1,0:T(8,128)}, f32[2]{0:T(128)S(1)}, f32[2]{0:T(128)S(1)}, /*index=5*/f32[...) while((s32[]{:T(128)}, bf16[2,512,2048]{2,1,0:T(8,128)(2,1)}, ...), condition=%wide.region_6.7_spmd.clone, body=%wide.region_2.6_spmd.clone.sunk | while | flops 4858055168 | bytes 44456268 | solution.py:44
  109.6 0.6 dynamic_slice.16
  110.9 12.7 %fusion.21 = (f32[]{:T(128)}, f32[]{:T(128)}, f32[]{:T(128)}, f32[512,2048]{1,0:T(8,128)}) fusion(f32[]{:T(128)} %get-tuple-element.270, f32[]{:T(128)} %get-tuple-element.275, s32[2048]{0:T(1024)S(1)} %iota_add_fusion.4, s32[512]{0:T(512)S(1)} %iota_add_fusion.5, bf16[2048,1152]{1,0:T(8,128)(2,1)} %get-tuple-element.274, ...), kind=kOutput, calls=%fused_computation.28.clone.1 | convolution fusion | flops 2437939200 | bytes 10103824 | tf_op jit(solution)/shard_map/while/body/eval_jaxpr/dot_general | solution.py:34
  123.5 0.7 dynamic_update_slice.32
  124.3 0.8 dynamic_update_slice.33
  125.0 0.8 dynamic_update_slice.34
  125.8 0.0 copy-start
  125.8 4.2 %bitcast_dynamic-update-slice_fusion.2 = bf16[2,512,2048]{2,1,0:T(8,128)(2,1)} fusion(bf16[2,512,2048]{2,1,0:T(8,128)(2,1)} %get-tuple-element.248, s32[]{:T(128)S(6)} %copy.20, f32[512,2048]{1,0:T(8,128)} %get-tuple-element.226, f32[]{:T(128)} %get-tuple-element.270), kind=kLoop, calls=%fused_computation.10.clone.1 | loop fusion | flops 2097152 | bytes 6291972 | tf_op jit(solution)/shard_map/while/body/jit(dynamic_update_index_in_dim)/dynamic_update_slice | solution.py:44
  130.0 0.0 copy-done
  130.0 6.6 %fusion.22 = f32[2,512,1152]{2,1,0:T(8,128)} fusion(f32[2,512,1152]{2,1,0:T(8,128)} %get-tuple-element.249, s32[]{:T(128)S(6)} %copy.20, bf16[2048,1152]{1,0:T(8,128)(2,1)} %get-tuple-element.274, f32[512,2048]{1,0:T(8,128)S(1)} %copy-done, f32[]{:T(128)} %get-tuple-element.270), kind=kOutput, calls=%fused_computation.9.clone.1 | convolution fusion | flops 2418016256 | bytes 11272708 | tf_op jit(solution)/shard_map/while/body/eval_jaxpr/dot_general | solution.py:41
  136.6 0.6 dynamic_slice.16
  137.8 12.7 %fusion.21 = (f32[]{:T(128)}, f32[]{:T(128)}, f32[]{:T(128)}, f32[512,2048]{1,0:T(8,128)}) fusion(f32[]{:T(128)} %get-tuple-element.270, f32[]{:T(128)} %get-tuple-element.275, s32[2048]{0:T(1024)S(1)} %iota_add_fusion.4, s32[512]{0:T(512)S(1)} %iota_add_fusion.5, bf16[2048,1152]{1,0:T(8,128)(2,1)} %get-tuple-element.274, ...), kind=kOutput, calls=%fused_computation.28.clone.1 | convolution fusion | flops 2437939200 | bytes 10103824 | tf_op jit(solution)/shard_map/while/body/eval_jaxpr/dot_general | solution.py:34
  150.5 0.7 dynamic_update_slice.32
  151.2 0.8 dynamic_update_slice.33
  152.0 0.8 dynamic_update_slice.34
  152.7 0.0 copy-start
  152.7 4.1 %bitcast_dynamic-update-slice_fusion.2 = bf16[2,512,2048]{2,1,0:T(8,128)(2,1)} fusion(bf16[2,512,2048]{2,1,0:T(8,128)(2,1)} %get-tuple-element.248, s32[]{:T(128)S(6)} %copy.20, f32[512,2048]{1,0:T(8,128)} %get-tuple-element.226, f32[]{:T(128)} %get-tuple-element.270), kind=kLoop, calls=%fused_computation.10.clone.1 | loop fusion | flops 2097152 | bytes 6291972 | tf_op jit(solution)/shard_map/while/body/jit(dynamic_update_index_in_dim)/dynamic_update_slice | solution.py:44
  156.9 0.0 copy-done
  156.9 6.7 %fusion.22 = f32[2,512,1152]{2,1,0:T(8,128)} fusion(f32[2,512,1152]{2,1,0:T(8,128)} %get-tuple-element.249, s32[]{:T(128)S(6)} %copy.20, bf16[2048,1152]{1,0:T(8,128)(2,1)} %get-tuple-element.274, f32[512,2048]{1,0:T(8,128)S(1)} %copy-done, f32[]{:T(128)} %get-tuple-element.270), kind=kOutput, calls=%fused_computation.9.clone.1 | convolution fusion | flops 2418016256 | bytes 11272708 | tf_op jit(solution)/shard_map/while/body/eval_jaxpr/dot_general | solution.py:41
  163.6 0.0 copy-start.4
  163.6 0.0 copy-start.3
  163.6 0.0 reduce-scatter.3.cloned.1.call-update
  163.6 0.2 reduce-scatter.5.cloned.1.call-start
  163.9 1.4 copy-done.3
  165.3 9.7 %fusion.10 = f32[2048,1152]{1,0:T(8,128)} fusion(bf16[1024,2048]{1,0:T(8,128)(2,1)} %bitcast.33, bf16[1024,1152]{1,0:T(8,128)(2,1)S(1)} %copy-done.3), kind=kOutput, calls=%fused_computation.29 | convolution fusion | flops 4831838208 | bytes 15990784 | tf_op jit(solution)/shard_map/dot_general | solution.py:53
  175.0 0.0 copy-done.4
  175.0 0.0 copy-start.5
  175.0 0.0 copy-start.1
  175.0 0.0 copy-start.2
  175.0 0.0 reduce-scatter.5.cloned.1.call-update
  175.0 0.6 reduce_sum.95
  175.6 0.0 copy-done.5
  175.6 0.6 reduce_sum.92
  176.2 0.6 reduce_sum.96
  176.8 75.2 %all-reduce = (f32[]{:T(128)}, f32[]{:T(128)}, f32[]{:T(128)}) all-reduce(f32[]{:T(128)} %reduce_sum.92, f32[]{:T(128)} %reduce_sum.95, f32[]{:T(128)} %reduce_sum.96), channel_id=1, replica_groups=mesh['img'=16,'txt'=8] {'img','txt'}, use_global_device_ids=true, to_apply=%region_8.9 | all-reduce | flops 3 | bytes 24 | tf_op jit(solution)/shard_map/psum | solution.py:49
  254.0 0.0 reduce-scatter.3.cloned.1.call-done
  254.1 0.0 copy-done.1
  254.1 1.3 multiply_reduce_fusion.2
  255.3 2.0 subtract_divide_fusion.1
  257.4 101.3 %reduce-scatter.5.cloned.1.call-done = f32[128,1152]{1,0:T(8,128)} async-done(((f32[2048,1152]{1,0:T(8,128)}), f32[128,1152]{1,0:T(8,128)}) %reduce-scatter.5.cloned.1.call-update) | async-done | bytes 589840 | tf_op jit(solution)/shard_map/reduce_scatter | solution.py:56
  358.7 0.0 copy-done.2
  358.7 1.3 multiply_reduce_fusion.1
  360.0 2.0 subtract_divide_fusion
  (12 shorter events, 0.0 us)
Async XLA Ops:
  7.2 63.1 %all-gather.3.cloned.1.call-start = ((), (), s32[]{:S(2)}) async-start(), calls=%async_computation.2 | async-start | bytes 2654208 | tf_op jit(solution)/shard_map/all_gather | solution.py:19
  10.3 99.3 %all-gather.5.cloned.1.call-start = ((), (), s32[]{:S(2)}) async-start(), calls=%async_computation.3 | async-start | bytes 5013504 | tf_op jit(solution)/shard_map/all_gather | solution.py:20
  13.5 240.6 %reduce-scatter.3.cloned.1.call-start = ((), (), s32[]{:S(2)}) async-start(), calls=%async_computation.4 | async-start | bytes 5308416 | tf_op jit(solution)/shard_map/reduce_scatter | solution.py:52
  125.8 4.2 %copy-start = (f32[512,2048]{1,0:T(8,128)S(1)}, f32[512,2048]{1,0:T(8,128)}, u32[]{:S(2)}) copy-start(f32[512,2048]{1,0:T(8,128)} %get-tuple-element.226) | copy-start | bytes 12582916 | tf_op jit(solution)/shard_map/while
  152.7 4.1 %copy-start = (f32[512,2048]{1,0:T(8,128)S(1)}, f32[512,2048]{1,0:T(8,128)}, u32[]{:S(2)}) copy-start(f32[512,2048]{1,0:T(8,128)} %get-tuple-element.226) | copy-start | bytes 12582916 | tf_op jit(solution)/shard_map/while
  163.6 11.4 %copy-start.4 = (f32[2]{0:T(128)}, f32[2]{0:T(128)S(1)}, u32[]{:S(2)}) copy-start(f32[2]{0:T(128)S(1)} %get-tuple-element.76) | copy-start | bytes 28
  163.6 1.7 copy-start.3
  163.6 195.1 %reduce-scatter.5.cloned.1.call-start = ((), (), s32[]{:S(2)}) async-start(), calls=%async_computation.5 | async-start | bytes 10027008 | tf_op jit(solution)/shard_map/reduce_scatter | solution.py:56
  175.0 0.7 copy-start.5
  175.0 79.1 %copy-start.1 = (f32[128,1152]{1,0:T(8,128)S(1)}, f32[128,1152]{1,0:T(8,128)}, u32[]{:S(2)}) copy-start(f32[128,1152]{1,0:T(8,128)} %param.6) | copy-start | bytes 1769476
  175.0 183.7 %copy-start.2 = (f32[128,1152]{1,0:T(8,128)S(1)}, f32[128,1152]{1,0:T(8,128)}, u32[]{:S(2)}) copy-start(f32[128,1152]{1,0:T(8,128)} %param.7) | copy-start | bytes 1769476
Sparse Core Ops, SparseCore 0:
  10.9 59.3 all-gather.2
  72.5 37.0 all-gather.4
  163.7 89.5 reduce-scatter.2
  255.7 102.9 reduce-scatter.4
where the time goes:
time: 376 us; the launch traced here: 372 us
  waiting for transfers between devices  197 us (52%)
  blocking collectives  75.2 us (20%)
  matrix products  48.4 us (13%)
  other arithmetic  22.9 us (6%)
  between operations  19.9 us (5%)
  local copies, waits for them, and re-layouts  7.11 us (2%)
    reduce_scatter x1, waiting for transfers between devices, local(): text_pull = lax.psum_scatter(terms, 'img', scatter_dimension=0, tiled=True)  101 us
    psum x1, blocking collectives, local(): lax.psum((jnp.sum(totals), jnp.sum(scale_parts), jnp.sum(bias_parts)), ('...  75.2 us
    all_gather x1, waiting for transfers between devices, local(): lax.all_gather(image_hat.astype(jnp.bfloat16), 'txt', axis=0, tiled=True)  56 us
    all_gather x1, waiting for transfers between devices, local(): lax.all_gather(text_hat.astype(jnp.bfloat16), 'img', axis=0, tiled=True)  39.4 us
    dot_general x2, matrix products, score(): similar = jnp.dot(rows, text_block.T, preferred_element_type=jnp.float32)  25.3 us
    dot_general x2, matrix products, score(): image_pull = jnp.dot(weight, text_block, preferred_element_type=jnp.float32)  13.3 us
    dot_general x1, matrix products, local(): lax.dot_general(weight_all, image_block, (((0,), (0,)), ((), ())), prefer...  9.72 us
    dynamic_update_slice x2, other arithmetic, local(): lax.map(score, jnp.arange(count, dtype=jnp.int32))  8.3 us
  transfers between devices with their start and end apart: 4, of which 3 were waited for; matrix products, arithmetic and copies ran while one was open for 5% of the time, Pallas kernels for 0%

commit v1 on v0

v1 whole, which is shorter than its diff:
```python
import jax
import jax.numpy as jnp
from jax import lax
from jax.experimental import pallas as pl
from jax.experimental.pallas import tpu as pltpu
from jax.sharding import PartitionSpec as P

BF = jnp.bfloat16
F32 = jnp.float32
LOG2E = 1.4426950408889634
ANY = pl.BlockSpec(memory_space=pl.ANY)
VM = pl.BlockSpec(memory_space=pltpu.VMEM)
SM = pl.BlockSpec(memory_space=pltpu.SMEM)
CHUNK = 512
STRIP = 64


def sds(shape, dtype):
    return jax.ShapeDtypeStruct(shape, dtype)


def params():
    return pltpu.CompilerParams(vmem_limit_bytes=56 * 1024 * 1024)


def encode(x):
    sq = x * x
    return (sq * sq * sq * x).astype(BF)


def decode(code):
    y = code.astype(F32)
    size = jnp.abs(y)
    root = jnp.exp2(jnp.log2(jnp.maximum(size, 1.2e-38)) * (1.0 / 7.0))
    root = jnp.where(size < 1.2e-38, 0.0, root)
    return jnp.where(y < 0, -root, root)


def normalize_kernel(a_ref, b_ref, a_out, b_out):
    for src, dst in ((a_ref, a_out), (b_ref, b_out)):
        x = src[...]
        norm = jnp.sqrt(jnp.sum(x * x, axis=1, keepdims=True) + 1e-06)
        dst[...] = (x / norm).astype(BF)


def normalize(a, b):
    return pl.pallas_call(
        normalize_kernel,
        out_shape=(sds(a.shape, BF), sds(b.shape, BF)),
        name="normalize",
    )(a, b)


def dot(a, b, dims):
    return lax.dot_general(a, b, (dims, ((), ())), preferred_element_type=F32)


def tile_kernel(ni, nt, rows, *refs):
    scal, diag = refs[0], refs[1]
    image_in, text_in = refs[2 : 2 + ni], refs[2 + ni : 2 + ni + nt]
    refs = refs[2 + ni + nt :]
    image_own, text_own = refs[0], refs[1]
    image_code, text_code, sums = refs[2], refs[3], refs[4]
    xs, ts, sim, wgt, pull, tp, isem, tsem, osem = refs[5:]
    m = ni * rows
    n = nt * rows
    copies_i = [
        pltpu.make_async_copy(r, xs.at[pl.ds(k * rows, rows)], isem.at[k]) for k, r in enumerate(image_in)
    ]
    copies_t = [
        pltpu.make_async_copy(r, ts.at[pl.ds(k * rows, rows)], tsem.at[k]) for k, r in enumerate(text_in)
    ]
    for c in copies_i + copies_t:
        c.start()
    for c in copies_i + copies_t:
        c.wait()
    scale = jnp.exp(jnp.full((1, 1), scal[0], F32))
    bias = scal[1]
    mult = scale * LOG2E
    shift = bias * LOG2E
    chunks = n // CHUNK
    half = chunks // 2
    per = CHUNK // rows
    sums[...] = jnp.zeros_like(sums)

    def step(c, carry):
        tc = ts[pl.ds(pl.multiple_of(c * CHUNK, CHUNK), CHUNK), :]
        sim[...] = dot(xs[...], tc, ((1,), (1,)))

        def strip(r, acc):
            loss, slope_sum, scale_sum = acc
            at = pl.ds(pl.multiple_of(r * STRIP, STRIP), STRIP)
            s = sim[at, :]
            e = jnp.exp2(s * mult + shift)
            u = e + 1.0
            r0 = pl.reciprocal(u, approx=True)
            sig = e * (r0 * (2.0 - u * r0))
            wgt[at, :] = (sig * scale).astype(BF)
            prod = u[0:8]
            for k in range(1, STRIP // 8):
                prod = prod * u[8 * k : 8 * k + 8]
            loss = loss + jnp.log(prod)
            ss = sig * s
            a, b = sig[0:8], ss[0:8]
            for k in range(1, STRIP // 8):
                a = a + sig[8 * k : 8 * k + 8]
                b = b + ss[8 * k : 8 * k + 8]
            return loss, slope_sum + a, scale_sum + b

        zero = jnp.zeros((8, CHUNK), F32)
        loss, slope_sum, scale_sum = lax.fori_loop(0, m // STRIP, strip, (zero, zero, zero))
        sums[0:8] += loss
        sums[8:16] += slope_sum
        sums[16:24] += scale_sum
        for b in range(ni):
            place = diag[b] - c * per

            @pl.when(jnp.logical_and(place >= 0, place < per))
            def _(b=b, place=place):
                at = (pl.ds(b * rows, rows), pl.ds(pl.multiple_of(place * rows, rows), rows))
                s = sim[at]
                eye = lax.broadcasted_iota(jnp.int32, s.shape, 0) == lax.broadcasted_iota(jnp.int32, s.shape, 1)
                z = scale * s + bias
                w = (-scale / (1.0 + jnp.exp(z))).astype(BF)
                wgt[at] = jnp.where(eye, w.astype(F32), wgt[at].astype(F32)).astype(BF)
                z = jnp.where(eye, z, 0.0)
                sd = jnp.where(eye, s, 0.0)
                one = jnp.where(eye, 1.0, 0.0)
                for row, v in ((0, z), (8, one), (16, sd)):
                    total = v[0:8]
                    for k in range(1, rows // 8):
                        total = total + v[8 * k : 8 * k + 8]
                    sums[row : row + 8, 0:rows] -= total

        tp[...] = dot(wgt[...], xs[...], ((0,), (0,)))

        @pl.when(c < half)
        def _():
            text_own[pl.ds(pl.multiple_of(c * CHUNK, CHUNK), CHUNK), :] = tp[...]

        @pl.when(c >= half)
        def _():
            text_code[pl.ds(pl.multiple_of((c - half) * CHUNK, CHUNK), CHUNK), :] = encode(tp[...])

        part = dot(wgt[...], tc, ((1,), (0,)))

        @pl.when(c == 0)
        def _():
            pull[...] = part

        @pl.when(c > 0)
        def _():
            pull[...] += part

        return carry

    lax.fori_loop(0, chunks, step, 0)
    copies = []
    for z in range(2):
        image_own[z * rows : (z + 1) * rows] = pull[4 * z * rows : (4 * z + 1) * rows]
        for k in range(1, 4):
            image_code[k - 1, z * rows : (z + 1) * rows] = encode(
                pull[(4 * z + k) * rows : (4 * z + k + 1) * rows]
            )


def tile(scal, diag, images, texts):
    rows, d = images[0].shape
    ni, nt = len(images), len(texts)
    m, n = ni * rows, nt * rows

    def body(*refs):
        k = 2 + ni + nt
        ins, rest = refs[:k], refs[k:]
        image_own, text_own, c1, c2, c3, text_code, sums = rest[:7]

        class Codes:
            def __setitem__(self, at, value):
                (c1, c2, c3)[at[0]][at[1], :] = value

        tile_kernel(ni, nt, rows, *ins, image_own, text_own, Codes(), text_code, sums, *rest[7:])

    return pl.pallas_call(
        body,
        in_specs=[SM, SM] + [ANY] * (ni + nt),
        out_specs=[VM] * 7,
        out_shape=(
            sds((2 * rows, d), F32),
            sds((n // 2, d), F32),
            sds((2 * rows, d), BF),
            sds((2 * rows, d), BF),
            sds((2 * rows, d), BF),
            sds((n // 2, d), BF),
            sds((24, CHUNK), F32),
        ),
        scratch_shapes=[
            pltpu.VMEM((m, d), BF),
            pltpu.VMEM((n, d), BF),
            pltpu.VMEM((m, CHUNK), F32),
            pltpu.VMEM((m, CHUNK), BF),
            pltpu.VMEM((m, d), F32),
            pltpu.VMEM((CHUNK, d), F32),
            pltpu.SemaphoreType.DMA((ni,)),
            pltpu.SemaphoreType.DMA((nt,)),
            pltpu.SemaphoreType.DMA((4,)),
        ],
        compiler_params=params(),
        cost_estimate=pl.CostEstimate(
            flops=6 * m * n * d, bytes_accessed=(m + n) * d * 8, transcendentals=3 * m * n
        ),
        name="tile",
    )(scal, diag, *images, *texts)


def fold_core_kernel(own_ref, code_ref, own_out, c1, c2, c3):
    rows = own_out.shape[0] // 2
    for z in range(2):
        for k in range(4):
            at = pl.ds((4 * z + k) * rows, rows)
            total = own_ref[at, :] + decode(code_ref[at, :])
            to = pl.ds(z * rows, rows)
            if k == 0:
                own_out[to, :] = total
            else:
                (c1, c2, c3)[k - 1][to, :] = encode(total)


def fold_core(own, code):
    rows, d = own.shape[0] // 4, own.shape[1]
    return pl.pallas_call(
        fold_core_kernel,
        out_shape=(sds((rows, d), F32),) + (sds((rows, d), BF),) * 3,
        compiler_params=params(),
        name="fold_core",
    )(own, code)


def fold_ring_kernel(own_ref, c1, c2, c3, own_out, code_out):
    rows = own_out.shape[0]
    for z in range(2):
        at = pl.ds(z * rows, rows)
        total = own_ref[at, :]
        for c in (c1, c2, c3):
            total = total + decode(c[at, :])
        if z == 0:
            own_out[...] = total
        else:
            code_out[...] = encode(total)


def fold_ring(own, codes):
    rows, d = own.shape[0] // 2, own.shape[1]
    return pl.pallas_call(
        fold_ring_kernel,
        out_shape=(sds((rows, d), F32), sds((rows, d), BF)),
        compiler_params=params(),
        name="fold_ring",
    )(own, *codes)


def finish_kernel(x_ref, own_ref, code_ref, out_ref):
    x = x_ref[...]
    norm = jnp.sqrt(jnp.sum(x * x, axis=1, keepdims=True) + 1e-06)
    hat = x / norm
    pull = own_ref[...] + decode(code_ref[...])
    out_ref[...] = (pull - hat * jnp.sum(hat * pull, axis=1, keepdims=True)) / norm


def finish(x, own, code):
    return pl.pallas_call(
        finish_kernel, out_shape=sds(x.shape, F32), compiler_params=params(), name="finish"
    )(x, own, code)


def img_index(y, z, c):
    return (y % 4) * 4 + (z % 2) * 2 + c % 2


def perm_x(shift):
    return [(i, ((i // 2 + shift) % 4) * 2 + i % 2) for i in range(8)]


def perm_y(shift):
    return [(i, img_index(i // 4 + shift, i // 2, i)) for i in range(16)]


PERM_ZHI = [(i, i ^ 1) for i in range(8)]
PERM_ZLO = [(i, i ^ 2) for i in range(16)]
PERM_CORE = [(i, i ^ 1) for i in range(16)]


def local(image_embed, text_embed, log_scale, logit_bias):
    image_low, text_low = normalize(image_embed, text_embed)
    send = lax.ppermute
    image_z = send(image_low, "txt", PERM_ZHI)
    text_z = send(text_low, "img", PERM_ZLO)
    images = [image_low] + [send(image_low, "txt", perm_x(k)) for k in (1, 2, 3)]
    texts = [text_low] + [send(text_low, "img", perm_y(k)) for k in (1, 2, 3)]
    images += [image_z] + [send(image_z, "txt", perm_x(k)) for k in (1, 2, 3)]
    texts += [text_z] + [send(text_z, "img", perm_y(k)) for k in (1, 2, 3)]
    texts += [send(t, "img", PERM_CORE) for t in texts]

    i, t = lax.axis_index("img"), lax.axis_index("txt")
    b = jnp.arange(8, dtype=jnp.int32)
    g = 8 * i + (((t // 2 - b % 4) % 4) * 2 + ((t % 2) ^ (b // 4)))
    o = g % 16
    place = ((i % 2) ^ (o % 2)) * 8 + (((i // 2) % 2) ^ ((o // 2) % 2)) * 4 + (i // 4 - o // 4) % 4
    diag = jnp.where(g // 16 == t, place, -1).astype(jnp.int32)
    scal = jnp.stack([log_scale, logit_bias])

    image_own, text_own, i1, i2, i3, text_code, sums = tile(scal, diag, images, texts)

    text_code = send(text_code, "img", PERM_CORE)
    codes = [send(c, "txt", perm_x(-k)) for k, c in ((1, i1), (2, i2), (3, i3))]
    text_own, t1, t2, t3 = fold_core(text_own, text_code)
    tcodes = [send(c, "img", perm_y(-k)) for k, c in ((1, t1), (2, t2), (3, t3))]

    v = jnp.sum(sums.reshape(3, 8, -1), axis=(1, 2))
    v = jnp.broadcast_to(v[:, None], (3, 128))
    v = (v + send(v, "txt", perm_x(2))) + (send(v, "txt", perm_x(1)) + send(v, "txt", perm_x(3)))
    v = (v + send(v, "img", perm_y(2))) + (send(v, "img", perm_y(1)) + send(v, "img", perm_y(3)))
    v = v + send(v, "txt", PERM_ZHI)
    v = v + send(v, "img", PERM_ZLO)
    v = v + send(v, "img", PERM_CORE)

    image_own, image_code = fold_ring(image_own, codes)
    image_code = send(image_code, "txt", PERM_ZHI)
    text_own, text_code = fold_ring(text_own, tcodes)
    text_code = send(text_code, "img", PERM_ZLO)
    image_grad = finish(image_embed, image_own, image_code)
    text_grad = finish(text_embed, text_own, text_code)
    pairs = F32(16384.0 * 16384.0)
    scale = jnp.exp(log_scale)
    return (v[0, 0] / pairs, image_grad, text_grad, v[2, 0] * scale / pairs, v[1, 0] / pairs)


def solution(mesh):
    placed = (P(("img", "txt"), None), P(("txt", "img"), None), P(), P())
    return jax.shard_map(
        local,
        mesh=mesh,
        in_specs=placed,
        out_specs=(P(), P(("img", "txt"), None), P(("txt", "img"), None), P(), P()),
        check_vma=False,
    )
```

time: 376 us -> 191 us (0.51)
  waiting for transfers between devices: 197 us -> 57.4 us
  blocking collectives: 75.2 us -> 0 us
  Pallas kernels: 0 us -> 58.5 us
  starting transfers between devices: 0.35 us -> 58.5 us
  matrix products: 48.4 us -> 0 us
  other arithmetic: 22.9 us -> 2.26 us
  between operations: 19.9 us -> 7.62 us
  local copies, waits for them, and re-layouts: 7.11 us -> 3 us
    reduce_scatter x2 -> x0, waiting for transfers between devices: 101 us -> none  [the longest x1 101 us: local(): text_pull = lax.psum_scatter(terms, 'img', scatter_dimension=0, tiled=True)]
    all_gather x2 -> x0, waiting for transfers between devices: 95.3 us -> none  [the longest x1 56 us: local(): lax.all_gather(image_hat.astype(jnp.bfloat16), 'txt', axis=0, tiled=True)]
    psum x1 -> x0, blocking collectives: 75.2 us -> none  [local(): lax.psum((jnp.sum(totals), jnp.sum(scale_parts), jnp.sum(bias_parts)), ('...]
    ppermute x0 -> x40, starting transfers between devices: none -> 58.5 us  [the longest x1 18.7 us: local(): image_code = send(image_code, 'txt', PERM_ZHI)]
    pallas_call x0 -> x7, Pallas kernels: none -> 58.5 us  [the longest x1 36.7 us: tile(): pl.pallas_call(body, in_specs=[SM, SM] + [ANY] * (ni + nt), out_specs=[VM...]
    ppermute x0 -> x40, waiting for transfers between devices: none -> 57.4 us  [the longest x1 11.5 us: local(): send(v, 'txt', perm_x(3))]
    dot_general x5 -> x0, matrix products: 48.4 us -> none  [the longest x2 25.3 us: score(): similar = jnp.dot(rows, text_block.T, preferred_element_type=jnp.float32)]
    dynamic_update_slice x2 -> x0, other arithmetic: 8.3 us -> none  [local(): lax.map(score, jnp.arange(count, dtype=jnp.int32))]
  transfers between devices with their start and end apart: 4 -> 40, of which waited for: 3 -> 15; matrix products, arithmetic and copies ran while one was open for 5% -> 2% of each run, Pallas kernels for 0% -> 9%
where the time goes in v1:
time: 191 us; the launch traced here: 187 us
  Pallas kernels  58.5 us (31%)
  starting transfers between devices  58.5 us (31%)
  waiting for transfers between devices  57.4 us (30%)
  between operations  7.62 us (4%)
  local copies, waits for them, and re-layouts  3 us (2%)
  other arithmetic  2.26 us (1%)
    pallas_call x1, Pallas kernels, tile(): pl.pallas_call(body, in_specs=[SM, SM] + [ANY] * (ni + nt), out_specs=[VM...  36.7 us
    ppermute x1, starting transfers between devices, local(): image_code = send(image_code, 'txt', PERM_ZHI)  18.7 us
    ppermute x1, waiting for transfers between devices, local(): send(v, 'txt', perm_x(3))  11.5 us
    ppermute x3, waiting for transfers between devices, local(): texts += [text_z] + [send(text_z, 'img', perm_y(k)) for k in (1, 2, 3)]  11.2 us
    ppermute x3, waiting for transfers between devices, local(): texts = [text_low] + [send(text_low, 'img', perm_y(k)) for k in (1, 2, 3)]  8.93 us
    pallas_call x2, Pallas kernels, fold_ring(): pl.pallas_call(fold_ring_kernel, out_shape=(sds((rows, d), F32), sds((row...  8.11 us
    ppermute x1, waiting for transfers between devices, local(): v = v + send(v, 'txt', PERM_ZHI)  7.09 us
    ppermute x3, waiting for transfers between devices, local(): send(image_low, 'txt', perm_x(k))  6.91 us
  transfers between devices with their start and end apart: 40, of which 15 were waited for; matrix products, arithmetic and copies ran while one was open for 2% of the time, Pallas kernels for 9%

profile of v1, /device:TPU:0, one launch (start us, length us, event | category | flops | bytes accessed | tf_op | source)
XLA Modules:
  0.0 187.3 jit_solution(4187429637260800321)
XLA Ops:
  0.6 2.2 %normalize.1 = (bf16[128,1152]{1,0:T(8,128)(2,1)}, bf16[128,1152]{1,0:T(8,128)(2,1)}) custom-call(f32[128,1152]{1,0:T(8,128)} %x_ref.2, f32[128,1152]{1,0:T(8,128)} %x_ref.3), custom_call_target="tpu_custom_call" | custom-call | tf_op jit(solution)/shard_map/normalize/pallas_call | solution.py:47
  2.8 4.0 %collective-permute-start.3 = (bf16[128,1152]{1,0:T(8,128)(2,1)}, bf16[128,1152]{1,0:T(8,128)(2,1)S(1)}, u32[]{:S(2)}, u32[]{:S(2)}) collective-permute-start(bf16[128,1152]{1,0:T(8,128)(2,1)} %get-tuple-element.22.refs_2_), channel_id=1, source_target_pairs={{0,1},{1,0},{2,3},{3,2},{4,5},{5,4},{6,7},{7,6},{8,9},{9,8},{10,11... | collective-permute-start | bytes 884744 | tf_op jit(solution)/shard_map/ppermute | solution.py:295
  6.8 2.8 %collective-permute-start.2 = (bf16[128,1152]{1,0:T(8,128)(2,1)}, bf16[128,1152]{1,0:T(8,128)(2,1)S(1)}, u32[]{:S(2)}, u32[]{:S(2)}) collective-permute-start(bf16[128,1152]{1,0:T(8,128)(2,1)} %get-tuple-element.22.refs_2_), channel_id=1, source_target_pairs={{0,6},{1,7},{2,0},{3,1},{4,2},{5,3},{6,4},{7,5},{8,14},{9,15},{10,... | collective-permute-start | bytes 884744 | tf_op jit(solution)/shard_map/ppermute | solution.py:297
  9.6 0.8 collective-permute-start.1
  10.4 0.9 collective-permute-start
  11.2 0.0 collective-permute-start.14
  11.3 2.8 %collective-permute-done.3.refs_6_ = bf16[128,1152]{1,0:T(8,128)(2,1)S(1)} collective-permute-done((bf16[128,1152]{1,0:T(8,128)(2,1)}, bf16[128,1152]{1,0:T(8,128)(2,1)S(1)}, u32[]{:S(2)}, u32[]{:S(2)}) %collective-permute-start.3) | collective-permute-done | bytes 294944 | tf_op jit(solution)/shard_map/ppermute | solution.py:295
  14.0 1.3 collective-permute-start.10
  15.3 6.9 %collective-permute-done.2.refs_5_ = bf16[128,1152]{1,0:T(8,128)(2,1)S(1)} collective-permute-done((bf16[128,1152]{1,0:T(8,128)(2,1)}, bf16[128,1152]{1,0:T(8,128)(2,1)S(1)}, u32[]{:S(2)}, u32[]{:S(2)}) %collective-permute-start.2) | collective-permute-done | bytes 294944 | tf_op jit(solution)/shard_map/ppermute | solution.py:297
  22.2 3.0 %collective-permute-start.9 = (bf16[128,1152]{1,0:T(8,128)(2,1)}, bf16[128,1152]{1,0:T(8,128)(2,1)S(1)}, u32[]{:S(2)}, u32[]{:S(2)}) collective-permute-start(bf16[128,1152]{1,0:T(8,128)(2,1)} %get-tuple-element.23.refs_10_), channel_id=1, source_target_pairs={{0,96},{8,104},{16,112},{24,120},{32,0},{40,8},{48,16},{56,24},{64... | collective-permute-start | bytes 884744 | tf_op jit(solution)/shard_map/ppermute | solution.py:298
  25.2 0.6 collective-permute-start.8
  25.9 0.0 collective-permute-done.refs_3_
  25.9 1.5 collective-permute-start.7
  27.4 3.0 %collective-permute-start.6 = (bf16[128,1152]{1,0:T(8,128)(2,1)S(1)}, bf16[128,1152]{1,0:T(8,128)(2,1)S(1)}, u32[]{:S(2)}, u32[]{:S(2)}) collective-permute-start(bf16[128,1152]{1,0:T(8,128)(2,1)S(1)} %collective-permute-done.3.refs_6_), channel_id=1, source_target_pairs={{0,6},{1,7},{2,0},{3,1},{4,2},{5,3},{6,4},{7,5},{8,14},{9,15},{10,... | collective-permute-start | bytes 884744 | tf_op jit(solution)/shard_map/ppermute | solution.py:299
  30.4 2.5 %collective-permute-done.9.refs_13_ = bf16[128,1152]{1,0:T(8,128)(2,1)S(1)} collective-permute-done((bf16[128,1152]{1,0:T(8,128)(2,1)}, bf16[128,1152]{1,0:T(8,128)(2,1)S(1)}, u32[]{:S(2)}, u32[]{:S(2)}) %collective-permute-start.9) | collective-permute-done | bytes 294944 | tf_op jit(solution)/shard_map/ppermute | solution.py:298
  33.0 3.4 %collective-permute-done.8.refs_12_ = bf16[128,1152]{1,0:T(8,128)(2,1)S(1)} collective-permute-done((bf16[128,1152]{1,0:T(8,128)(2,1)}, bf16[128,1152]{1,0:T(8,128)(2,1)S(1)}, u32[]{:S(2)}, u32[]{:S(2)}) %collective-permute-start.8) | collective-permute-done | bytes 294944 | tf_op jit(solution)/shard_map/ppermute | solution.py:298
  36.4 3.0 %collective-permute-done.7.refs_11_ = bf16[128,1152]{1,0:T(8,128)(2,1)S(1)} collective-permute-done((bf16[128,1152]{1,0:T(8,128)(2,1)}, bf16[128,1152]{1,0:T(8,128)(2,1)S(1)}, u32[]{:S(2)}, u32[]{:S(2)}) %collective-permute-start.7) | collective-permute-done | bytes 294944 | tf_op jit(solution)/shard_map/ppermute | solution.py:298
  39.4 1.2 collective-permute-start.13
  40.6 0.6 collective-permute-start.12
  41.2 1.3 collective-permute-start.11
  42.5 1.4 collective-permute-done.4.refs_7_
  44.0 0.5 collective-permute-start.16
  44.5 4.9 %collective-permute-done.13.refs_17_ = bf16[128,1152]{1,0:T(8,128)(2,1)} collective-permute-done((bf16[128,1152]{1,0:T(8,128)(2,1)S(1)}, bf16[128,1152]{1,0:T(8,128)(2,1)}, u32[]{:S(2)}, u32[]{:S(2)}) %collective-permute-start.13) | collective-permute-done | bytes 294944 | tf_op jit(solution)/shard_map/ppermute | solution.py:300
  49.4 2.7 %collective-permute-done.12.refs_16_ = bf16[128,1152]{1,0:T(8,128)(2,1)} collective-permute-done((bf16[128,1152]{1,0:T(8,128)(2,1)S(1)}, bf16[128,1152]{1,0:T(8,128)(2,1)}, u32[]{:S(2)}, u32[]{:S(2)}) %collective-permute-start.12) | collective-permute-done | bytes 294944 | tf_op jit(solution)/shard_map/ppermute | solution.py:300
  52.2 3.5 %collective-permute-done.11.refs_15_ = bf16[128,1152]{1,0:T(8,128)(2,1)} collective-permute-done((bf16[128,1152]{1,0:T(8,128)(2,1)S(1)}, bf16[128,1152]{1,0:T(8,128)(2,1)}, u32[]{:S(2)}, u32[]{:S(2)}) %collective-permute-start.11) | collective-permute-done | bytes 294944 | tf_op jit(solution)/shard_map/ppermute | solution.py:300
  55.7 0.0 collective-permute-start.20
  55.7 0.7 collective-permute-start.19
  57.8 0.6 pad_maximum_fusion.refs_0_
  58.4 0.6 compare_select_fusion.6.refs_1_
  59.1 36.7 %tile.1 = (f32[256,1152]{1,0:T(8,128)}, f32[1024,1152]{1,0:T(8,128)}, bf16[256,1152]{1,0:T(8,128)(2,1)}, bf16[256,1152]{1,0:T(8,128)(2,1)}, bf16[256,1152]{1,0:T...) custom-call(f32[2]{0:T(128)} %pad_maximum_fusion.refs_0_, s32[8]{0:T(128)} %compare_select_fusion.6.refs_1_, ...), custom_call_target="tpu_custom_call" | custom-call | flops 14495514624 | bytes 28311552 | tf_op jit(solution)/shard_map/tile/pallas_call | solution.py:183
  95.7 0.5 collective-permute-start.35
  96.3 1.9 collective-permute-start.31
  98.1 0.9 reduce_sum.10
  99.1 0.1 reduce_sum.14
  99.1 0.1 reduce_sum.18
  99.3 0.1 broadcast_in_dim.4
  99.3 0.2 collective-permute-start.23
  99.5 3.1 %collective-permute-start.24 = (f32[3,128]{1,0:T(4,128)S(1)}, f32[3,128]{1,0:T(4,128)S(1)}, u32[]{:S(2)}, u32[]{:S(2)}) collective-permute-start(f32[3,128]{1,0:T(4,128)S(1)} %broadcast_in_dim.4), channel_id=1, source_target_pairs={{0,6},{1,7},{2,0},{3,1},{4,2},{5,3},{6,4},{7,5},{8,14},{9,15},{10,... | collective-permute-start | bytes 4616 | tf_op jit(solution)/shard_map/ppermute | solution.py:320
  102.6 3.5 %collective-permute-start.32 = (bf16[256,1152]{1,0:T(8,128)(2,1)}, bf16[256,1152]{1,0:T(8,128)(2,1)S(1)}, u32[]{:S(2)}, u32[]{:S(2)}) collective-permute-start(bf16[256,1152]{1,0:T(8,128)(2,1)} %get-tuple-element.27), channel_id=1, source_target_pairs={{0,4},{1,5},{2,6},{3,7},{4,0},{5,1},{6,2},{7,3},{8,12},{9,13},{10,... | collective-permute-start | bytes 1769480 | tf_op jit(solution)/shard_map/ppermute | solution.py:314
  106.1 6.3 %fold_core.1 = (f32[256,1152]{1,0:T(8,128)}, bf16[256,1152]{1,0:T(8,128)(2,1)}, bf16[256,1152]{1,0:T(8,128)(2,1)}, bf16[256,1152]{1,0:T(8,128)(2,1)}) custom-call(f32[1024,1152]{1,0:T(8,128)} %get-tuple-element.31.own_ref, bf16[1024,1152]{1,0:T(8,128)(2,1)} %copy-done), custom_call_target="tpu_custom_call" | custom-call | tf_op jit(solution)/shard_map/fold_core/pallas_call | solution.py:230
  112.4 0.1 collective-permute-start.33
  112.5 11.5 %collective-permute-done.24 = f32[3,128]{1,0:T(4,128)S(1)} collective-permute-done((f32[3,128]{1,0:T(4,128)S(1)}, f32[3,128]{1,0:T(4,128)S(1)}, u32[]{:S(2)}, u32[]{:S(2)}) %collective-permute-start.24) | collective-permute-done | bytes 1568 | tf_op jit(solution)/shard_map/ppermute | solution.py:320
  124.1 0.0 copy-start.1
  124.1 2.1 %collective-permute-start.38 = (bf16[256,1152]{1,0:T(8,128)(2,1)}, bf16[256,1152]{1,0:T(8,128)(2,1)S(1)}, u32[]{:S(2)}, u32[]{:S(2)}) collective-permute-start(bf16[256,1152]{1,0:T(8,128)(2,1)} %get-tuple-element.36), channel_id=1, source_target_pairs={{0,32},{8,40},{16,48},{24,56},{32,64},{40,72},{48,80},{56,88},{64,... | collective-permute-start | bytes 1769480 | tf_op jit(solution)/shard_map/ppermute | solution.py:316
  126.1 0.1 add_add_fusion.1
  126.2 2.8 %collective-permute-start.27 = (f32[3,128]{1,0:T(4,128)S(1)}, f32[3,128]{1,0:T(4,128)S(1)}, u32[]{:S(2)}, u32[]{:S(2)}) collective-permute-start(f32[3,128]{1,0:T(4,128)S(1)} %add_add_fusion.1), channel_id=1, source_target_pairs={{0,96},{8,104},{16,112},{24,120},{32,0},{40,8},{48,16},{56,24},{64... | collective-permute-start | bytes 4616 | tf_op jit(solution)/shard_map/ppermute | solution.py:321
  129.1 2.4 %collective-permute-done.33.c3 = bf16[256,1152]{1,0:T(8,128)(2,1)S(1)} collective-permute-done((bf16[256,1152]{1,0:T(8,128)(2,1)S(1)}, bf16[256,1152]{1,0:T(8,128)(2,1)S(1)}, u32[]{:S(2)}, u32[]{:S(2)}) %collective-permute-start.33) | collective-permute-done | bytes 589856 | tf_op jit(solution)/shard_map/ppermute | solution.py:314
  131.5 1.1 collective-permute-start.26
  132.6 1.5 collective-permute-done.36.c1
  134.2 4.2 %fold_ring.2 = (f32[128,1152]{1,0:T(8,128)}, bf16[128,1152]{1,0:T(8,128)(2,1)}) custom-call(f32[256,1152]{1,0:T(8,128)} %get-tuple-element.25.own_ref, bf16[256,1152]{1,0:T(8,128)(2,1)} %copy-done.1, bf16[256,1152]{1,0:T(8,128)(2,1)} %copy-done.2, bf16[256,1152]{1,0:T(8,128)(2,1)} %copy-done.5), custom_call_target="tpu_custom_call" | custom-call | tf_op jit(solution)/shard_map/fold_ring/pallas_call | solution.py:253
  138.3 18.7 %collective-permute-start.34 = (bf16[128,1152]{1,0:T(8,128)(2,1)}, bf16[128,1152]{1,0:T(8,128)(2,1)S(1)}, u32[]{:S(2)}, u32[]{:S(2)}) collective-permute-start(bf16[128,1152]{1,0:T(8,128)(2,1)} %get-tuple-element.30), channel_id=1, source_target_pairs={{0,1},{1,0},{2,3},{3,2},{4,5},{5,4},{6,7},{7,6},{8,9},{9,8},{10,11... | collective-permute-start | bytes 884744 | tf_op jit(solution)/shard_map/ppermute | solution.py:327
  157.1 0.8 copy-done.6
  157.9 4.0 %fold_ring.3 = (f32[128,1152]{1,0:T(8,128)}, bf16[128,1152]{1,0:T(8,128)(2,1)}) custom-call(f32[256,1152]{1,0:T(8,128)} %get-tuple-element.33.own_ref, bf16[256,1152]{1,0:T(8,128)(2,1)} %copy-done.3, bf16[256,1152]{1,0:T(8,128)(2,1)} %copy-done.4, bf16[256,1152]{1,0:T(8,128)(2,1)} %copy-done.6), custom_call_target="tpu_custom_call" | custom-call | tf_op jit(solution)/shard_map/fold_ring/pallas_call | solution.py:253
  161.9 1.1 collective-permute-start.28
  163.0 7.1 %collective-permute-done.28 = f32[3,128]{1,0:T(4,128)S(1)} collective-permute-done((f32[3,128]{1,0:T(4,128)S(1)}, f32[3,128]{1,0:T(4,128)S(1)}, u32[]{:S(2)}, u32[]{:S(2)}) %collective-permute-start.28) | collective-permute-done | bytes 1568 | tf_op jit(solution)/shard_map/ppermute | solution.py:322
  170.1 1.2 collective-permute-start.29
  171.2 2.4 %collective-permute-done.29 = f32[3,128]{1,0:T(4,128)S(1)} collective-permute-done((f32[3,128]{1,0:T(4,128)S(1)}, f32[3,128]{1,0:T(4,128)S(1)}, u32[]{:S(2)}, u32[]{:S(2)}) %collective-permute-start.29) | collective-permute-done | bytes 1568 | tf_op jit(solution)/shard_map/ppermute | solution.py:323
  173.7 1.1 collective-permute-done.30
  174.8 0.5 fusion.14
  177.3 0.0 copy-start.7
  177.3 0.7 copy-done.7
  178.0 2.6 %finish.2 = f32[128,1152]{1,0:T(8,128)} custom-call(f32[128,1152]{1,0:T(8,128)} %x_ref.2, f32[128,1152]{1,0:T(8,128)} %get-tuple-element.29.own_ref, bf16[128,1152]{1,0:T(8,128)(2,1)} %copy-done.7), custom_call_target="tpu_custom_call" | custom-call | tf_op jit(solution)/shard_map/finish/pallas_call | solution.py:270
  180.6 0.7 copy-done.8
  181.3 2.6 %finish.3 = f32[128,1152]{1,0:T(8,128)} custom-call(f32[128,1152]{1,0:T(8,128)} %x_ref.3, f32[128,1152]{1,0:T(8,128)} %get-tuple-element.37.own_ref, bf16[128,1152]{1,0:T(8,128)(2,1)} %copy-done.8), custom_call_target="tpu_custom_call" | custom-call | tf_op jit(solution)/shard_map/finish/pallas_call | solution.py:270
  (83 shorter events, 0.2 us)
Async XLA Ops:
  2.8 11.2 %collective-permute-start.3 = (bf16[128,1152]{1,0:T(8,128)(2,1)}, bf16[128,1152]{1,0:T(8,128)(2,1)S(1)}, u32[]{:S(2)}, u32[]{:S(2)}) collective-permute-start(bf16[128,1152]{1,0:T(8,128)(2,1)} %get-tuple-element.22.refs_2_), channel_id=1, source_target_pairs={{0,1},{1,0},{2,3},{3,2},{4,5},{5,4},{6,7},{7,6},{8,9},{9,8},{10,11... | collective-permute-start | bytes 884744 | tf_op jit(solution)/shard_map/ppermute | solution.py:295
  6.8 15.4 %collective-permute-start.2 = (bf16[128,1152]{1,0:T(8,128)(2,1)}, bf16[128,1152]{1,0:T(8,128)(2,1)S(1)}, u32[]{:S(2)}, u32[]{:S(2)}) collective-permute-start(bf16[128,1152]{1,0:T(8,128)(2,1)} %get-tuple-element.22.refs_2_), channel_id=1, source_target_pairs={{0,6},{1,7},{2,0},{3,1},{4,2},{5,3},{6,4},{7,5},{8,14},{9,15},{10,... | collective-permute-start | bytes 884744 | tf_op jit(solution)/shard_map/ppermute | solution.py:297
  9.6 15.7 %collective-permute-start.1 = (bf16[128,1152]{1,0:T(8,128)(2,1)}, bf16[128,1152]{1,0:T(8,128)(2,1)S(1)}, u32[]{:S(2)}, u32[]{:S(2)}) collective-permute-start(bf16[128,1152]{1,0:T(8,128)(2,1)} %get-tuple-element.22.refs_2_), channel_id=1, source_target_pairs={{0,4},{1,5},{2,6},{3,7},{4,0},{5,1},{6,2},{7,3},{8,12},{9,13},{10,... | collective-permute-start | bytes 884744 | tf_op jit(solution)/shard_map/ppermute | solution.py:297
  10.4 15.5 %collective-permute-start = (bf16[128,1152]{1,0:T(8,128)(2,1)}, bf16[128,1152]{1,0:T(8,128)(2,1)S(1)}, u32[]{:S(2)}, u32[]{:S(2)}) collective-permute-start(bf16[128,1152]{1,0:T(8,128)(2,1)} %get-tuple-element.22.refs_2_), channel_id=1, source_target_pairs={{0,2},{1,3},{2,4},{3,5},{4,6},{5,7},{6,0},{7,1},{8,10},{9,11},{10,... | collective-permute-start | bytes 884744 | tf_op jit(solution)/shard_map/ppermute | solution.py:297
  11.2 16.1 %collective-permute-start.14 = (bf16[128,1152]{1,0:T(8,128)(2,1)}, bf16[128,1152]{1,0:T(8,128)(2,1)S(1)}, u32[]{:S(2)}, u32[]{:S(2)}) collective-permute-start(bf16[128,1152]{1,0:T(8,128)(2,1)} %get-tuple-element.23.refs_10_), channel_id=1, source_target_pairs={{0,8},{8,0},{16,24},{24,16},{32,40},{40,32},{48,56},{56,48},{64,72... | collective-permute-start | bytes 884744 | tf_op jit(solution)/shard_map/ppermute | solution.py:301
  14.0 44.9 %copy-start.10 = (bf16[128,1152]{1,0:T(8,128)(2,1)}, bf16[128,1152]{1,0:T(8,128)(2,1)S(1)}, u32[]{:S(2)}) copy-start(bf16[128,1152]{1,0:T(8,128)(2,1)S(1)} %collective-permute-done.3.refs_6_) | copy-start | bytes 884740
  14.0 16.4 %collective-permute-start.10 = (bf16[128,1152]{1,0:T(8,128)(2,1)}, bf16[128,1152]{1,0:T(8,128)(2,1)S(1)}, u32[]{:S(2)}, u32[]{:S(2)}) collective-permute-start(bf16[128,1152]{1,0:T(8,128)(2,1)} %get-tuple-element.23.refs_10_), channel_id=1, source_target_pairs={{0,16},{8,24},{16,0},{24,8},{32,48},{40,56},{48,32},{56,40},{64,80... | collective-permute-start | bytes 884744 | tf_op jit(solution)/shard_map/ppermute | solution.py:296
  22.2 36.7 %copy-start.11 = (bf16[128,1152]{1,0:T(8,128)(2,1)}, bf16[128,1152]{1,0:T(8,128)(2,1)S(1)}, u32[]{:S(2)}) copy-start(bf16[128,1152]{1,0:T(8,128)(2,1)S(1)} %collective-permute-done.2.refs_5_) | copy-start | bytes 884740
  22.2 10.7 %collective-permute-start.9 = (bf16[128,1152]{1,0:T(8,128)(2,1)}, bf16[128,1152]{1,0:T(8,128)(2,1)S(1)}, u32[]{:S(2)}, u32[]{:S(2)}) collective-permute-start(bf16[128,1152]{1,0:T(8,128)(2,1)} %get-tuple-element.23.refs_10_), channel_id=1, source_target_pairs={{0,96},{8,104},{16,112},{24,120},{32,0},{40,8},{48,16},{56,24},{64... | collective-permute-start | bytes 884744 | tf_op jit(solution)/shard_map/ppermute | solution.py:298
  25.2 33.7 %copy-start.12 = (bf16[128,1152]{1,0:T(8,128)(2,1)}, bf16[128,1152]{1,0:T(8,128)(2,1)S(1)}, u32[]{:S(2)}) copy-start(bf16[128,1152]{1,0:T(8,128)(2,1)S(1)} %collective-permute-done.1.refs_4_) | copy-start | bytes 884740
  25.2 11.1 %collective-permute-start.8 = (bf16[128,1152]{1,0:T(8,128)(2,1)}, bf16[128,1152]{1,0:T(8,128)(2,1)S(1)}, u32[]{:S(2)}, u32[]{:S(2)}) collective-permute-start(bf16[128,1152]{1,0:T(8,128)(2,1)} %get-tuple-element.23.refs_10_), channel_id=1, source_target_pairs={{0,64},{8,72},{16,80},{24,88},{32,96},{40,104},{48,112},{56,120},{... | collective-permute-start | bytes 884744 | tf_op jit(solution)/shard_map/ppermute | solution.py:298
  25.9 33.1 %copy-start.13 = (bf16[128,1152]{1,0:T(8,128)(2,1)}, bf16[128,1152]{1,0:T(8,128)(2,1)S(1)}, u32[]{:S(2)}) copy-start(bf16[128,1152]{1,0:T(8,128)(2,1)S(1)} %collective-permute-done.refs_3_) | copy-start | bytes 884740
  25.9 13.5 %collective-permute-start.7 = (bf16[128,1152]{1,0:T(8,128)(2,1)}, bf16[128,1152]{1,0:T(8,128)(2,1)S(1)}, u32[]{:S(2)}, u32[]{:S(2)}) collective-permute-start(bf16[128,1152]{1,0:T(8,128)(2,1)} %get-tuple-element.23.refs_10_), channel_id=1, source_target_pairs={{0,32},{8,40},{16,48},{24,56},{32,64},{40,72},{48,80},{56,88},{64,... | collective-permute-start | bytes 884744 | tf_op jit(solution)/shard_map/ppermute | solution.py:298
  27.4 31.6 %copy-start.14 = (bf16[128,1152]{1,0:T(8,128)(2,1)}, bf16[128,1152]{1,0:T(8,128)(2,1)S(1)}, u32[]{:S(2)}) copy-start(bf16[128,1152]{1,0:T(8,128)(2,1)S(1)} %collective-permute-done.14.refs_18_) | copy-start | bytes 884740
  27.4 13.2 %collective-permute-start.6 = (bf16[128,1152]{1,0:T(8,128)(2,1)S(1)}, bf16[128,1152]{1,0:T(8,128)(2,1)S(1)}, u32[]{:S(2)}, u32[]{:S(2)}) collective-permute-start(bf16[128,1152]{1,0:T(8,128)(2,1)S(1)} %collective-permute-done.3.refs_6_), channel_id=1, source_target_pairs={{0,6},{1,7},{2,0},{3,1},{4,2},{5,3},{6,4},{7,5},{8,14},{9,15},{10,... | collective-permute-start | bytes 884744 | tf_op jit(solution)/shard_map/ppermute | solution.py:299
  30.4 28.6 %copy-start.15 = (bf16[128,1152]{1,0:T(8,128)(2,1)}, bf16[128,1152]{1,0:T(8,128)(2,1)S(1)}, u32[]{:S(2)}) copy-start(bf16[128,1152]{1,0:T(8,128)(2,1)S(1)} %collective-permute-done.10.refs_14_) | copy-start | bytes 884740
  30.4 10.8 %collective-permute-start.5 = (bf16[128,1152]{1,0:T(8,128)(2,1)S(1)}, bf16[128,1152]{1,0:T(8,128)(2,1)S(1)}, u32[]{:S(2)}, u32[]{:S(2)}) collective-permute-start(bf16[128,1152]{1,0:T(8,128)(2,1)S(1)} %collective-permute-done.3.refs_6_), channel_id=1, source_target_pairs={{0,4},{1,5},{2,6},{3,7},{4,0},{5,1},{6,2},{7,3},{8,12},{9,13},{10,... | collective-permute-start | bytes 884744 | tf_op jit(solution)/shard_map/ppermute | solution.py:299
  33.0 26.1 %copy-start.16 = (bf16[128,1152]{1,0:T(8,128)(2,1)}, bf16[128,1152]{1,0:T(8,128)(2,1)S(1)}, u32[]{:S(2)}) copy-start(bf16[128,1152]{1,0:T(8,128)(2,1)S(1)} %collective-permute-done.9.refs_13_) | copy-start | bytes 884740
  33.0 11.0 %collective-permute-start.4 = (bf16[128,1152]{1,0:T(8,128)(2,1)S(1)}, bf16[128,1152]{1,0:T(8,128)(2,1)S(1)}, u32[]{:S(2)}, u32[]{:S(2)}) collective-permute-start(bf16[128,1152]{1,0:T(8,128)(2,1)S(1)} %collective-permute-done.3.refs_6_), channel_id=1, source_target_pairs={{0,2},{1,3},{2,4},{3,5},{4,6},{5,7},{6,0},{7,1},{8,10},{9,11},{10,... | collective-permute-start | bytes 884744 | tf_op jit(solution)/shard_map/ppermute | solution.py:299
  36.4 22.7 %copy-start.17 = (bf16[128,1152]{1,0:T(8,128)(2,1)}, bf16[128,1152]{1,0:T(8,128)(2,1)S(1)}, u32[]{:S(2)}) copy-start(bf16[128,1152]{1,0:T(8,128)(2,1)S(1)} %collective-permute-done.8.refs_12_) | copy-start | bytes 884740
  36.4 7.6 %collective-permute-start.18 = (bf16[128,1152]{1,0:T(8,128)(2,1)S(1)}, bf16[128,1152]{1,0:T(8,128)(2,1)S(1)}, u32[]{:S(2)}, u32[]{:S(2)}) collective-permute-start(bf16[128,1152]{1,0:T(8,128)(2,1)S(1)} %collective-permute-done.10.refs_14_), channel_id=1, source_target_pairs={{0,8},{8,0},{16,24},{24,16},{32,40},{40,32},{48,56},{56,48},{64,72... | collective-permute-start | bytes 884744 | tf_op jit(solution)/shard_map/ppermute | solution.py:301
  39.4 19.7 %copy-start.18 = (bf16[128,1152]{1,0:T(8,128)(2,1)}, bf16[128,1152]{1,0:T(8,128)(2,1)S(1)}, u32[]{:S(2)}) copy-start(bf16[128,1152]{1,0:T(8,128)(2,1)S(1)} %collective-permute-done.7.refs_11_) | copy-start | bytes 884740
  39.4 10.1 %collective-permute-start.13 = (bf16[128,1152]{1,0:T(8,128)(2,1)S(1)}, bf16[128,1152]{1,0:T(8,128)(2,1)}, u32[]{:S(2)}, u32[]{:S(2)}) collective-permute-start(bf16[128,1152]{1,0:T(8,128)(2,1)S(1)} %collective-permute-done.10.refs_14_), channel_id=1, source_target_pairs={{0,96},{8,104},{16,112},{24,120},{32,0},{40,8},{48,16},{56,24},{64... | collective-permute-start | bytes 884744 | tf_op jit(solution)/shard_map/ppermute | solution.py:300
  40.6 18.5 %copy-start.19 = (bf16[128,1152]{1,0:T(8,128)(2,1)}, bf16[128,1152]{1,0:T(8,128)(2,1)S(1)}, u32[]{:S(2)}) copy-start(bf16[128,1152]{1,0:T(8,128)(2,1)S(1)} %collective-permute-done.6.refs_9_) | copy-start | bytes 884740
  40.6 11.6 %collective-permute-start.12 = (bf16[128,1152]{1,0:T(8,128)(2,1)S(1)}, bf16[128,1152]{1,0:T(8,128)(2,1)}, u32[]{:S(2)}, u32[]{:S(2)}) collective-permute-start(bf16[128,1152]{1,0:T(8,128)(2,1)S(1)} %collective-permute-done.10.refs_14_), channel_id=1, source_target_pairs={{0,64},{8,72},{16,80},{24,88},{32,96},{40,104},{48,112},{56,120},{... | collective-permute-start | bytes 884744 | tf_op jit(solution)/shard_map/ppermute | solution.py:300
  41.2 17.8 %copy-start.20 = (bf16[128,1152]{1,0:T(8,128)(2,1)}, bf16[128,1152]{1,0:T(8,128)(2,1)S(1)}, u32[]{:S(2)}) copy-start(bf16[128,1152]{1,0:T(8,128)(2,1)S(1)} %collective-permute-done.5.refs_8_) | copy-start | bytes 884740
  41.2 14.5 %collective-permute-start.11 = (bf16[128,1152]{1,0:T(8,128)(2,1)S(1)}, bf16[128,1152]{1,0:T(8,128)(2,1)}, u32[]{:S(2)}, u32[]{:S(2)}) collective-permute-start(bf16[128,1152]{1,0:T(8,128)(2,1)S(1)} %collective-permute-done.10.refs_14_), channel_id=1, source_target_pairs={{0,32},{8,40},{16,48},{24,56},{32,64},{40,72},{48,80},{56,88},{64,... | collective-permute-start | bytes 884744 | tf_op jit(solution)/shard_map/ppermute | solution.py:300
  44.0 15.1 %copy-start.21 = (bf16[128,1152]{1,0:T(8,128)(2,1)}, bf16[128,1152]{1,0:T(8,128)(2,1)S(1)}, u32[]{:S(2)}) copy-start(bf16[128,1152]{1,0:T(8,128)(2,1)S(1)} %collective-permute-done.4.refs_7_) | copy-start | bytes 884740
  44.0 11.8 %collective-permute-start.17 = (bf16[128,1152]{1,0:T(8,128)(2,1)S(1)}, bf16[128,1152]{1,0:T(8,128)(2,1)S(1)}, u32[]{:S(2)}, u32[]{:S(2)}) collective-permute-start(bf16[128,1152]{1,0:T(8,128)(2,1)S(1)} %collective-permute-done.9.refs_13_), channel_id=1, source_target_pairs={{0,8},{8,0},{16,24},{24,16},{32,40},{40,32},{48,56},{56,48},{64,72... | collective-permute-start | bytes 884744 | tf_op jit(solution)/shard_map/ppermute | solution.py:301
  44.0 11.7 %copy-start.22 = (bf16[128,1152]{1,0:T(8,128)(2,1)}, bf16[128,1152]{1,0:T(8,128)(2,1)S(1)}, u32[]{:S(2)}) copy-start(bf16[128,1152]{1,0:T(8,128)(2,1)S(1)} %collective-permute-done.18.refs_22_) | copy-start | bytes 884740
  44.0 14.9 %collective-permute-start.16 = (bf16[128,1152]{1,0:T(8,128)(2,1)S(1)}, bf16[128,1152]{1,0:T(8,128)(2,1)}, u32[]{:S(2)}, u32[]{:S(2)}) collective-permute-start(bf16[128,1152]{1,0:T(8,128)(2,1)S(1)} %collective-permute-done.8.refs_12_), channel_id=1, source_target_pairs={{0,8},{8,0},{16,24},{24,16},{32,40},{40,32},{48,56},{56,48},{64,72... | collective-permute-start | bytes 884744 | tf_op jit(solution)/shard_map/ppermute | solution.py:301
  49.4 9.5 %collective-permute-start.15 = (bf16[128,1152]{1,0:T(8,128)(2,1)S(1)}, bf16[128,1152]{1,0:T(8,128)(2,1)}, u32[]{:S(2)}, u32[]{:S(2)}) collective-permute-start(bf16[128,1152]{1,0:T(8,128)(2,1)S(1)} %collective-permute-done.7.refs_11_), channel_id=1, source_target_pairs={{0,8},{8,0},{16,24},{24,16},{32,40},{40,32},{48,56},{56,48},{64,72... | collective-permute-start | bytes 884744 | tf_op jit(solution)/shard_map/ppermute | solution.py:301
  52.2 6.8 %collective-permute-start.21 = (bf16[128,1152]{1,0:T(8,128)(2,1)}, bf16[128,1152]{1,0:T(8,128)(2,1)}, u32[]{:S(2)}, u32[]{:S(2)}) collective-permute-start(bf16[128,1152]{1,0:T(8,128)(2,1)} %collective-permute-done.13.refs_17_), channel_id=1, source_target_pairs={{0,8},{8,0},{16,24},{24,16},{32,40},{40,32},{48,56},{56,48},{64,72... | collective-permute-start | bytes 884744 | tf_op jit(solution)/shard_map/ppermute | solution.py:301
  55.7 3.2 %collective-permute-start.20 = (bf16[128,1152]{1,0:T(8,128)(2,1)}, bf16[128,1152]{1,0:T(8,128)(2,1)}, u32[]{:S(2)}, u32[]{:S(2)}) collective-permute-start(bf16[128,1152]{1,0:T(8,128)(2,1)} %collective-permute-done.12.refs_16_), channel_id=1, source_target_pairs={{0,8},{8,0},{16,24},{24,16},{32,40},{40,32},{48,56},{56,48},{64,72... | collective-permute-start | bytes 884744 | tf_op jit(solution)/shard_map/ppermute | solution.py:301
  55.7 0.8 copy-start.23
  55.7 3.2 %collective-permute-start.19 = (bf16[128,1152]{1,0:T(8,128)(2,1)}, bf16[128,1152]{1,0:T(8,128)(2,1)}, u32[]{:S(2)}, u32[]{:S(2)}) collective-permute-start(bf16[128,1152]{1,0:T(8,128)(2,1)} %collective-permute-done.11.refs_15_), channel_id=1, source_target_pairs={{0,8},{8,0},{16,24},{24,16},{32,40},{40,32},{48,56},{56,48},{64,72... | collective-permute-start | bytes 884744 | tf_op jit(solution)/shard_map/ppermute | solution.py:301
  95.7 6.8 %collective-permute-start.35 = (bf16[1024,1152]{1,0:T(8,128)(2,1)}, bf16[1024,1152]{1,0:T(8,128)(2,1)S(1)}, u32[]{:S(2)}, u32[]{:S(2)}) collective-permute-start(bf16[1024,1152]{1,0:T(8,128)(2,1)} %get-tuple-element.32), channel_id=1, source_target_pairs={{0,8},{8,0},{16,24},{24,16},{32,40},{40,32},{48,56},{56,48},{64,72... | collective-permute-start | bytes 7077896 | tf_op jit(solution)/shard_map/ppermute | solution.py:313
  96.3 27.8 %collective-permute-start.31 = (bf16[256,1152]{1,0:T(8,128)(2,1)}, bf16[256,1152]{1,0:T(8,128)(2,1)S(1)}, u32[]{:S(2)}, u32[]{:S(2)}) collective-permute-start(bf16[256,1152]{1,0:T(8,128)(2,1)} %get-tuple-element.26), channel_id=1, source_target_pairs={{0,6},{1,7},{2,0},{3,1},{4,2},{5,3},{6,4},{7,5},{8,14},{9,15},{10,... | collective-permute-start | bytes 1769480 | tf_op jit(solution)/shard_map/ppermute | solution.py:314
  99.3 13.1 %collective-permute-start.23 = (f32[3,128]{1,0:T(4,128)S(1)}, f32[3,128]{1,0:T(4,128)S(1)}, u32[]{:S(2)}, u32[]{:S(2)}) collective-permute-start(f32[3,128]{1,0:T(4,128)S(1)} %broadcast_in_dim.4), channel_id=1, source_target_pairs={{0,2},{1,3},{2,4},{3,5},{4,6},{5,7},{6,0},{7,1},{8,10},{9,11},{10,... | collective-permute-start | bytes 4616 | tf_op jit(solution)/shard_map/ppermute | solution.py:320
  99.5 24.5 %collective-permute-start.24 = (f32[3,128]{1,0:T(4,128)S(1)}, f32[3,128]{1,0:T(4,128)S(1)}, u32[]{:S(2)}, u32[]{:S(2)}) collective-permute-start(f32[3,128]{1,0:T(4,128)S(1)} %broadcast_in_dim.4), channel_id=1, source_target_pairs={{0,6},{1,7},{2,0},{3,1},{4,2},{5,3},{6,4},{7,5},{8,14},{9,15},{10,... | collective-permute-start | bytes 4616 | tf_op jit(solution)/shard_map/ppermute | solution.py:320
  102.6 21.5 %collective-permute-start.22 = (f32[3,128]{1,0:T(4,128)S(1)}, f32[3,128]{1,0:T(4,128)S(1)}, u32[]{:S(2)}, u32[]{:S(2)}) collective-permute-start(f32[3,128]{1,0:T(4,128)S(1)} %broadcast_in_dim.4), channel_id=1, source_target_pairs={{0,4},{1,5},{2,6},{3,7},{4,0},{5,1},{6,2},{7,3},{8,12},{9,13},{10,... | collective-permute-start | bytes 4616 | tf_op jit(solution)/shard_map/ppermute | solution.py:320
  102.6 3.5 %copy-start = (bf16[1024,1152]{1,0:T(8,128)(2,1)}, bf16[1024,1152]{1,0:T(8,128)(2,1)S(1)}, u32[]{:S(2)}) copy-start(bf16[1024,1152]{1,0:T(8,128)(2,1)S(1)} %collective-permute-done.35.code_ref) | copy-start | bytes 7077892
  102.6 23.6 %collective-permute-start.32 = (bf16[256,1152]{1,0:T(8,128)(2,1)}, bf16[256,1152]{1,0:T(8,128)(2,1)S(1)}, u32[]{:S(2)}, u32[]{:S(2)}) collective-permute-start(bf16[256,1152]{1,0:T(8,128)(2,1)} %get-tuple-element.27), channel_id=1, source_target_pairs={{0,4},{1,5},{2,6},{3,7},{4,0},{5,1},{6,2},{7,3},{8,12},{9,13},{10,... | collective-permute-start | bytes 1769480 | tf_op jit(solution)/shard_map/ppermute | solution.py:314
  106.1 6.3 %copy-start.9 = (bf16[256,1152]{1,0:T(8,128)(2,1)S(1)}, bf16[256,1152]{1,0:T(8,128)(2,1)}, u32[]{:S(2)}) copy-start(bf16[256,1152]{1,0:T(8,128)(2,1)} %get-tuple-element.28) | copy-start | bytes 1769476
  112.4 19.1 %collective-permute-start.33 = (bf16[256,1152]{1,0:T(8,128)(2,1)S(1)}, bf16[256,1152]{1,0:T(8,128)(2,1)S(1)}, u32[]{:S(2)}, u32[]{:S(2)}) collective-permute-start(bf16[256,1152]{1,0:T(8,128)(2,1)S(1)} %copy-done.9), channel_id=1, source_target_pairs={{0,2},{1,3},{2,4},{3,5},{4,6},{5,7},{6,0},{7,1},{8,10},{9,11},{10,... | collective-permute-start | bytes 1769480 | tf_op jit(solution)/shard_map/ppermute | solution.py:314
  124.0 10.1 %collective-permute-start.36 = (bf16[256,1152]{1,0:T(8,128)(2,1)}, bf16[256,1152]{1,0:T(8,128)(2,1)S(1)}, u32[]{:S(2)}, u32[]{:S(2)}) collective-permute-start(bf16[256,1152]{1,0:T(8,128)(2,1)} %get-tuple-element.34), channel_id=1, source_target_pairs={{0,96},{8,104},{16,112},{24,120},{32,0},{40,8},{48,16},{56,24},{64... | collective-permute-start | bytes 1769480 | tf_op jit(solution)/shard_map/ppermute | solution.py:316
  124.0 14.3 %collective-permute-start.37 = (bf16[256,1152]{1,0:T(8,128)(2,1)}, bf16[256,1152]{1,0:T(8,128)(2,1)S(1)}, u32[]{:S(2)}, u32[]{:S(2)}) collective-permute-start(bf16[256,1152]{1,0:T(8,128)(2,1)} %get-tuple-element.35), channel_id=1, source_target_pairs={{0,64},{8,72},{16,80},{24,88},{32,96},{40,104},{48,112},{56,120},{... | collective-permute-start | bytes 1769480 | tf_op jit(solution)/shard_map/ppermute | solution.py:316
  124.1 10.1 %copy-start.1 = (bf16[256,1152]{1,0:T(8,128)(2,1)}, bf16[256,1152]{1,0:T(8,128)(2,1)S(1)}, u32[]{:S(2)}) copy-start(bf16[256,1152]{1,0:T(8,128)(2,1)S(1)} %collective-permute-done.31.c1) | copy-start | bytes 1769476
  124.1 33.0 %collective-permute-start.38 = (bf16[256,1152]{1,0:T(8,128)(2,1)}, bf16[256,1152]{1,0:T(8,128)(2,1)S(1)}, u32[]{:S(2)}, u32[]{:S(2)}) collective-permute-start(bf16[256,1152]{1,0:T(8,128)(2,1)} %get-tuple-element.36), channel_id=1, source_target_pairs={{0,32},{8,40},{16,48},{24,56},{32,64},{40,72},{48,80},{56,88},{64,... | collective-permute-start | bytes 1769480 | tf_op jit(solution)/shard_map/ppermute | solution.py:316
  126.2 7.9 %copy-start.2 = (bf16[256,1152]{1,0:T(8,128)(2,1)}, bf16[256,1152]{1,0:T(8,128)(2,1)S(1)}, u32[]{:S(2)}) copy-start(bf16[256,1152]{1,0:T(8,128)(2,1)S(1)} %collective-permute-done.32.c2) | copy-start | bytes 1769476
  126.2 35.6 %collective-permute-start.27 = (f32[3,128]{1,0:T(4,128)S(1)}, f32[3,128]{1,0:T(4,128)S(1)}, u32[]{:S(2)}, u32[]{:S(2)}) collective-permute-start(f32[3,128]{1,0:T(4,128)S(1)} %add_add_fusion.1), channel_id=1, source_target_pairs={{0,96},{8,104},{16,112},{24,120},{32,0},{40,8},{48,16},{56,24},{64... | collective-permute-start | bytes 4616 | tf_op jit(solution)/shard_map/ppermute | solution.py:321
  131.5 2.6 %copy-start.5 = (bf16[256,1152]{1,0:T(8,128)(2,1)}, bf16[256,1152]{1,0:T(8,128)(2,1)S(1)}, u32[]{:S(2)}) copy-start(bf16[256,1152]{1,0:T(8,128)(2,1)S(1)} %collective-permute-done.33.c3) | copy-start | bytes 1769476
  131.5 30.3 %collective-permute-start.26 = (f32[3,128]{1,0:T(4,128)S(1)}, f32[3,128]{1,0:T(4,128)S(1)}, u32[]{:S(2)}, u32[]{:S(2)}) collective-permute-start(f32[3,128]{1,0:T(4,128)S(1)} %add_add_fusion.1), channel_id=1, source_target_pairs={{0,32},{8,40},{16,48},{24,56},{32,64},{40,72},{48,80},{56,88},{64,... | collective-permute-start | bytes 4616 | tf_op jit(solution)/shard_map/ppermute | solution.py:321
  134.1 22.9 %copy-start.3 = (bf16[256,1152]{1,0:T(8,128)(2,1)}, bf16[256,1152]{1,0:T(8,128)(2,1)S(1)}, u32[]{:S(2)}) copy-start(bf16[256,1152]{1,0:T(8,128)(2,1)S(1)} %collective-permute-done.36.c1) | copy-start | bytes 1769476
  134.1 27.7 %collective-permute-start.25 = (f32[3,128]{1,0:T(4,128)S(1)}, f32[3,128]{1,0:T(4,128)S(1)}, u32[]{:S(2)}, u32[]{:S(2)}) collective-permute-start(f32[3,128]{1,0:T(4,128)S(1)} %add_add_fusion.1), channel_id=1, source_target_pairs={{0,64},{8,72},{16,80},{24,88},{32,96},{40,104},{48,112},{56,120},{... | collective-permute-start | bytes 4616 | tf_op jit(solution)/shard_map/ppermute | solution.py:321
  138.3 18.8 %copy-start.4 = (bf16[256,1152]{1,0:T(8,128)(2,1)}, bf16[256,1152]{1,0:T(8,128)(2,1)S(1)}, u32[]{:S(2)}) copy-start(bf16[256,1152]{1,0:T(8,128)(2,1)S(1)} %collective-permute-done.37.c2) | copy-start | bytes 1769476
  138.3 39.0 %collective-permute-start.34 = (bf16[128,1152]{1,0:T(8,128)(2,1)}, bf16[128,1152]{1,0:T(8,128)(2,1)S(1)}, u32[]{:S(2)}, u32[]{:S(2)}) collective-permute-start(bf16[128,1152]{1,0:T(8,128)(2,1)} %get-tuple-element.30), channel_id=1, source_target_pairs={{0,1},{1,0},{2,3},{3,2},{4,5},{5,4},{6,7},{7,6},{8,9},{9,8},{10,11... | collective-permute-start | bytes 884744 | tf_op jit(solution)/shard_map/ppermute | solution.py:327
  157.1 0.8 copy-start.6
  161.8 18.8 %collective-permute-start.39 = (bf16[128,1152]{1,0:T(8,128)(2,1)}, bf16[128,1152]{1,0:T(8,128)(2,1)S(1)}, u32[]{:S(2)}, u32[]{:S(2)}) collective-permute-start(bf16[128,1152]{1,0:T(8,128)(2,1)} %get-tuple-element.38), channel_id=1, source_target_pairs={{0,16},{8,24},{16,0},{24,8},{32,48},{40,56},{48,32},{56,40},{64,80... | collective-permute-start | bytes 884744 | tf_op jit(solution)/shard_map/ppermute | solution.py:329
  161.9 8.2 %collective-permute-start.28 = (f32[3,128]{1,0:T(4,128)S(1)}, f32[3,128]{1,0:T(4,128)S(1)}, u32[]{:S(2)}, u32[]{:S(2)}) collective-permute-start(f32[3,128]{1,0:T(4,128)S(1)} %add_add_fusion), channel_id=1, source_target_pairs={{0,1},{1,0},{2,3},{3,2},{4,5},{5,4},{6,7},{7,6},{8,9},{9,8},{10,11... | collective-permute-start | bytes 4616 | tf_op jit(solution)/shard_map/ppermute | solution.py:322
  170.1 3.6 %collective-permute-start.29 = (f32[3,128]{1,0:T(4,128)S(1)}, f32[3,128]{1,0:T(4,128)S(1)}, u32[]{:S(2)}, u32[]{:S(2)}) collective-permute-start(f32[3,128]{1,0:T(4,128)S(1)} %add.105), channel_id=1, source_target_pairs={{0,16},{8,24},{16,0},{24,8},{32,48},{40,56},{48,32},{56,40},{64,80... | collective-permute-start | bytes 4616 | tf_op jit(solution)/shard_map/ppermute | solution.py:323
  173.6 1.2 collective-permute-start.30
  177.3 0.7 copy-start.7
  180.6 0.7 copy-start.8

commit v2 on v0

v2 whole, which is shorter than its diff:
```python
import jax
import jax.numpy as jnp
from jax import lax
from jax.experimental import pallas as pl
from jax.experimental.pallas import tpu as pltpu
from jax.sharding import PartitionSpec as P

BF = jnp.bfloat16
F32 = jnp.float32
LOG2E = 1.4426950408889634
ANY = pl.BlockSpec(memory_space=pl.ANY)
VM = pl.BlockSpec(memory_space=pltpu.VMEM)
SM = pl.BlockSpec(memory_space=pltpu.SMEM)
STRIP = 256
PIECE = 512
SLOT = {2: 0, 1: 1, 3: 2, 0: 3}


def sds(shape, dtype):
    return jax.ShapeDtypeStruct(shape, dtype)


def params():
    return pltpu.CompilerParams(vmem_limit_bytes=56 * 1024 * 1024)


def encode(x):
    sq = x * x
    return (sq * sq * sq * x).astype(BF)


def decode(code):
    y = code.astype(F32)
    return y * jnp.exp2(jnp.log2(jnp.maximum(jnp.abs(y), 1.2e-38)) * (-6.0 / 7.0))


def dot(a, b, dims):
    return lax.dot_general(a, b, (dims, ((), ())), preferred_element_type=F32)


def normalize_kernel(a_ref, b_ref, a_out, b_out):
    for src, dst in ((a_ref, a_out), (b_ref, b_out)):
        x = src[...]
        norm = jnp.sqrt(jnp.sum(x * x, axis=1, keepdims=True) + 1e-06)
        dst[...] = (x / norm).astype(BF)


def normalize(a, b):
    return pl.pallas_call(
        normalize_kernel, out_shape=(sds(a.shape, BF), sds(b.shape, BF)), name="normalize"
    )(a, b)


def loads(refs, dest, sems, base=0):
    out, at = [], base
    for n, r in enumerate(refs):
        out.append(pltpu.make_async_copy(r, dest.at[pl.ds(at, r.shape[0])], sems.at[n]))
        at += r.shape[0]
    return out


def start(copies):
    for c in copies:
        c.start()


def wait(copies):
    for c in copies:
        c.wait()


def scores(scal, diag, first, xs, ts, sim, wgt, sums):
    m, n, rows = xs.shape[0], ts.shape[0], xs.shape[0] // 8
    scale = jnp.exp(jnp.full((1, 1), scal[0], F32))
    bias = scal[1]
    mult = scale * LOG2E
    shift = bias * LOG2E
    pieces = [(r, c) for r in range(0, m, STRIP) for c in range(0, n, PIECE)]

    def score(r, c):
        sim[r : r + STRIP, c : c + PIECE] = dot(xs[r : r + STRIP, :], ts[c : c + PIECE, :], ((1,), (1,)))

    acc = [jnp.zeros((8, PIECE), F32) for _ in range(3)]
    score(*pieces[0])
    for p, (r, c) in enumerate(pieces):
        if p + 1 < len(pieces):
            score(*pieces[p + 1])
        prod = None
        for i in range(0, STRIP, 16):
            s = sim[r + i : r + i + 16, c : c + PIECE]
            e = jnp.exp2(s * mult + shift)
            u = e + 1.0
            r0 = pl.reciprocal(u, approx=True)
            sig = e * (r0 * (2.0 - u * r0))
            wgt[r + i : r + i + 16, c : c + PIECE] = (sig * scale).astype(BF)
            both = u[0:8] * u[8:16]
            prod = both if prod is None else prod * both
            if i % 64 == 48:
                acc[0] = acc[0] + jnp.log(prod)
                prod = None
            ss = sig * s
            acc[1] = acc[1] + (sig[0:8] + sig[8:16])
            acc[2] = acc[2] + (ss[0:8] + ss[8:16])
    for k in range(3):
        sums[8 * k : 8 * k + 8] = acc[k]

    for b in range(8):
        place = diag[b] - first

        @pl.when(jnp.logical_and(place >= 0, place < n // rows))
        def _(b=b, place=place):
            at = (pl.ds(b * rows, rows), pl.ds(pl.multiple_of(place * rows, rows), rows))
            s = sim[at]
            eye = lax.broadcasted_iota(jnp.int32, s.shape, 0) == lax.broadcasted_iota(jnp.int32, s.shape, 1)
            z = scale * s + bias
            w = -scale / (1.0 + jnp.exp(z))
            wgt[at] = jnp.where(eye, w, wgt[at].astype(F32)).astype(BF)
            z = jnp.where(eye, z, 0.0)
            sd = jnp.where(eye, s, 0.0)
            one = jnp.where(eye, 1.0, 0.0)
            for row, v in ((0, z), (8, one), (16, sd)):
                total = v[0:8]
                for k in range(1, rows // 8):
                    total = total + v[8 * k : 8 * k + 8]
                sums[row : row + 8, 0:rows] -= total


def first_kernel(ni, nt, scal, diag, *refs):
    images, texts = refs[:ni], refs[ni : ni + nt]
    w_out, tp_out, sums, xs, ts, sim, wgt, tp, isem, tsem, osem = refs[ni + nt :]
    copies = loads(texts, ts, tsem) + loads(images, xs, isem)
    start(copies)
    wait(copies)
    scores(scal, diag, 0, xs, ts, sim, wgt, sums)
    w_copy = pltpu.make_async_copy(wgt, w_out, osem.at[0])
    w_copy.start()
    outs = [w_copy]
    for n, r in enumerate(range(0, ts.shape[0], STRIP)):
        tp[r : r + STRIP, :] = dot(wgt[:, r : r + STRIP], xs[...], ((0,), (0,)))
        c = pltpu.make_async_copy(tp.at[pl.ds(r, STRIP)], tp_out.at[pl.ds(r, STRIP)], osem.at[1 + n])
        c.start()
        outs.append(c)
    wait(outs)


def first(scal, diag, images, texts, m, n, d):
    ni, nt = len(images), len(texts)
    return pl.pallas_call(
        lambda *refs: first_kernel(ni, nt, *refs),
        in_specs=[SM, SM] + [ANY] * (ni + nt),
        out_specs=[ANY, ANY, VM],
        out_shape=(sds((m, n), BF), sds((n, d), F32), sds((24, PIECE), F32)),
        scratch_shapes=[
            pltpu.VMEM((m, d), BF),
            pltpu.VMEM((n, d), BF),
            pltpu.VMEM((m, n), F32),
            pltpu.VMEM((m, n), BF),
            pltpu.VMEM((n, d), F32),
            pltpu.SemaphoreType.DMA((ni,)),
            pltpu.SemaphoreType.DMA((nt,)),
            pltpu.SemaphoreType.DMA((1 + n // STRIP,)),
        ],
        compiler_params=params(),
        cost_estimate=pl.CostEstimate(
            flops=4 * m * n * d, bytes_accessed=(m + n) * d * 4, transcendentals=3 * m * n
        ),
        name="other_half",
    )(scal, diag, *images, *texts)


def put_groups(pulls, rows, far_a, far_b, k1, k3, own):
    far = pulls(SLOT[2])
    far_a[...] = encode(far[:rows])
    far_b[...] = encode(far[rows:])
    for k, ref in ((1, k1), (3, k3), (0, own)):
        ref[...] = pulls(SLOT[k])


def second_kernel(ni, nt, scal, diag, *refs):
    images, own, other = refs[:ni], refs[ni : ni + nt], refs[ni + nt : ni + 2 * nt]
    w_in = refs[ni + 2 * nt]
    w_out, far_a, far_b, k1, k3, k0, sums = refs[ni + 2 * nt + 1 : ni + 2 * nt + 8]
    xs, ts, to, sim, wgt, wo, isem, tsem, osem, wsem = refs[ni + 2 * nt + 8 :]
    now = loads(own, ts, tsem) + loads(images, xs, isem)
    later = loads(other, to, osem) + [pltpu.make_async_copy(w_in, wo, wsem.at[0])]
    start(now)
    start(later)
    wait(now)
    scores(scal, diag, 8, xs, ts, sim, wgt, sums)
    w_copy = pltpu.make_async_copy(wgt, w_out, wsem.at[1])
    w_copy.start()
    wait(later)

    def pulls(slot):
        at = slice(slot * STRIP, (slot + 1) * STRIP)
        return dot(wgt[at, :], ts[...], ((1,), (0,))) + dot(wo[at, :], to[...], ((1,), (0,)))

    put_groups(pulls, xs.shape[0] // 8, far_a, far_b, k1, k3, k0)
    w_copy.wait()


def group_shapes(rows, d):
    return (sds((rows, d), BF),) * 2 + (sds((2 * rows, d), F32),) * 3


def second(scal, diag, images, own, other, w_other, n, d):
    ni, nt = len(images), len(own)
    m = w_other.shape[0]
    return pl.pallas_call(
        lambda *refs: second_kernel(ni, nt, *refs),
        in_specs=[SM, SM] + [ANY] * (ni + 2 * nt + 1),
        out_specs=[ANY] + [VM] * 6,
        out_shape=(sds((m, n), BF),) + group_shapes(m // 8, d) + (sds((24, PIECE), F32),),
        scratch_shapes=[
            pltpu.VMEM((m, d), BF),
            pltpu.VMEM((n, d), BF),
            pltpu.VMEM((n, d), BF),
            pltpu.VMEM((m, n), F32),
            pltpu.VMEM((m, n), BF),
            pltpu.VMEM((m, n), BF),
            pltpu.SemaphoreType.DMA((ni,)),
            pltpu.SemaphoreType.DMA((nt,)),
            pltpu.SemaphoreType.DMA((nt,)),
            pltpu.SemaphoreType.DMA((2,)),
        ],
        compiler_params=params(),
        cost_estimate=pl.CostEstimate(
            flops=6 * m * n * d, bytes_accessed=(m + 2 * n) * d * 4, transcendentals=3 * m * n
        ),
        name="own_half",
    )(scal, diag, *images, *own, *other, w_other)


def third_kernel(ni, *refs):
    images, w_in, tp_in = refs[:ni], refs[ni], refs[ni + 1]
    far_a, far_b, k1, k3, k0, xs, wgt, tp, isem, wsem = refs[ni + 2 :]
    copies = loads(images, xs, isem) + [pltpu.make_async_copy(w_in, wgt, wsem.at[0])]
    later = pltpu.make_async_copy(tp_in, tp, wsem.at[1])
    start(copies)
    later.start()
    wait(copies)
    later.wait()

    def pulls(slot):
        at = slice(slot * STRIP, (slot + 1) * STRIP)
        return dot(wgt[:, at], xs[...], ((0,), (0,))) + tp[at, :]

    put_groups(pulls, wgt.shape[1] // 8, far_a, far_b, k1, k3, k0)


def third(images, w_own, tp):
    ni = len(images)
    (m, n), d = w_own.shape, tp.shape[1]
    return pl.pallas_call(
        lambda *refs: third_kernel(ni, *refs),
        in_specs=[ANY] * (ni + 2),
        out_specs=[VM] * 5,
        out_shape=group_shapes(n // 8, d),
        scratch_shapes=[
            pltpu.VMEM((m, d), BF),
            pltpu.VMEM((m, n), BF),
            pltpu.VMEM((n, d), F32),
            pltpu.SemaphoreType.DMA((ni,)),
            pltpu.SemaphoreType.DMA((2,)),
        ],
        compiler_params=params(),
        cost_estimate=pl.CostEstimate(
            flops=2 * m * n * d, bytes_accessed=(m + 2 * n) * d * 4, transcendentals=0
        ),
        name="own_text_pull",
    )(*images, w_own, tp)


def relay_kernel(k1, k3, via1, via3, c1, c3):
    rows = via1.shape[0]
    c1[:rows, :] = encode(k1[:rows, :])
    c1[rows:, :] = encode(k1[rows:, :] + decode(via1[...]))
    c3[:rows, :] = encode(k3[:rows, :] + decode(via3[...]))
    c3[rows:, :] = encode(k3[rows:, :])


def relay(k1, k3, via1, via3):
    return pl.pallas_call(
        relay_kernel, out_shape=(sds(k1.shape, BF),) * 2, compiler_params=params(), name="relay"
    )(k1, k3, via1, via3)


def partner_kernel(own, c1, c3, out):
    out[...] = encode(own[...] + decode(c1[...]) + decode(c3[...]))


def fold_partner(own, c1, c3):
    rows, d = own.shape[0] // 2, own.shape[1]
    half = pl.BlockSpec((rows, d), lambda i: (1, 0))
    return pl.pallas_call(
        partner_kernel,
        grid=(1,),
        in_specs=[half] * 3,
        out_specs=pl.BlockSpec((rows, d), lambda i: (0, 0)),
        out_shape=sds((rows, d), BF),
        compiler_params=params(),
        name="fold_partner",
    )(own, c1, c3)


def finish_kernel(x_ref, own, c1, c3, code_ref, out_ref):
    x = x_ref[...]
    norm = jnp.sqrt(jnp.sum(x * x, axis=1, keepdims=True) + 1e-06)
    hat = x / norm
    pull = own[...] + decode(c1[...]) + decode(c3[...]) + decode(code_ref[...])
    out_ref[...] = (pull - hat * jnp.sum(hat * pull, axis=1, keepdims=True)) / norm


def finish(x, own, c1, c3, code):
    whole = pl.BlockSpec(x.shape, lambda i: (0, 0))
    return pl.pallas_call(
        finish_kernel,
        grid=(1,),
        in_specs=[whole] * 5,
        out_specs=whole,
        out_shape=sds(x.shape, F32),
        compiler_params=params(),
        name="finish",
    )(x, own, c1, c3, code)


def img_index(y, z, c):
    return (y % 4) * 4 + (z % 2) * 2 + c % 2


def perm_x(shift):
    return [(i, ((i // 2 + shift) % 4) * 2 + i % 2) for i in range(8)]


def perm_y(shift):
    return [(i, img_index(i // 4 + shift, i // 2, i)) for i in range(16)]


PERM_ZHI = [(i, i ^ 1) for i in range(8)]
PERM_ZLO = [(i, i ^ 2) for i in range(16)]
PERM_CORE = [(i, i ^ 1) for i in range(16)]


def local(image_embed, text_embed, log_scale, logit_bias):
    send = lax.ppermute
    rows, d = image_embed.shape
    image_low, text_low = normalize(image_embed, text_embed)

    i0 = jnp.concatenate([image_low, send(image_low, "txt", PERM_ZHI)], 0)
    t0 = jnp.concatenate([text_low, send(text_low, "img", PERM_ZLO)], 0)
    i1, i3 = send(i0, "txt", perm_x(1)), send(i0, "txt", perm_x(-1))
    t1, t3 = send(t0, "img", perm_y(1)), send(t0, "img", perm_y(-1))
    i2 = [send(i1[:rows], "txt", perm_x(1)), send(i3[rows:], "txt", perm_x(-1))]
    t2 = [send(t1[:rows], "img", perm_y(1)), send(t3[rows:], "img", perm_y(-1))]
    images = i2 + [i1, i3, i0]
    own = t2 + [t1, t3, t0]
    other = [send(t, "img", PERM_CORE) for t in own]

    i, t = lax.axis_index("img"), lax.axis_index("txt")
    b = jnp.arange(8, dtype=jnp.int32)
    ring = jnp.array([2, 1, 3, 0], jnp.int32)
    g = 8 * i + ((t // 2 - ring[b // 2]) % 4) * 2 + ((t % 2) ^ (b % 2))
    o = g % 16
    slot = jnp.array([3, 1, 0, 2], jnp.int32)[(i // 4 - o // 4) % 4]
    mine = 1 - ((i % 2) ^ (o % 2))
    place = mine * 8 + slot * 2 + (((i // 2) % 2) ^ ((o // 2) % 2))
    diag = jnp.where(g // 16 == t, place, -1).astype(jnp.int32)
    scal = jnp.stack([log_scale, logit_bias])

    w_other, tp, sums = first(scal, diag, images, other, 8 * rows, 8 * rows, d)
    tp = send(tp, "img", PERM_CORE)
    w_own, ia, ib, k1, k3, k0, more = second(scal, diag, images, own, other, w_other, 8 * rows, d)

    ia, ib = send(ia, "txt", perm_x(1)), send(ib, "txt", perm_x(-1))
    ta, tb, q1, q3, q0 = third(images, w_own, tp)
    ta, tb = send(ta, "img", perm_y(1)), send(tb, "img", perm_y(-1))
    c1, c3 = relay(k1, k3, ib, ia)
    c1, c3 = send(c1, "txt", perm_x(-1)), send(c3, "txt", perm_x(1))
    e1, e3 = relay(q1, q3, tb, ta)
    e1, e3 = send(e1, "img", perm_y(-1)), send(e3, "img", perm_y(1))

    v = jnp.sum((sums + more).reshape(3, 8, -1), axis=(1, 2))
    v = jnp.broadcast_to(v[:, None], (3, 128))
    v = v + send(v, "img", PERM_CORE)
    for bit in (2, 4):
        v = v + send(v, "txt", [(i, i ^ bit) for i in range(8)])
    for bit in (4, 8):
        v = v + send(v, "img", [(i, i ^ bit) for i in range(16)])
    v = v + send(v, "txt", PERM_ZHI)
    v = v + send(v, "img", PERM_ZLO)

    image_code = send(fold_partner(k0, c1, c3), "txt", PERM_ZHI)
    text_code = send(fold_partner(q0, e1, e3), "img", PERM_ZLO)
    image_grad = finish(image_embed, k0, c1, c3, image_code)
    text_grad = finish(text_embed, q0, e1, e3, text_code)
    pairs = F32(128.0 * rows) * F32(128.0 * rows)
    scale = jnp.exp(log_scale)
    return (v[0, 0] / pairs, image_grad, text_grad, v[2, 0] * scale / pairs, v[1, 0] / pairs)


def solution(mesh):
    placed = (P(("img", "txt"), None), P(("txt", "img"), None), P(), P())
    return jax.shard_map(
        local,
        mesh=mesh,
        in_specs=placed,
        out_specs=(P(), P(("img", "txt"), None), P(("txt", "img"), None), P(), P()),
        check_vma=False,
    )
```

time: 376 us -> 172 us (0.46)
  waiting for transfers between devices: 197 us -> 58.3 us
  blocking collectives: 75.2 us -> 0 us
  Pallas kernels: 0 us -> 56.4 us
  matrix products: 48.4 us -> 0 us
  starting transfers between devices: 0.35 us -> 33.1 us
  other arithmetic: 22.9 us -> 1.59 us
  between operations: 19.9 us -> 7.66 us
  local copies, waits for them, and re-layouts: 7.11 us -> 14.2 us
    reduce_scatter x2 -> x0, waiting for transfers between devices: 101 us -> none  [the longest x1 101 us: local(): text_pull = lax.psum_scatter(terms, 'img', scatter_dimension=0, tiled=True)]
    all_gather x2 -> x0, waiting for transfers between devices: 95.3 us -> none  [the longest x1 56 us: local(): lax.all_gather(image_hat.astype(jnp.bfloat16), 'txt', axis=0, tiled=True)]
    psum x1 -> x0, blocking collectives: 75.2 us -> none  [local(): lax.psum((jnp.sum(totals), jnp.sum(scale_parts), jnp.sum(bias_parts)), ('...]
    ppermute x0 -> x33, waiting for transfers between devices: none -> 58.3 us  [the longest x1 10.6 us: local(): t0 = jnp.concatenate([text_low, send(text_low, 'img', PERM_ZLO)], 0)]
    pallas_call x0 -> x10, Pallas kernels: none -> 56.4 us  [the longest x1 16.6 us: second(): pl.pallas_call(lambda *refs: second_kernel(ni, nt, *refs), in_specs=[SM,...]
    dot_general x5 -> x0, matrix products: 48.4 us -> none  [the longest x2 25.3 us: score(): similar = jnp.dot(rows, text_block.T, preferred_element_type=jnp.float32)]
    ppermute x0 -> x33, starting transfers between devices: none -> 33.1 us  [the longest x1 3.96 us: local(): i0 = jnp.concatenate([image_low, send(image_low, 'txt', PERM_ZHI)], 0)]
    unnamed x10 -> x48, local copies, waits for them, and re-layouts: 1.44 us -> 10.4 us
  transfers between devices with their start and end apart: 4 -> 33, of which waited for: 3 -> 17; matrix products, arithmetic and copies ran while one was open for 5% -> 5% of each run, Pallas kernels for 0% -> 23%
where the time goes in v2:
time: 172 us; the launch traced here: 171 us
  waiting for transfers between devices  58.3 us (34%)
  Pallas kernels  56.4 us (33%)
  starting transfers between devices  33.1 us (19%)
  local copies, waits for them, and re-layouts  14.2 us (8%)
  between operations  7.66 us (4%)
    pallas_call x1, Pallas kernels, second(): pl.pallas_call(lambda *refs: second_kernel(ni, nt, *refs), in_specs=[SM,...  16.6 us
    pallas_call x1, Pallas kernels, first(): pl.pallas_call(lambda *refs: first_kernel(ni, nt, *refs), in_specs=[SM, S...  12.4 us
    ppermute x1, waiting for transfers between devices, local(): t0 = jnp.concatenate([text_low, send(text_low, 'img', PERM_ZLO)], 0)  10.6 us
    unnamed x48, local copies, waits for them, and re-layouts  10.4 us
    ppermute x2, waiting for transfers between devices, local(): v = v + send(v, 'img', [(i, i ^ bit) for i in range(16)])  8.12 us
    pallas_call x1, Pallas kernels, third(): pl.pallas_call(lambda *refs: third_kernel(ni, *refs), in_specs=[ANY] * (n...  7.92 us
    ppermute x2, waiting for transfers between devices, local(): t1, t3 = (send(t0, 'img', perm_y(1)), send(t0, 'img', perm_y(-1)))  7.14 us
    pallas_call x2, Pallas kernels, relay(): pl.pallas_call(relay_kernel, out_shape=(sds(k1.shape, BF),) * 2, compiler...  6.48 us
  transfers between devices with their start and end apart: 33, of which 17 were waited for; matrix products, arithmetic and copies ran while one was open for 5% of the time, Pallas kernels for 23%

profile of v2, /device:TPU:0, one launch (start us, length us, event | category | flops | bytes accessed | tf_op | source)
XLA Modules:
  0.0 171.2 jit_solution(14562279635284225392)
XLA Ops:
  0.6 2.2 %normalize.1 = (bf16[128,1152]{1,0:T(8,128)(2,1)}, bf16[128,1152]{1,0:T(8,128)(2,1)}) custom-call(f32[128,1152]{1,0:T(8,128)} %x_ref.2, f32[128,1152]{1,0:T(8,128)} %x_ref.3), custom_call_target="tpu_custom_call" | custom-call | tf_op jit(solution)/shard_map/normalize/pallas_call | solution.py:49
  2.8 4.0 %collective-permute-start = (bf16[128,1152]{1,0:T(8,128)(2,1)}, bf16[128,1152]{1,0:T(8,128)(2,1)S(1)}, u32[]{:S(2)}, u32[]{:S(2)}) collective-permute-start(bf16[128,1152]{1,0:T(8,128)(2,1)} %get-tuple-element.26), channel_id=1, source_target_pairs={{0,1},{1,0},{2,3},{3,2},{4,5},{5,4},{6,7},{7,6},{8,9},{9,8},{10,11... | collective-permute-start | bytes 884744 | tf_op jit(solution)/shard_map/ppermute | solution.py:349
  6.8 1.0 collective-permute-start.5
  7.8 1.0 constant_dynamic-update-slice_fusion.1
  8.8 1.7 constant_dynamic-update-slice_fusion.3
  10.5 10.6 %collective-permute-done.5 = bf16[128,1152]{1,0:T(8,128)(2,1)S(1)} collective-permute-done((bf16[128,1152]{1,0:T(8,128)(2,1)}, bf16[128,1152]{1,0:T(8,128)(2,1)S(1)}, u32[]{:S(2)}, u32[]{:S(2)}) %collective-permute-start.5) | collective-permute-done | bytes 294944 | tf_op jit(solution)/shard_map/ppermute | solution.py:350
  21.1 0.7 constant_dynamic-update-slice_fusion.2.refs_11_
  21.8 3.0 %collective-permute-start.9 = (bf16[256,1152]{1,0:T(8,128)(2,1)}, bf16[256,1152]{1,0:T(8,128)(2,1)S(1)}, u32[]{:S(2)}, u32[]{:S(2)}) collective-permute-start(bf16[256,1152]{1,0:T(8,128)(2,1)} %constant_dynamic-update-slice_fusion.2.refs_11_), channel_id=1, source_target_pairs={{0,96},{8,104},{16,112},{24,120},{32,0},{40,8},{48,16},{56,24},{64... | collective-permute-start | bytes 1769480 | tf_op jit(solution)/shard_map/ppermute | solution.py:352
  24.9 2.8 %collective-permute-start.3 = (bf16[256,1152]{1,0:T(8,128)(2,1)S(1)}, bf16[256,1152]{1,0:T(8,128)(2,1)S(1)}, u32[]{:S(2)}, u32[]{:S(2)}) collective-permute-start(bf16[256,1152]{1,0:T(8,128)(2,1)S(1)} %constant_dynamic-update-slice_fusion.refs_6_.refs_4_), channel_id=1, source_target_pairs={{0,6},{1,7},{2,0},{3,1},{4,2},{5,3},{6,4},{7,5},{8,14},{9,15},{10,... | collective-permute-start | bytes 1769480 | tf_op jit(solution)/shard_map/ppermute | solution.py:351
  29.1 0.6 gather_fusion
  29.7 7.1 %collective-permute-done.9.refs_10_ = bf16[256,1152]{1,0:T(8,128)(2,1)S(1)} collective-permute-done((bf16[256,1152]{1,0:T(8,128)(2,1)}, bf16[256,1152]{1,0:T(8,128)(2,1)S(1)}, u32[]{:S(2)}, u32[]{:S(2)}) %collective-permute-start.9) | collective-permute-done | bytes 589856 | tf_op jit(solution)/shard_map/ppermute | solution.py:352
  36.9 3.7 %collective-permute-start.10 = (bf16[128,1152]{1,0:T(8,128)(2,1)S(1)}, bf16[128,1152]{1,0:T(8,128)(2,1)}, u32[]{:S(2)}, u32[]{:S(2)}) collective-permute-start(bf16[128,1152]{1,0:T(8,128)(2,1)S(1)} %slice.35), channel_id=1, source_target_pairs={{0,96},{8,104},{16,112},{24,120},{32,0},{40,8},{48,16},{56,24},{64... | collective-permute-start | bytes 884744 | tf_op jit(solution)/shard_map/ppermute | solution.py:354
  40.5 1.0 slice.34
  41.7 2.8 %collective-permute-start.4 = (bf16[128,1152]{1,0:T(8,128)(2,1)S(1)}, bf16[128,1152]{1,0:T(8,128)(2,1)S(1)}, u32[]{:S(2)}, u32[]{:S(2)}) collective-permute-start(bf16[128,1152]{1,0:T(8,128)(2,1)S(1)} %slice.33), channel_id=1, source_target_pairs={{0,6},{1,7},{2,0},{3,1},{4,2},{5,3},{6,4},{7,5},{8,14},{9,15},{10,... | collective-permute-start | bytes 884744 | tf_op jit(solution)/shard_map/ppermute | solution.py:353
  44.6 0.4 collective-permute-start.12
  45.1 0.6 gather_fusion.1
  45.8 0.7 collective-permute-start.2
  46.5 3.1 %collective-permute-done.7.refs_7_ = bf16[128,1152]{1,0:T(8,128)(2,1)} collective-permute-done((bf16[128,1152]{1,0:T(8,128)(2,1)S(1)}, bf16[128,1152]{1,0:T(8,128)(2,1)}, u32[]{:S(2)}, u32[]{:S(2)}) %collective-permute-start.7) | collective-permute-done | bytes 294944 | tf_op jit(solution)/shard_map/ppermute | solution.py:354
  49.6 0.5 collective-permute-start.8
  50.1 0.6 pad_maximum_fusion.refs_0_
  50.7 0.5 compare_select_fusion.12.refs_1_
  51.3 4.8 %collective-permute-done.2.refs_2_.refs_0_ = bf16[128,1152]{1,0:T(8,128)(2,1)S(1)} collective-permute-done((bf16[128,1152]{1,0:T(8,128)(2,1)S(1)}, bf16[128,1152]{1,0:T(8,128)(2,1)S(1)}, u32[]{:S(2)}, u32[]{:S(2)}) %collective-permute-start.2) | collective-permute-done | bytes 294944 | tf_op jit(solution)/shard_map/ppermute | solution.py:353
  56.2 0.6 copy-done.11
  57.0 12.4 %other_half.1 = (bf16[1024,1024]{1,0:T(8,128)(2,1)}, f32[1024,1152]{1,0:T(8,128)}, f32[24,512]{1,0:T(8,128)}) custom-call(f32[2]{0:T(128)} %pad_maximum_fusion.refs_0_, s32[8]{0:T(128)} %compare_select_fusion.12.refs_1_, bf16[128,1152]{1,0:T(8,128)(2,1)} %copy-done.11, bf16[128,1152]{1,0:T(8,128)(2,1)} %copy-done.10, bf16[256,1152]{1,0:T(8,128)(2,1)} %copy-done.8, ...), custom_call_target="tpu_custom_call" | custom-call | flops 4831838208 | bytes 9437184 | tf_op jit(solution)/shard_map/other_half/pallas_call | solution.py:148
  69.5 16.6 %own_half.1 = (bf16[1024,1024]{1,0:T(8,128)(2,1)}, bf16[128,1152]{1,0:T(8,128)(2,1)}, bf16[128,1152]{1,0:T(8,128)(2,1)}, f32[256,1152]{1,0:T(8,128)}, f32[256,11...) custom-call(f32[2]{0:T(128)} %pad_maximum_fusion.refs_0_, s32[8]{0:T(128)} %compare_select_fusion.12.refs_1_, ...), custom_call_target="tpu_custom_call" | custom-call | flops 7247757312 | bytes 14155776 | tf_op jit(solution)/shard_map/own_half/pallas_call | solution.py:209
  86.3 2.0 %collective-permute-start.23 = (bf16[128,1152]{1,0:T(8,128)(2,1)}, bf16[128,1152]{1,0:T(8,128)(2,1)S(1)}, u32[]{:S(2)}, u32[]{:S(2)}) collective-permute-start(bf16[128,1152]{1,0:T(8,128)(2,1)} %get-tuple-element.35), channel_id=1, source_target_pairs={{0,2},{1,3},{2,4},{3,5},{4,6},{5,7},{6,0},{7,1},{8,10},{9,11},{10,... | collective-permute-start | bytes 884744 | tf_op jit(solution)/shard_map/ppermute | solution.py:374
  88.3 2.2 %copy-done.2 = f32[1024,1152]{1,0:T(8,128)} copy-done((f32[1024,1152]{1,0:T(8,128)}, f32[1024,1152]{1,0:T(8,128)S(1)}, u32[]{:S(2)}) %copy-start.2) | copy-done | bytes 4718616
  90.5 7.9 %own_text_pull.1 = (bf16[128,1152]{1,0:T(8,128)(2,1)}, bf16[128,1152]{1,0:T(8,128)(2,1)}, f32[256,1152]{1,0:T(8,128)}, f32[256,1152]{1,0:T(8,128)}, f32[256,1152]{1,0:T(8,128)}) custom-call(bf16[128,1152]{1,0:T(8,128)(2,1)} %copy-done.11, bf16[128,1152]{1,0:T(8,128)(2,1)} %copy-done.10, bf16[256,1152]{1,0:T(8,128)(2,1)} %copy-done.8, ...), custom_call_target="tpu_custom_call" | custom-call | flops 2415919104 | bytes 14155776 | tf_op jit(solution)/shard_map/own_text_pull/pallas_call | solution.py:254
  98.4 2.9 %collective-permute-start.28 = (bf16[128,1152]{1,0:T(8,128)(2,1)}, bf16[128,1152]{1,0:T(8,128)(2,1)S(1)}, u32[]{:S(2)}, u32[]{:S(2)}) collective-permute-start(bf16[128,1152]{1,0:T(8,128)(2,1)} %get-tuple-element.43), channel_id=1, source_target_pairs={{0,96},{8,104},{16,112},{24,120},{32,0},{40,8},{48,16},{56,24},{64... | collective-permute-start | bytes 884744 | tf_op jit(solution)/shard_map/ppermute | solution.py:376
  101.4 0.7 copy-done.12
  102.1 3.2 %relay.2 = (bf16[256,1152]{1,0:T(8,128)(2,1)}, bf16[256,1152]{1,0:T(8,128)(2,1)}) custom-call(f32[256,1152]{1,0:T(8,128)} %get-tuple-element.32.k1, f32[256,1152]{1,0:T(8,128)} %get-tuple-element.33.k3, bf16[128,1152]{1,0:T(8,128)(2,1)} %copy-done.12, bf16[128,1152]{1,0:T(8,128)(2,1)} %copy-done.14), custom_call_target="tpu_custom_call" | custom-call | tf_op jit(solution)/shard_map/relay/pallas_call | solution.py:283
  105.4 1.5 collective-permute-start.24
  106.9 0.5 collective-permute-start.25
  107.4 0.6 collective-permute-done.28.via1
  108.0 3.3 %collective-permute-done.29.via3 = bf16[128,1152]{1,0:T(8,128)(2,1)S(1)} collective-permute-done((bf16[128,1152]{1,0:T(8,128)(2,1)}, bf16[128,1152]{1,0:T(8,128)(2,1)S(1)}, u32[]{:S(2)}, u32[]{:S(2)}) %collective-permute-start.29) | collective-permute-done | bytes 294944 | tf_op jit(solution)/shard_map/ppermute | solution.py:376
  111.3 0.7 copy-done.15
  112.0 3.2 %relay.3 = (bf16[256,1152]{1,0:T(8,128)(2,1)}, bf16[256,1152]{1,0:T(8,128)(2,1)}) custom-call(f32[256,1152]{1,0:T(8,128)} %get-tuple-element.41.k1, f32[256,1152]{1,0:T(8,128)} %get-tuple-element.42.k3, bf16[128,1152]{1,0:T(8,128)(2,1)} %copy-done.13, bf16[128,1152]{1,0:T(8,128)(2,1)} %copy-done.15), custom_call_target="tpu_custom_call" | custom-call | tf_op jit(solution)/shard_map/relay/pallas_call | solution.py:283
  115.3 0.4 collective-permute-start.30
  115.6 1.6 collective-permute-start.31
  117.7 1.1 collective-permute-done.15
  119.2 1.2 collective-permute-done.24.c1
  120.4 2.7 %collective-permute-done.25.c3 = bf16[256,1152]{1,0:T(8,128)(2,1)S(1)} collective-permute-done((bf16[256,1152]{1,0:T(8,128)(2,1)}, bf16[256,1152]{1,0:T(8,128)(2,1)S(1)}, u32[]{:S(2)}, u32[]{:S(2)}) %collective-permute-start.25) | collective-permute-done | bytes 589856 | tf_op jit(solution)/shard_map/ppermute | solution.py:378
  123.2 0.8 copy-done.4
  124.0 2.3 %fold_partner.2 = bf16[128,1152]{1,0:T(8,128)(2,1)} custom-call(f32[256,1152]{1,0:T(8,128)} %get-tuple-element.31.own, bf16[256,1152]{1,0:T(8,128)(2,1)} %copy-done.3, bf16[256,1152]{1,0:T(8,128)(2,1)} %copy-done.4), custom_call_target="tpu_custom_call" | custom-call | tf_op jit(solution)/shard_map/fold_partner/pallas_call | solution.py:295
  126.3 1.2 collective-permute-start.26
  127.5 1.9 %collective-permute-done.30.c1 = bf16[256,1152]{1,0:T(8,128)(2,1)S(1)} collective-permute-done((bf16[256,1152]{1,0:T(8,128)(2,1)}, bf16[256,1152]{1,0:T(8,128)(2,1)S(1)}, u32[]{:S(2)}, u32[]{:S(2)}) %collective-permute-start.30) | collective-permute-done | bytes 589856 | tf_op jit(solution)/shard_map/ppermute | solution.py:380
  129.4 1.6 collective-permute-done.31.c3
  131.1 0.8 copy-done.6
  131.9 2.3 %fold_partner.3 = bf16[128,1152]{1,0:T(8,128)(2,1)} custom-call(f32[256,1152]{1,0:T(8,128)} %get-tuple-element.40.own, bf16[256,1152]{1,0:T(8,128)(2,1)} %copy-done.5, bf16[256,1152]{1,0:T(8,128)(2,1)} %copy-done.6), custom_call_target="tpu_custom_call" | custom-call | tf_op jit(solution)/shard_map/fold_partner/pallas_call | solution.py:295
  134.2 1.0 collective-permute-start.32
  135.3 0.3 collective-permute-start.17
  135.7 4.7 %collective-permute-done.17 = f32[3,128]{1,0:T(4,128)S(1)} collective-permute-done((f32[3,128]{1,0:T(4,128)S(1)}, f32[3,128]{1,0:T(4,128)S(1)}, u32[]{:S(2)}, u32[]{:S(2)}) %collective-permute-start.17) | collective-permute-done | bytes 1568 | tf_op jit(solution)/shard_map/ppermute | solution.py:386
  140.6 3.5 %collective-permute-done.18 = f32[3,128]{1,0:T(4,128)S(1)} collective-permute-done((f32[3,128]{1,0:T(4,128)S(1)}, f32[3,128]{1,0:T(4,128)S(1)}, u32[]{:S(2)}, u32[]{:S(2)}) %collective-permute-start.18) | collective-permute-done | bytes 1568 | tf_op jit(solution)/shard_map/ppermute | solution.py:388
  144.0 0.4 collective-permute-start.19
  144.5 4.7 %collective-permute-done.19 = f32[3,128]{1,0:T(4,128)S(1)} collective-permute-done((f32[3,128]{1,0:T(4,128)S(1)}, f32[3,128]{1,0:T(4,128)S(1)}, u32[]{:S(2)}, u32[]{:S(2)}) %collective-permute-start.19) | collective-permute-done | bytes 1568 | tf_op jit(solution)/shard_map/ppermute | solution.py:388
  149.1 0.5 collective-permute-start.20
  149.6 4.6 %collective-permute-done.20 = f32[3,128]{1,0:T(4,128)S(1)} collective-permute-done((f32[3,128]{1,0:T(4,128)S(1)}, f32[3,128]{1,0:T(4,128)S(1)}, u32[]{:S(2)}, u32[]{:S(2)}) %collective-permute-start.20) | collective-permute-done | bytes 1568 | tf_op jit(solution)/shard_map/ppermute | solution.py:389
  154.2 1.0 collective-permute-start.21
  155.3 2.5 %collective-permute-done.21 = f32[3,128]{1,0:T(4,128)S(1)} collective-permute-done((f32[3,128]{1,0:T(4,128)S(1)}, f32[3,128]{1,0:T(4,128)S(1)}, u32[]{:S(2)}, u32[]{:S(2)}) %collective-permute-start.21) | collective-permute-done | bytes 1568 | tf_op jit(solution)/shard_map/ppermute | solution.py:390
  157.8 0.5 fusion.21
  160.3 0.7 copy-done.16
  161.0 3.0 %finish.2 = f32[128,1152]{1,0:T(8,128)} custom-call(f32[128,1152]{1,0:T(8,128)} %x_ref.2, f32[256,1152]{1,0:T(8,128)} %get-tuple-element.31.own, bf16[256,1152]{1,0:T(8,128)(2,1)} %copy-done.3, bf16[256,1152]{1,0:T(8,128)(2,1)} %copy-done.4, bf16[128,1152]{1,0:T(8,128)(2,1)} %copy-done.16), custom_call_target="tpu_custom_call" | custom-call | tf_op jit(solution)/shard_map/finish/pallas_call | solution.py:316
  164.1 0.7 copy-done.17
  164.8 3.0 %finish.3 = f32[128,1152]{1,0:T(8,128)} custom-call(f32[128,1152]{1,0:T(8,128)} %x_ref.3, f32[256,1152]{1,0:T(8,128)} %get-tuple-element.40.own, bf16[256,1152]{1,0:T(8,128)(2,1)} %copy-done.5, bf16[256,1152]{1,0:T(8,128)(2,1)} %copy-done.6, bf16[128,1152]{1,0:T(8,128)(2,1)} %copy-done.17), custom_call_target="tpu_custom_call" | custom-call | tf_op jit(solution)/shard_map/finish/pallas_call | solution.py:316
  (86 shorter events, 2.0 us)
Async XLA Ops:
  2.8 22.0 %collective-permute-start = (bf16[128,1152]{1,0:T(8,128)(2,1)}, bf16[128,1152]{1,0:T(8,128)(2,1)S(1)}, u32[]{:S(2)}, u32[]{:S(2)}) collective-permute-start(bf16[128,1152]{1,0:T(8,128)(2,1)} %get-tuple-element.26), channel_id=1, source_target_pairs={{0,1},{1,0},{2,3},{3,2},{4,5},{5,4},{6,7},{7,6},{8,9},{9,8},{10,11... | collective-permute-start | bytes 884744 | tf_op jit(solution)/shard_map/ppermute | solution.py:349
  6.8 22.3 %copy-start.1 = (s32[4]{0:T(128)S(1)}, s32[4]{0:T(128)}, u32[]{:S(2)}) copy-start(s32[4]{0:T(128)} %constant.164.clone) | copy-start | bytes 52
  6.8 14.3 %collective-permute-start.5 = (bf16[128,1152]{1,0:T(8,128)(2,1)}, bf16[128,1152]{1,0:T(8,128)(2,1)S(1)}, u32[]{:S(2)}, u32[]{:S(2)}) collective-permute-start(bf16[128,1152]{1,0:T(8,128)(2,1)} %get-tuple-element.27), channel_id=1, source_target_pairs={{0,16},{8,24},{16,0},{24,8},{32,48},{40,56},{48,32},{56,40},{64,80... | collective-permute-start | bytes 884744 | tf_op jit(solution)/shard_map/ppermute | solution.py:350
  21.8 15.0 %collective-permute-start.9 = (bf16[256,1152]{1,0:T(8,128)(2,1)}, bf16[256,1152]{1,0:T(8,128)(2,1)S(1)}, u32[]{:S(2)}, u32[]{:S(2)}) collective-permute-start(bf16[256,1152]{1,0:T(8,128)(2,1)} %constant_dynamic-update-slice_fusion.2.refs_11_), channel_id=1, source_target_pairs={{0,96},{8,104},{16,112},{24,120},{32,0},{40,8},{48,16},{56,24},{64... | collective-permute-start | bytes 1769480 | tf_op jit(solution)/shard_map/ppermute | solution.py:352
  24.8 15.7 %collective-permute-start.6 = (bf16[256,1152]{1,0:T(8,128)(2,1)}, bf16[256,1152]{1,0:T(8,128)(2,1)}, u32[]{:S(2)}, u32[]{:S(2)}) collective-permute-start(bf16[256,1152]{1,0:T(8,128)(2,1)} %constant_dynamic-update-slice_fusion.2.refs_11_), channel_id=1, source_target_pairs={{0,32},{8,40},{16,48},{24,56},{32,64},{40,72},{48,80},{56,88},{64,... | collective-permute-start | bytes 1769480 | tf_op jit(solution)/shard_map/ppermute | solution.py:352
  24.9 16.8 %copy-start.9 = (bf16[256,1152]{1,0:T(8,128)(2,1)}, bf16[256,1152]{1,0:T(8,128)(2,1)S(1)}, u32[]{:S(2)}) copy-start(bf16[256,1152]{1,0:T(8,128)(2,1)S(1)} %constant_dynamic-update-slice_fusion.refs_6_.refs_4_) | copy-start | bytes 1769476
  24.9 16.7 %collective-permute-start.3 = (bf16[256,1152]{1,0:T(8,128)(2,1)S(1)}, bf16[256,1152]{1,0:T(8,128)(2,1)S(1)}, u32[]{:S(2)}, u32[]{:S(2)}) collective-permute-start(bf16[256,1152]{1,0:T(8,128)(2,1)S(1)} %constant_dynamic-update-slice_fusion.refs_6_.refs_4_), channel_id=1, source_target_pairs={{0,6},{1,7},{2,0},{3,1},{4,2},{5,3},{6,4},{7,5},{8,14},{9,15},{10,... | collective-permute-start | bytes 1769480 | tf_op jit(solution)/shard_map/ppermute | solution.py:351
  27.7 16.8 %collective-permute-start.14 = (bf16[256,1152]{1,0:T(8,128)(2,1)}, bf16[256,1152]{1,0:T(8,128)(2,1)}, u32[]{:S(2)}, u32[]{:S(2)}) collective-permute-start(bf16[256,1152]{1,0:T(8,128)(2,1)} %constant_dynamic-update-slice_fusion.2.refs_11_), channel_id=1, source_target_pairs={{0,8},{8,0},{16,24},{24,16},{32,40},{40,32},{48,56},{56,48},{64,72... | collective-permute-start | bytes 1769480 | tf_op jit(solution)/shard_map/ppermute | solution.py:357
  27.7 17.0 %collective-permute-start.1 = (bf16[256,1152]{1,0:T(8,128)(2,1)S(1)}, bf16[256,1152]{1,0:T(8,128)(2,1)S(1)}, u32[]{:S(2)}, u32[]{:S(2)}) collective-permute-start(bf16[256,1152]{1,0:T(8,128)(2,1)S(1)} %constant_dynamic-update-slice_fusion.refs_6_.refs_4_), channel_id=1, source_target_pairs={{0,2},{1,3},{2,4},{3,5},{4,6},{5,7},{6,0},{7,1},{8,10},{9,11},{10,... | collective-permute-start | bytes 1769480 | tf_op jit(solution)/shard_map/ppermute | solution.py:351
  27.7 17.4 %copy-start = (s32[4]{0:T(128)S(1)}, s32[4]{0:T(128)}, u32[]{:S(2)}) copy-start(s32[4]{0:T(128)} %constant.165.clone) | copy-start | bytes 52
  36.8 8.9 %copy-start.18 = (bf16[256,1152]{1,0:T(8,128)(2,1)}, bf16[256,1152]{1,0:T(8,128)(2,1)S(1)}, u32[]{:S(2)}) copy-start(bf16[256,1152]{1,0:T(8,128)(2,1)S(1)} %collective-permute-done.9.refs_10_) | copy-start | bytes 1769476
  36.9 8.9 %collective-permute-start.10 = (bf16[128,1152]{1,0:T(8,128)(2,1)S(1)}, bf16[128,1152]{1,0:T(8,128)(2,1)}, u32[]{:S(2)}, u32[]{:S(2)}) collective-permute-start(bf16[128,1152]{1,0:T(8,128)(2,1)S(1)} %slice.35), channel_id=1, source_target_pairs={{0,96},{8,104},{16,112},{24,120},{32,0},{40,8},{48,16},{56,24},{64... | collective-permute-start | bytes 884744 | tf_op jit(solution)/shard_map/ppermute | solution.py:354
  41.5 8.1 %collective-permute-start.7 = (bf16[128,1152]{1,0:T(8,128)(2,1)S(1)}, bf16[128,1152]{1,0:T(8,128)(2,1)}, u32[]{:S(2)}, u32[]{:S(2)}) collective-permute-start(bf16[128,1152]{1,0:T(8,128)(2,1)S(1)} %slice.34), channel_id=1, source_target_pairs={{0,32},{8,40},{16,48},{24,56},{32,64},{40,72},{48,80},{56,88},{64,... | collective-permute-start | bytes 884744 | tf_op jit(solution)/shard_map/ppermute | solution.py:354
  41.6 14.5 %copy-start.7 = (bf16[256,1152]{1,0:T(8,128)(2,1)}, bf16[256,1152]{1,0:T(8,128)(2,1)S(1)}, u32[]{:S(2)}) copy-start(bf16[256,1152]{1,0:T(8,128)(2,1)S(1)} %collective-permute-done.3.refs_5_.refs_3_) | copy-start | bytes 1769476
  41.7 8.0 %collective-permute-start.4 = (bf16[128,1152]{1,0:T(8,128)(2,1)S(1)}, bf16[128,1152]{1,0:T(8,128)(2,1)S(1)}, u32[]{:S(2)}, u32[]{:S(2)}) collective-permute-start(bf16[128,1152]{1,0:T(8,128)(2,1)S(1)} %slice.33), channel_id=1, source_target_pairs={{0,6},{1,7},{2,0},{3,1},{4,2},{5,3},{6,4},{7,5},{8,14},{9,15},{10,... | collective-permute-start | bytes 884744 | tf_op jit(solution)/shard_map/ppermute | solution.py:353
  44.5 11.6 %collective-permute-start.13 = (bf16[256,1152]{1,0:T(8,128)(2,1)S(1)}, bf16[256,1152]{1,0:T(8,128)(2,1)}, u32[]{:S(2)}, u32[]{:S(2)}) collective-permute-start(bf16[256,1152]{1,0:T(8,128)(2,1)S(1)} %collective-permute-done.9.refs_10_), channel_id=1, source_target_pairs={{0,8},{8,0},{16,24},{24,16},{32,40},{40,32},{48,56},{56,48},{64,72... | collective-permute-start | bytes 1769480 | tf_op jit(solution)/shard_map/ppermute | solution.py:357
  44.6 11.5 %copy-start.8 = (bf16[256,1152]{1,0:T(8,128)(2,1)}, bf16[256,1152]{1,0:T(8,128)(2,1)S(1)}, u32[]{:S(2)}) copy-start(bf16[256,1152]{1,0:T(8,128)(2,1)S(1)} %collective-permute-done.1.refs_4_.refs_2_) | copy-start | bytes 1769476
  44.6 11.5 %collective-permute-start.12 = (bf16[256,1152]{1,0:T(8,128)(2,1)}, bf16[256,1152]{1,0:T(8,128)(2,1)}, u32[]{:S(2)}, u32[]{:S(2)}) collective-permute-start(bf16[256,1152]{1,0:T(8,128)(2,1)} %collective-permute-done.6.refs_9_), channel_id=1, source_target_pairs={{0,8},{8,0},{16,24},{24,16},{32,40},{40,32},{48,56},{56,48},{64,72... | collective-permute-start | bytes 1769480 | tf_op jit(solution)/shard_map/ppermute | solution.py:357
  45.8 10.3 %collective-permute-start.2 = (bf16[128,1152]{1,0:T(8,128)(2,1)S(1)}, bf16[128,1152]{1,0:T(8,128)(2,1)S(1)}, u32[]{:S(2)}, u32[]{:S(2)}) collective-permute-start(bf16[128,1152]{1,0:T(8,128)(2,1)S(1)} %slice.32), channel_id=1, source_target_pairs={{0,2},{1,3},{2,4},{3,5},{4,6},{5,7},{6,0},{7,1},{8,10},{9,11},{10,... | collective-permute-start | bytes 884744 | tf_op jit(solution)/shard_map/ppermute | solution.py:353
  49.6 6.5 %collective-permute-start.11 = (bf16[128,1152]{1,0:T(8,128)(2,1)}, bf16[128,1152]{1,0:T(8,128)(2,1)S(1)}, u32[]{:S(2)}, u32[]{:S(2)}) collective-permute-start(bf16[128,1152]{1,0:T(8,128)(2,1)} %collective-permute-done.10.refs_8_), channel_id=1, source_target_pairs={{0,8},{8,0},{16,24},{24,16},{32,40},{40,32},{48,56},{56,48},{64,72... | collective-permute-start | bytes 884744 | tf_op jit(solution)/shard_map/ppermute | solution.py:357
  49.6 6.5 %copy-start.10 = (bf16[128,1152]{1,0:T(8,128)(2,1)}, bf16[128,1152]{1,0:T(8,128)(2,1)S(1)}, u32[]{:S(2)}) copy-start(bf16[128,1152]{1,0:T(8,128)(2,1)S(1)} %collective-permute-done.4.refs_3_.refs_1_) | copy-start | bytes 884740
  49.6 6.5 %collective-permute-start.8 = (bf16[128,1152]{1,0:T(8,128)(2,1)}, bf16[128,1152]{1,0:T(8,128)(2,1)S(1)}, u32[]{:S(2)}, u32[]{:S(2)}) collective-permute-start(bf16[128,1152]{1,0:T(8,128)(2,1)} %collective-permute-done.7.refs_7_), channel_id=1, source_target_pairs={{0,8},{8,0},{16,24},{24,16},{32,40},{40,32},{48,56},{56,48},{64,72... | collective-permute-start | bytes 884744 | tf_op jit(solution)/shard_map/ppermute | solution.py:357
  56.1 0.7 copy-start.11
  56.1 0.8 copy-start.21
  56.1 0.9 copy-start.22
  69.5 18.8 %collective-permute-start.27 = (f32[1024,1152]{1,0:T(8,128)}, f32[1024,1152]{1,0:T(8,128)S(1)}, u32[]{:S(2)}, u32[]{:S(2)}) collective-permute-start(f32[1024,1152]{1,0:T(8,128)} %get-tuple-element.39), channel_id=1, source_target_pairs={{0,8},{8,0},{16,24},{24,16},{32,40},{40,32},{48,56},{56,48},{64,72... | collective-permute-start | bytes 14155784 | tf_op jit(solution)/shard_map/ppermute | solution.py:371
  86.2 15.1 %collective-permute-start.22 = (bf16[128,1152]{1,0:T(8,128)(2,1)}, bf16[128,1152]{1,0:T(8,128)(2,1)S(1)}, u32[]{:S(2)}, u32[]{:S(2)}) collective-permute-start(bf16[128,1152]{1,0:T(8,128)(2,1)} %get-tuple-element.34), channel_id=1, source_target_pairs={{0,6},{1,7},{2,0},{3,1},{4,2},{5,3},{6,4},{7,5},{8,14},{9,15},{10,... | collective-permute-start | bytes 884744 | tf_op jit(solution)/shard_map/ppermute | solution.py:374
  86.3 15.1 %collective-permute-start.23 = (bf16[128,1152]{1,0:T(8,128)(2,1)}, bf16[128,1152]{1,0:T(8,128)(2,1)S(1)}, u32[]{:S(2)}, u32[]{:S(2)}) collective-permute-start(bf16[128,1152]{1,0:T(8,128)(2,1)} %get-tuple-element.35), channel_id=1, source_target_pairs={{0,2},{1,3},{2,4},{3,5},{4,6},{5,7},{6,0},{7,1},{8,10},{9,11},{10,... | collective-permute-start | bytes 884744 | tf_op jit(solution)/shard_map/ppermute | solution.py:374
  88.3 2.2 %copy-start.2 = (f32[1024,1152]{1,0:T(8,128)}, f32[1024,1152]{1,0:T(8,128)S(1)}, u32[]{:S(2)}) copy-start(f32[1024,1152]{1,0:T(8,128)S(1)} %collective-permute-done.27.refs_6_) | copy-start | bytes 14155780
  98.4 9.6 %collective-permute-start.28 = (bf16[128,1152]{1,0:T(8,128)(2,1)}, bf16[128,1152]{1,0:T(8,128)(2,1)S(1)}, u32[]{:S(2)}, u32[]{:S(2)}) collective-permute-start(bf16[128,1152]{1,0:T(8,128)(2,1)} %get-tuple-element.43), channel_id=1, source_target_pairs={{0,96},{8,104},{16,112},{24,120},{32,0},{40,8},{48,16},{56,24},{64... | collective-permute-start | bytes 884744 | tf_op jit(solution)/shard_map/ppermute | solution.py:376
  101.3 10.0 %collective-permute-start.29 = (bf16[128,1152]{1,0:T(8,128)(2,1)}, bf16[128,1152]{1,0:T(8,128)(2,1)S(1)}, u32[]{:S(2)}, u32[]{:S(2)}) collective-permute-start(bf16[128,1152]{1,0:T(8,128)(2,1)} %get-tuple-element.44), channel_id=1, source_target_pairs={{0,32},{8,40},{16,48},{24,56},{32,64},{40,72},{48,80},{56,88},{64,... | collective-permute-start | bytes 884744 | tf_op jit(solution)/shard_map/ppermute | solution.py:376
  101.3 0.7 copy-start.12
  101.3 0.8 copy-start.14
  105.4 15.1 %collective-permute-start.24 = (bf16[256,1152]{1,0:T(8,128)(2,1)}, bf16[256,1152]{1,0:T(8,128)(2,1)S(1)}, u32[]{:S(2)}, u32[]{:S(2)}) collective-permute-start(bf16[256,1152]{1,0:T(8,128)(2,1)} %get-tuple-element.36), channel_id=1, source_target_pairs={{0,6},{1,7},{2,0},{3,1},{4,2},{5,3},{6,4},{7,5},{8,14},{9,15},{10,... | collective-permute-start | bytes 1769480 | tf_op jit(solution)/shard_map/ppermute | solution.py:378
  106.9 16.3 %collective-permute-start.25 = (bf16[256,1152]{1,0:T(8,128)(2,1)}, bf16[256,1152]{1,0:T(8,128)(2,1)S(1)}, u32[]{:S(2)}, u32[]{:S(2)}) collective-permute-start(bf16[256,1152]{1,0:T(8,128)(2,1)} %get-tuple-element.37), channel_id=1, source_target_pairs={{0,2},{1,3},{2,4},{3,5},{4,6},{5,7},{6,0},{7,1},{8,10},{9,11},{10,... | collective-permute-start | bytes 1769480 | tf_op jit(solution)/shard_map/ppermute | solution.py:378
  108.0 3.3 %copy-start.13 = (bf16[128,1152]{1,0:T(8,128)(2,1)}, bf16[128,1152]{1,0:T(8,128)(2,1)S(1)}, u32[]{:S(2)}) copy-start(bf16[128,1152]{1,0:T(8,128)(2,1)S(1)} %collective-permute-done.28.via1) | copy-start | bytes 884740
  111.3 0.7 copy-start.15
  112.0 5.3 %copy-start.19 = (f32[24,512]{1,0:T(8,128)S(1)}, f32[24,512]{1,0:T(8,128)}, u32[]{:S(2)}) copy-start(f32[24,512]{1,0:T(8,128)} %get-tuple-element.28) | copy-start | bytes 147460
  112.0 5.3 %copy-start.20 = (f32[24,512]{1,0:T(8,128)S(1)}, f32[24,512]{1,0:T(8,128)}, u32[]{:S(2)}) copy-start(f32[24,512]{1,0:T(8,128)} %get-tuple-element.30) | copy-start | bytes 147460
  115.3 14.2 %collective-permute-start.30 = (bf16[256,1152]{1,0:T(8,128)(2,1)}, bf16[256,1152]{1,0:T(8,128)(2,1)S(1)}, u32[]{:S(2)}, u32[]{:S(2)}) collective-permute-start(bf16[256,1152]{1,0:T(8,128)(2,1)} %get-tuple-element.45), channel_id=1, source_target_pairs={{0,96},{8,104},{16,112},{24,120},{32,0},{40,8},{48,16},{56,24},{64... | collective-permute-start | bytes 1769480 | tf_op jit(solution)/shard_map/ppermute | solution.py:380
  115.6 15.4 %collective-permute-start.31 = (bf16[256,1152]{1,0:T(8,128)(2,1)}, bf16[256,1152]{1,0:T(8,128)(2,1)S(1)}, u32[]{:S(2)}, u32[]{:S(2)}) collective-permute-start(bf16[256,1152]{1,0:T(8,128)(2,1)} %get-tuple-element.46), channel_id=1, source_target_pairs={{0,32},{8,40},{16,48},{24,56},{32,64},{40,72},{48,80},{56,88},{64,... | collective-permute-start | bytes 1769480 | tf_op jit(solution)/shard_map/ppermute | solution.py:380
  117.7 1.2 collective-permute-start.15
  118.9 16.3 %collective-permute-start.16 = (f32[3,128]{1,0:T(4,128)S(1)}, f32[3,128]{1,0:T(4,128)S(1)}, u32[]{:S(2)}, u32[]{:S(2)}) collective-permute-start(f32[3,128]{1,0:T(4,128)S(1)} %broadcast_add_fusion), channel_id=1, source_target_pairs={{0,2},{1,3},{2,0},{3,1},{4,6},{5,7},{6,4},{7,5},{8,10},{9,11},{10,... | collective-permute-start | bytes 4616 | tf_op jit(solution)/shard_map/ppermute | solution.py:386
  120.4 2.7 %copy-start.3 = (bf16[256,1152]{1,0:T(8,128)(2,1)}, bf16[256,1152]{1,0:T(8,128)(2,1)S(1)}, u32[]{:S(2)}) copy-start(bf16[256,1152]{1,0:T(8,128)(2,1)S(1)} %collective-permute-done.24.c1) | copy-start | bytes 1769476
  123.2 0.8 copy-start.4
  126.3 33.9 %collective-permute-start.26 = (bf16[128,1152]{1,0:T(8,128)(2,1)}, bf16[128,1152]{1,0:T(8,128)(2,1)S(1)}, u32[]{:S(2)}, u32[]{:S(2)}) collective-permute-start(bf16[128,1152]{1,0:T(8,128)(2,1)} %fold_partner.2), channel_id=1, source_target_pairs={{0,1},{1,0},{2,3},{3,2},{4,5},{5,4},{6,7},{7,6},{8,9},{9,8},{10,11... | collective-permute-start | bytes 884744 | tf_op jit(solution)/shard_map/ppermute | solution.py:392
  129.4 1.6 copy-start.5
  131.1 0.8 copy-start.6
  134.2 29.9 %collective-permute-start.32 = (bf16[128,1152]{1,0:T(8,128)(2,1)}, bf16[128,1152]{1,0:T(8,128)(2,1)S(1)}, u32[]{:S(2)}, u32[]{:S(2)}) collective-permute-start(bf16[128,1152]{1,0:T(8,128)(2,1)} %fold_partner.3), channel_id=1, source_target_pairs={{0,16},{8,24},{16,0},{24,8},{32,48},{40,56},{48,32},{56,40},{64,80... | collective-permute-start | bytes 884744 | tf_op jit(solution)/shard_map/ppermute | solution.py:393
  135.3 5.1 %collective-permute-start.17 = (f32[3,128]{1,0:T(4,128)S(1)}, f32[3,128]{1,0:T(4,128)S(1)}, u32[]{:S(2)}, u32[]{:S(2)}) collective-permute-start(f32[3,128]{1,0:T(4,128)S(1)} %fusion.22), channel_id=1, source_target_pairs={{0,4},{1,5},{2,6},{3,7},{4,0},{5,1},{6,2},{7,3},{8,12},{9,13},{10,... | collective-permute-start | bytes 4616 | tf_op jit(solution)/shard_map/ppermute | solution.py:386
  140.4 3.6 %collective-permute-start.18 = (f32[3,128]{1,0:T(4,128)S(1)}, f32[3,128]{1,0:T(4,128)S(1)}, u32[]{:S(2)}, u32[]{:S(2)}) collective-permute-start(f32[3,128]{1,0:T(4,128)S(1)} %add.195), channel_id=1, source_target_pairs={{0,32},{8,40},{16,48},{24,56},{32,0},{40,8},{48,16},{56,24},{64,96... | collective-permute-start | bytes 4616 | tf_op jit(solution)/shard_map/ppermute | solution.py:388
  144.0 5.1 %collective-permute-start.19 = (f32[3,128]{1,0:T(4,128)S(1)}, f32[3,128]{1,0:T(4,128)S(1)}, u32[]{:S(2)}, u32[]{:S(2)}) collective-permute-start(f32[3,128]{1,0:T(4,128)S(1)} %add.196), channel_id=1, source_target_pairs={{0,64},{8,72},{16,80},{24,88},{32,96},{40,104},{48,112},{56,120},{... | collective-permute-start | bytes 4616 | tf_op jit(solution)/shard_map/ppermute | solution.py:388
  149.1 5.1 %collective-permute-start.20 = (f32[3,128]{1,0:T(4,128)S(1)}, f32[3,128]{1,0:T(4,128)S(1)}, u32[]{:S(2)}, u32[]{:S(2)}) collective-permute-start(f32[3,128]{1,0:T(4,128)S(1)} %add.197), channel_id=1, source_target_pairs={{0,1},{1,0},{2,3},{3,2},{4,5},{5,4},{6,7},{7,6},{8,9},{9,8},{10,11... | collective-permute-start | bytes 4616 | tf_op jit(solution)/shard_map/ppermute | solution.py:389
  154.2 3.6 %collective-permute-start.21 = (f32[3,128]{1,0:T(4,128)S(1)}, f32[3,128]{1,0:T(4,128)S(1)}, u32[]{:S(2)}, u32[]{:S(2)}) collective-permute-start(f32[3,128]{1,0:T(4,128)S(1)} %add.198), channel_id=1, source_target_pairs={{0,16},{8,24},{16,0},{24,8},{32,48},{40,56},{48,32},{56,40},{64,80... | collective-permute-start | bytes 4616 | tf_op jit(solution)/shard_map/ppermute | solution.py:390
  160.3 0.8 copy-start.16
  164.1 0.7 copy-start.17

commit v3 on v0

v3 whole, which is shorter than its diff:
```python
import jax
import jax.numpy as jnp
from jax import lax
from jax.experimental import pallas as pl
from jax.experimental.pallas import tpu as pltpu
from jax.sharding import PartitionSpec as P

BF = jnp.bfloat16
F32 = jnp.float32
LOG2E = 1.4426950408889634
ANY = pl.BlockSpec(memory_space=pl.ANY)
VM = pl.BlockSpec(memory_space=pltpu.VMEM)
SM = pl.BlockSpec(memory_space=pltpu.SMEM)
STRIP = 256
TALL = 512
PIECE = 512
SLOT = {2: 0, 1: 1, 3: 2, 0: 3}


def sds(shape, dtype):
    return jax.ShapeDtypeStruct(shape, dtype)


def params():
    return pltpu.CompilerParams(vmem_limit_bytes=56 * 1024 * 1024)


def encode(x):
    sq = x * x
    return (sq * sq * sq * x).astype(BF)


def decode(code):
    y = code.astype(F32)
    return y * jnp.exp2(jnp.log2(jnp.maximum(jnp.abs(y), 1.2e-38)) * (-6.0 / 7.0))


def dot(a, b, dims):
    return lax.dot_general(a, b, (dims, ((), ())), preferred_element_type=F32)


def normalize_kernel(a_ref, b_ref, a_out, b_out):
    for src, dst in ((a_ref, a_out), (b_ref, b_out)):
        x = src[...]
        norm = jnp.sqrt(jnp.sum(x * x, axis=1, keepdims=True) + 1e-06)
        dst[...] = (x / norm).astype(BF)


def normalize(a, b):
    return pl.pallas_call(
        normalize_kernel, out_shape=(sds(a.shape, BF), sds(b.shape, BF)), name="normalize"
    )(a, b)


RING = (0, 1, 3, 2)


def block_copies(pair, dest, sems, base=0):
    out = {}
    for zz, ref in enumerate(pair):
        rows = ref.shape[0] // 4
        for j, k in enumerate(RING):
            at = base + (2 * SLOT[k] + zz) * rows
            out[at] = pltpu.make_async_copy(
                ref.at[pl.ds(j * rows, rows)], dest.at[pl.ds(at, rows)], sems.at[4 * zz + j]
            )
    return [out[at] for at in sorted(out)]


class Pending:
    def __init__(self, copies, rows):
        self.copies, self.rows, self.done = copies, rows, 0

    def start(self):
        for c in self.copies:
            c.start()

    def upto(self, row):
        while self.done < len(self.copies) and self.done * self.rows < row:
            self.copies[self.done].wait()
            self.done += 1


def scores(scal, diag, first, xs, ts, sim, wgt, sums, need):
    m, n, rows = xs.shape[0], ts.shape[0], xs.shape[0] // 8
    scale, bias, mult, shift = scal[0], scal[1], scal[2], scal[3]
    pieces = [(r, c) for r in range(0, m, TALL) for c in range(0, n, PIECE)]

    def score(r, c):
        need(r + TALL, c + PIECE)
        sim[r : r + TALL, c : c + PIECE] = dot(xs[r : r + TALL, :], ts[c : c + PIECE, :], ((1,), (1,)))

    acc = [jnp.zeros((8, PIECE), F32) for _ in range(3)]
    score(*pieces[0])
    for p, (r, c) in enumerate(pieces):
        if p + 1 < len(pieces):
            score(*pieces[p + 1])
        prod = None
        for i in range(0, TALL, 16):
            s = sim[r + i : r + i + 16, c : c + PIECE]
            e = jnp.exp2(s * mult + shift)
            u = e + 1.0
            r0 = pl.reciprocal(u, approx=True)
            sig = e * (r0 * (2.0 - u * r0))
            wgt[r + i : r + i + 16, c : c + PIECE] = (sig * scale).astype(BF)
            both = u[0:8] * u[8:16]
            prod = both if prod is None else prod * both
            if i % 64 == 48:
                acc[0] = acc[0] + jnp.log(prod)
                prod = None
            ss = sig * s
            acc[1] = acc[1] + (sig[0:8] + sig[8:16])
            acc[2] = acc[2] + (ss[0:8] + ss[8:16])
    for k in range(3):
        sums[8 * k : 8 * k + 8] = acc[k]

    for b in range(8):
        place = diag[b] - first

        @pl.when(jnp.logical_and(place >= 0, place < n // rows))
        def _(b=b, place=place):
            at = (pl.ds(b * rows, rows), pl.ds(pl.multiple_of(place * rows, rows), rows))
            s = sim[at]
            eye = lax.broadcasted_iota(jnp.int32, s.shape, 0) == lax.broadcasted_iota(jnp.int32, s.shape, 1)
            z = scale * s + bias
            w = -scale / (1.0 + jnp.exp(z))
            wgt[at] = jnp.where(eye, w, wgt[at].astype(F32)).astype(BF)
            z = jnp.where(eye, z, 0.0)
            sd = jnp.where(eye, s, 0.0)
            one = jnp.where(eye, 1.0, 0.0)
            for row, v in ((0, z), (8, one), (16, sd)):
                total = v[0:8]
                for k in range(1, rows // 8):
                    total = total + v[8 * k : 8 * k + 8]
                sums[row : row + 8, 0:rows] -= total


def scores_kernel(first, scal, diag, xa, xb, ta, tb, *refs):
    before = refs[:1] if len(refs) == 9 else ()
    wgt, out_sums, xs, ts, sim, sums, xsem, tsem = refs[-8:]
    rows = xa.shape[0] // 4
    x, t = Pending(block_copies((xa, xb), xs, xsem), rows), Pending(block_copies((ta, tb), ts, tsem), rows)
    for n in range(8):
        t.copies[n].start()
        x.copies[n].start()

    def need(r, c):
        x.upto(r)
        t.upto(c)

    scores(scal, diag, first, xs, ts, sim, wgt, sums, need)
    if before:
        total = sums[...] + before[0][...]
        lane = lax.broadcasted_iota(jnp.int32, (8, 128), 1)
        out = jnp.zeros((8, 128), F32)
        for k in range(3):
            out = jnp.where(lane == k, jnp.sum(total[8 * k : 8 * k + 8], keepdims=True), out)
        out_sums[...] = out[0:1]
    else:
        out_sums[...] = sums[...]


def score_half(first, scal, diag, images, texts, before=()):
    rows, d = images[0].shape[0] // 4, images[0].shape[1]
    m = n = 8 * rows
    return pl.pallas_call(
        lambda *refs: scores_kernel(first, *refs),
        in_specs=[SM, SM] + [ANY] * 4 + [VM] * len(before),
        out_specs=[VM, VM],
        out_shape=(sds((m, n), BF), sds((1, 128) if before else (24, PIECE), F32)),
        scratch_shapes=[
            pltpu.VMEM((m, d), BF),
            pltpu.VMEM((n, d), BF),
            pltpu.VMEM((m, n), F32),
            pltpu.VMEM((24, PIECE), F32),
            pltpu.SemaphoreType.DMA((8,)),
            pltpu.SemaphoreType.DMA((8,)),
        ],
        compiler_params=params(),
        cost_estimate=pl.CostEstimate(
            flops=2 * m * n * d, bytes_accessed=(m + n) * d * 2, transcendentals=3 * m * n
        ),
        name="scores",
    )(scal, diag, *images, *texts, *before)


def far_kernel(dims, l0, l1, r0a, r0b, r1a, r1b, out, lhs, rhs, lsem, s0, s1):
    n = rhs.shape[0] // 2
    p0 = Pending(block_copies((r0a, r0b), rhs, s0), n // 8)
    p1 = Pending(block_copies((r1a, r1b), rhs, s1, n), n // 8)
    cut = (pl.ds(0, STRIP), slice(None)) if dims == 1 else (slice(None), pl.ds(0, STRIP))
    lc = [pltpu.make_async_copy(l.at[cut], lhs.at[k], lsem.at[k]) for k, l in enumerate((l0, l1))]
    lc[0].start()
    p0.start()
    lc[1].start()
    p1.start()
    lc[0].wait()
    p0.upto(n)
    part = dot(lhs[0], rhs[:n, :], ((dims,), (0,)))
    lc[1].wait()
    p1.upto(n)
    out[...] = encode(part + dot(lhs[1], rhs[n:, :], ((dims,), (0,))))


def far_pull(dims, w0, w1, rows0, rows1, name):
    d = rows0[0].shape[1]
    n = w0.shape[dims]
    return pl.pallas_call(
        lambda *refs: far_kernel(dims, *refs),
        in_specs=[ANY] * 6,
        out_specs=VM,
        out_shape=sds((STRIP, d), BF),
        scratch_shapes=[
            pltpu.VMEM((2, STRIP, n) if dims == 1 else (2, n, STRIP), BF),
            pltpu.VMEM((2 * n, d), BF),
            pltpu.SemaphoreType.DMA((2,)),
            pltpu.SemaphoreType.DMA((8,)),
            pltpu.SemaphoreType.DMA((8,)),
        ],
        compiler_params=params(),
        cost_estimate=pl.CostEstimate(
            flops=4 * STRIP * n * d, bytes_accessed=4 * n * d + 4 * STRIP * n, transcendentals=0
        ),
        name=name,
    )(w0, w1, *rows0, *rows1)


def near_kernel(dims, l0, l1, r0a, r0b, r1a, r1b, *refs):
    o1, o3, own, w0, w1, rhs, pull, lsem, s0, s1 = refs
    n = rhs.shape[0] // 2
    p0 = Pending(block_copies((r0a, r0b), rhs, s0), n // 8)
    p1 = Pending(block_copies((r1a, r1b), rhs, s1, n), n // 8)
    lc = [pltpu.make_async_copy(s, w, lsem.at[k]) for k, (s, w) in enumerate(((l0, w0), (l1, w1)))]
    lc[0].start()
    p0.start()
    lc[1].start()
    p1.start()
    groups = [slice(SLOT[k] * STRIP, (SLOT[k] + 1) * STRIP) for k in (1, 3, 0)]
    cut = (lambda w, at: w[at, :]) if dims == 1 else (lambda w, at: w[:, at])
    lc[0].wait()
    p0.upto(n)
    for k, at in enumerate(groups):
        pull[k] = dot(cut(w0, at), rhs[:n, :], ((dims,), (0,)))
    lc[1].wait()
    p1.upto(n)
    for k, at in enumerate(groups):
        total = pull[k] + dot(cut(w1, at), rhs[n:, :], ((dims,), (0,)))
        (o1, o3, own)[k][...] = encode(total) if k < 2 else total


def near_pulls(dims, w0, w1, rows0, rows1, name):
    m, d = w0.shape[0], rows0[0].shape[1]
    return pl.pallas_call(
        lambda *refs: near_kernel(dims, *refs),
        in_specs=[ANY] * 6,
        out_specs=[VM] * 3,
        out_shape=(sds((STRIP, d), BF), sds((STRIP, d), BF), sds((STRIP, d), F32)),
        scratch_shapes=[pltpu.VMEM((m, m), BF)] * 2
        + [pltpu.VMEM((2 * m, d), BF), pltpu.VMEM((3, STRIP, d), F32), pltpu.SemaphoreType.DMA((2,))]
        + [pltpu.SemaphoreType.DMA((8,))] * 2,
        compiler_params=params(),
        cost_estimate=pl.CostEstimate(
            flops=3 * m * m * d, bytes_accessed=4 * m * d + 4 * m * m, transcendentals=0
        ),
        name=name,
    )(w0, w1, *rows0, *rows1)


def partner_kernel(own, c1, c2, c3, out):
    out[...] = encode(own[...] + decode(c1[...]) + decode(c2[...]) + decode(c3[...]))


def fold_partner(own, *codes):
    rows, d = own.shape[0] // 2, own.shape[1]
    half = pl.BlockSpec((rows, d), lambda i: (1, 0))
    return pl.pallas_call(
        partner_kernel,
        grid=(1,),
        in_specs=[half] * 4,
        out_specs=pl.BlockSpec((rows, d), lambda i: (0, 0)),
        out_shape=sds((rows, d), BF),
        compiler_params=params(),
        name="fold_partner",
    )(own, *codes)


def own_kernel(own, c1, c2, c3, out):
    out[...] = own[...] + decode(c1[...]) + decode(c2[...]) + decode(c3[...])


def fold_own(own, *codes):
    rows, d = own.shape[0] // 2, own.shape[1]
    half = pl.BlockSpec((rows, d), lambda i: (0, 0))
    return pl.pallas_call(
        own_kernel,
        grid=(1,),
        in_specs=[half] * 4,
        out_specs=half,
        out_shape=sds((rows, d), F32),
        compiler_params=params(),
        name="fold_own",
    )(own, *codes)


def finish_kernel(x_ref, own, code_ref, out_ref):
    x = x_ref[...]
    norm = jnp.sqrt(jnp.sum(x * x, axis=1, keepdims=True) + 1e-06)
    hat = x / norm
    pull = own[...] + decode(code_ref[...])
    out_ref[...] = (pull - hat * jnp.sum(hat * pull, axis=1, keepdims=True)) / norm


def finish(x, own, code):
    return pl.pallas_call(
        finish_kernel, out_shape=sds(x.shape, F32), compiler_params=params(), name="finish"
    )(x, own, code)


def img_index(y, z, c):
    return (y % 4) * 4 + (z % 2) * 2 + c % 2


def perm_x(shift):
    return [(i, ((i // 2 + shift) % 4) * 2 + i % 2) for i in range(8)]


def perm_y(shift):
    return [(i, img_index(i // 4 + shift, i // 2, i)) for i in range(16)]


PERM_ZHI = [(i, i ^ 1) for i in range(8)]
PERM_ZLO = [(i, i ^ 2) for i in range(16)]
PERM_CORE = [(i, i ^ 1) for i in range(16)]
send = lax.ppermute


def after(x, *others):
    return lax.optimization_barrier((x, *others))[0]


def gather(low, axis, perm, perm_z):
    a1, a3 = send(low, axis, perm(1)), send(low, axis, perm(-1))
    z = send(low, axis, perm_z)
    a2 = send(a1, axis, perm(1))
    z1, z3 = send(z, axis, perm(1)), send(z, axis, perm(-1))
    z2 = send(z3, axis, perm(-1))
    return jnp.concatenate([low, a1, a3, a2], 0), jnp.concatenate([z, z1, z3, z2], 0)


def exchange_sum(v, axis, bit):
    size = {"img": 16, "txt": 8}[axis]
    return v + send(v, axis, [(i, i ^ bit) for i in range(size)])


def local(image_embed, text_embed, log_scale, logit_bias):
    rows, d = image_embed.shape
    image_low, text_low = normalize(image_embed, text_embed)
    images = gather(image_low, "txt", perm_x, PERM_ZHI)
    own = gather(text_low, "img", perm_y, PERM_ZLO)
    other = [send(t, "img", PERM_CORE) for t in own]
    partner = [send(x, "img", PERM_CORE) for x in images]

    i, t = lax.axis_index("img"), lax.axis_index("txt")
    b = jnp.arange(8, dtype=jnp.int32)
    slot = b // 2
    ring = jnp.where(slot == 0, 2, jnp.where(slot == 1, 1, jnp.where(slot == 2, 3, 0)))
    g = 8 * i + ((t // 2 - ring) % 4) * 2 + ((t % 2) ^ (b % 2))
    o = g % 16
    k = (i // 4 - o // 4) % 4
    slot = jnp.where(k == 2, 0, jnp.where(k == 1, 1, jnp.where(k == 3, 2, 3)))
    mine = 1 - ((i % 2) ^ (o % 2))
    place = mine * 8 + slot * 2 + (((i // 2) % 2) ^ ((o // 2) % 2))
    diag = jnp.where(g // 16 == t, place, -1).astype(jnp.int32)
    scale = jnp.exp(log_scale)
    scal = jnp.stack([scale, logit_bias, scale * LOG2E, logit_bias * LOG2E])

    w_oth, sums = score_half(0, scal, diag, images, other)
    w_rec = send(w_oth, "img", PERM_CORE)
    w_own, v = score_half(8, scal, diag, images, own, (sums,))

    u = exchange_sum(v, "img", 4)
    i2 = far_pull(1, w_own, w_oth, own, other, "far_image")
    u = after(u, i2)
    i2 = send(i2, "txt", perm_x(2))
    v = exchange_sum(u, "img", 8)
    t2 = far_pull(0, after(w_own, u), w_rec, images, partner, "far_text")
    v = after(v, t2)
    t2 = send(t2, "img", perm_y(2))
    u = exchange_sum(v, "img", 2)
    i1, i3, i0 = near_pulls(1, after(w_own, v), w_oth, own, other, "near_image")
    u = after(u, i0)
    i1, i3 = after(i1, i2), after(i3, i2)
    i1, i3 = send(i1, "txt", perm_x(-1)), send(i3, "txt", perm_x(1))
    v = exchange_sum(u, "txt", 1)
    t1, t3, t0 = near_pulls(0, after(w_own, u), w_rec, images, partner, "near_text")
    v = after(v, t0)
    t1, t3 = after(t1, t2), after(t3, t2)
    t1, t3 = send(t1, "img", perm_y(-1)), send(t3, "img", perm_y(1))
    v = exchange_sum(v, "img", 1)
    v = after(v, i1, i3)
    v = exchange_sum(exchange_sum(v, "txt", 2), "txt", 4)
    t0 = after(t0, v)

    icodes, tcodes = (i1, i2, i3), (t1, t2, t3)
    image_code = send(fold_partner(i0, *icodes), "txt", PERM_ZHI)
    text_code = send(fold_partner(t0, *tcodes), "img", PERM_ZLO)
    image_grad = finish(image_embed, fold_own(i0, *icodes), image_code)
    text_grad = finish(text_embed, fold_own(t0, *tcodes), text_code)
    pairs = F32(128.0 * rows) * F32(128.0 * rows)
    return (v[0, 0] / pairs, image_grad, text_grad, v[0, 2] * scale / pairs, v[0, 1] / pairs)


def solution(mesh):
    placed = (P(("img", "txt"), None), P(("txt", "img"), None), P(), P())
    return jax.shard_map(
        local,
        mesh=mesh,
        in_specs=placed,
        out_specs=(P(), P(("img", "txt"), None), P(("txt", "img"), None), P(), P()),
        check_vma=False,
    )
```

time: 376 us -> 159 us (0.42)
  waiting for transfers between devices: 197 us -> 39 us
  blocking collectives: 75.2 us -> 0 us
  Pallas kernels: 0 us -> 62 us
  matrix products: 48.4 us -> 0 us
  starting transfers between devices: 0.35 us -> 38.4 us
  other arithmetic: 22.9 us -> 1.18 us
  between operations: 19.9 us -> 7.75 us
    reduce_scatter x2 -> x0, waiting for transfers between devices: 101 us -> none  [the longest x1 101 us: local(): text_pull = lax.psum_scatter(terms, 'img', scatter_dimension=0, tiled=True)]
    all_gather x2 -> x0, waiting for transfers between devices: 95.3 us -> none  [the longest x1 56 us: local(): lax.all_gather(image_hat.astype(jnp.bfloat16), 'txt', axis=0, tiled=True)]
    psum x1 -> x0, blocking collectives: 75.2 us -> none  [local(): lax.psum((jnp.sum(totals), jnp.sum(scale_parts), jnp.sum(bias_parts)), ('...]
    pallas_call x0 -> x13, Pallas kernels: none -> 62 us  [the longest x2 17.2 us: near_pulls(): pl.pallas_call(lambda *refs: near_kernel(dims, *refs), in_specs=[ANY] * 6...]
    dot_general x5 -> x0, matrix products: 48.4 us -> none  [the longest x2 25.3 us: score(): similar = jnp.dot(rows, text_block.T, preferred_element_type=jnp.float32)]
    ppermute x0 -> x34, waiting for transfers between devices: none -> 39 us  [the longest x7 13.2 us: exchange_sum(): return v + send(v, axis, [(i, i ^ bit) for i in range(size)])]
    ppermute x0 -> x34, starting transfers between devices: none -> 38.4 us  [the longest x7 7.55 us: exchange_sum(): return v + send(v, axis, [(i, i ^ bit) for i in range(size)])]
    dynamic_update_slice x2 -> x0, other arithmetic: 8.3 us -> none  [local(): lax.map(score, jnp.arange(count, dtype=jnp.int32))]
  transfers between devices with their start and end apart: 4 -> 34, of which waited for: 3 -> 12; matrix products, arithmetic and copies ran while one was open for 5% -> 2% of each run, Pallas kernels for 0% -> 31%
where the time goes in v3:
time: 159 us; the launch traced here: 158 us
  Pallas kernels  62 us (39%)
  waiting for transfers between devices  39 us (25%)
  starting transfers between devices  38.4 us (24%)
  local copies, waits for them, and re-layouts  9.34 us (6%)
  between operations  7.75 us (5%)
    pallas_call x2, Pallas kernels, near_pulls(): pl.pallas_call(lambda *refs: near_kernel(dims, *refs), in_specs=[ANY] * 6...  17.2 us
    pallas_call x2, Pallas kernels, score_half(): pl.pallas_call(lambda *refs: scores_kernel(first, *refs), in_specs=[SM, S...  16.8 us
    ppermute x7, waiting for transfers between devices, exchange_sum(): return v + send(v, axis, [(i, i ^ bit) for i in range(size)])  13.2 us
    pallas_call x2, Pallas kernels, far_pull(): pl.pallas_call(lambda *refs: far_kernel(dims, *refs), in_specs=[ANY] * 6,...  10.3 us
    ppermute x2, waiting for transfers between devices, gather(): a2 = send(a1, axis, perm(1))  9.26 us
    unnamed x47, local copies, waits for them, and re-layouts  8.63 us
    ppermute x4, waiting for transfers between devices, gather(): z1, z3 = (send(z, axis, perm(1)), send(z, axis, perm(-1)))  8.46 us
    ppermute x7, starting transfers between devices, exchange_sum(): return v + send(v, axis, [(i, i ^ bit) for i in range(size)])  7.55 us
  transfers between devices with their start and end apart: 34, of which 12 were waited for; matrix products, arithmetic and copies ran while one was open for 2% of the time, Pallas kernels for 31%

profile of v3, /device:TPU:0, one launch (start us, length us, event | category | flops | bytes accessed | tf_op | source)
XLA Modules:
  0.0 157.7 jit_solution(8646623826217659535)
XLA Ops:
  0.6 2.2 %normalize.1 = (bf16[128,1152]{1,0:T(8,128)(2,1)}, bf16[128,1152]{1,0:T(8,128)(2,1)}) custom-call(f32[128,1152]{1,0:T(8,128)} %x_ref.2, f32[128,1152]{1,0:T(8,128)} %x_ref.3), custom_call_target="tpu_custom_call" | custom-call | tf_op jit(solution)/shard_map/normalize/pallas_call | solution.py:50
  2.8 4.0 %collective-permute-start.3 = (bf16[128,1152]{1,0:T(8,128)(2,1)}, bf16[128,1152]{1,0:T(8,128)(2,1)S(1)}, u32[]{:S(2)}, u32[]{:S(2)}) collective-permute-start(bf16[128,1152]{1,0:T(8,128)(2,1)} %get-tuple-element.30), channel_id=1, source_target_pairs={{0,1},{1,0},{2,3},{3,2},{4,5},{5,4},{6,7},{7,6},{8,9},{9,8},{10,11... | collective-permute-start | bytes 884744 | tf_op jit(solution)/shard_map/ppermute | solution.py:343
  6.8 2.8 %collective-permute-start.1 = (bf16[128,1152]{1,0:T(8,128)(2,1)}, bf16[128,1152]{1,0:T(8,128)(2,1)S(1)}, u32[]{:S(2)}, u32[]{:S(2)}) collective-permute-start(bf16[128,1152]{1,0:T(8,128)(2,1)} %get-tuple-element.30), channel_id=1, source_target_pairs={{0,6},{1,7},{2,0},{3,1},{4,2},{5,3},{6,4},{7,5},{8,14},{9,15},{10,... | collective-permute-start | bytes 884744 | tf_op jit(solution)/shard_map/ppermute | solution.py:342
  9.6 1.0 collective-permute-start.10
  10.6 3.0 %collective-permute-start.8 = (bf16[128,1152]{1,0:T(8,128)(2,1)}, bf16[128,1152]{1,0:T(8,128)(2,1)S(1)}, u32[]{:S(2)}, u32[]{:S(2)}) collective-permute-start(bf16[128,1152]{1,0:T(8,128)(2,1)} %get-tuple-element.31), channel_id=1, source_target_pairs={{0,96},{8,104},{16,112},{24,120},{32,0},{40,8},{48,16},{56,24},{64... | collective-permute-start | bytes 884744 | tf_op jit(solution)/shard_map/ppermute | solution.py:342
  15.0 0.6 pad_maximum_fusion.refs_0_
  15.6 1.1 constant_dynamic-update-slice_fusion.3
  16.7 0.6 compare_select_fusion.9.refs_1_
  17.3 3.8 %collective-permute-done.10 = bf16[128,1152]{1,0:T(8,128)(2,1)S(1)} collective-permute-done((bf16[128,1152]{1,0:T(8,128)(2,1)}, bf16[128,1152]{1,0:T(8,128)(2,1)S(1)}, u32[]{:S(2)}, u32[]{:S(2)}) %collective-permute-start.10) | collective-permute-done | bytes 294944 | tf_op jit(solution)/shard_map/ppermute | solution.py:343
  21.1 2.8 %collective-permute-start.5 = (bf16[128,1152]{1,0:T(8,128)(2,1)S(1)}, bf16[128,1152]{1,0:T(8,128)(2,1)S(1)}, u32[]{:S(2)}, u32[]{:S(2)}) collective-permute-start(bf16[128,1152]{1,0:T(8,128)(2,1)S(1)} %collective-permute-done.3), channel_id=1, source_target_pairs={{0,6},{1,7},{2,0},{3,1},{4,2},{5,3},{6,4},{7,5},{8,14},{9,15},{10,... | collective-permute-start | bytes 884744 | tf_op jit(solution)/shard_map/ppermute | solution.py:345
  23.9 3.1 %collective-permute-start.12 = (bf16[128,1152]{1,0:T(8,128)(2,1)S(1)}, bf16[128,1152]{1,0:T(8,128)(2,1)S(1)}, u32[]{:S(2)}, u32[]{:S(2)}) collective-permute-start(bf16[128,1152]{1,0:T(8,128)(2,1)S(1)} %collective-permute-done.10), channel_id=1, source_target_pairs={{0,96},{8,104},{16,112},{24,120},{32,0},{40,8},{48,16},{56,24},{64... | collective-permute-start | bytes 884744 | tf_op jit(solution)/shard_map/ppermute | solution.py:345
  27.0 0.1 collective-permute-start.11
  27.1 0.1 collective-permute-start.4
  27.2 4.8 %collective-permute-done.12 = bf16[128,1152]{1,0:T(8,128)(2,1)S(1)} collective-permute-done((bf16[128,1152]{1,0:T(8,128)(2,1)S(1)}, bf16[128,1152]{1,0:T(8,128)(2,1)S(1)}, u32[]{:S(2)}, u32[]{:S(2)}) %collective-permute-start.12) | collective-permute-done | bytes 294944 | tf_op jit(solution)/shard_map/ppermute | solution.py:345
  32.1 1.0 collective-permute-start.9
  33.1 3.6 %collective-permute-done.11 = bf16[128,1152]{1,0:T(8,128)(2,1)S(1)} collective-permute-done((bf16[128,1152]{1,0:T(8,128)(2,1)S(1)}, bf16[128,1152]{1,0:T(8,128)(2,1)S(1)}, u32[]{:S(2)}, u32[]{:S(2)}) %collective-permute-start.11) | collective-permute-done | bytes 294944 | tf_op jit(solution)/shard_map/ppermute | solution.py:345
  36.8 5.1 %collective-permute-done.9 = bf16[128,1152]{1,0:T(8,128)(2,1)S(1)} collective-permute-done((bf16[128,1152]{1,0:T(8,128)(2,1)S(1)}, bf16[128,1152]{1,0:T(8,128)(2,1)S(1)}, u32[]{:S(2)}, u32[]{:S(2)}) %collective-permute-start.9) | collective-permute-done | bytes 294944 | tf_op jit(solution)/shard_map/ppermute | solution.py:344
  42.0 1.5 collective-permute-done.13
  43.5 0.6 collective-permute-start.15
  44.2 2.0 %collective-permute-start.6 = (bf16[128,1152]{1,0:T(8,128)(2,1)S(1)}, bf16[128,1152]{1,0:T(8,128)(2,1)S(1)}, u32[]{:S(2)}, u32[]{:S(2)}) collective-permute-start(bf16[128,1152]{1,0:T(8,128)(2,1)S(1)} %collective-permute-done.5), channel_id=1, source_target_pairs={{0,6},{1,7},{2,0},{3,1},{4,2},{5,3},{6,4},{7,5},{8,14},{9,15},{10,... | collective-permute-start | bytes 884744 | tf_op jit(solution)/shard_map/ppermute | solution.py:346
  46.2 4.2 %collective-permute-done.2 = bf16[128,1152]{1,0:T(8,128)(2,1)S(1)} collective-permute-done((bf16[128,1152]{1,0:T(8,128)(2,1)S(1)}, bf16[128,1152]{1,0:T(8,128)(2,1)S(1)}, u32[]{:S(2)}, u32[]{:S(2)}) %collective-permute-start.2) | collective-permute-done | bytes 294944 | tf_op jit(solution)/shard_map/ppermute | solution.py:344
  50.4 2.7 %collective-permute-done.6 = bf16[128,1152]{1,0:T(8,128)(2,1)S(1)} collective-permute-done((bf16[128,1152]{1,0:T(8,128)(2,1)S(1)}, bf16[128,1152]{1,0:T(8,128)(2,1)S(1)}, u32[]{:S(2)}, u32[]{:S(2)}) %collective-permute-start.6) | collective-permute-done | bytes 294944 | tf_op jit(solution)/shard_map/ppermute | solution.py:346
  53.2 1.0 copy-done.7
  54.2 0.4 copy-done.11
  54.6 8.3 %scores.2 = (bf16[1024,1024]{1,0:T(8,128)(2,1)}, f32[24,512]{1,0:T(8,128)}) custom-call(f32[4]{0:T(128)} %pad_maximum_fusion.refs_0_, s32[8]{0:T(128)} %compare_select_fusion.9.refs_1_, bf16[512,1152]{1,0:T(8,128)(2,1)} %copy-done.10, bf16[512,1152]{1,0:T(8,128)(2,1)} %copy-done.7, bf16[512,1152]{1,0:T(8,128)(2,1)} %copy-done.11, ...), custom_call_target="tpu_custom_call" | custom-call | flops 2415919104 | bytes 4718592 | tf_op jit(solution)/shard_map/scores/pallas_call | solution.py:166
  63.0 0.1 collective-permute-start.18
  63.1 0.5 collective-permute-start.19
  63.6 0.1 collective-permute-start.20
  63.7 8.5 %scores.3 = (bf16[1024,1024]{1,0:T(8,128)(2,1)}, f32[1,128]{1,0:T(1,128)}) custom-call(f32[4]{0:T(128)} %pad_maximum_fusion.refs_0_, s32[8]{0:T(128)} %compare_select_fusion.9.refs_1_, bf16[512,1152]{1,0:T(8,128)(2,1)} %copy-done.10, bf16[512,1152]{1,0:T(8,128)(2,1)} %copy-done.7, bf16[512,1152]{1,0:T(8,128)(2,1)} %copy-done.9, bf16[512,1152]{1,0:T(8,128)(2,1)} %copy-done.8, ...), custom_call_target="tpu_custom_call" | custom-call | flops 2415919104 | bytes 4718592 | tf_op jit(solution)/shard_map/scores/pallas_call | solution.py:166
  72.1 5.1 %far_image.1 = bf16[256,1152]{1,0:T(8,128)(2,1)} custom-call(bf16[1024,1024]{1,0:T(8,128)(2,1)} %get-tuple-element.42.refs_0_, bf16[1024,1024]{1,0:T(8,128)(2,1)} %get-tuple-element.35.refs_1_, bf16[512,1152]{1,0:T(8,128)(2,1)} %copy-done.9, bf16[512,1152]{1,0:T(8,128)(2,1)} %copy-done.8, bf16[512,1152]{1,0:T(8,128)(2,1)} %copy-done.11, ...), custom_call_target="tpu_custom_call" | custom-call | flops 1207959552 | bytes 5767168 | tf_op jit(solution)/shard_map/far_image/pallas_call | solution.py:208
  77.3 1.4 collective-permute-start.24
  78.6 3.5 %collective-permute-done.16 = f32[1,128]{1,0:T(1,128)S(1)} collective-permute-done((f32[1,128]{1,0:T(1,128)S(1)}, f32[1,128]{1,0:T(1,128)S(1)}, u32[]{:S(2)}, u32[]{:S(2)}) %collective-permute-start.16) | collective-permute-done | bytes 544 | tf_op jit(solution)/shard_map/ppermute | solution.py:352
  82.2 0.7 collective-permute-start.17
  82.8 4.4 %collective-permute-done.17 = f32[1,128]{1,0:T(1,128)S(1)} collective-permute-done((f32[1,128]{1,0:T(1,128)S(1)}, f32[1,128]{1,0:T(1,128)S(1)}, u32[]{:S(2)}, u32[]{:S(2)}) %collective-permute-start.17) | collective-permute-done | bytes 544 | tf_op jit(solution)/shard_map/ppermute | solution.py:352
  87.3 1.0 copy-done.12
  88.3 0.4 copy-done.13
  88.7 1.4 copy-done.6
  90.0 5.2 %far_text.1 = bf16[256,1152]{1,0:T(8,128)(2,1)} custom-call(bf16[1024,1024]{1,0:T(8,128)(2,1)} %get-tuple-element.42.refs_0_, bf16[1024,1024]{1,0:T(8,128)(2,1)} %copy-done.6, bf16[512,1152]{1,0:T(8,128)(2,1)} %copy-done.10, bf16[512,1152]{1,0:T(8,128)(2,1)} %copy-done.7, bf16[512,1152]{1,0:T(8,128)(2,1)} %copy-done.12, bf16[512,1152]{1,0:T(8,128)(2,1)} %copy-done.13), custom_call_target="tpu_custom_call" | custom-call | flops 1207959552 | bytes 5767168 | tf_op jit(solution)/shard_map/far_text/pallas_call | solution.py:208
  95.2 1.1 collective-permute-start.21
  96.3 0.6 collective-permute-start.30
  96.9 8.5 %near_image.1 = (bf16[256,1152]{1,0:T(8,128)(2,1)}, bf16[256,1152]{1,0:T(8,128)(2,1)}, f32[256,1152]{1,0:T(8,128)}) custom-call(bf16[1024,1024]{1,0:T(8,128)(2,1)} %get-tuple-element.42.refs_0_, bf16[1024,1024]{1,0:T(8,128)(2,1)} %get-tuple-element.35.refs_1_, bf16[512,1152]{1,0:T(8,128)(2,1)} %copy-done.9, bf16[512,1152]{1,0:T(8,128)(2,1)} %copy-done.8, ...), custom_call_target="tpu_custom_call" | custom-call | flops 3623878656 | bytes 8912896 | tf_op jit(solution)/shard_map/near_image/pallas_call | solution.py:253
  105.5 2.6 %collective-permute-start.26 = (bf16[256,1152]{1,0:T(8,128)(2,1)}, bf16[256,1152]{1,0:T(8,128)(2,1)S(1)}, u32[]{:S(2)}, u32[]{:S(2)}) collective-permute-start(bf16[256,1152]{1,0:T(8,128)(2,1)} %get-tuple-element.48), channel_id=1, source_target_pairs={{0,2},{1,3},{2,4},{3,5},{4,6},{5,7},{6,0},{7,1},{8,10},{9,11},{10,... | collective-permute-start | bytes 1769480 | tf_op jit(solution)/shard_map/ppermute | solution.py:393
  108.1 0.9 collective-permute-start.25
  109.0 8.7 %near_text.1 = (bf16[256,1152]{1,0:T(8,128)(2,1)}, bf16[256,1152]{1,0:T(8,128)(2,1)}, f32[256,1152]{1,0:T(8,128)}) custom-call(bf16[1024,1024]{1,0:T(8,128)(2,1)} %get-tuple-element.42.refs_0_, bf16[1024,1024]{1,0:T(8,128)(2,1)} %copy-done.6, bf16[512,1152]{1,0:T(8,128)(2,1)} %copy-done.10, bf16[512,1152]{1,0:T(8,128)(2,1)} %copy-done.7, ...), custom_call_target="tpu_custom_call" | custom-call | flops 3623878656 | bytes 8912896 | tf_op jit(solution)/shard_map/near_text/pallas_call | solution.py:253
  117.7 2.1 %collective-permute-start.31 = (bf16[256,1152]{1,0:T(8,128)(2,1)}, bf16[256,1152]{1,0:T(8,128)(2,1)S(1)}, u32[]{:S(2)}, u32[]{:S(2)}) collective-permute-start(bf16[256,1152]{1,0:T(8,128)(2,1)} %get-tuple-element.52), channel_id=1, source_target_pairs={{0,96},{8,104},{16,112},{24,120},{32,0},{40,8},{48,16},{56,24},{64... | collective-permute-start | bytes 1769480 | tf_op jit(solution)/shard_map/ppermute | solution.py:398
  119.8 3.3 %collective-permute-start.22 = (f32[1,128]{1,0:T(1,128)S(1)}, f32[1,128]{1,0:T(1,128)S(1)}, u32[]{:S(2)}, u32[]{:S(2)}) collective-permute-start(f32[1,128]{1,0:T(1,128)S(1)} %add.95), channel_id=1, source_target_pairs={{0,1},{1,0},{2,3},{3,2},{4,5},{5,4},{6,7},{7,6},{8,9},{9,8},{10,11... | collective-permute-start | bytes 1544 | tf_op jit(solution)/shard_map/ppermute | solution.py:352
  123.2 1.7 %collective-permute-done.22 = f32[1,128]{1,0:T(1,128)S(1)} collective-permute-done((f32[1,128]{1,0:T(1,128)S(1)}, f32[1,128]{1,0:T(1,128)S(1)}, u32[]{:S(2)}, u32[]{:S(2)}) %collective-permute-start.22) | collective-permute-done | bytes 544 | tf_op jit(solution)/shard_map/ppermute | solution.py:352
  124.9 1.1 collective-permute-done.23
  126.1 1.2 collective-permute-start.27
  127.3 2.4 %collective-permute-done.27 = f32[1,128]{1,0:T(1,128)S(1)} collective-permute-done((f32[1,128]{1,0:T(1,128)S(1)}, f32[1,128]{1,0:T(1,128)S(1)}, u32[]{:S(2)}, u32[]{:S(2)}) %collective-permute-start.27) | collective-permute-done | bytes 544 | tf_op jit(solution)/shard_map/ppermute | solution.py:352
  129.7 1.3 collective-permute-start.28
  130.9 2.6 %fold_partner.2 = bf16[128,1152]{1,0:T(8,128)(2,1)} custom-call(f32[256,1152]{1,0:T(8,128)} %get-tuple-element.40.own, bf16[256,1152]{1,0:T(8,128)(2,1)} %copy-done.4, bf16[256,1152]{1,0:T(8,128)(2,1)} %copy-done, bf16[256,1152]{1,0:T(8,128)(2,1)} %copy-done.2), custom_call_target="tpu_custom_call" | custom-call | tf_op jit(solution)/shard_map/fold_partner/pallas_call | solution.py:276
  133.5 2.1 %collective-permute-start.29 = (bf16[128,1152]{1,0:T(8,128)(2,1)}, bf16[128,1152]{1,0:T(8,128)(2,1)S(1)}, u32[]{:S(2)}, u32[]{:S(2)}) collective-permute-start(bf16[128,1152]{1,0:T(8,128)(2,1)} %fold_partner.2), channel_id=1, source_target_pairs={{0,1},{1,0},{2,3},{3,2},{4,5},{5,4},{6,7},{7,6},{8,9},{9,8},{10,11... | collective-permute-start | bytes 884744 | tf_op jit(solution)/shard_map/ppermute | solution.py:405
  135.7 0.8 copy-done.3
  136.5 0.8 copy-done.5
  137.3 2.6 %fold_partner.3 = bf16[128,1152]{1,0:T(8,128)(2,1)} custom-call(f32[256,1152]{1,0:T(8,128)} %get-tuple-element.50.own, bf16[256,1152]{1,0:T(8,128)(2,1)} %copy-done.3, bf16[256,1152]{1,0:T(8,128)(2,1)} %copy-done.1, bf16[256,1152]{1,0:T(8,128)(2,1)} %copy-done.5), custom_call_target="tpu_custom_call" | custom-call | tf_op jit(solution)/shard_map/fold_partner/pallas_call | solution.py:276
  139.9 0.1 collective-permute-start.33
  140.0 2.6 %fold_own.2.own = f32[128,1152]{1,0:T(8,128)} custom-call(f32[256,1152]{1,0:T(8,128)} %get-tuple-element.40.own, bf16[256,1152]{1,0:T(8,128)(2,1)} %copy-done.4, bf16[256,1152]{1,0:T(8,128)(2,1)} %copy-done, bf16[256,1152]{1,0:T(8,128)(2,1)} %copy-done.2), custom_call_target="tpu_custom_call" | custom-call | tf_op jit(solution)/shard_map/fold_own/pallas_call | solution.py:294
  142.6 0.6 fusion.15
  145.2 0.7 copy-done.15
  145.9 2.5 %finish.2 = f32[128,1152]{1,0:T(8,128)} custom-call(f32[128,1152]{1,0:T(8,128)} %x_ref.2, f32[128,1152]{1,0:T(8,128)} %fold_own.2.own, bf16[128,1152]{1,0:T(8,128)(2,1)} %copy-done.15), custom_call_target="tpu_custom_call" | custom-call | tf_op jit(solution)/shard_map/finish/pallas_call | solution.py:314
  148.4 2.6 %fold_own.3.own = f32[128,1152]{1,0:T(8,128)} custom-call(f32[256,1152]{1,0:T(8,128)} %get-tuple-element.50.own, bf16[256,1152]{1,0:T(8,128)(2,1)} %copy-done.3, bf16[256,1152]{1,0:T(8,128)(2,1)} %copy-done.1, bf16[256,1152]{1,0:T(8,128)(2,1)} %copy-done.5), custom_call_target="tpu_custom_call" | custom-call | tf_op jit(solution)/shard_map/fold_own/pallas_call | solution.py:294
  151.0 0.7 copy-done.16
  151.8 2.5 %finish.3 = f32[128,1152]{1,0:T(8,128)} custom-call(f32[128,1152]{1,0:T(8,128)} %x_ref.3, f32[128,1152]{1,0:T(8,128)} %fold_own.3.own, bf16[128,1152]{1,0:T(8,128)(2,1)} %copy-done.16), custom_call_target="tpu_custom_call" | custom-call | tf_op jit(solution)/shard_map/finish/pallas_call | solution.py:314
  (78 shorter events, 0.6 us)
Async XLA Ops:
  2.8 14.4 %copy-start.14 = (bf16[128,1152]{1,0:T(8,128)(2,1)S(1)}, bf16[128,1152]{1,0:T(8,128)(2,1)}, u32[]{:S(2)}) copy-start(bf16[128,1152]{1,0:T(8,128)(2,1)} %get-tuple-element.31) | copy-start | bytes 884740
  2.8 14.4 %collective-permute-start.3 = (bf16[128,1152]{1,0:T(8,128)(2,1)}, bf16[128,1152]{1,0:T(8,128)(2,1)S(1)}, u32[]{:S(2)}, u32[]{:S(2)}) collective-permute-start(bf16[128,1152]{1,0:T(8,128)(2,1)} %get-tuple-element.30), channel_id=1, source_target_pairs={{0,1},{1,0},{2,3},{3,2},{4,5},{5,4},{6,7},{7,6},{8,9},{9,8},{10,11... | collective-permute-start | bytes 884744 | tf_op jit(solution)/shard_map/ppermute | solution.py:343
  6.8 36.7 %collective-permute-start.1 = (bf16[128,1152]{1,0:T(8,128)(2,1)}, bf16[128,1152]{1,0:T(8,128)(2,1)S(1)}, u32[]{:S(2)}, u32[]{:S(2)}) collective-permute-start(bf16[128,1152]{1,0:T(8,128)(2,1)} %get-tuple-element.30), channel_id=1, source_target_pairs={{0,6},{1,7},{2,0},{3,1},{4,2},{5,3},{6,4},{7,5},{8,14},{9,15},{10,... | collective-permute-start | bytes 884744 | tf_op jit(solution)/shard_map/ppermute | solution.py:342
  9.6 14.3 %collective-permute-start = (bf16[128,1152]{1,0:T(8,128)(2,1)}, bf16[128,1152]{1,0:T(8,128)(2,1)S(1)}, u32[]{:S(2)}, u32[]{:S(2)}) collective-permute-start(bf16[128,1152]{1,0:T(8,128)(2,1)} %get-tuple-element.30), channel_id=1, source_target_pairs={{0,2},{1,3},{2,4},{3,5},{4,6},{5,7},{6,0},{7,1},{8,10},{9,11},{10,... | collective-permute-start | bytes 884744 | tf_op jit(solution)/shard_map/ppermute | solution.py:342
  9.6 11.5 %collective-permute-start.10 = (bf16[128,1152]{1,0:T(8,128)(2,1)}, bf16[128,1152]{1,0:T(8,128)(2,1)S(1)}, u32[]{:S(2)}, u32[]{:S(2)}) collective-permute-start(bf16[128,1152]{1,0:T(8,128)(2,1)} %get-tuple-element.31), channel_id=1, source_target_pairs={{0,16},{8,24},{16,0},{24,8},{32,48},{40,56},{48,32},{56,40},{64,80... | collective-permute-start | bytes 884744 | tf_op jit(solution)/shard_map/ppermute | solution.py:343
  10.6 16.5 %collective-permute-start.8 = (bf16[128,1152]{1,0:T(8,128)(2,1)}, bf16[128,1152]{1,0:T(8,128)(2,1)S(1)}, u32[]{:S(2)}, u32[]{:S(2)}) collective-permute-start(bf16[128,1152]{1,0:T(8,128)(2,1)} %get-tuple-element.31), channel_id=1, source_target_pairs={{0,96},{8,104},{16,112},{24,120},{32,0},{40,8},{48,16},{56,24},{64... | collective-permute-start | bytes 884744 | tf_op jit(solution)/shard_map/ppermute | solution.py:342
  17.2 9.8 %collective-permute-start.7 = (bf16[128,1152]{1,0:T(8,128)(2,1)S(1)}, bf16[128,1152]{1,0:T(8,128)(2,1)S(1)}, u32[]{:S(2)}, u32[]{:S(2)}) collective-permute-start(bf16[128,1152]{1,0:T(8,128)(2,1)S(1)} %copy-done.14), channel_id=1, source_target_pairs={{0,32},{8,40},{16,48},{24,56},{32,64},{40,72},{48,80},{56,88},{64,... | collective-permute-start | bytes 884744 | tf_op jit(solution)/shard_map/ppermute | solution.py:342
  21.1 23.1 %collective-permute-start.5 = (bf16[128,1152]{1,0:T(8,128)(2,1)S(1)}, bf16[128,1152]{1,0:T(8,128)(2,1)S(1)}, u32[]{:S(2)}, u32[]{:S(2)}) collective-permute-start(bf16[128,1152]{1,0:T(8,128)(2,1)S(1)} %collective-permute-done.3), channel_id=1, source_target_pairs={{0,6},{1,7},{2,0},{3,1},{4,2},{5,3},{6,4},{7,5},{8,14},{9,15},{10,... | collective-permute-start | bytes 884744 | tf_op jit(solution)/shard_map/ppermute | solution.py:345
  23.9 8.2 %collective-permute-start.12 = (bf16[128,1152]{1,0:T(8,128)(2,1)S(1)}, bf16[128,1152]{1,0:T(8,128)(2,1)S(1)}, u32[]{:S(2)}, u32[]{:S(2)}) collective-permute-start(bf16[128,1152]{1,0:T(8,128)(2,1)S(1)} %collective-permute-done.10), channel_id=1, source_target_pairs={{0,96},{8,104},{16,112},{24,120},{32,0},{40,8},{48,16},{56,24},{64... | collective-permute-start | bytes 884744 | tf_op jit(solution)/shard_map/ppermute | solution.py:345
  27.0 9.7 %collective-permute-start.11 = (bf16[128,1152]{1,0:T(8,128)(2,1)S(1)}, bf16[128,1152]{1,0:T(8,128)(2,1)S(1)}, u32[]{:S(2)}, u32[]{:S(2)}) collective-permute-start(bf16[128,1152]{1,0:T(8,128)(2,1)S(1)} %collective-permute-done.10), channel_id=1, source_target_pairs={{0,32},{8,40},{16,48},{24,56},{32,64},{40,72},{48,80},{56,88},{64,... | collective-permute-start | bytes 884744 | tf_op jit(solution)/shard_map/ppermute | solution.py:345
  27.1 19.0 %collective-permute-start.4 = (bf16[128,1152]{1,0:T(8,128)(2,1)S(1)}, bf16[128,1152]{1,0:T(8,128)(2,1)S(1)}, u32[]{:S(2)}, u32[]{:S(2)}) collective-permute-start(bf16[128,1152]{1,0:T(8,128)(2,1)S(1)} %collective-permute-done.3), channel_id=1, source_target_pairs={{0,2},{1,3},{2,4},{3,5},{4,6},{5,7},{6,0},{7,1},{8,10},{9,11},{10,... | collective-permute-start | bytes 884744 | tf_op jit(solution)/shard_map/ppermute | solution.py:345
  32.1 9.8 %collective-permute-start.9 = (bf16[128,1152]{1,0:T(8,128)(2,1)S(1)}, bf16[128,1152]{1,0:T(8,128)(2,1)S(1)}, u32[]{:S(2)}, u32[]{:S(2)}) collective-permute-start(bf16[128,1152]{1,0:T(8,128)(2,1)S(1)} %collective-permute-done.7), channel_id=1, source_target_pairs={{0,32},{8,40},{16,48},{24,56},{32,64},{40,72},{48,80},{56,88},{64,... | collective-permute-start | bytes 884744 | tf_op jit(solution)/shard_map/ppermute | solution.py:344
  36.7 6.7 %collective-permute-start.13 = (bf16[128,1152]{1,0:T(8,128)(2,1)S(1)}, bf16[128,1152]{1,0:T(8,128)(2,1)S(1)}, u32[]{:S(2)}, u32[]{:S(2)}) collective-permute-start(bf16[128,1152]{1,0:T(8,128)(2,1)S(1)} %collective-permute-done.12), channel_id=1, source_target_pairs={{0,96},{8,104},{16,112},{24,120},{32,0},{40,8},{48,16},{56,24},{64... | collective-permute-start | bytes 884744 | tf_op jit(solution)/shard_map/ppermute | solution.py:346
  41.9 8.5 %collective-permute-start.2 = (bf16[128,1152]{1,0:T(8,128)(2,1)S(1)}, bf16[128,1152]{1,0:T(8,128)(2,1)S(1)}, u32[]{:S(2)}, u32[]{:S(2)}) collective-permute-start(bf16[128,1152]{1,0:T(8,128)(2,1)S(1)} %collective-permute-done), channel_id=1, source_target_pairs={{0,2},{1,3},{2,4},{3,5},{4,6},{5,7},{6,0},{7,1},{8,10},{9,11},{10,... | collective-permute-start | bytes 884744 | tf_op jit(solution)/shard_map/ppermute | solution.py:344
  41.9 4.2 %copy-start.9 = (bf16[512,1152]{1,0:T(8,128)(2,1)}, bf16[512,1152]{1,0:T(8,128)(2,1)S(1)}, u32[]{:S(2)}) copy-start(bf16[512,1152]{1,0:T(8,128)(2,1)S(1)} %constant_dynamic-update-slice_fusion.8.refs_4_.refs_2_) | copy-start | bytes 3538948
  43.5 9.7 %collective-permute-start.14 = (bf16[512,1152]{1,0:T(8,128)(2,1)S(1)}, bf16[512,1152]{1,0:T(8,128)(2,1)S(1)}, u32[]{:S(2)}, u32[]{:S(2)}) collective-permute-start(bf16[512,1152]{1,0:T(8,128)(2,1)S(1)} %constant_dynamic-update-slice_fusion.8.refs_4_.refs_2_), channel_id=1, source_target_pairs={{0,8},{8,0},{16,24},{24,16},{32,40},{40,32},{48,56},{56,48},{64,72... | collective-permute-start | bytes 3538952 | tf_op jit(solution)/shard_map/ppermute | solution.py:360
  43.5 6.9 %copy-start.8 = (bf16[512,1152]{1,0:T(8,128)(2,1)}, bf16[512,1152]{1,0:T(8,128)(2,1)S(1)}, u32[]{:S(2)}) copy-start(bf16[512,1152]{1,0:T(8,128)(2,1)S(1)} %constant_dynamic-update-slice_fusion.12.refs_5_.refs_3_) | copy-start | bytes 3538948
  43.5 9.7 %collective-permute-start.15 = (bf16[512,1152]{1,0:T(8,128)(2,1)S(1)}, bf16[512,1152]{1,0:T(8,128)(2,1)}, u32[]{:S(2)}, u32[]{:S(2)}) collective-permute-start(bf16[512,1152]{1,0:T(8,128)(2,1)S(1)} %constant_dynamic-update-slice_fusion.12.refs_5_.refs_3_), channel_id=1, source_target_pairs={{0,8},{8,0},{16,24},{24,16},{32,40},{40,32},{48,56},{56,48},{64,72... | collective-permute-start | bytes 3538952 | tf_op jit(solution)/shard_map/ppermute | solution.py:360
  44.2 9.0 %collective-permute-start.6 = (bf16[128,1152]{1,0:T(8,128)(2,1)S(1)}, bf16[128,1152]{1,0:T(8,128)(2,1)S(1)}, u32[]{:S(2)}, u32[]{:S(2)}) collective-permute-start(bf16[128,1152]{1,0:T(8,128)(2,1)S(1)} %collective-permute-done.5), channel_id=1, source_target_pairs={{0,6},{1,7},{2,0},{3,1},{4,2},{5,3},{6,4},{7,5},{8,14},{9,15},{10,... | collective-permute-start | bytes 884744 | tf_op jit(solution)/shard_map/ppermute | solution.py:346
  50.4 2.8 %copy-start.10 = (bf16[512,1152]{1,0:T(8,128)(2,1)}, bf16[512,1152]{1,0:T(8,128)(2,1)S(1)}, u32[]{:S(2)}) copy-start(bf16[512,1152]{1,0:T(8,128)(2,1)S(1)} %constant_dynamic-update-slice_fusion.refs_2_) | copy-start | bytes 3538948
  53.2 1.0 copy-start.7
  53.2 1.4 copy-start.11
  63.0 24.3 %collective-permute-start.18 = (bf16[1024,1024]{1,0:T(8,128)(2,1)}, bf16[1024,1024]{1,0:T(8,128)(2,1)S(1)}, u32[]{:S(2)}, u32[]{:S(2)}) collective-permute-start(bf16[1024,1024]{1,0:T(8,128)(2,1)} %get-tuple-element.35.refs_1_), channel_id=1, source_target_pairs={{0,8},{8,0},{16,24},{24,16},{32,40},{40,32},{48,56},{56,48},{64,72... | collective-permute-start | bytes 6291464 | tf_op jit(solution)/shard_map/ppermute | solution.py:378
  63.1 24.2 %collective-permute-start.19 = (bf16[512,1152]{1,0:T(8,128)(2,1)}, bf16[512,1152]{1,0:T(8,128)(2,1)S(1)}, u32[]{:S(2)}, u32[]{:S(2)}) collective-permute-start(bf16[512,1152]{1,0:T(8,128)(2,1)} %copy-done.10), channel_id=1, source_target_pairs={{0,8},{8,0},{16,24},{24,16},{32,40},{40,32},{48,56},{56,48},{64,72... | collective-permute-start | bytes 3538952 | tf_op jit(solution)/shard_map/ppermute | solution.py:361
  63.6 23.7 %collective-permute-start.20 = (bf16[512,1152]{1,0:T(8,128)(2,1)}, bf16[512,1152]{1,0:T(8,128)(2,1)S(1)}, u32[]{:S(2)}, u32[]{:S(2)}) collective-permute-start(bf16[512,1152]{1,0:T(8,128)(2,1)} %copy-done.7), channel_id=1, source_target_pairs={{0,8},{8,0},{16,24},{24,16},{32,40},{40,32},{48,56},{56,48},{64,72... | collective-permute-start | bytes 3538952 | tf_op jit(solution)/shard_map/ppermute | solution.py:361
  72.1 6.5 %copy-start.17 = (f32[1,128]{1,0:T(1,128)S(1)}, f32[1,128]{1,0:T(1,128)}, u32[]{:S(2)}) copy-start(f32[1,128]{1,0:T(1,128)} %get-tuple-element.33) | copy-start | bytes 1540
  77.3 28.2 %collective-permute-start.24 = (bf16[256,1152]{1,0:T(8,128)(2,1)}, bf16[256,1152]{1,0:T(8,128)(2,1)S(1)}, u32[]{:S(2)}, u32[]{:S(2)}) collective-permute-start(bf16[256,1152]{1,0:T(8,128)(2,1)} %far_image.1), channel_id=1, source_target_pairs={{0,4},{1,5},{2,6},{3,7},{4,0},{5,1},{6,2},{7,3},{8,12},{9,13},{10,... | collective-permute-start | bytes 1769480 | tf_op jit(solution)/shard_map/ppermute | solution.py:384
  78.6 3.5 %collective-permute-start.16 = (f32[1,128]{1,0:T(1,128)S(1)}, f32[1,128]{1,0:T(1,128)S(1)}, u32[]{:S(2)}, u32[]{:S(2)}) collective-permute-start(f32[1,128]{1,0:T(1,128)S(1)} %copy-done.17), channel_id=1, source_target_pairs={{0,32},{8,40},{16,48},{24,56},{32,0},{40,8},{48,16},{56,24},{64,96... | collective-permute-start | bytes 1544 | tf_op jit(solution)/shard_map/ppermute | solution.py:352
  82.2 5.0 %collective-permute-start.17 = (f32[1,128]{1,0:T(1,128)S(1)}, f32[1,128]{1,0:T(1,128)S(1)}, u32[]{:S(2)}, u32[]{:S(2)}) collective-permute-start(f32[1,128]{1,0:T(1,128)S(1)} %add.93), channel_id=1, source_target_pairs={{0,64},{8,72},{16,80},{24,88},{32,96},{40,104},{48,112},{56,120},{... | collective-permute-start | bytes 1544 | tf_op jit(solution)/shard_map/ppermute | solution.py:352
  87.2 1.0 copy-start.12
  87.2 1.4 copy-start.13
  88.7 1.4 copy-start.6
  95.2 13.8 %collective-permute-start.21 = (f32[1,128]{1,0:T(1,128)S(1)}, f32[1,128]{1,0:T(1,128)S(1)}, u32[]{:S(2)}, u32[]{:S(2)}) collective-permute-start(f32[1,128]{1,0:T(1,128)S(1)} %add.94), channel_id=1, source_target_pairs={{0,16},{8,24},{16,0},{24,8},{32,48},{40,56},{48,32},{56,40},{64,80... | collective-permute-start | bytes 1544 | tf_op jit(solution)/shard_map/ppermute | solution.py:352
  96.3 21.4 %collective-permute-start.30 = (bf16[256,1152]{1,0:T(8,128)(2,1)}, bf16[256,1152]{1,0:T(8,128)(2,1)S(1)}, u32[]{:S(2)}, u32[]{:S(2)}) collective-permute-start(bf16[256,1152]{1,0:T(8,128)(2,1)} %far_text.1), channel_id=1, source_target_pairs={{0,64},{8,72},{16,80},{24,88},{32,96},{40,104},{48,112},{56,120},{... | collective-permute-start | bytes 1769480 | tf_op jit(solution)/shard_map/ppermute | solution.py:388
  105.5 12.2 %copy-start = (bf16[256,1152]{1,0:T(8,128)(2,1)}, bf16[256,1152]{1,0:T(8,128)(2,1)S(1)}, u32[]{:S(2)}) copy-start(bf16[256,1152]{1,0:T(8,128)(2,1)S(1)} %collective-permute-done.24.c2) | copy-start | bytes 1769476
  105.5 20.5 %collective-permute-start.26 = (bf16[256,1152]{1,0:T(8,128)(2,1)}, bf16[256,1152]{1,0:T(8,128)(2,1)S(1)}, u32[]{:S(2)}, u32[]{:S(2)}) collective-permute-start(bf16[256,1152]{1,0:T(8,128)(2,1)} %get-tuple-element.48), channel_id=1, source_target_pairs={{0,2},{1,3},{2,4},{3,5},{4,6},{5,7},{6,0},{7,1},{8,10},{9,11},{10,... | collective-permute-start | bytes 1769480 | tf_op jit(solution)/shard_map/ppermute | solution.py:393
  108.1 17.9 %collective-permute-start.25 = (bf16[256,1152]{1,0:T(8,128)(2,1)}, bf16[256,1152]{1,0:T(8,128)(2,1)S(1)}, u32[]{:S(2)}, u32[]{:S(2)}) collective-permute-start(bf16[256,1152]{1,0:T(8,128)(2,1)} %get-tuple-element.46), channel_id=1, source_target_pairs={{0,6},{1,7},{2,0},{3,1},{4,2},{5,3},{6,4},{7,5},{8,14},{9,15},{10,... | collective-permute-start | bytes 1769480 | tf_op jit(solution)/shard_map/ppermute | solution.py:393
  117.7 15.8 %copy-start.1 = (bf16[256,1152]{1,0:T(8,128)(2,1)}, bf16[256,1152]{1,0:T(8,128)(2,1)S(1)}, u32[]{:S(2)}) copy-start(bf16[256,1152]{1,0:T(8,128)(2,1)S(1)} %collective-permute-done.30.c2) | copy-start | bytes 1769476
  117.7 17.9 %collective-permute-start.31 = (bf16[256,1152]{1,0:T(8,128)(2,1)}, bf16[256,1152]{1,0:T(8,128)(2,1)S(1)}, u32[]{:S(2)}, u32[]{:S(2)}) collective-permute-start(bf16[256,1152]{1,0:T(8,128)(2,1)} %get-tuple-element.52), channel_id=1, source_target_pairs={{0,96},{8,104},{16,112},{24,120},{32,0},{40,8},{48,16},{56,24},{64... | collective-permute-start | bytes 1769480 | tf_op jit(solution)/shard_map/ppermute | solution.py:398
  119.8 15.8 %collective-permute-start.32 = (bf16[256,1152]{1,0:T(8,128)(2,1)}, bf16[256,1152]{1,0:T(8,128)(2,1)S(1)}, u32[]{:S(2)}, u32[]{:S(2)}) collective-permute-start(bf16[256,1152]{1,0:T(8,128)(2,1)} %get-tuple-element.54), channel_id=1, source_target_pairs={{0,32},{8,40},{16,48},{24,56},{32,64},{40,72},{48,80},{56,88},{64,... | collective-permute-start | bytes 1769480 | tf_op jit(solution)/shard_map/ppermute | solution.py:398
  119.8 5.0 %collective-permute-start.22 = (f32[1,128]{1,0:T(1,128)S(1)}, f32[1,128]{1,0:T(1,128)S(1)}, u32[]{:S(2)}, u32[]{:S(2)}) collective-permute-start(f32[1,128]{1,0:T(1,128)S(1)} %add.95), channel_id=1, source_target_pairs={{0,1},{1,0},{2,3},{3,2},{4,5},{5,4},{6,7},{7,6},{8,9},{9,8},{10,11... | collective-permute-start | bytes 1544 | tf_op jit(solution)/shard_map/ppermute | solution.py:352
  124.9 1.1 collective-permute-start.23
  126.0 4.9 %copy-start.2 = (bf16[256,1152]{1,0:T(8,128)(2,1)}, bf16[256,1152]{1,0:T(8,128)(2,1)S(1)}, u32[]{:S(2)}) copy-start(bf16[256,1152]{1,0:T(8,128)(2,1)S(1)} %collective-permute-done.26.c3) | copy-start | bytes 1769476
  126.0 4.9 %copy-start.4 = (bf16[256,1152]{1,0:T(8,128)(2,1)}, bf16[256,1152]{1,0:T(8,128)(2,1)S(1)}, u32[]{:S(2)}) copy-start(bf16[256,1152]{1,0:T(8,128)(2,1)S(1)} %collective-permute-done.25.c1) | copy-start | bytes 1769476
  126.1 3.6 %collective-permute-start.27 = (f32[1,128]{1,0:T(1,128)S(1)}, f32[1,128]{1,0:T(1,128)S(1)}, u32[]{:S(2)}, u32[]{:S(2)}) collective-permute-start(f32[1,128]{1,0:T(1,128)S(1)} %add.97), channel_id=1, source_target_pairs={{0,2},{1,3},{2,0},{3,1},{4,6},{5,7},{6,4},{7,5},{8,10},{9,11},{10,... | collective-permute-start | bytes 1544 | tf_op jit(solution)/shard_map/ppermute | solution.py:352
  129.7 6.0 %collective-permute-start.28 = (f32[1,128]{1,0:T(1,128)S(1)}, f32[1,128]{1,0:T(1,128)S(1)}, u32[]{:S(2)}, u32[]{:S(2)}) collective-permute-start(f32[1,128]{1,0:T(1,128)S(1)} %add.98), channel_id=1, source_target_pairs={{0,4},{1,5},{2,6},{3,7},{4,0},{5,1},{6,2},{7,3},{8,12},{9,13},{10,... | collective-permute-start | bytes 1544 | tf_op jit(solution)/shard_map/ppermute | solution.py:352
  133.5 11.6 %collective-permute-start.29 = (bf16[128,1152]{1,0:T(8,128)(2,1)}, bf16[128,1152]{1,0:T(8,128)(2,1)S(1)}, u32[]{:S(2)}, u32[]{:S(2)}) collective-permute-start(bf16[128,1152]{1,0:T(8,128)(2,1)} %fold_partner.2), channel_id=1, source_target_pairs={{0,1},{1,0},{2,3},{3,2},{4,5},{5,4},{6,7},{7,6},{8,9},{9,8},{10,11... | collective-permute-start | bytes 884744 | tf_op jit(solution)/shard_map/ppermute | solution.py:405
  135.7 0.8 copy-start.3
  136.5 0.8 copy-start.5
  139.9 11.1 %collective-permute-start.33 = (bf16[128,1152]{1,0:T(8,128)(2,1)}, bf16[128,1152]{1,0:T(8,128)(2,1)S(1)}, u32[]{:S(2)}, u32[]{:S(2)}) collective-permute-start(bf16[128,1152]{1,0:T(8,128)(2,1)} %fold_partner.3), channel_id=1, source_target_pairs={{0,16},{8,24},{16,0},{24,8},{32,48},{40,56},{48,32},{56,40},{64,80... | collective-permute-start | bytes 884744 | tf_op jit(solution)/shard_map/ppermute | solution.py:406
  145.2 0.7 copy-start.15
  151.0 0.7 copy-start.16

commit v4 on v3

v4 whole, which is shorter than its diff:
```python
import jax
import jax.numpy as jnp
from jax import lax
from jax.experimental import pallas as pl
from jax.experimental.pallas import tpu as pltpu
from jax.sharding import PartitionSpec as P

BF = jnp.bfloat16
F32 = jnp.float32
LOG2E = 1.4426950408889634
VM = pl.BlockSpec(memory_space=pltpu.VMEM)
SM = pl.BlockSpec(memory_space=pltpu.SMEM)
PIECE = 512


def sds(shape, dtype):
    return jax.ShapeDtypeStruct(shape, dtype)


def params():
    return pltpu.CompilerParams(vmem_limit_bytes=24 * 1024 * 1024)


def small():
    return pltpu.CompilerParams(vmem_limit_bytes=8 * 1024 * 1024)


def encode(x):
    sq = x * x
    return (sq * sq * sq * x).astype(BF)


def decode(code):
    y = code.astype(F32)
    return y * jnp.exp2(jnp.log2(jnp.maximum(jnp.abs(y), 1.2e-38)) * (-6.0 / 7.0))


def dot(a, b, dims):
    return lax.dot_general(a, b, (dims, ((), ())), preferred_element_type=F32)


def normalize_kernel(a_ref, b_ref, a_out, b_out):
    for src, dst in ((a_ref, a_out), (b_ref, b_out)):
        x = src[...]
        norm = jnp.sqrt(jnp.sum(x * x, axis=1, keepdims=True) + 1e-06)
        dst[...] = (x / norm).astype(BF)


def normalize(a, b):
    return pl.pallas_call(
        normalize_kernel, out_shape=(sds(a.shape, BF), sds(b.shape, BF)), out_specs=[VM, VM], name="normalize"
    )(a, b)


RING = (0, 1, 3, 2)


def scores(scal, diag, first, xs, ts, sim, wgt, sums):
    tall, n, rows = xs[0].shape[0], 2 * ts[0].shape[0], xs[0].shape[0] // 4
    scale, bias, mult, shift = scal[0], scal[1], scal[2], scal[3]
    pieces = [(r, c) for r in range(2) for c in range(2)]

    def score(r, c):
        sim[r * tall : (r + 1) * tall, c * PIECE : (c + 1) * PIECE] = dot(xs[r][...], ts[c][...], ((1,), (1,)))

    acc = [jnp.zeros((8, PIECE), F32) for _ in range(3)]
    score(*pieces[0])
    for p, (r, c) in enumerate(pieces):
        if p + 1 < len(pieces):
            score(*pieces[p + 1])
        prod = None
        r, c = r * tall, c * PIECE
        for i in range(0, tall, 16):
            s = sim[r + i : r + i + 16, c : c + PIECE]
            e = jnp.exp2(s * mult + shift)
            u = e + 1.0
            r0 = pl.reciprocal(u, approx=True)
            sig = e * (r0 * (2.0 - u * r0))
            wgt[r + i : r + i + 16, c : c + PIECE] = (sig * scale).astype(BF)
            both = u[0:8] * u[8:16]
            prod = both if prod is None else prod * both
            if i % 64 == 48:
                acc[0] = acc[0] + jnp.log(prod)
                prod = None
            ss = sig * s
            acc[1] = acc[1] + (sig[0:8] + sig[8:16])
            acc[2] = acc[2] + (ss[0:8] + ss[8:16])
    for k in range(3):
        sums[8 * k : 8 * k + 8] = acc[k]

    for b in range(8):
        place = diag[b] - first

        @pl.when(jnp.logical_and(place >= 0, place < n // rows))
        def _(b=b, place=place):
            at = (pl.ds(b * rows, rows), pl.ds(pl.multiple_of(place * rows, rows), rows))
            s = sim[at]
            eye = lax.broadcasted_iota(jnp.int32, s.shape, 0) == lax.broadcasted_iota(jnp.int32, s.shape, 1)
            z = scale * s + bias
            w = -scale / (1.0 + jnp.exp(z))
            wgt[at] = jnp.where(eye, w, wgt[at].astype(F32)).astype(BF)
            z = jnp.where(eye, z, 0.0)
            sd = jnp.where(eye, s, 0.0)
            one = jnp.where(eye, 1.0, 0.0)
            for row, v in ((0, z), (8, one), (16, sd)):
                total = v[0:8]
                for k in range(1, rows // 8):
                    total = total + v[8 * k : 8 * k + 8]
                sums[row : row + 8, 0:rows] -= total


def here(*arrays):
    return [pltpu.with_memory_space_constraint(a, pltpu.VMEM) for a in arrays]


def scores_kernel(first, scal, diag, xa, xb, ta, tb, *refs):
    before = refs[:1] if len(refs) == 5 else ()
    wgt, out_sums, sim, sums = refs[-4:]
    scores(scal, diag, first, (xa, xb), (ta, tb), sim, wgt, sums)
    if before:
        total = sums[...] + before[0][...]
        lane = lax.broadcasted_iota(jnp.int32, (8, 128), 1)
        out = jnp.zeros((8, 128), F32)
        for k in range(3):
            out = jnp.where(lane == k, jnp.sum(total[8 * k : 8 * k + 8], keepdims=True), out)
        out_sums[...] = out[0:1]
    else:
        out_sums[...] = sums[...]


def score_half(first, scal, diag, images, texts, before=()):
    d = images[0].shape[1]
    m = n = 2 * images[0].shape[0]
    return pl.pallas_call(
        lambda *refs: scores_kernel(first, *refs),
        in_specs=[SM, SM] + [VM] * (4 + len(before)),
        out_specs=[VM, VM],
        out_shape=(sds((m, n), BF), sds((1, 128) if before else (24, PIECE), F32)),
        scratch_shapes=[pltpu.VMEM((m, n), F32), pltpu.VMEM((24, PIECE), F32)],
        compiler_params=params(),
        cost_estimate=pl.CostEstimate(
            flops=2 * m * n * d, bytes_accessed=(m + n) * d * 2, transcendentals=3 * m * n
        ),
        name="scores",
    )(scal, diag, *here(*images, *texts, *before))


def group_pull(dims, j, weights, pairs):
    total = None
    for w, pair in zip(weights, pairs):
        tall = pair[0].shape[0]
        rows = tall // 4
        one, two = slice(j * rows, (j + 1) * rows), slice(tall + j * rows, tall + (j + 1) * rows)
        for h, r in enumerate(pair):
            at = slice(h * tall, (h + 1) * tall)
            if dims == 1:
                lhs = jnp.concatenate([w[one, at], w[two, at]], 0)
            else:
                lhs = jnp.concatenate([w[at, one], w[at, two]], 1)
            part = dot(lhs, r[...], ((dims,), (0,)))
            total = part if total is None else total + part
    return total


def pulls_kernel(dims, groups, w0, w1, r0a, r0b, r1a, r1b, *outs):
    for j, out in zip(groups, outs):
        total = group_pull(dims, j, (w0, w1), ((r0a, r0b), (r1a, r1b)))
        out[...] = encode(total) if j else total


def pulls(dims, groups, w0, w1, rows0, rows1, name):
    rows, d = rows0[0].shape[0] // 4, rows0[0].shape[1]
    n = w0.shape[dims]
    out = pl.pallas_call(
        lambda *refs: pulls_kernel(dims, groups, *refs),
        in_specs=[VM] * 6,
        out_specs=[VM] * len(groups),
        out_shape=[sds((2 * rows, d), BF if j else F32) for j in groups],
        compiler_params=params(),
        cost_estimate=pl.CostEstimate(
            flops=8 * len(groups) * rows * n * d, bytes_accessed=4 * n * d, transcendentals=0
        ),
        name=name,
    )(*here(w0, w1, *rows0, *rows1))
    return out[0] if len(groups) == 1 else out


def partner_kernel(own, c1, c2, c3, out):
    at = pl.ds(out.shape[0], out.shape[0])
    out[...] = encode(own[at, :] + decode(c1[at, :]) + decode(c2[at, :]) + decode(c3[at, :]))


def fold_partner(own, *codes):
    rows, d = own.shape[0] // 2, own.shape[1]
    return pl.pallas_call(
        partner_kernel,
        in_specs=[VM] * 4,
        out_specs=VM,
        out_shape=sds((rows, d), BF),
        compiler_params=small(),
        name="fold_partner",
    )(*here(own, *codes))


def own_kernel(own, c1, c2, c3, out):
    at = pl.ds(0, out.shape[0])
    out[...] = own[at, :] + decode(c1[at, :]) + decode(c2[at, :]) + decode(c3[at, :])


def fold_own(own, *codes):
    rows, d = own.shape[0] // 2, own.shape[1]
    return pl.pallas_call(
        own_kernel,
        in_specs=[VM] * 4,
        out_specs=VM,
        out_shape=sds((rows, d), F32),
        compiler_params=small(),
        name="fold_own",
    )(*here(own, *codes))


def finish_kernel(x_ref, own, code_ref, out_ref):
    x = x_ref[...]
    norm = jnp.sqrt(jnp.sum(x * x, axis=1, keepdims=True) + 1e-06)
    hat = x / norm
    pull = own[...] + decode(code_ref[...])
    out_ref[...] = (pull - hat * jnp.sum(hat * pull, axis=1, keepdims=True)) / norm


def finish(x, own, code):
    return pl.pallas_call(
        finish_kernel,
        in_specs=[VM] * 3,
        out_specs=VM,
        out_shape=sds(x.shape, F32),
        compiler_params=small(),
        name="finish",
    )(x, *here(own, code))


def img_index(y, z, c):
    return (y % 4) * 4 + (z % 2) * 2 + c % 2


def perm_x(shift):
    return [(i, ((i // 2 + shift) % 4) * 2 + i % 2) for i in range(8)]


def perm_y(shift):
    return [(i, img_index(i // 4 + shift, i // 2, i)) for i in range(16)]


PERM_ZHI = [(i, i ^ 1) for i in range(8)]
PERM_ZLO = [(i, i ^ 2) for i in range(16)]
PERM_CORE = [(i, i ^ 1) for i in range(16)]
send = lax.ppermute


def after(x, *others):
    return lax.optimization_barrier((x, *others))[0]


def gather(low, axis, perm, perm_z):
    a1, a3 = send(low, axis, perm(1)), send(low, axis, perm(-1))
    z = send(low, axis, perm_z)
    a2 = send(a1, axis, perm(1))
    z1, z3 = send(z, axis, perm(1)), send(z, axis, perm(-1))
    z2 = send(z3, axis, perm(-1))
    return jnp.concatenate([low, a1, a3, a2], 0), jnp.concatenate([z, z1, z3, z2], 0)


def exchange_sum(v, axis, bit):
    size = {"img": 16, "txt": 8}[axis]
    return v + send(v, axis, [(i, i ^ bit) for i in range(size)])


def local(image_embed, text_embed, log_scale, logit_bias):
    rows, d = image_embed.shape
    image_low, text_low = normalize(image_embed, text_embed)
    images = gather(image_low, "txt", perm_x, PERM_ZHI)
    own = gather(text_low, "img", perm_y, PERM_ZLO)
    other = [send(t, "img", PERM_CORE) for t in own]
    partner = [send(x, "img", PERM_CORE) for x in images]

    i, t = lax.axis_index("img"), lax.axis_index("txt")
    b = jnp.arange(8, dtype=jnp.int32)
    j, zz = b % 4, b // 4
    ring = jnp.where(j == 2, 3, jnp.where(j == 3, 2, j))
    g = 8 * i + ((t // 2 - ring) % 4) * 2 + ((t % 2) ^ zz)
    o = g % 16
    k = (i // 4 - o // 4) % 4
    mine = 1 - ((i % 2) ^ (o % 2))
    place = mine * 8 + (((i // 2) % 2) ^ ((o // 2) % 2)) * 4 + jnp.where(k == 2, 3, jnp.where(k == 3, 2, k))
    diag = jnp.where(g // 16 == t, place, -1).astype(jnp.int32)
    scale = jnp.exp(log_scale)
    scal = jnp.stack([scale, logit_bias, scale * LOG2E, logit_bias * LOG2E])

    w_oth, sums = score_half(0, scal, diag, images, other)
    w_rec = send(w_oth, "img", PERM_CORE)
    w_own, v = score_half(8, scal, diag, images, own, (sums,))

    u = exchange_sum(v, "img", 4)
    i2 = pulls(1, (3,), w_own, w_oth, own, other, "far_image")
    u = after(u, i2)
    i2 = send(i2, "txt", perm_x(2))
    v = exchange_sum(u, "img", 8)
    t2 = pulls(0, (3,), after(w_own, u), w_rec, images, partner, "far_text")
    v = after(v, t2)
    t2 = send(t2, "img", perm_y(2))
    u = exchange_sum(v, "img", 2)
    i1, i3, i0 = pulls(1, (1, 2, 0), after(w_own, v), w_oth, own, other, "near_image")
    u = after(u, i0)
    i1, i3 = after(i1, i2), after(i3, i2)
    i1, i3 = send(i1, "txt", perm_x(-1)), send(i3, "txt", perm_x(1))
    v = exchange_sum(u, "txt", 1)
    t1, t3, t0 = pulls(0, (1, 2, 0), after(w_own, u), w_rec, images, partner, "near_text")
    v = after(v, t0)
    t1, t3 = after(t1, t2), after(t3, t2)
    t1, t3 = send(t1, "img", perm_y(-1)), send(t3, "img", perm_y(1))
    v = exchange_sum(v, "img", 1)
    v = after(v, i1, i3)
    v = exchange_sum(exchange_sum(v, "txt", 2), "txt", 4)
    t0 = after(t0, v)

    icodes, tcodes = (i1, i2, i3), (t1, t2, t3)
    image_code = send(fold_partner(i0, *icodes), "txt", PERM_ZHI)
    text_code = send(fold_partner(t0, *tcodes), "img", PERM_ZLO)
    image_grad = finish(image_embed, fold_own(i0, *icodes), image_code)
    text_grad = finish(text_embed, fold_own(t0, *tcodes), text_code)
    pairs = F32(128.0 * rows) * F32(128.0 * rows)
    return (v[0, 0] / pairs, image_grad, text_grad, v[0, 2] * scale / pairs, v[0, 1] / pairs)


def solution(mesh):
    placed = (P(("img", "txt"), None), P(("txt", "img"), None), P(), P())
    return jax.shard_map(
        local,
        mesh=mesh,
        in_specs=placed,
        out_specs=(P(), P(("img", "txt"), None), P(("txt", "img"), None), P(), P()),
        check_vma=False,
    )
```

time: 159 us -> 130 us (0.82)
  Pallas kernels: 62 us -> 32.4 us
  waiting for transfers between devices: 39 us -> 49.5 us
  local copies, waits for them, and re-layouts: 9.34 us -> 3.74 us
  starting transfers between devices: 38.4 us -> 36.2 us
    pallas_call x10, Pallas kernels: 43 us -> 19.6 us  [the longest x4 11.8 us: pulls(): pl.pallas_call(lambda *refs: pulls_kernel(dims, groups, *refs), in_specs=...]
    pallas_call x2, Pallas kernels: 16.8 us -> 10.6 us  [score_half(): pl.pallas_call(lambda *refs: scores_kernel(first, *refs), in_specs=[SM, S...]
    unnamed x47 -> x17, local copies, waits for them, and re-layouts: 8.63 us -> 3.02 us
    ppermute x1, waiting for transfers between devices: 0.01 us -> 4.04 us  [local(): image_code = send(fold_partner(i0, *icodes), 'txt', PERM_ZHI)]
    ppermute x7, waiting for transfers between devices: 13.2 us -> 16 us  [exchange_sum(): return v + send(v, axis, [(i, i ^ bit) for i in range(size)])]
    ppermute x1, waiting for transfers between devices: 0.01 us -> 2.29 us  [local(): t2 = send(t2, 'img', perm_y(2))]
  transfers between devices with their start and end apart: 34 -> 34, of which waited for: 12 -> 16; matrix products, arithmetic and copies ran while one was open for 2% -> 2% of each run, Pallas kernels for 31% -> 18%
where the time goes in v4:
time: 130 us
  waiting for transfers between devices  49.5 us (38%)
  starting transfers between devices  36.2 us (28%)
  Pallas kernels  32.4 us (25%)
  between operations  7.58 us (6%)
  local copies, waits for them, and re-layouts  3.74 us (3%)
    ppermute x7, waiting for transfers between devices, exchange_sum(): return v + send(v, axis, [(i, i ^ bit) for i in range(size)])  16 us
    pallas_call x4, Pallas kernels, pulls(): pl.pallas_call(lambda *refs: pulls_kernel(dims, groups, *refs), in_specs=...  11.8 us
    pallas_call x2, Pallas kernels, score_half(): pl.pallas_call(lambda *refs: scores_kernel(first, *refs), in_specs=[SM, S...  10.6 us
    ppermute x2, waiting for transfers between devices, gather(): a2 = send(a1, axis, perm(1))  9.38 us
    ppermute x4, waiting for transfers between devices, gather(): z1, z3 = (send(z, axis, perm(1)), send(z, axis, perm(-1)))  8.46 us
    ppermute x7, starting transfers between devices, exchange_sum(): return v + send(v, axis, [(i, i ^ bit) for i in range(size)])  6.89 us
    ppermute x4, starting transfers between devices, gather(): a1, a3 = (send(low, axis, perm(1)), send(low, axis, perm(-1)))  6 us
    ppermute x4, starting transfers between devices, gather(): z1, z3 = (send(z, axis, perm(1)), send(z, axis, perm(-1)))  5.99 us
  transfers between devices with their start and end apart: 34, of which 16 were waited for; matrix products, arithmetic and copies ran while one was open for 2% of the time, Pallas kernels for 18%

profile of v4, /device:TPU:0, one launch (start us, length us, event | category | flops | bytes accessed | tf_op | source)
XLA Modules:
  0.0 129.6 jit_solution(12735714933911849063)
XLA Ops:
  0.6 2.2 %normalize.1 = (bf16[128,1152]{1,0:T(8,128)(2,1)}, bf16[128,1152]{1,0:T(8,128)(2,1)}) custom-call(f32[128,1152]{1,0:T(8,128)} %x_ref.2, f32[128,1152]{1,0:T(8,128)} %x_ref.3), custom_call_target="tpu_custom_call" | custom-call | tf_op jit(solution)/shard_map/normalize/pallas_call | solution.py:50
  2.8 4.0 %collective-permute-start.3 = (bf16[128,1152]{1,0:T(8,128)(2,1)}, bf16[128,1152]{1,0:T(8,128)(2,1)S(1)}, u32[]{:S(2)}, u32[]{:S(2)}) collective-permute-start(bf16[128,1152]{1,0:T(8,128)(2,1)} %get-tuple-element.30), channel_id=1, source_target_pairs={{0,1},{1,0},{2,3},{3,2},{4,5},{5,4},{6,7},{7,6},{8,9},{9,8},{10,11... | collective-permute-start | bytes 884744 | tf_op jit(solution)/shard_map/ppermute | solution.py:265
  6.8 2.8 %collective-permute-start.1 = (bf16[128,1152]{1,0:T(8,128)(2,1)}, bf16[128,1152]{1,0:T(8,128)(2,1)S(1)}, u32[]{:S(2)}, u32[]{:S(2)}) collective-permute-start(bf16[128,1152]{1,0:T(8,128)(2,1)} %get-tuple-element.30), channel_id=1, source_target_pairs={{0,6},{1,7},{2,0},{3,1},{4,2},{5,3},{6,4},{7,5},{8,14},{9,15},{10,... | collective-permute-start | bytes 884744 | tf_op jit(solution)/shard_map/ppermute | solution.py:264
  9.6 0.0 collective-permute-start
  9.6 1.0 collective-permute-start.10
  10.6 3.0 %collective-permute-start.8 = (bf16[128,1152]{1,0:T(8,128)(2,1)}, bf16[128,1152]{1,0:T(8,128)(2,1)S(1)}, u32[]{:S(2)}, u32[]{:S(2)}) collective-permute-start(bf16[128,1152]{1,0:T(8,128)(2,1)} %get-tuple-element.31), channel_id=1, source_target_pairs={{0,96},{8,104},{16,112},{24,120},{32,0},{40,8},{48,16},{56,24},{64... | collective-permute-start | bytes 884744 | tf_op jit(solution)/shard_map/ppermute | solution.py:264
  15.0 0.1 pad_maximum_fusion.refs_0_
  15.0 1.1 constant_dynamic-update-slice_fusion.3
  16.2 0.0 collective-permute-done.3
  16.2 0.2 collective-permute-start.7
  16.5 4.6 %collective-permute-done.10 = bf16[128,1152]{1,0:T(8,128)(2,1)S(1)} collective-permute-done((bf16[128,1152]{1,0:T(8,128)(2,1)}, bf16[128,1152]{1,0:T(8,128)(2,1)S(1)}, u32[]{:S(2)}, u32[]{:S(2)}) %collective-permute-start.10) | collective-permute-done | bytes 294944 | tf_op jit(solution)/shard_map/ppermute | solution.py:265
  21.1 2.8 %collective-permute-start.5 = (bf16[128,1152]{1,0:T(8,128)(2,1)S(1)}, bf16[128,1152]{1,0:T(8,128)(2,1)S(1)}, u32[]{:S(2)}, u32[]{:S(2)}) collective-permute-start(bf16[128,1152]{1,0:T(8,128)(2,1)S(1)} %collective-permute-done.3), channel_id=1, source_target_pairs={{0,6},{1,7},{2,0},{3,1},{4,2},{5,3},{6,4},{7,5},{8,14},{9,15},{10,... | collective-permute-start | bytes 884744 | tf_op jit(solution)/shard_map/ppermute | solution.py:267
  23.9 3.1 %collective-permute-start.12 = (bf16[128,1152]{1,0:T(8,128)(2,1)S(1)}, bf16[128,1152]{1,0:T(8,128)(2,1)S(1)}, u32[]{:S(2)}, u32[]{:S(2)}) collective-permute-start(bf16[128,1152]{1,0:T(8,128)(2,1)S(1)} %collective-permute-done.10), channel_id=1, source_target_pairs={{0,96},{8,104},{16,112},{24,120},{32,0},{40,8},{48,16},{56,24},{64... | collective-permute-start | bytes 884744 | tf_op jit(solution)/shard_map/ppermute | solution.py:267
  27.0 0.1 collective-permute-start.11
  27.1 0.1 collective-permute-start.4
  27.2 4.8 %collective-permute-done.12 = bf16[128,1152]{1,0:T(8,128)(2,1)S(1)} collective-permute-done((bf16[128,1152]{1,0:T(8,128)(2,1)S(1)}, bf16[128,1152]{1,0:T(8,128)(2,1)S(1)}, u32[]{:S(2)}, u32[]{:S(2)}) %collective-permute-start.12) | collective-permute-done | bytes 294944 | tf_op jit(solution)/shard_map/ppermute | solution.py:267
  32.1 1.0 collective-permute-start.9
  33.1 3.6 %collective-permute-done.11 = bf16[128,1152]{1,0:T(8,128)(2,1)S(1)} collective-permute-done((bf16[128,1152]{1,0:T(8,128)(2,1)S(1)}, bf16[128,1152]{1,0:T(8,128)(2,1)S(1)}, u32[]{:S(2)}, u32[]{:S(2)}) %collective-permute-start.11) | collective-permute-done | bytes 294944 | tf_op jit(solution)/shard_map/ppermute | solution.py:267
  36.8 5.1 %collective-permute-done.9 = bf16[128,1152]{1,0:T(8,128)(2,1)S(1)} collective-permute-done((bf16[128,1152]{1,0:T(8,128)(2,1)S(1)}, bf16[128,1152]{1,0:T(8,128)(2,1)S(1)}, u32[]{:S(2)}, u32[]{:S(2)}) %collective-permute-start.9) | collective-permute-done | bytes 294944 | tf_op jit(solution)/shard_map/ppermute | solution.py:266
  41.9 1.5 %collective-permute-done.13 = bf16[128,1152]{1,0:T(8,128)(2,1)S(1)} collective-permute-done((bf16[128,1152]{1,0:T(8,128)(2,1)S(1)}, bf16[128,1152]{1,0:T(8,128)(2,1)S(1)}, u32[]{:S(2)}, u32[]{:S(2)}) %collective-permute-start.13) | collective-permute-done | bytes 294944 | tf_op jit(solution)/shard_map/ppermute | solution.py:268
  43.5 0.6 collective-permute-start.15
  44.1 1.9 %collective-permute-start.6 = (bf16[128,1152]{1,0:T(8,128)(2,1)S(1)}, bf16[128,1152]{1,0:T(8,128)(2,1)S(1)}, u32[]{:S(2)}, u32[]{:S(2)}) collective-permute-start(bf16[128,1152]{1,0:T(8,128)(2,1)S(1)} %collective-permute-done.5), channel_id=1, source_target_pairs={{0,6},{1,7},{2,0},{3,1},{4,2},{5,3},{6,4},{7,5},{8,14},{9,15},{10,... | collective-permute-start | bytes 884744 | tf_op jit(solution)/shard_map/ppermute | solution.py:268
  46.1 4.3 %collective-permute-done.2 = bf16[128,1152]{1,0:T(8,128)(2,1)S(1)} collective-permute-done((bf16[128,1152]{1,0:T(8,128)(2,1)S(1)}, bf16[128,1152]{1,0:T(8,128)(2,1)S(1)}, u32[]{:S(2)}, u32[]{:S(2)}) %collective-permute-start.2) | collective-permute-done | bytes 294944 | tf_op jit(solution)/shard_map/ppermute | solution.py:266
  50.4 2.7 %collective-permute-done.6 = bf16[128,1152]{1,0:T(8,128)(2,1)S(1)} collective-permute-done((bf16[128,1152]{1,0:T(8,128)(2,1)S(1)}, bf16[128,1152]{1,0:T(8,128)(2,1)S(1)}, u32[]{:S(2)}, u32[]{:S(2)}) %collective-permute-start.6) | collective-permute-done | bytes 294944 | tf_op jit(solution)/shard_map/ppermute | solution.py:268
  53.2 5.2 %scores.2 = (bf16[1024,1024]{1,0:T(8,128)(2,1)S(1)}, f32[24,512]{1,0:T(8,128)S(1)}) custom-call(f32[4]{0:T(128)S(1)} %pad_maximum_fusion.refs_0_, s32[8]{0:T(128)S(1)} %compare_select_fusion.9.refs_1_, bf16[512,1152]{1,0:T(8,128)(2,1)S(1)} %constant_dynamic-update-slice_fusion.refs_2_, bf16[512,1152]{1,0:T(8,128)(2,1)S(1)} %constant_dynamic-update-slice_fusion.4.refs_3_, ...), custom_call_target="tpu_custom_call" | custom-call | flops 2415919104 | bytes 4718592 | tf_op jit(solution)/shard_map/scores/pallas_call | solution.py:134
  58.4 0.1 collective-permute-start.18
  58.5 0.5 collective-permute-start.19
  59.0 0.1 collective-permute-start.20
  59.1 5.4 %scores.3 = (bf16[1024,1024]{1,0:T(8,128)(2,1)S(1)}, f32[1,128]{1,0:T(1,128)S(1)}) custom-call(f32[4]{0:T(128)S(1)} %pad_maximum_fusion.refs_0_, s32[8]{0:T(128)S(1)} %compare_select_fusion.9.refs_1_, bf16[512,1152]{1,0:T(8,128)(2,1)S(1)} %constant_dynamic-update-slice_fusion.refs_2_, bf16[512,1152]{1,0:T(8,128)(2,1)S(1)} %constant_dynamic-update-slice_fusion.4.refs_3_, ...), custom_call_target="tpu_custom_call" | custom-call | flops 2415919104 | bytes 4718592 | tf_op jit(solution)/shard_map/scores/pallas_call | solution.py:134
  64.5 1.5 %far_image.1 = bf16[256,1152]{1,0:T(8,128)(2,1)S(1)} custom-call(bf16[1024,1024]{1,0:T(8,128)(2,1)S(1)} %get-tuple-element.42.refs_0_, bf16[1024,1024]{1,0:T(8,128)(2,1)S(1)} %get-tuple-element.35.refs_1_, bf16[512,1152]{1,0:T(8,128)(2,1)S(1)} %constant_dynamic-update-slice_fusion.8.refs_4_.refs_2_, ...), custom_call_target="tpu_custom_call" | custom-call | flops 1207959552 | bytes 4718592 | tf_op jit(solution)/shard_map/far_image/pallas_call | solution.py:174
  66.0 1.3 collective-permute-start.24
  67.3 3.5 %collective-permute-done.16 = f32[1,128]{1,0:T(1,128)S(1)} collective-permute-done((f32[1,128]{1,0:T(1,128)S(1)}, f32[1,128]{1,0:T(1,128)S(1)}, u32[]{:S(2)}, u32[]{:S(2)}) %collective-permute-start.16) | collective-permute-done | bytes 544 | tf_op jit(solution)/shard_map/ppermute | solution.py:274
  70.8 0.1 collective-permute-start.17
  70.9 4.9 %collective-permute-done.17 = f32[1,128]{1,0:T(1,128)S(1)} collective-permute-done((f32[1,128]{1,0:T(1,128)S(1)}, f32[1,128]{1,0:T(1,128)S(1)}, u32[]{:S(2)}, u32[]{:S(2)}) %collective-permute-start.17) | collective-permute-done | bytes 544 | tf_op jit(solution)/shard_map/ppermute | solution.py:274
  75.9 1.6 %far_text.1 = bf16[256,1152]{1,0:T(8,128)(2,1)S(1)} custom-call(bf16[1024,1024]{1,0:T(8,128)(2,1)S(1)} %get-tuple-element.42.refs_0_, bf16[1024,1024]{1,0:T(8,128)(2,1)S(1)} %collective-permute-done.18.refs_1_, bf16[512,1152]{1,0:T(8,128)(2,1)S(1)} %constant_dynamic-update-slice_fusion.refs_2_, ...), custom_call_target="tpu_custom_call" | custom-call | flops 1207959552 | bytes 4718592 | tf_op jit(solution)/shard_map/far_text/pallas_call | solution.py:174
  77.5 1.1 collective-permute-start.21
  78.6 0.0 collective-permute-start.30
  78.6 4.3 %near_image.1 = (bf16[256,1152]{1,0:T(8,128)(2,1)S(1)}, bf16[256,1152]{1,0:T(8,128)(2,1)S(1)}, f32[256,1152]{1,0:T(8,128)S(1)}) custom-call(bf16[1024,1024]{1,0:T(8,128)(2,1)S(1)} %get-tuple-element.42.refs_0_, bf16[1024,1024]{1,0:T(8,128)(2,1)S(1)} %get-tuple-element.35.refs_1_, bf16[512,1152]{1,0:T(8,128)(2,1)S(1)} %constant_dynamic-update-slice_fusion.8.refs_4_.refs_2_, ...), custom_call_target="tpu_custom_call" | custom-call | flops 3623878656 | bytes 4718592 | tf_op jit(solution)/shard_map/near_image/pallas_call | solution.py:174
  82.9 0.4 collective-permute-done.24.c2
  83.3 2.0 %collective-permute-start.26 = (bf16[256,1152]{1,0:T(8,128)(2,1)S(1)}, bf16[256,1152]{1,0:T(8,128)(2,1)S(1)}, u32[]{:S(2)}, u32[]{:S(2)}) collective-permute-start(bf16[256,1152]{1,0:T(8,128)(2,1)S(1)} %get-tuple-element.48), channel_id=1, source_target_pairs={{0,2},{1,3},{2,4},{3,5},{4,6},{5,7},{6,0},{7,1},{8,10},{9,11},{10,... | collective-permute-start | bytes 1769480 | tf_op jit(solution)/shard_map/ppermute | solution.py:314
  85.3 1.2 collective-permute-start.25
  86.5 4.4 %near_text.1 = (bf16[256,1152]{1,0:T(8,128)(2,1)S(1)}, bf16[256,1152]{1,0:T(8,128)(2,1)S(1)}, f32[256,1152]{1,0:T(8,128)S(1)}) custom-call(bf16[1024,1024]{1,0:T(8,128)(2,1)S(1)} %get-tuple-element.42.refs_0_, bf16[1024,1024]{1,0:T(8,128)(2,1)S(1)} %collective-permute-done.18.refs_1_, bf16[512,1152]{1,0:T(8,128)(2,1)S(1)} %constant_dynamic-update-slice_fusion.refs_2_, ...), custom_call_target="tpu_custom_call" | custom-call | flops 3623878656 | bytes 4718592 | tf_op jit(solution)/shard_map/near_text/pallas_call | solution.py:174
  90.9 2.3 %collective-permute-done.30.c2 = bf16[256,1152]{1,0:T(8,128)(2,1)S(1)} collective-permute-done((bf16[256,1152]{1,0:T(8,128)(2,1)S(1)}, bf16[256,1152]{1,0:T(8,128)(2,1)S(1)}, u32[]{:S(2)}, u32[]{:S(2)}) %collective-permute-start.30) | collective-permute-done | bytes 589856 | tf_op jit(solution)/shard_map/ppermute | solution.py:309
  93.2 0.6 collective-permute-start.31
  93.7 1.5 %collective-permute-start.32 = (bf16[256,1152]{1,0:T(8,128)(2,1)S(1)}, bf16[256,1152]{1,0:T(8,128)(2,1)S(1)}, u32[]{:S(2)}, u32[]{:S(2)}) collective-permute-start(bf16[256,1152]{1,0:T(8,128)(2,1)S(1)} %get-tuple-element.54), channel_id=1, source_target_pairs={{0,32},{8,40},{16,48},{24,56},{32,64},{40,72},{48,80},{56,88},{64,... | collective-permute-start | bytes 1769480 | tf_op jit(solution)/shard_map/ppermute | solution.py:319
  95.2 1.9 %collective-permute-start.22 = (f32[1,128]{1,0:T(1,128)S(1)}, f32[1,128]{1,0:T(1,128)S(1)}, u32[]{:S(2)}, u32[]{:S(2)}) collective-permute-start(f32[1,128]{1,0:T(1,128)S(1)} %add.95), channel_id=1, source_target_pairs={{0,1},{1,0},{2,3},{3,2},{4,5},{5,4},{6,7},{7,6},{8,9},{9,8},{10,11... | collective-permute-start | bytes 1544 | tf_op jit(solution)/shard_map/ppermute | solution.py:274
  97.1 3.2 %collective-permute-done.22 = f32[1,128]{1,0:T(1,128)S(1)} collective-permute-done((f32[1,128]{1,0:T(1,128)S(1)}, f32[1,128]{1,0:T(1,128)S(1)}, u32[]{:S(2)}, u32[]{:S(2)}) %collective-permute-start.22) | collective-permute-done | bytes 544 | tf_op jit(solution)/shard_map/ppermute | solution.py:274
  100.3 1.1 collective-permute-done.23
  101.4 2.4 %collective-permute-start.27 = (f32[1,128]{1,0:T(1,128)S(1)}, f32[1,128]{1,0:T(1,128)S(1)}, u32[]{:S(2)}, u32[]{:S(2)}) collective-permute-start(f32[1,128]{1,0:T(1,128)S(1)} %add.97), channel_id=1, source_target_pairs={{0,2},{1,3},{2,0},{3,1},{4,6},{5,7},{6,4},{7,5},{8,10},{9,11},{10,... | collective-permute-start | bytes 1544 | tf_op jit(solution)/shard_map/ppermute | solution.py:274
  103.8 1.5 %collective-permute-done.27 = f32[1,128]{1,0:T(1,128)S(1)} collective-permute-done((f32[1,128]{1,0:T(1,128)S(1)}, f32[1,128]{1,0:T(1,128)S(1)}, u32[]{:S(2)}, u32[]{:S(2)}) %collective-permute-start.27) | collective-permute-done | bytes 544 | tf_op jit(solution)/shard_map/ppermute | solution.py:274
  105.3 1.4 %collective-permute-start.28 = (f32[1,128]{1,0:T(1,128)S(1)}, f32[1,128]{1,0:T(1,128)S(1)}, u32[]{:S(2)}, u32[]{:S(2)}) collective-permute-start(f32[1,128]{1,0:T(1,128)S(1)} %add.98), channel_id=1, source_target_pairs={{0,4},{1,5},{2,6},{3,7},{4,0},{5,1},{6,2},{7,3},{8,12},{9,13},{10,... | collective-permute-start | bytes 1544 | tf_op jit(solution)/shard_map/ppermute | solution.py:274
  106.7 1.3 fold_partner.2
  108.0 0.6 collective-permute-start.29
  108.6 1.8 %collective-permute-done.28 = f32[1,128]{1,0:T(1,128)S(1)} collective-permute-done((f32[1,128]{1,0:T(1,128)S(1)}, f32[1,128]{1,0:T(1,128)S(1)}, u32[]{:S(2)}, u32[]{:S(2)}) %collective-permute-start.28) | collective-permute-done | bytes 544 | tf_op jit(solution)/shard_map/ppermute | solution.py:274
  110.4 1.3 fold_partner.3
  111.7 1.0 collective-permute-start.33
  112.7 0.5 fold_own.2.own
  113.2 0.6 fusion.15
  115.7 4.0 %collective-permute-done.29.code_ref = bf16[128,1152]{1,0:T(8,128)(2,1)} collective-permute-done((bf16[128,1152]{1,0:T(8,128)(2,1)}, bf16[128,1152]{1,0:T(8,128)(2,1)}, u32[]{:S(2)}, u32[]{:S(2)}) %collective-permute-start.29) | collective-permute-done | bytes 294944 | tf_op jit(solution)/shard_map/ppermute | solution.py:326
  119.8 1.1 copy-done
  120.8 2.2 %finish.2 = f32[128,1152]{1,0:T(8,128)} custom-call(f32[128,1152]{1,0:T(8,128)S(1)} %copy-done, f32[128,1152]{1,0:T(8,128)S(1)} %fold_own.2.own, bf16[128,1152]{1,0:T(8,128)(2,1)} %collective-permute-done.29.code_ref), custom_call_target="tpu_custom_call" | custom-call | tf_op jit(solution)/shard_map/finish/pallas_call | solution.py:231
  123.0 0.5 fold_own.3.own
  123.5 0.6 copy-done.1
  124.1 2.2 %finish.3 = f32[128,1152]{1,0:T(8,128)} custom-call(f32[128,1152]{1,0:T(8,128)S(1)} %copy-done.1, f32[128,1152]{1,0:T(8,128)S(1)} %fold_own.3.own, bf16[128,1152]{1,0:T(8,128)(2,1)} %collective-permute-done.33.code_ref), custom_call_target="tpu_custom_call" | custom-call | tf_op jit(solution)/shard_map/finish/pallas_call | solution.py:231
  (48 shorter events, 0.5 us)
Async XLA Ops:
  2.8 13.4 %copy-start.2 = (bf16[128,1152]{1,0:T(8,128)(2,1)S(1)}, bf16[128,1152]{1,0:T(8,128)(2,1)}, u32[]{:S(2)}) copy-start(bf16[128,1152]{1,0:T(8,128)(2,1)} %get-tuple-element.31) | copy-start | bytes 884740
  2.8 13.3 %collective-permute-start.3 = (bf16[128,1152]{1,0:T(8,128)(2,1)}, bf16[128,1152]{1,0:T(8,128)(2,1)S(1)}, u32[]{:S(2)}, u32[]{:S(2)}) collective-permute-start(bf16[128,1152]{1,0:T(8,128)(2,1)} %get-tuple-element.30), channel_id=1, source_target_pairs={{0,1},{1,0},{2,3},{3,2},{4,5},{5,4},{6,7},{7,6},{8,9},{9,8},{10,11... | collective-permute-start | bytes 884744 | tf_op jit(solution)/shard_map/ppermute | solution.py:265
  6.8 36.7 %collective-permute-start.1 = (bf16[128,1152]{1,0:T(8,128)(2,1)}, bf16[128,1152]{1,0:T(8,128)(2,1)S(1)}, u32[]{:S(2)}, u32[]{:S(2)}) collective-permute-start(bf16[128,1152]{1,0:T(8,128)(2,1)} %get-tuple-element.30), channel_id=1, source_target_pairs={{0,6},{1,7},{2,0},{3,1},{4,2},{5,3},{6,4},{7,5},{8,14},{9,15},{10,... | collective-permute-start | bytes 884744 | tf_op jit(solution)/shard_map/ppermute | solution.py:264
  9.6 14.3 %collective-permute-start = (bf16[128,1152]{1,0:T(8,128)(2,1)}, bf16[128,1152]{1,0:T(8,128)(2,1)S(1)}, u32[]{:S(2)}, u32[]{:S(2)}) collective-permute-start(bf16[128,1152]{1,0:T(8,128)(2,1)} %get-tuple-element.30), channel_id=1, source_target_pairs={{0,2},{1,3},{2,4},{3,5},{4,6},{5,7},{6,0},{7,1},{8,10},{9,11},{10,... | collective-permute-start | bytes 884744 | tf_op jit(solution)/shard_map/ppermute | solution.py:264
  9.6 11.5 %collective-permute-start.10 = (bf16[128,1152]{1,0:T(8,128)(2,1)}, bf16[128,1152]{1,0:T(8,128)(2,1)S(1)}, u32[]{:S(2)}, u32[]{:S(2)}) collective-permute-start(bf16[128,1152]{1,0:T(8,128)(2,1)} %get-tuple-element.31), channel_id=1, source_target_pairs={{0,16},{8,24},{16,0},{24,8},{32,48},{40,56},{48,32},{56,40},{64,80... | collective-permute-start | bytes 884744 | tf_op jit(solution)/shard_map/ppermute | solution.py:265
  10.6 16.5 %collective-permute-start.8 = (bf16[128,1152]{1,0:T(8,128)(2,1)}, bf16[128,1152]{1,0:T(8,128)(2,1)S(1)}, u32[]{:S(2)}, u32[]{:S(2)}) collective-permute-start(bf16[128,1152]{1,0:T(8,128)(2,1)} %get-tuple-element.31), channel_id=1, source_target_pairs={{0,96},{8,104},{16,112},{24,120},{32,0},{40,8},{48,16},{56,24},{64... | collective-permute-start | bytes 884744 | tf_op jit(solution)/shard_map/ppermute | solution.py:264
  16.2 10.8 %collective-permute-start.7 = (bf16[128,1152]{1,0:T(8,128)(2,1)S(1)}, bf16[128,1152]{1,0:T(8,128)(2,1)S(1)}, u32[]{:S(2)}, u32[]{:S(2)}) collective-permute-start(bf16[128,1152]{1,0:T(8,128)(2,1)S(1)} %copy-done.2), channel_id=1, source_target_pairs={{0,32},{8,40},{16,48},{24,56},{32,64},{40,72},{48,80},{56,88},{64,... | collective-permute-start | bytes 884744 | tf_op jit(solution)/shard_map/ppermute | solution.py:264
  21.1 23.1 %collective-permute-start.5 = (bf16[128,1152]{1,0:T(8,128)(2,1)S(1)}, bf16[128,1152]{1,0:T(8,128)(2,1)S(1)}, u32[]{:S(2)}, u32[]{:S(2)}) collective-permute-start(bf16[128,1152]{1,0:T(8,128)(2,1)S(1)} %collective-permute-done.3), channel_id=1, source_target_pairs={{0,6},{1,7},{2,0},{3,1},{4,2},{5,3},{6,4},{7,5},{8,14},{9,15},{10,... | collective-permute-start | bytes 884744 | tf_op jit(solution)/shard_map/ppermute | solution.py:267
  23.9 8.2 %collective-permute-start.12 = (bf16[128,1152]{1,0:T(8,128)(2,1)S(1)}, bf16[128,1152]{1,0:T(8,128)(2,1)S(1)}, u32[]{:S(2)}, u32[]{:S(2)}) collective-permute-start(bf16[128,1152]{1,0:T(8,128)(2,1)S(1)} %collective-permute-done.10), channel_id=1, source_target_pairs={{0,96},{8,104},{16,112},{24,120},{32,0},{40,8},{48,16},{56,24},{64... | collective-permute-start | bytes 884744 | tf_op jit(solution)/shard_map/ppermute | solution.py:267
  27.0 9.7 %collective-permute-start.11 = (bf16[128,1152]{1,0:T(8,128)(2,1)S(1)}, bf16[128,1152]{1,0:T(8,128)(2,1)S(1)}, u32[]{:S(2)}, u32[]{:S(2)}) collective-permute-start(bf16[128,1152]{1,0:T(8,128)(2,1)S(1)} %collective-permute-done.10), channel_id=1, source_target_pairs={{0,32},{8,40},{16,48},{24,56},{32,64},{40,72},{48,80},{56,88},{64,... | collective-permute-start | bytes 884744 | tf_op jit(solution)/shard_map/ppermute | solution.py:267
  27.1 18.9 %collective-permute-start.4 = (bf16[128,1152]{1,0:T(8,128)(2,1)S(1)}, bf16[128,1152]{1,0:T(8,128)(2,1)S(1)}, u32[]{:S(2)}, u32[]{:S(2)}) collective-permute-start(bf16[128,1152]{1,0:T(8,128)(2,1)S(1)} %collective-permute-done.3), channel_id=1, source_target_pairs={{0,2},{1,3},{2,4},{3,5},{4,6},{5,7},{6,0},{7,1},{8,10},{9,11},{10,... | collective-permute-start | bytes 884744 | tf_op jit(solution)/shard_map/ppermute | solution.py:267
  32.1 9.8 %collective-permute-start.9 = (bf16[128,1152]{1,0:T(8,128)(2,1)S(1)}, bf16[128,1152]{1,0:T(8,128)(2,1)S(1)}, u32[]{:S(2)}, u32[]{:S(2)}) collective-permute-start(bf16[128,1152]{1,0:T(8,128)(2,1)S(1)} %collective-permute-done.7), channel_id=1, source_target_pairs={{0,32},{8,40},{16,48},{24,56},{32,64},{40,72},{48,80},{56,88},{64,... | collective-permute-start | bytes 884744 | tf_op jit(solution)/shard_map/ppermute | solution.py:266
  36.7 6.7 %collective-permute-start.13 = (bf16[128,1152]{1,0:T(8,128)(2,1)S(1)}, bf16[128,1152]{1,0:T(8,128)(2,1)S(1)}, u32[]{:S(2)}, u32[]{:S(2)}) collective-permute-start(bf16[128,1152]{1,0:T(8,128)(2,1)S(1)} %collective-permute-done.12), channel_id=1, source_target_pairs={{0,96},{8,104},{16,112},{24,120},{32,0},{40,8},{48,16},{56,24},{64... | collective-permute-start | bytes 884744 | tf_op jit(solution)/shard_map/ppermute | solution.py:268
  41.9 8.5 %collective-permute-start.2 = (bf16[128,1152]{1,0:T(8,128)(2,1)S(1)}, bf16[128,1152]{1,0:T(8,128)(2,1)S(1)}, u32[]{:S(2)}, u32[]{:S(2)}) collective-permute-start(bf16[128,1152]{1,0:T(8,128)(2,1)S(1)} %collective-permute-done), channel_id=1, source_target_pairs={{0,2},{1,3},{2,4},{3,5},{4,6},{5,7},{6,0},{7,1},{8,10},{9,11},{10,... | collective-permute-start | bytes 884744 | tf_op jit(solution)/shard_map/ppermute | solution.py:266
  43.5 9.7 %collective-permute-start.14 = (bf16[512,1152]{1,0:T(8,128)(2,1)S(1)}, bf16[512,1152]{1,0:T(8,128)(2,1)S(1)}, u32[]{:S(2)}, u32[]{:S(2)}) collective-permute-start(bf16[512,1152]{1,0:T(8,128)(2,1)S(1)} %constant_dynamic-update-slice_fusion.8.refs_4_.refs_2_), channel_id=1, source_target_pairs={{0,8},{8,0},{16,24},{24,16},{32,40},{40,32},{48,56},{56,48},{64,72... | collective-permute-start | bytes 3538952 | tf_op jit(solution)/shard_map/ppermute | solution.py:282
  43.5 9.7 %collective-permute-start.15 = (bf16[512,1152]{1,0:T(8,128)(2,1)S(1)}, bf16[512,1152]{1,0:T(8,128)(2,1)S(1)}, u32[]{:S(2)}, u32[]{:S(2)}) collective-permute-start(bf16[512,1152]{1,0:T(8,128)(2,1)S(1)} %constant_dynamic-update-slice_fusion.12.refs_5_.refs_3_), channel_id=1, source_target_pairs={{0,8},{8,0},{16,24},{24,16},{32,40},{40,32},{48,56},{56,48},{64,72... | collective-permute-start | bytes 3538952 | tf_op jit(solution)/shard_map/ppermute | solution.py:282
  44.1 9.0 %collective-permute-start.6 = (bf16[128,1152]{1,0:T(8,128)(2,1)S(1)}, bf16[128,1152]{1,0:T(8,128)(2,1)S(1)}, u32[]{:S(2)}, u32[]{:S(2)}) collective-permute-start(bf16[128,1152]{1,0:T(8,128)(2,1)S(1)} %collective-permute-done.5), channel_id=1, source_target_pairs={{0,6},{1,7},{2,0},{3,1},{4,2},{5,3},{6,4},{7,5},{8,14},{9,15},{10,... | collective-permute-start | bytes 884744 | tf_op jit(solution)/shard_map/ppermute | solution.py:268
  58.4 17.5 %collective-permute-start.18 = (bf16[1024,1024]{1,0:T(8,128)(2,1)S(1)}, bf16[1024,1024]{1,0:T(8,128)(2,1)S(1)}, u32[]{:S(2)}, u32[]{:S(2)}) collective-permute-start(bf16[1024,1024]{1,0:T(8,128)(2,1)S(1)} %get-tuple-element.35.refs_1_), channel_id=1, source_target_pairs={{0,8},{8,0},{16,24},{24,16},{32,40},{40,32},{48,56},{56,48},{64,72... | collective-permute-start | bytes 6291464 | tf_op jit(solution)/shard_map/ppermute | solution.py:299
  58.5 17.4 %collective-permute-start.19 = (bf16[512,1152]{1,0:T(8,128)(2,1)S(1)}, bf16[512,1152]{1,0:T(8,128)(2,1)S(1)}, u32[]{:S(2)}, u32[]{:S(2)}) collective-permute-start(bf16[512,1152]{1,0:T(8,128)(2,1)S(1)} %constant_dynamic-update-slice_fusion.refs_2_), channel_id=1, source_target_pairs={{0,8},{8,0},{16,24},{24,16},{32,40},{40,32},{48,56},{56,48},{64,72... | collective-permute-start | bytes 3538952 | tf_op jit(solution)/shard_map/ppermute | solution.py:283
  59.0 16.9 %collective-permute-start.20 = (bf16[512,1152]{1,0:T(8,128)(2,1)S(1)}, bf16[512,1152]{1,0:T(8,128)(2,1)S(1)}, u32[]{:S(2)}, u32[]{:S(2)}) collective-permute-start(bf16[512,1152]{1,0:T(8,128)(2,1)S(1)} %constant_dynamic-update-slice_fusion.4.refs_3_), channel_id=1, source_target_pairs={{0,8},{8,0},{16,24},{24,16},{32,40},{40,32},{48,56},{56,48},{64,72... | collective-permute-start | bytes 3538952 | tf_op jit(solution)/shard_map/ppermute | solution.py:283
  66.0 17.2 %collective-permute-start.24 = (bf16[256,1152]{1,0:T(8,128)(2,1)S(1)}, bf16[256,1152]{1,0:T(8,128)(2,1)S(1)}, u32[]{:S(2)}, u32[]{:S(2)}) collective-permute-start(bf16[256,1152]{1,0:T(8,128)(2,1)S(1)} %far_image.1), channel_id=1, source_target_pairs={{0,4},{1,5},{2,6},{3,7},{4,0},{5,1},{6,2},{7,3},{8,12},{9,13},{10,... | collective-permute-start | bytes 1769480 | tf_op jit(solution)/shard_map/ppermute | solution.py:305
  67.3 3.5 %collective-permute-start.16 = (f32[1,128]{1,0:T(1,128)S(1)}, f32[1,128]{1,0:T(1,128)S(1)}, u32[]{:S(2)}, u32[]{:S(2)}) collective-permute-start(f32[1,128]{1,0:T(1,128)S(1)} %get-tuple-element.33), channel_id=1, source_target_pairs={{0,32},{8,40},{16,48},{24,56},{32,0},{40,8},{48,16},{56,24},{64,96... | collective-permute-start | bytes 1544 | tf_op jit(solution)/shard_map/ppermute | solution.py:274
  70.8 5.0 %collective-permute-start.17 = (f32[1,128]{1,0:T(1,128)S(1)}, f32[1,128]{1,0:T(1,128)S(1)}, u32[]{:S(2)}, u32[]{:S(2)}) collective-permute-start(f32[1,128]{1,0:T(1,128)S(1)} %add.93), channel_id=1, source_target_pairs={{0,64},{8,72},{16,80},{24,88},{32,96},{40,104},{48,112},{56,120},{... | collective-permute-start | bytes 1544 | tf_op jit(solution)/shard_map/ppermute | solution.py:274
  77.5 9.0 %collective-permute-start.21 = (f32[1,128]{1,0:T(1,128)S(1)}, f32[1,128]{1,0:T(1,128)S(1)}, u32[]{:S(2)}, u32[]{:S(2)}) collective-permute-start(f32[1,128]{1,0:T(1,128)S(1)} %add.94), channel_id=1, source_target_pairs={{0,16},{8,24},{16,0},{24,8},{32,48},{40,56},{48,32},{56,40},{64,80... | collective-permute-start | bytes 1544 | tf_op jit(solution)/shard_map/ppermute | solution.py:274
  78.6 14.6 %collective-permute-start.30 = (bf16[256,1152]{1,0:T(8,128)(2,1)S(1)}, bf16[256,1152]{1,0:T(8,128)(2,1)S(1)}, u32[]{:S(2)}, u32[]{:S(2)}) collective-permute-start(bf16[256,1152]{1,0:T(8,128)(2,1)S(1)} %far_text.1), channel_id=1, source_target_pairs={{0,64},{8,72},{16,80},{24,88},{32,96},{40,104},{48,112},{56,120},{... | collective-permute-start | bytes 1769480 | tf_op jit(solution)/shard_map/ppermute | solution.py:309
  83.3 18.1 %collective-permute-start.26 = (bf16[256,1152]{1,0:T(8,128)(2,1)S(1)}, bf16[256,1152]{1,0:T(8,128)(2,1)S(1)}, u32[]{:S(2)}, u32[]{:S(2)}) collective-permute-start(bf16[256,1152]{1,0:T(8,128)(2,1)S(1)} %get-tuple-element.48), channel_id=1, source_target_pairs={{0,2},{1,3},{2,4},{3,5},{4,6},{5,7},{6,0},{7,1},{8,10},{9,11},{10,... | collective-permute-start | bytes 1769480 | tf_op jit(solution)/shard_map/ppermute | solution.py:314
  85.3 16.1 %collective-permute-start.25 = (bf16[256,1152]{1,0:T(8,128)(2,1)S(1)}, bf16[256,1152]{1,0:T(8,128)(2,1)S(1)}, u32[]{:S(2)}, u32[]{:S(2)}) collective-permute-start(bf16[256,1152]{1,0:T(8,128)(2,1)S(1)} %get-tuple-element.46), channel_id=1, source_target_pairs={{0,6},{1,7},{2,0},{3,1},{4,2},{5,3},{6,4},{7,5},{8,14},{9,15},{10,... | collective-permute-start | bytes 1769480 | tf_op jit(solution)/shard_map/ppermute | solution.py:314
  93.2 17.2 %collective-permute-start.31 = (bf16[256,1152]{1,0:T(8,128)(2,1)S(1)}, bf16[256,1152]{1,0:T(8,128)(2,1)S(1)}, u32[]{:S(2)}, u32[]{:S(2)}) collective-permute-start(bf16[256,1152]{1,0:T(8,128)(2,1)S(1)} %get-tuple-element.52), channel_id=1, source_target_pairs={{0,96},{8,104},{16,112},{24,120},{32,0},{40,8},{48,16},{56,24},{64... | collective-permute-start | bytes 1769480 | tf_op jit(solution)/shard_map/ppermute | solution.py:319
  93.7 16.7 %collective-permute-start.32 = (bf16[256,1152]{1,0:T(8,128)(2,1)S(1)}, bf16[256,1152]{1,0:T(8,128)(2,1)S(1)}, u32[]{:S(2)}, u32[]{:S(2)}) collective-permute-start(bf16[256,1152]{1,0:T(8,128)(2,1)S(1)} %get-tuple-element.54), channel_id=1, source_target_pairs={{0,32},{8,40},{16,48},{24,56},{32,64},{40,72},{48,80},{56,88},{64,... | collective-permute-start | bytes 1769480 | tf_op jit(solution)/shard_map/ppermute | solution.py:319
  95.2 5.0 %collective-permute-start.22 = (f32[1,128]{1,0:T(1,128)S(1)}, f32[1,128]{1,0:T(1,128)S(1)}, u32[]{:S(2)}, u32[]{:S(2)}) collective-permute-start(f32[1,128]{1,0:T(1,128)S(1)} %add.95), channel_id=1, source_target_pairs={{0,1},{1,0},{2,3},{3,2},{4,5},{5,4},{6,7},{7,6},{8,9},{9,8},{10,11... | collective-permute-start | bytes 1544 | tf_op jit(solution)/shard_map/ppermute | solution.py:274
  100.3 1.1 collective-permute-start.23
  101.4 3.9 %collective-permute-start.27 = (f32[1,128]{1,0:T(1,128)S(1)}, f32[1,128]{1,0:T(1,128)S(1)}, u32[]{:S(2)}, u32[]{:S(2)}) collective-permute-start(f32[1,128]{1,0:T(1,128)S(1)} %add.97), channel_id=1, source_target_pairs={{0,2},{1,3},{2,0},{3,1},{4,6},{5,7},{6,4},{7,5},{8,10},{9,11},{10,... | collective-permute-start | bytes 1544 | tf_op jit(solution)/shard_map/ppermute | solution.py:274
  105.3 5.0 %collective-permute-start.28 = (f32[1,128]{1,0:T(1,128)S(1)}, f32[1,128]{1,0:T(1,128)S(1)}, u32[]{:S(2)}, u32[]{:S(2)}) collective-permute-start(f32[1,128]{1,0:T(1,128)S(1)} %add.98), channel_id=1, source_target_pairs={{0,4},{1,5},{2,6},{3,7},{4,0},{5,1},{6,2},{7,3},{8,12},{9,13},{10,... | collective-permute-start | bytes 1544 | tf_op jit(solution)/shard_map/ppermute | solution.py:274
  108.0 11.8 %collective-permute-start.29 = (bf16[128,1152]{1,0:T(8,128)(2,1)}, bf16[128,1152]{1,0:T(8,128)(2,1)}, u32[]{:S(2)}, u32[]{:S(2)}) collective-permute-start(bf16[128,1152]{1,0:T(8,128)(2,1)} %fold_partner.2), channel_id=1, source_target_pairs={{0,1},{1,0},{2,3},{3,2},{4,5},{5,4},{6,7},{7,6},{8,9},{9,8},{10,11... | collective-permute-start | bytes 884744 | tf_op jit(solution)/shard_map/ppermute | solution.py:326
  111.7 11.8 %collective-permute-start.33 = (bf16[128,1152]{1,0:T(8,128)(2,1)}, bf16[128,1152]{1,0:T(8,128)(2,1)}, u32[]{:S(2)}, u32[]{:S(2)}) collective-permute-start(bf16[128,1152]{1,0:T(8,128)(2,1)} %fold_partner.3), channel_id=1, source_target_pairs={{0,16},{8,24},{16,0},{24,8},{32,48},{40,56},{48,32},{56,40},{64,80... | collective-permute-start | bytes 884744 | tf_op jit(solution)/shard_map/ppermute | solution.py:327
  119.8 1.1 copy-start
  123.0 1.1 copy-start.1

commit v5 on v4

--- a/solution.py
+++ b/solution.py
@@ -1,3 +1,5 @@
+import functools
+
 import jax
 import jax.numpy as jnp
 from jax import lax
@@ -35,24 +37,31 @@
     return y * jnp.exp2(jnp.log2(jnp.maximum(jnp.abs(y), 1.2e-38)) * (-6.0 / 7.0))
 
 
+def normalize_kernel(a_ref, b_ref, *outs):
+    for src, low, hat_out, norm_out in ((a_ref, *outs[:3]), (b_ref, *outs[3:])):
+        x = src[...]
+        norm = jnp.sqrt(jnp.sum(x * x, axis=1, keepdims=True) + 1e-06)
+        hat = x / norm
+        low[...] = hat.astype(BF)
+        hat_out[...] = hat
+        norm_out[...] = norm
+
+
+def normalize(a, b):
+    one = lambda x: (sds(x.shape, BF), sds(x.shape, F32), sds((x.shape[0], 1), F32))
+    out = pl.pallas_call(
+        normalize_kernel, out_shape=one(a) + one(b), out_specs=[VM] * 6, name="normalize"
+    )(a, b)
+    return out[:3], out[3:]
+
+
 def dot(a, b, dims):
     return lax.dot_general(a, b, (dims, ((), ())), preferred_element_type=F32)
 
 
-def normalize_kernel(a_ref, b_ref, a_out, b_out):
-    for src, dst in ((a_ref, a_out), (b_ref, b_out)):
-        x = src[...]
-        norm = jnp.sqrt(jnp.sum(x * x, axis=1, keepdims=True) + 1e-06)
-        dst[...] = (x / norm).astype(BF)
-
-
-def normalize(a, b):
-    return pl.pallas_call(
-        normalize_kernel, out_shape=(sds(a.shape, BF), sds(b.shape, BF)), out_specs=[VM, VM], name="normalize"
-    )(a, b)
-
-
-RING = (0, 1, 3, 2)
+RING = (0, 1, 3, 2, 0, 1, 3, 2)
+PARTNER = (0, 0, 0, 0, 1, 1, 1, 1)
+GROUP = {0: (0, 4), 1: (1, 5), 2: (3, 7), 3: (2, 6)}
 
 
 def scores(scal, diag, first, xs, ts, sim, wgt, sums):
@@ -145,12 +154,12 @@
     )(scal, diag, *here(*images, *texts, *before))
 
 
-def group_pull(dims, j, weights, pairs):
+def group_pull(dims, k, weights, pairs):
     total = None
     for w, pair in zip(weights, pairs):
         tall = pair[0].shape[0]
         rows = tall // 4
-        one, two = slice(j * rows, (j + 1) * rows), slice(tall + j * rows, tall + (j + 1) * rows)
+        one, two = (slice(b * rows, (b + 1) * rows) for b in GROUP[k])
         for h, r in enumerate(pair):
             at = slice(h * tall, (h + 1) * tall)
             if dims == 1:
@@ -162,80 +171,83 @@
     return total
 
 
-def pulls_kernel(dims, groups, w0, w1, r0a, r0b, r1a, r1b, *outs):
-    for j, out in zip(groups, outs):
-        total = group_pull(dims, j, (w0, w1), ((r0a, r0b), (r1a, r1b)))
-        out[...] = encode(total) if j else total
-
-
-def pulls(dims, groups, w0, w1, rows0, rows1, name):
+def far_kernel(dims, w0, w1, r0a, r0b, r1a, r1b, out_a, out_b):
+    total = group_pull(dims, 2, (w0, w1), ((r0a, r0b), (r1a, r1b)))
+    rows = out_a.shape[0]
+    out_a[...] = encode(total[:rows])
+    out_b[...] = encode(total[rows:])
+
+
+def near_kernel(dims, w0, w1, r0a, r0b, r1a, r1b, via_a, via_b, o1, o3, own):
+    rows = via_a.shape[0]
+    for k, out in ((1, o1), (3, o3), (0, own)):
+        total = group_pull(dims, k, (w0, w1), ((r0a, r0b), (r1a, r1b)))
+        one, two = total[:rows], total[rows:]
+        if k == 0:
+            out[...] = total
+            continue
+        if k == 1:
+            two = two + decode(via_b[...])
+        else:
+            one = one + decode(via_a[...])
+        out[:rows, :] = encode(one)
+        out[rows:, :] = encode(two)
+
+
+def pulls(dims, w0, w1, rows0, rows1, name, via=()):
     rows, d = rows0[0].shape[0] // 4, rows0[0].shape[1]
     n = w0.shape[dims]
-    out = pl.pallas_call(
-        lambda *refs: pulls_kernel(dims, groups, *refs),
-        in_specs=[VM] * 6,
-        out_specs=[VM] * len(groups),
-        out_shape=[sds((2 * rows, d), BF if j else F32) for j in groups],
+    shapes = [sds((2 * rows, d), BF)] * 2 + [sds((2 * rows, d), F32)] if via else [sds((rows, d), BF)] * 2
+    return pl.pallas_call(
+        functools.partial(near_kernel if via else far_kernel, dims),
+        in_specs=[VM] * (6 + len(via)),
+        out_specs=[VM] * len(shapes),
+        out_shape=shapes,
         compiler_params=params(),
         cost_estimate=pl.CostEstimate(
-            flops=8 * len(groups) * rows * n * d, bytes_accessed=4 * n * d, transcendentals=0
+            flops=8 * (3 if via else 1) * rows * n * d, bytes_accessed=4 * n * d, transcendentals=0
         ),
         name=name,
-    )(*here(w0, w1, *rows0, *rows1))
-    return out[0] if len(groups) == 1 else out
-
-
-def partner_kernel(own, c1, c2, c3, out):
+    )(*here(w0, w1, *rows0, *rows1, *via))
+
+
+def partner_kernel(own, c1, c3, out):
     at = pl.ds(out.shape[0], out.shape[0])
-    out[...] = encode(own[at, :] + decode(c1[at, :]) + decode(c2[at, :]) + decode(c3[at, :]))
-
-
-def fold_partner(own, *codes):
+    out[...] = encode(own[at, :] + decode(c1[at, :]) + decode(c3[at, :]))
+
+
+def own_kernel(own, c1, c3, out):
+    at = pl.ds(0, out.shape[0])
+    out[...] = own[at, :] + decode(c1[at, :]) + decode(c3[at, :])
+
+
+def fold(kernel, own, codes, dtype, name):
     rows, d = own.shape[0] // 2, own.shape[1]
     return pl.pallas_call(
-        partner_kernel,
+        kernel,
+        in_specs=[VM] * 3,
+        out_specs=VM,
+        out_shape=sds((rows, d), dtype),
+        compiler_params=small(),
+        name=name,
+    )(*here(own, *codes))
+
+
+def finish_kernel(hat_ref, norm_ref, own, code_ref, out_ref):
+    hat = hat_ref[...]
+    pull = own[...] + decode(code_ref[...])
+    out_ref[...] = (pull - hat * jnp.sum(hat * pull, axis=1, keepdims=True)) / norm_ref[...]
+
+
+def finish(hat, norm, own, code):
+    return pl.pallas_call(
+        finish_kernel,
         in_specs=[VM] * 4,
         out_specs=VM,
-        out_shape=sds((rows, d), BF),
-        compiler_params=small(),
-        name="fold_partner",
-    )(*here(own, *codes))
-
-
-def own_kernel(own, c1, c2, c3, out):
-    at = pl.ds(0, out.shape[0])
-    out[...] = own[at, :] + decode(c1[at, :]) + decode(c2[at, :]) + decode(c3[at, :])
-
-
-def fold_own(own, *codes):
-    rows, d = own.shape[0] // 2, own.shape[1]
-    return pl.pallas_call(
-        own_kernel,
-        in_specs=[VM] * 4,
-        out_specs=VM,
-        out_shape=sds((rows, d), F32),
-        compiler_params=small(),
-        name="fold_own",
-    )(*here(own, *codes))
-
-
-def finish_kernel(x_ref, own, code_ref, out_ref):
-    x = x_ref[...]
-    norm = jnp.sqrt(jnp.sum(x * x, axis=1, keepdims=True) + 1e-06)
-    hat = x / norm
-    pull = own[...] + decode(code_ref[...])
-    out_ref[...] = (pull - hat * jnp.sum(hat * pull, axis=1, keepdims=True)) / norm
-
-
-def finish(x, own, code):
-    return pl.pallas_call(
-        finish_kernel,
-        in_specs=[VM] * 3,
-        out_specs=VM,
-        out_shape=sds(x.shape, F32),
+        out_shape=sds(hat.shape, F32),
         compiler_params=small(),
         name="finish",
-    )(x, *here(own, code))
+    )(*here(hat, norm, own, code))
 
 
 def img_index(y, z, c):
@@ -260,73 +272,77 @@
     return lax.optimization_barrier((x, *others))[0]
 
 
-def gather(low, axis, perm, perm_z):
-    a1, a3 = send(low, axis, perm(1)), send(low, axis, perm(-1))
-    z = send(low, axis, perm_z)
-    a2 = send(a1, axis, perm(1))
-    z1, z3 = send(z, axis, perm(1)), send(z, axis, perm(-1))
-    z2 = send(z3, axis, perm(-1))
-    return jnp.concatenate([low, a1, a3, a2], 0), jnp.concatenate([z, z1, z3, z2], 0)
-
-
-def exchange_sum(v, axis, bit):
-    size = {"img": 16, "txt": 8}[axis]
-    return v + send(v, axis, [(i, i ^ bit) for i in range(size)])
+def gather(image, text):
+    ways = ((image, "txt", perm_x, PERM_ZHI), (text, "img", perm_y, PERM_ZLO))
+    z = [send(low, axis, pz) for low, axis, _, pz in ways]
+    a1 = [send(low, axis, perm(1)) for low, axis, perm, _ in ways]
+    a3 = [send(low, axis, perm(-1)) for low, axis, perm, _ in ways]
+    a2 = [send(a, axis, perm(1)) for a, (_, axis, perm, _) in zip(a1, ways)]
+    z, a1, a3, a2 = lax.optimization_barrier((z, a1, a3, a2))
+    z3 = [send(b, axis, perm(-1)) for b, (_, axis, perm, _) in zip(z, ways)]
+    z1 = [send(b, axis, perm(1)) for b, (_, axis, perm, _) in zip(z, ways)]
+    z3, z1 = lax.optimization_barrier((z3, z1))
+    z2 = lax.optimization_barrier([send(b, axis, perm(-1)) for b, (_, axis, perm, _) in zip(z3, ways)])
+    return [
+        (jnp.concatenate([w[0], a1[n], a3[n], a2[n]], 0), jnp.concatenate([z[n], z1[n], z3[n], z2[n]], 0))
+        for n, w in enumerate(ways)
+    ]
+
+
+def exchange_sum(v, axis, *perms):
+    got = [send(v, a, p) for a, p in zip(axis, perms)]
+    return v + got[0] if len(got) == 1 else (v + got[1]) + (got[0] + got[2])
 
 
 def local(image_embed, text_embed, log_scale, logit_bias):
     rows, d = image_embed.shape
-    image_low, text_low = normalize(image_embed, text_embed)
-    images = gather(image_low, "txt", perm_x, PERM_ZHI)
-    own = gather(text_low, "img", perm_y, PERM_ZLO)
+    (image_low, image_hat, image_norm), (text_low, text_hat, text_norm) = normalize(image_embed, text_embed)
+    images, own = gather(image_low, text_low)
     other = [send(t, "img", PERM_CORE) for t in own]
     partner = [send(x, "img", PERM_CORE) for x in images]
 
     i, t = lax.axis_index("img"), lax.axis_index("txt")
-    b = jnp.arange(8, dtype=jnp.int32)
-    j, zz = b % 4, b // 4
-    ring = jnp.where(j == 2, 3, jnp.where(j == 3, 2, j))
+    ring, zz = jnp.array(RING, jnp.int32), jnp.array(PARTNER, jnp.int32)
     g = 8 * i + ((t // 2 - ring) % 4) * 2 + ((t % 2) ^ zz)
     o = g % 16
-    k = (i // 4 - o // 4) % 4
+    k, z = (i // 4 - o // 4) % 4, ((i // 2) % 2) ^ ((o // 2) % 2)
     mine = 1 - ((i % 2) ^ (o % 2))
-    place = mine * 8 + (((i // 2) % 2) ^ ((o // 2) % 2)) * 4 + jnp.where(k == 2, 3, jnp.where(k == 3, 2, k))
+    found = jnp.logical_and(k[:, None] == ring[None, :], z[:, None] == zz[None, :])
+    place = mine * 8 + jnp.sum(jnp.where(found, jnp.arange(8, dtype=jnp.int32)[None, :], 0), 1)
     diag = jnp.where(g // 16 == t, place, -1).astype(jnp.int32)
     scale = jnp.exp(log_scale)
     scal = jnp.stack([scale, logit_bias, scale * LOG2E, logit_bias * LOG2E])
 
-    w_oth, sums = score_half(0, scal, diag, images, other)
+    w_own, sums = score_half(8, scal, diag, images, own)
+    w_oth, v = score_half(0, scal, diag, images, other, (sums,))
     w_rec = send(w_oth, "img", PERM_CORE)
-    w_own, v = score_half(8, scal, diag, images, own, (sums,))
-
-    u = exchange_sum(v, "img", 4)
-    i2 = pulls(1, (3,), w_own, w_oth, own, other, "far_image")
-    u = after(u, i2)
-    i2 = send(i2, "txt", perm_x(2))
-    v = exchange_sum(u, "img", 8)
-    t2 = pulls(0, (3,), after(w_own, u), w_rec, images, partner, "far_text")
-    v = after(v, t2)
-    t2 = send(t2, "img", perm_y(2))
-    u = exchange_sum(v, "img", 2)
-    i1, i3, i0 = pulls(1, (1, 2, 0), after(w_own, v), w_oth, own, other, "near_image")
-    u = after(u, i0)
-    i1, i3 = after(i1, i2), after(i3, i2)
+
+    ia, ib = pulls(1, w_own, w_oth, own, other, "far_image")
+    ia, ib = send(ia, "txt", perm_x(1)), send(ib, "txt", perm_x(-1))
+    ta, tb = pulls(0, w_own, w_rec, images, partner, "far_text")
+    v = after(v, ta)
+    ta, tb = send(ta, "img", perm_y(1)), send(tb, "img", perm_y(-1))
+    v = exchange_sum(v, ("img",), PERM_CORE)
+    i1, i3, i0 = pulls(1, w_own, w_oth, own, other, "near_image", (ia, ib))
+    v = after(v, i0)
     i1, i3 = send(i1, "txt", perm_x(-1)), send(i3, "txt", perm_x(1))
-    v = exchange_sum(u, "txt", 1)
-    t1, t3, t0 = pulls(0, (1, 2, 0), after(w_own, u), w_rec, images, partner, "near_text")
+    both = [(n, n ^ 17) for n in range(128)]
+    v = exchange_sum(v, ("img", ("img", "txt"), "txt"), PERM_ZLO, both, PERM_ZHI)
+    t1, t3, t0 = pulls(0, after(w_own, i0), w_rec, images, partner, "near_text", (ta, tb))
     v = after(v, t0)
-    t1, t3 = after(t1, t2), after(t3, t2)
     t1, t3 = send(t1, "img", perm_y(-1)), send(t3, "img", perm_y(1))
-    v = exchange_sum(v, "img", 1)
+
+    image_code = send(fold(partner_kernel, i0, (i1, i3), BF, "fold_partner"), "txt", PERM_ZHI)
+    image_own = fold(own_kernel, i0, (i1, i3), F32, "fold_own")
     v = after(v, i1, i3)
-    v = exchange_sum(exchange_sum(v, "txt", 2), "txt", 4)
-    t0 = after(t0, v)
-
-    icodes, tcodes = (i1, i2, i3), (t1, t2, t3)
-    image_code = send(fold_partner(i0, *icodes), "txt", PERM_ZHI)
-    text_code = send(fold_partner(t0, *tcodes), "img", PERM_ZLO)
-    image_grad = finish(image_embed, fold_own(i0, *icodes), image_code)
-    text_grad = finish(text_embed, fold_own(t0, *tcodes), text_code)
+    v = exchange_sum(v, ("txt",) * 3, perm_x(1), perm_x(2), perm_x(-1))
+    text_code = fold(partner_kernel, t0, (t1, t3), BF, "fold_partner")
+    v = after(v, text_code)
+    text_code = send(text_code, "img", PERM_ZLO)
+    text_own = fold(own_kernel, t0, (t1, t3), F32, "fold_own")
+    v = exchange_sum(v, ("img",) * 3, perm_y(1), perm_y(2), perm_y(-1))
+    image_grad = finish(image_hat, image_norm, image_own, image_code)
+    text_grad = finish(text_hat, text_norm, after(text_own, v), text_code)
     pairs = F32(128.0 * rows) * F32(128.0 * rows)
     return (v[0, 0] / pairs, image_grad, text_grad, v[0, 2] * scale / pairs, v[0, 1] / pairs)
 

time: 130 us -> 127 us (0.977)
  starting transfers between devices: 36.2 us -> 54.5 us
  waiting for transfers between devices: 49.5 us -> 32.7 us
  Pallas kernels: 32.4 us -> 29.3 us
  local copies, waits for them, and re-layouts: 3.74 us -> 2.15 us
    ppermute x25 -> x30, waiting for transfers between devices: 49.5 us -> 28.1 us  [the longest x10 8 us: exchange_sum(): got = [send(v, a, p) for a, p in zip(axis, perms)]]
    ppermute x25 -> x30, starting transfers between devices: 29.7 us -> 46.5 us  [the longest x10 12.5 us: exchange_sum(): got = [send(v, a, p) for a, p in zip(axis, perms)]]
    pallas_call x11, Pallas kernels: 21.8 us -> 18.5 us  [the longest x4 12.1 us: pulls(): pl.pallas_call(functools.partial(near_kernel if via else far_kernel, dims...]
    ppermute x2, waiting for transfers between devices: 0.01 us -> 2.82 us  [local(): i1, i3 = (send(i1, 'txt', perm_x(-1)), send(i3, 'txt', perm_x(1)))]
    ppermute x2, waiting for transfers between devices: 0.01 us -> 1.8 us  [local(): partner = [send(x, 'img', PERM_CORE) for x in images]]
    unnamed x17 -> x24, local copies, waits for them, and re-layouts: 3.02 us -> 1.43 us
    ppermute x2, starting transfers between devices: 2.03 us -> 3.42 us  [local(): t1, t3 = (send(t1, 'img', perm_y(-1)), send(t3, 'img', perm_y(1)))]
  transfers between devices with their start and end apart: 34 -> 39, of which waited for: 16 -> 18; matrix products, arithmetic and copies ran while one was open for 2% -> 2% of each run, Pallas kernels for 18% -> 16%
where the time goes in v5:
time: 127 us
  starting transfers between devices  54.5 us (43%)
  waiting for transfers between devices  32.7 us (26%)
  Pallas kernels  29.3 us (23%)
  between operations  7.67 us (6%)
  local copies, waits for them, and re-layouts  2.15 us (2%)
    ppermute x10, starting transfers between devices, exchange_sum(): got = [send(v, a, p) for a, p in zip(axis, perms)]  12.5 us
    pallas_call x4, Pallas kernels, pulls(): pl.pallas_call(functools.partial(near_kernel if via else far_kernel, dims...  12.1 us
    pallas_call x2, Pallas kernels, score_half(): pl.pallas_call(lambda *refs: scores_kernel(first, *refs), in_specs=[SM, S...  10.8 us
    ppermute x10, waiting for transfers between devices, exchange_sum(): got = [send(v, a, p) for a, p in zip(axis, perms)]  8 us
    ppermute x2, waiting for transfers between devices, gather(): a2 = [send(a, axis, perm(1)) for a, (_, axis, perm, _) in zip(a1, ways)]  5.43 us
    ppermute x2, starting transfers between devices, gather(): z3 = [send(b, axis, perm(-1)) for b, (_, axis, perm, _) in zip(z, ways)]  5.27 us
    ppermute x2, starting transfers between devices, gather(): z = [send(low, axis, pz) for low, axis, _, pz in ways]  4.89 us
    ppermute x2, waiting for transfers between devices, gather(): z1 = [send(b, axis, perm(1)) for b, (_, axis, perm, _) in zip(z, ways)]  4.4 us
  transfers between devices with their start and end apart: 39, of which 18 were waited for; matrix products, arithmetic and copies ran while one was open for 2% of the time, Pallas kernels for 16%

profile of v5, /device:TPU:0, one launch (start us, length us, event | category | flops | bytes accessed | tf_op | source)
XLA Modules:
  0.0 126.7 jit_solution(12798230544510124325)
XLA Ops:
  0.7 2.6 %normalize.1 = (bf16[128,1152]{1,0:T(8,128)(2,1)}, f32[128,1152]{1,0:T(8,128)}, f32[128,1]{1,0:T(8,128)}, bf16[128,1152]{1,0:T(8,128)(2,1)}, f32[128,1152]{1,0:T(8,128)}, /*index=5*/f32[128,1]{1,0:T(8,128)}) custom-call(f32[128,1152]{1,0:T(8,128)} %a_ref.1, f32[128,1152]{1,0:T(8,128)} %b_ref.1), custom_call_target="tpu_custom_call" | custom-call | tf_op jit(solution)/shard_map/normalize/pallas_call | solution.py:52
  3.3 1.6 %collective-permute-start.2 = (bf16[128,1152]{1,0:T(8,128)(2,1)}, bf16[128,1152]{1,0:T(8,128)(2,1)S(1)}, u32[]{:S(2)}, u32[]{:S(2)}) collective-permute-start(bf16[128,1152]{1,0:T(8,128)(2,1)} %get-tuple-element.46), channel_id=1, source_target_pairs={{0,2},{1,3},{2,4},{3,5},{4,6},{5,7},{6,0},{7,1},{8,10},{9,11},{10,... | collective-permute-start | bytes 884744 | tf_op jit(solution)/shard_map/ppermute | solution.py:278
  4.9 3.9 %collective-permute-start = (bf16[128,1152]{1,0:T(8,128)(2,1)}, bf16[128,1152]{1,0:T(8,128)(2,1)S(1)}, u32[]{:S(2)}, u32[]{:S(2)}) collective-permute-start(bf16[128,1152]{1,0:T(8,128)(2,1)} %get-tuple-element.46), channel_id=1, source_target_pairs={{0,1},{1,0},{2,3},{3,2},{4,5},{5,4},{6,7},{7,6},{8,9},{9,8},{10,11... | collective-permute-start | bytes 884744 | tf_op jit(solution)/shard_map/ppermute | solution.py:277
  8.8 1.6 %collective-permute-start.3 = (bf16[128,1152]{1,0:T(8,128)(2,1)}, bf16[128,1152]{1,0:T(8,128)(2,1)S(1)}, u32[]{:S(2)}, u32[]{:S(2)}) collective-permute-start(bf16[128,1152]{1,0:T(8,128)(2,1)} %get-tuple-element.47), channel_id=1, source_target_pairs={{0,32},{8,40},{16,48},{24,56},{32,64},{40,72},{48,80},{56,88},{64,... | collective-permute-start | bytes 884744 | tf_op jit(solution)/shard_map/ppermute | solution.py:278
  10.3 1.0 collective-permute-start.1
  11.4 1.7 %collective-permute-start.4 = (bf16[128,1152]{1,0:T(8,128)(2,1)}, bf16[128,1152]{1,0:T(8,128)(2,1)S(1)}, u32[]{:S(2)}, u32[]{:S(2)}) collective-permute-start(bf16[128,1152]{1,0:T(8,128)(2,1)} %get-tuple-element.46), channel_id=1, source_target_pairs={{0,6},{1,7},{2,0},{3,1},{4,2},{5,3},{6,4},{7,5},{8,14},{9,15},{10,... | collective-permute-start | bytes 884744 | tf_op jit(solution)/shard_map/ppermute | solution.py:279
  14.6 0.2 select_reduce_fusion
  14.8 1.8 %collective-permute-start.5 = (bf16[128,1152]{1,0:T(8,128)(2,1)}, bf16[128,1152]{1,0:T(8,128)(2,1)S(1)}, u32[]{:S(2)}, u32[]{:S(2)}) collective-permute-start(bf16[128,1152]{1,0:T(8,128)(2,1)} %get-tuple-element.47), channel_id=1, source_target_pairs={{0,96},{8,104},{16,112},{24,120},{32,0},{40,8},{48,16},{56,24},{64... | collective-permute-start | bytes 884744 | tf_op jit(solution)/shard_map/ppermute | solution.py:279
  16.6 1.9 %collective-permute-done.3 = bf16[128,1152]{1,0:T(8,128)(2,1)S(1)} collective-permute-done((bf16[128,1152]{1,0:T(8,128)(2,1)}, bf16[128,1152]{1,0:T(8,128)(2,1)S(1)}, u32[]{:S(2)}, u32[]{:S(2)}) %collective-permute-start.3) | collective-permute-done | bytes 294944 | tf_op jit(solution)/shard_map/ppermute | solution.py:278
  18.4 1.5 %collective-permute-start.6 = (bf16[128,1152]{1,0:T(8,128)(2,1)S(1)}, bf16[128,1152]{1,0:T(8,128)(2,1)S(1)}, u32[]{:S(2)}, u32[]{:S(2)}) collective-permute-start(bf16[128,1152]{1,0:T(8,128)(2,1)S(1)} %collective-permute-done.2), channel_id=1, source_target_pairs={{0,2},{1,3},{2,4},{3,5},{4,6},{5,7},{6,0},{7,1},{8,10},{9,11},{10,... | collective-permute-start | bytes 884744 | tf_op jit(solution)/shard_map/ppermute | solution.py:280
  19.9 0.3 collective-permute-start.7
  20.3 1.1 constant_dynamic-update-slice_fusion.3
  21.4 1.3 %collective-permute-done.1 = bf16[128,1152]{1,0:T(8,128)(2,1)S(1)} collective-permute-done((bf16[128,1152]{1,0:T(8,128)(2,1)}, bf16[128,1152]{1,0:T(8,128)(2,1)S(1)}, u32[]{:S(2)}, u32[]{:S(2)}) %collective-permute-start.1) | collective-permute-done | bytes 294944 | tf_op jit(solution)/shard_map/ppermute | solution.py:277
  22.8 4.2 %collective-permute-done.6 = bf16[128,1152]{1,0:T(8,128)(2,1)S(1)} collective-permute-done((bf16[128,1152]{1,0:T(8,128)(2,1)S(1)}, bf16[128,1152]{1,0:T(8,128)(2,1)S(1)}, u32[]{:S(2)}, u32[]{:S(2)}) %collective-permute-start.6) | collective-permute-done | bytes 294944 | tf_op jit(solution)/shard_map/ppermute | solution.py:280
  27.0 1.2 collective-permute-done.7
  28.2 1.2 collective-permute-start.10
  29.4 2.0 %collective-permute-start.8 = (bf16[128,1152]{1,0:T(8,128)(2,1)S(1)}, bf16[128,1152]{1,0:T(8,128)(2,1)S(1)}, u32[]{:S(2)}, u32[]{:S(2)}) collective-permute-start(bf16[128,1152]{1,0:T(8,128)(2,1)S(1)} %collective-permute-done), channel_id=1, source_target_pairs={{0,6},{1,7},{2,0},{3,1},{4,2},{5,3},{6,4},{7,5},{8,14},{9,15},{10,... | collective-permute-start | bytes 884744 | tf_op jit(solution)/shard_map/ppermute | solution.py:282
  31.4 3.2 %collective-permute-start.9 = (bf16[128,1152]{1,0:T(8,128)(2,1)S(1)}, bf16[128,1152]{1,0:T(8,128)(2,1)S(1)}, u32[]{:S(2)}, u32[]{:S(2)}) collective-permute-start(bf16[128,1152]{1,0:T(8,128)(2,1)S(1)} %collective-permute-done.1), channel_id=1, source_target_pairs={{0,96},{8,104},{16,112},{24,120},{32,0},{40,8},{48,16},{56,24},{64... | collective-permute-start | bytes 884744 | tf_op jit(solution)/shard_map/ppermute | solution.py:282
  35.0 1.2 collective-permute-done.10
  36.1 3.2 %collective-permute-done.11 = bf16[128,1152]{1,0:T(8,128)(2,1)S(1)} collective-permute-done((bf16[128,1152]{1,0:T(8,128)(2,1)S(1)}, bf16[128,1152]{1,0:T(8,128)(2,1)S(1)}, u32[]{:S(2)}, u32[]{:S(2)}) %collective-permute-start.11) | collective-permute-done | bytes 294944 | tf_op jit(solution)/shard_map/ppermute | solution.py:283
  39.4 0.7 collective-permute-start.12
  40.0 3.7 %collective-permute-start.13 = (bf16[128,1152]{1,0:T(8,128)(2,1)S(1)}, bf16[128,1152]{1,0:T(8,128)(2,1)S(1)}, u32[]{:S(2)}, u32[]{:S(2)}) collective-permute-start(bf16[128,1152]{1,0:T(8,128)(2,1)S(1)} %collective-permute-done.9), channel_id=1, source_target_pairs={{0,96},{8,104},{16,112},{24,120},{32,0},{40,8},{48,16},{56,24},{64... | collective-permute-start | bytes 884744 | tf_op jit(solution)/shard_map/ppermute | solution.py:285
  43.8 2.3 %collective-permute-done.12 = bf16[128,1152]{1,0:T(8,128)(2,1)S(1)} collective-permute-done((bf16[128,1152]{1,0:T(8,128)(2,1)S(1)}, bf16[128,1152]{1,0:T(8,128)(2,1)S(1)}, u32[]{:S(2)}, u32[]{:S(2)}) %collective-permute-start.12) | collective-permute-done | bytes 294944 | tf_op jit(solution)/shard_map/ppermute | solution.py:285
  46.1 1.9 %collective-permute-done.13 = bf16[128,1152]{1,0:T(8,128)(2,1)S(1)} collective-permute-done((bf16[128,1152]{1,0:T(8,128)(2,1)S(1)}, bf16[128,1152]{1,0:T(8,128)(2,1)S(1)}, u32[]{:S(2)}, u32[]{:S(2)}) %collective-permute-start.13) | collective-permute-done | bytes 294944 | tf_op jit(solution)/shard_map/ppermute | solution.py:285
  48.3 5.4 %scores.2 = (bf16[1024,1024]{1,0:T(8,128)(2,1)S(1)}, f32[24,512]{1,0:T(8,128)S(1)}) custom-call(f32[4]{0:T(128)S(1)} %pad_maximum_fusion.refs_0_, s32[8]{0:T(128)S(1)} %compare_select_fusion.6.refs_1_, bf16[512,1152]{1,0:T(8,128)(2,1)S(1)} %constant_dynamic-update-slice_fusion.refs_2_.r0a, ...), custom_call_target="tpu_custom_call" | custom-call | flops 2415919104 | bytes 4718592 | tf_op jit(solution)/shard_map/scores/pallas_call | solution.py:143
  53.7 5.4 %scores.3 = (bf16[1024,1024]{1,0:T(8,128)(2,1)S(1)}, f32[1,128]{1,0:T(1,128)S(1)}) custom-call(f32[4]{0:T(128)S(1)} %pad_maximum_fusion.refs_0_, s32[8]{0:T(128)S(1)} %compare_select_fusion.6.refs_1_, bf16[512,1152]{1,0:T(8,128)(2,1)S(1)} %constant_dynamic-update-slice_fusion.refs_2_.r0a, ...), custom_call_target="tpu_custom_call" | custom-call | flops 2415919104 | bytes 4718592 | tf_op jit(solution)/shard_map/scores/pallas_call | solution.py:143
  59.1 0.6 collective-permute-start.16
  59.8 0.4 collective-permute-start.18
  60.2 1.5 %far_image.1 = (bf16[128,1152]{1,0:T(8,128)(2,1)S(1)}, bf16[128,1152]{1,0:T(8,128)(2,1)S(1)}) custom-call(bf16[1024,1024]{1,0:T(8,128)(2,1)S(1)} %get-tuple-element.72.w0, bf16[1024,1024]{1,0:T(8,128)(2,1)S(1)} %get-tuple-element.65.w1, bf16[512,1152]{1,0:T(8,128)(2,1)S(1)} %constant_dynamic-update-slice_fusion.8.refs_4_.r0a, ...), custom_call_target="tpu_custom_call" | custom-call | flops 1207959552 | bytes 4718592 | tf_op jit(solution)/shard_map/far_image/pallas_call | solution.py:201
  61.7 1.0 collective-permute-start.20
  62.7 2.3 %collective-permute-start.21 = (bf16[128,1152]{1,0:T(8,128)(2,1)S(1)}, bf16[128,1152]{1,0:T(8,128)(2,1)S(1)}, u32[]{:S(2)}, u32[]{:S(2)}) collective-permute-start(bf16[128,1152]{1,0:T(8,128)(2,1)S(1)} %get-tuple-element.69), channel_id=1, source_target_pairs={{0,6},{1,7},{2,0},{3,1},{4,2},{5,3},{6,4},{7,5},{8,14},{9,15},{10,... | collective-permute-start | bytes 884744 | tf_op jit(solution)/shard_map/ppermute | solution.py:321
  65.0 0.1 collective-permute-done.17.r1a
  65.2 1.7 %collective-permute-done.18.r1b = bf16[512,1152]{1,0:T(8,128)(2,1)S(1)} collective-permute-done((bf16[512,1152]{1,0:T(8,128)(2,1)S(1)}, bf16[512,1152]{1,0:T(8,128)(2,1)S(1)}, u32[]{:S(2)}, u32[]{:S(2)}) %collective-permute-start.18) | collective-permute-done | bytes 1179680 | tf_op jit(solution)/shard_map/ppermute | solution.py:302
  66.9 1.6 %far_text.1 = (bf16[128,1152]{1,0:T(8,128)(2,1)S(1)}, bf16[128,1152]{1,0:T(8,128)(2,1)S(1)}) custom-call(bf16[1024,1024]{1,0:T(8,128)(2,1)S(1)} %get-tuple-element.72.w0, bf16[1024,1024]{1,0:T(8,128)(2,1)S(1)} %collective-permute-done.16.w1, bf16[512,1152]{1,0:T(8,128)(2,1)S(1)} %constant_dynamic-update-slice_fusion.refs_2_.r0a, ...), custom_call_target="tpu_custom_call" | custom-call | flops 1207959552 | bytes 4718592 | tf_op jit(solution)/shard_map/far_text/pallas_call | solution.py:201
  68.5 3.4 %collective-permute-start.26 = (bf16[128,1152]{1,0:T(8,128)(2,1)S(1)}, bf16[128,1152]{1,0:T(8,128)(2,1)S(1)}, u32[]{:S(2)}, u32[]{:S(2)}) collective-permute-start(bf16[128,1152]{1,0:T(8,128)(2,1)S(1)} %get-tuple-element.73), channel_id=1, source_target_pairs={{0,96},{8,104},{16,112},{24,120},{32,0},{40,8},{48,16},{56,24},{64... | collective-permute-start | bytes 884744 | tf_op jit(solution)/shard_map/ppermute | solution.py:324
  72.0 4.5 %near_image.1 = (bf16[256,1152]{1,0:T(8,128)(2,1)S(1)}, bf16[256,1152]{1,0:T(8,128)(2,1)S(1)}, f32[256,1152]{1,0:T(8,128)S(1)}) custom-call(bf16[1024,1024]{1,0:T(8,128)(2,1)S(1)} %get-tuple-element.72.w0, bf16[1024,1024]{1,0:T(8,128)(2,1)S(1)} %get-tuple-element.65.w1, bf16[512,1152]{1,0:T(8,128)(2,1)S(1)} %constant_dynamic-update-slice_fusion.8.refs_4_.r0a, ...), custom_call_target="tpu_custom_call" | custom-call | flops 3623878656 | bytes 4718592 | tf_op jit(solution)/shard_map/near_image/pallas_call | solution.py:201
  76.5 3.2 %collective-permute-start.27 = (bf16[256,1152]{1,0:T(8,128)(2,1)S(1)}, bf16[256,1152]{1,0:T(8,128)(2,1)S(1)}, u32[]{:S(2)}, u32[]{:S(2)}) collective-permute-start(bf16[256,1152]{1,0:T(8,128)(2,1)S(1)} %get-tuple-element.76), channel_id=1, source_target_pairs={{0,6},{1,7},{2,0},{3,1},{4,2},{5,3},{6,4},{7,5},{8,14},{9,15},{10,... | collective-permute-start | bytes 1769480 | tf_op jit(solution)/shard_map/ppermute | solution.py:328
  79.7 4.5 %near_text.1 = (bf16[256,1152]{1,0:T(8,128)(2,1)S(1)}, bf16[256,1152]{1,0:T(8,128)(2,1)S(1)}, f32[256,1152]{1,0:T(8,128)S(1)}) custom-call(bf16[1024,1024]{1,0:T(8,128)(2,1)S(1)} %get-tuple-element.72.w0, bf16[1024,1024]{1,0:T(8,128)(2,1)S(1)} %collective-permute-done.16.w1, bf16[512,1152]{1,0:T(8,128)(2,1)S(1)} %constant_dynamic-update-slice_fusion.refs_2_.r0a, ...), custom_call_target="tpu_custom_call" | custom-call | flops 3623878656 | bytes 4718592 | tf_op jit(solution)/shard_map/near_text/pallas_call | solution.py:201
  84.3 3.4 %collective-permute-start.32 = (bf16[256,1152]{1,0:T(8,128)(2,1)S(1)}, bf16[256,1152]{1,0:T(8,128)(2,1)S(1)}, u32[]{:S(2)}, u32[]{:S(2)}) collective-permute-start(bf16[256,1152]{1,0:T(8,128)(2,1)S(1)} %get-tuple-element.79), channel_id=1, source_target_pairs={{0,96},{8,104},{16,112},{24,120},{32,0},{40,8},{48,16},{56,24},{64... | collective-permute-start | bytes 1769480 | tf_op jit(solution)/shard_map/ppermute | solution.py:333
  87.7 1.1 collective-permute-done.19
  88.8 2.2 %collective-permute-start.22 = (f32[1,128]{1,0:T(1,128)S(1)}, f32[1,128]{1,0:T(1,128)S(1)}, u32[]{:S(2)}, u32[]{:S(2)}) collective-permute-start(f32[1,128]{1,0:T(1,128)S(1)} %add.92), channel_id=1, source_target_pairs={{0,17},{1,16},{2,19},{3,18},{4,21},{5,20},{6,23},{7,22},{8,25},{9,... | collective-permute-start | bytes 1544 | tf_op jit(solution)/shard_map/ppermute | solution.py:293
  91.0 1.0 collective-permute-done.27.c1
  92.0 1.0 collective-permute-start.23
  93.0 1.8 %collective-permute-done.28.c3 = bf16[256,1152]{1,0:T(8,128)(2,1)S(1)} collective-permute-done((bf16[256,1152]{1,0:T(8,128)(2,1)S(1)}, bf16[256,1152]{1,0:T(8,128)(2,1)S(1)}, u32[]{:S(2)}, u32[]{:S(2)}) %collective-permute-start.28) | collective-permute-done | bytes 589856 | tf_op jit(solution)/shard_map/ppermute | solution.py:328
  94.8 1.7 %collective-permute-start.24 = (f32[1,128]{1,0:T(1,128)S(1)}, f32[1,128]{1,0:T(1,128)S(1)}, u32[]{:S(2)}, u32[]{:S(2)}) collective-permute-start(f32[1,128]{1,0:T(1,128)S(1)} %add.92), channel_id=1, source_target_pairs={{0,1},{1,0},{2,3},{3,2},{4,5},{5,4},{6,7},{7,6},{8,9},{9,8},{10,11... | collective-permute-start | bytes 1544 | tf_op jit(solution)/shard_map/ppermute | solution.py:293
  96.5 0.4 fold_partner.3
  96.9 1.9 %collective-permute-start.37 = (bf16[128,1152]{1,0:T(8,128)(2,1)S(1)}, bf16[128,1152]{1,0:T(8,128)(2,1)S(1)}, u32[]{:S(2)}, u32[]{:S(2)}) collective-permute-start(bf16[128,1152]{1,0:T(8,128)(2,1)S(1)} %fold_partner.3), channel_id=1, source_target_pairs={{0,1},{1,0},{2,3},{3,2},{4,5},{5,4},{6,7},{7,6},{8,9},{9,8},{10,11... | collective-permute-start | bytes 884744 | tf_op jit(solution)/shard_map/ppermute | solution.py:335
  98.9 1.0 collective-permute-done.24
  99.9 0.2 collective-permute-start.29
  100.1 1.6 %collective-permute-start.30 = (f32[1,128]{1,0:T(1,128)S(1)}, f32[1,128]{1,0:T(1,128)S(1)}, u32[]{:S(2)}, u32[]{:S(2)}) collective-permute-start(f32[1,128]{1,0:T(1,128)S(1)} %add_add_fusion.2), channel_id=1, source_target_pairs={{0,2},{1,3},{2,4},{3,5},{4,6},{5,7},{6,0},{7,1},{8,10},{9,11},{10,... | collective-permute-start | bytes 1544 | tf_op jit(solution)/shard_map/ppermute | solution.py:293
  101.7 3.2 %collective-permute-done.29 = f32[1,128]{1,0:T(1,128)S(1)} collective-permute-done((f32[1,128]{1,0:T(1,128)S(1)}, f32[1,128]{1,0:T(1,128)S(1)}, u32[]{:S(2)}, u32[]{:S(2)}) %collective-permute-start.29) | collective-permute-done | bytes 544 | tf_op jit(solution)/shard_map/ppermute | solution.py:293
  104.9 1.0 collective-permute-start.31
  105.9 2.6 %collective-permute-done.31 = f32[1,128]{1,0:T(1,128)S(1)} collective-permute-done((f32[1,128]{1,0:T(1,128)S(1)}, f32[1,128]{1,0:T(1,128)S(1)}, u32[]{:S(2)}, u32[]{:S(2)}) %collective-permute-start.31) | collective-permute-done | bytes 544 | tf_op jit(solution)/shard_map/ppermute | solution.py:293
  108.5 0.4 fold_partner.2
  108.9 1.7 %collective-permute-start.34 = (f32[1,128]{1,0:T(1,128)S(1)}, f32[1,128]{1,0:T(1,128)S(1)}, u32[]{:S(2)}, u32[]{:S(2)}) collective-permute-start(f32[1,128]{1,0:T(1,128)S(1)} %add_add_fusion.1), channel_id=1, source_target_pairs={{0,64},{8,72},{16,80},{24,88},{32,96},{40,104},{48,112},{56,120},{... | collective-permute-start | bytes 1544 | tf_op jit(solution)/shard_map/ppermute | solution.py:293
  110.6 2.6 %collective-permute-start.35 = (f32[1,128]{1,0:T(1,128)S(1)}, f32[1,128]{1,0:T(1,128)S(1)}, u32[]{:S(2)}, u32[]{:S(2)}) collective-permute-start(f32[1,128]{1,0:T(1,128)S(1)} %add_add_fusion.1), channel_id=1, source_target_pairs={{0,32},{8,40},{16,48},{24,56},{32,64},{40,72},{48,80},{56,88},{64,... | collective-permute-start | bytes 1544 | tf_op jit(solution)/shard_map/ppermute | solution.py:293
  113.2 0.6 collective-permute-start.36
  113.8 0.3 fold_own.2.own
  114.2 1.2 finish.2
  115.4 1.0 collective-permute-start.38
  116.4 0.3 fold_own.3.own
  116.8 0.6 fusion.12
  119.3 2.8 %collective-permute-done.38.code_ref = bf16[128,1152]{1,0:T(8,128)(2,1)S(1)} collective-permute-done((bf16[128,1152]{1,0:T(8,128)(2,1)S(1)}, bf16[128,1152]{1,0:T(8,128)(2,1)S(1)}, u32[]{:S(2)}, u32[]{:S(2)}) %collective-permute-start.38) | collective-permute-done | bytes 294944 | tf_op jit(solution)/shard_map/ppermute | solution.py:341
  122.1 1.2 finish.3
  (65 shorter events, 1.1 us)
Async XLA Ops:
  0.6 13.8 %copy-start.4 = (s32[8]{0:T(128)S(1)}, s32[8]{0:T(128)}, u32[]{:S(2)}) copy-start(s32[8]{0:T(128)} %constant.142.clone) | copy-start | bytes 100
  0.6 13.8 %copy-start.6 = (s32[8]{0:T(128)S(1)}, s32[8]{0:T(128)}, u32[]{:S(2)}) copy-start(s32[8]{0:T(128)} %constant.143) | copy-start | bytes 100
  0.7 13.9 %copy-start.5 = (s32[8]{0:T(128)S(1)}, s32[8]{0:T(128)}, u32[]{:S(2)}) copy-start(s32[8]{0:T(128)} %constant.141.clone) | copy-start | bytes 100
  3.3 11.4 %collective-permute-start.2 = (bf16[128,1152]{1,0:T(8,128)(2,1)}, bf16[128,1152]{1,0:T(8,128)(2,1)S(1)}, u32[]{:S(2)}, u32[]{:S(2)}) collective-permute-start(bf16[128,1152]{1,0:T(8,128)(2,1)} %get-tuple-element.46), channel_id=1, source_target_pairs={{0,2},{1,3},{2,4},{3,5},{4,6},{5,7},{6,0},{7,1},{8,10},{9,11},{10,... | collective-permute-start | bytes 884744 | tf_op jit(solution)/shard_map/ppermute | solution.py:278
  4.9 15.0 %collective-permute-start = (bf16[128,1152]{1,0:T(8,128)(2,1)}, bf16[128,1152]{1,0:T(8,128)(2,1)S(1)}, u32[]{:S(2)}, u32[]{:S(2)}) collective-permute-start(bf16[128,1152]{1,0:T(8,128)(2,1)} %get-tuple-element.46), channel_id=1, source_target_pairs={{0,1},{1,0},{2,3},{3,2},{4,5},{5,4},{6,7},{7,6},{8,9},{9,8},{10,11... | collective-permute-start | bytes 884744 | tf_op jit(solution)/shard_map/ppermute | solution.py:277
  8.8 9.7 %collective-permute-start.3 = (bf16[128,1152]{1,0:T(8,128)(2,1)}, bf16[128,1152]{1,0:T(8,128)(2,1)S(1)}, u32[]{:S(2)}, u32[]{:S(2)}) collective-permute-start(bf16[128,1152]{1,0:T(8,128)(2,1)} %get-tuple-element.47), channel_id=1, source_target_pairs={{0,32},{8,40},{16,48},{24,56},{32,64},{40,72},{48,80},{56,88},{64,... | collective-permute-start | bytes 884744 | tf_op jit(solution)/shard_map/ppermute | solution.py:278
  10.3 12.4 %collective-permute-start.1 = (bf16[128,1152]{1,0:T(8,128)(2,1)}, bf16[128,1152]{1,0:T(8,128)(2,1)S(1)}, u32[]{:S(2)}, u32[]{:S(2)}) collective-permute-start(bf16[128,1152]{1,0:T(8,128)(2,1)} %get-tuple-element.47), channel_id=1, source_target_pairs={{0,16},{8,24},{16,0},{24,8},{32,48},{40,56},{48,32},{56,40},{64,80... | collective-permute-start | bytes 884744 | tf_op jit(solution)/shard_map/ppermute | solution.py:277
  11.4 11.4 %collective-permute-start.4 = (bf16[128,1152]{1,0:T(8,128)(2,1)}, bf16[128,1152]{1,0:T(8,128)(2,1)S(1)}, u32[]{:S(2)}, u32[]{:S(2)}) collective-permute-start(bf16[128,1152]{1,0:T(8,128)(2,1)} %get-tuple-element.46), channel_id=1, source_target_pairs={{0,6},{1,7},{2,0},{3,1},{4,2},{5,3},{6,4},{7,5},{8,14},{9,15},{10,... | collective-permute-start | bytes 884744 | tf_op jit(solution)/shard_map/ppermute | solution.py:279
  14.8 8.0 %collective-permute-start.5 = (bf16[128,1152]{1,0:T(8,128)(2,1)}, bf16[128,1152]{1,0:T(8,128)(2,1)S(1)}, u32[]{:S(2)}, u32[]{:S(2)}) collective-permute-start(bf16[128,1152]{1,0:T(8,128)(2,1)} %get-tuple-element.47), channel_id=1, source_target_pairs={{0,96},{8,104},{16,112},{24,120},{32,0},{40,8},{48,16},{56,24},{64... | collective-permute-start | bytes 884744 | tf_op jit(solution)/shard_map/ppermute | solution.py:279
  18.4 8.5 %collective-permute-start.6 = (bf16[128,1152]{1,0:T(8,128)(2,1)S(1)}, bf16[128,1152]{1,0:T(8,128)(2,1)S(1)}, u32[]{:S(2)}, u32[]{:S(2)}) collective-permute-start(bf16[128,1152]{1,0:T(8,128)(2,1)S(1)} %collective-permute-done.2), channel_id=1, source_target_pairs={{0,2},{1,3},{2,4},{3,5},{4,6},{5,7},{6,0},{7,1},{8,10},{9,11},{10,... | collective-permute-start | bytes 884744 | tf_op jit(solution)/shard_map/ppermute | solution.py:280
  19.9 8.3 %collective-permute-start.7 = (bf16[128,1152]{1,0:T(8,128)(2,1)S(1)}, bf16[128,1152]{1,0:T(8,128)(2,1)S(1)}, u32[]{:S(2)}, u32[]{:S(2)}) collective-permute-start(bf16[128,1152]{1,0:T(8,128)(2,1)S(1)} %collective-permute-done.3), channel_id=1, source_target_pairs={{0,32},{8,40},{16,48},{24,56},{32,64},{40,72},{48,80},{56,88},{64,... | collective-permute-start | bytes 884744 | tf_op jit(solution)/shard_map/ppermute | solution.py:280
  28.2 7.9 %collective-permute-start.10 = (bf16[128,1152]{1,0:T(8,128)(2,1)S(1)}, bf16[128,1152]{1,0:T(8,128)(2,1)S(1)}, u32[]{:S(2)}, u32[]{:S(2)}) collective-permute-start(bf16[128,1152]{1,0:T(8,128)(2,1)S(1)} %collective-permute-done), channel_id=1, source_target_pairs={{0,2},{1,3},{2,4},{3,5},{4,6},{5,7},{6,0},{7,1},{8,10},{9,11},{10,... | collective-permute-start | bytes 884744 | tf_op jit(solution)/shard_map/ppermute | solution.py:283
  29.4 10.0 %collective-permute-start.8 = (bf16[128,1152]{1,0:T(8,128)(2,1)S(1)}, bf16[128,1152]{1,0:T(8,128)(2,1)S(1)}, u32[]{:S(2)}, u32[]{:S(2)}) collective-permute-start(bf16[128,1152]{1,0:T(8,128)(2,1)S(1)} %collective-permute-done), channel_id=1, source_target_pairs={{0,6},{1,7},{2,0},{3,1},{4,2},{5,3},{6,4},{7,5},{8,14},{9,15},{10,... | collective-permute-start | bytes 884744 | tf_op jit(solution)/shard_map/ppermute | solution.py:282
  31.4 7.9 %collective-permute-start.11 = (bf16[128,1152]{1,0:T(8,128)(2,1)S(1)}, bf16[128,1152]{1,0:T(8,128)(2,1)S(1)}, u32[]{:S(2)}, u32[]{:S(2)}) collective-permute-start(bf16[128,1152]{1,0:T(8,128)(2,1)S(1)} %collective-permute-done.1), channel_id=1, source_target_pairs={{0,32},{8,40},{16,48},{24,56},{32,64},{40,72},{48,80},{56,88},{64,... | collective-permute-start | bytes 884744 | tf_op jit(solution)/shard_map/ppermute | solution.py:283
  31.4 7.9 %collective-permute-start.9 = (bf16[128,1152]{1,0:T(8,128)(2,1)S(1)}, bf16[128,1152]{1,0:T(8,128)(2,1)S(1)}, u32[]{:S(2)}, u32[]{:S(2)}) collective-permute-start(bf16[128,1152]{1,0:T(8,128)(2,1)S(1)} %collective-permute-done.1), channel_id=1, source_target_pairs={{0,96},{8,104},{16,112},{24,120},{32,0},{40,8},{48,16},{56,24},{64... | collective-permute-start | bytes 884744 | tf_op jit(solution)/shard_map/ppermute | solution.py:282
  34.8 18.9 %collective-permute-start.14 = (bf16[512,1152]{1,0:T(8,128)(2,1)S(1)}, bf16[512,1152]{1,0:T(8,128)(2,1)S(1)}, u32[]{:S(2)}, u32[]{:S(2)}) collective-permute-start(bf16[512,1152]{1,0:T(8,128)(2,1)S(1)} %constant_dynamic-update-slice_fusion.8.refs_4_.r0a), channel_id=1, source_target_pairs={{0,8},{8,0},{16,24},{24,16},{32,40},{40,32},{48,56},{56,48},{64,72... | collective-permute-start | bytes 3538952 | tf_op jit(solution)/shard_map/ppermute | solution.py:301
  39.4 6.7 %collective-permute-start.12 = (bf16[128,1152]{1,0:T(8,128)(2,1)S(1)}, bf16[128,1152]{1,0:T(8,128)(2,1)S(1)}, u32[]{:S(2)}, u32[]{:S(2)}) collective-permute-start(bf16[128,1152]{1,0:T(8,128)(2,1)S(1)} %collective-permute-done.8), channel_id=1, source_target_pairs={{0,6},{1,7},{2,0},{3,1},{4,2},{5,3},{6,4},{7,5},{8,14},{9,15},{10,... | collective-permute-start | bytes 884744 | tf_op jit(solution)/shard_map/ppermute | solution.py:285
  40.0 7.9 %collective-permute-start.13 = (bf16[128,1152]{1,0:T(8,128)(2,1)S(1)}, bf16[128,1152]{1,0:T(8,128)(2,1)S(1)}, u32[]{:S(2)}, u32[]{:S(2)}) collective-permute-start(bf16[128,1152]{1,0:T(8,128)(2,1)S(1)} %collective-permute-done.9), channel_id=1, source_target_pairs={{0,96},{8,104},{16,112},{24,120},{32,0},{40,8},{48,16},{56,24},{64... | collective-permute-start | bytes 884744 | tf_op jit(solution)/shard_map/ppermute | solution.py:285
  48.0 5.7 %collective-permute-start.15 = (bf16[512,1152]{1,0:T(8,128)(2,1)S(1)}, bf16[512,1152]{1,0:T(8,128)(2,1)S(1)}, u32[]{:S(2)}, u32[]{:S(2)}) collective-permute-start(bf16[512,1152]{1,0:T(8,128)(2,1)S(1)} %constant_dynamic-update-slice_fusion.12.refs_5_.r0b), channel_id=1, source_target_pairs={{0,8},{8,0},{16,24},{24,16},{32,40},{40,32},{48,56},{56,48},{64,72... | collective-permute-start | bytes 3538952 | tf_op jit(solution)/shard_map/ppermute | solution.py:301
  59.1 7.7 %collective-permute-start.16 = (bf16[1024,1024]{1,0:T(8,128)(2,1)S(1)}, bf16[1024,1024]{1,0:T(8,128)(2,1)S(1)}, u32[]{:S(2)}, u32[]{:S(2)}) collective-permute-start(bf16[1024,1024]{1,0:T(8,128)(2,1)S(1)} %get-tuple-element.65.w1), channel_id=1, source_target_pairs={{0,8},{8,0},{16,24},{24,16},{32,40},{40,32},{48,56},{56,48},{64,72... | collective-permute-start | bytes 6291464 | tf_op jit(solution)/shard_map/ppermute | solution.py:318
  59.7 5.5 %collective-permute-start.17 = (bf16[512,1152]{1,0:T(8,128)(2,1)S(1)}, bf16[512,1152]{1,0:T(8,128)(2,1)S(1)}, u32[]{:S(2)}, u32[]{:S(2)}) collective-permute-start(bf16[512,1152]{1,0:T(8,128)(2,1)S(1)} %constant_dynamic-update-slice_fusion.refs_2_.r0a), channel_id=1, source_target_pairs={{0,8},{8,0},{16,24},{24,16},{32,40},{40,32},{48,56},{56,48},{64,72... | collective-permute-start | bytes 3538952 | tf_op jit(solution)/shard_map/ppermute | solution.py:302
  59.8 7.1 %collective-permute-start.18 = (bf16[512,1152]{1,0:T(8,128)(2,1)S(1)}, bf16[512,1152]{1,0:T(8,128)(2,1)S(1)}, u32[]{:S(2)}, u32[]{:S(2)}) collective-permute-start(bf16[512,1152]{1,0:T(8,128)(2,1)S(1)} %constant_dynamic-update-slice_fusion.4.refs_3_.r0b), channel_id=1, source_target_pairs={{0,8},{8,0},{16,24},{24,16},{32,40},{40,32},{48,56},{56,48},{64,72... | collective-permute-start | bytes 3538952 | tf_op jit(solution)/shard_map/ppermute | solution.py:302
  61.7 10.3 %collective-permute-start.20 = (bf16[128,1152]{1,0:T(8,128)(2,1)S(1)}, bf16[128,1152]{1,0:T(8,128)(2,1)S(1)}, u32[]{:S(2)}, u32[]{:S(2)}) collective-permute-start(bf16[128,1152]{1,0:T(8,128)(2,1)S(1)} %get-tuple-element.68), channel_id=1, source_target_pairs={{0,2},{1,3},{2,4},{3,5},{4,6},{5,7},{6,0},{7,1},{8,10},{9,11},{10,... | collective-permute-start | bytes 884744 | tf_op jit(solution)/shard_map/ppermute | solution.py:321
  62.7 9.3 %collective-permute-start.21 = (bf16[128,1152]{1,0:T(8,128)(2,1)S(1)}, bf16[128,1152]{1,0:T(8,128)(2,1)S(1)}, u32[]{:S(2)}, u32[]{:S(2)}) collective-permute-start(bf16[128,1152]{1,0:T(8,128)(2,1)S(1)} %get-tuple-element.69), channel_id=1, source_target_pairs={{0,6},{1,7},{2,0},{3,1},{4,2},{5,3},{6,4},{7,5},{8,14},{9,15},{10,... | collective-permute-start | bytes 884744 | tf_op jit(solution)/shard_map/ppermute | solution.py:321
  68.4 11.3 %collective-permute-start.25 = (bf16[128,1152]{1,0:T(8,128)(2,1)S(1)}, bf16[128,1152]{1,0:T(8,128)(2,1)S(1)}, u32[]{:S(2)}, u32[]{:S(2)}) collective-permute-start(bf16[128,1152]{1,0:T(8,128)(2,1)S(1)} %get-tuple-element.66), channel_id=1, source_target_pairs={{0,32},{8,40},{16,48},{24,56},{32,64},{40,72},{48,80},{56,88},{64,... | collective-permute-start | bytes 884744 | tf_op jit(solution)/shard_map/ppermute | solution.py:324
  68.5 11.3 %collective-permute-start.26 = (bf16[128,1152]{1,0:T(8,128)(2,1)S(1)}, bf16[128,1152]{1,0:T(8,128)(2,1)S(1)}, u32[]{:S(2)}, u32[]{:S(2)}) collective-permute-start(bf16[128,1152]{1,0:T(8,128)(2,1)S(1)} %get-tuple-element.73), channel_id=1, source_target_pairs={{0,96},{8,104},{16,112},{24,120},{32,0},{40,8},{48,16},{56,24},{64... | collective-permute-start | bytes 884744 | tf_op jit(solution)/shard_map/ppermute | solution.py:324
  76.5 15.5 %collective-permute-start.27 = (bf16[256,1152]{1,0:T(8,128)(2,1)S(1)}, bf16[256,1152]{1,0:T(8,128)(2,1)S(1)}, u32[]{:S(2)}, u32[]{:S(2)}) collective-permute-start(bf16[256,1152]{1,0:T(8,128)(2,1)S(1)} %get-tuple-element.76), channel_id=1, source_target_pairs={{0,6},{1,7},{2,0},{3,1},{4,2},{5,3},{6,4},{7,5},{8,14},{9,15},{10,... | collective-permute-start | bytes 1769480 | tf_op jit(solution)/shard_map/ppermute | solution.py:328
  79.7 15.1 %collective-permute-start.28 = (bf16[256,1152]{1,0:T(8,128)(2,1)S(1)}, bf16[256,1152]{1,0:T(8,128)(2,1)S(1)}, u32[]{:S(2)}, u32[]{:S(2)}) collective-permute-start(bf16[256,1152]{1,0:T(8,128)(2,1)S(1)} %get-tuple-element.77), channel_id=1, source_target_pairs={{0,2},{1,3},{2,4},{3,5},{4,6},{5,7},{6,0},{7,1},{8,10},{9,11},{10,... | collective-permute-start | bytes 1769480 | tf_op jit(solution)/shard_map/ppermute | solution.py:328
  84.3 24.2 %collective-permute-start.32 = (bf16[256,1152]{1,0:T(8,128)(2,1)S(1)}, bf16[256,1152]{1,0:T(8,128)(2,1)S(1)}, u32[]{:S(2)}, u32[]{:S(2)}) collective-permute-start(bf16[256,1152]{1,0:T(8,128)(2,1)S(1)} %get-tuple-element.79), channel_id=1, source_target_pairs={{0,96},{8,104},{16,112},{24,120},{32,0},{40,8},{48,16},{56,24},{64... | collective-permute-start | bytes 1769480 | tf_op jit(solution)/shard_map/ppermute | solution.py:333
  87.7 20.8 %collective-permute-start.33 = (bf16[256,1152]{1,0:T(8,128)(2,1)S(1)}, bf16[256,1152]{1,0:T(8,128)(2,1)S(1)}, u32[]{:S(2)}, u32[]{:S(2)}) collective-permute-start(bf16[256,1152]{1,0:T(8,128)(2,1)S(1)} %get-tuple-element.80), channel_id=1, source_target_pairs={{0,32},{8,40},{16,48},{24,56},{32,64},{40,72},{48,80},{56,88},{64,... | collective-permute-start | bytes 1769480 | tf_op jit(solution)/shard_map/ppermute | solution.py:333
  87.7 1.1 collective-permute-start.19
  88.8 8.1 %collective-permute-start.22 = (f32[1,128]{1,0:T(1,128)S(1)}, f32[1,128]{1,0:T(1,128)S(1)}, u32[]{:S(2)}, u32[]{:S(2)}) collective-permute-start(f32[1,128]{1,0:T(1,128)S(1)} %add.92), channel_id=1, source_target_pairs={{0,17},{1,16},{2,19},{3,18},{4,21},{5,20},{6,23},{7,22},{8,25},{9,... | collective-permute-start | bytes 1544 | tf_op jit(solution)/shard_map/ppermute | solution.py:293
  92.0 6.9 %collective-permute-start.23 = (f32[1,128]{1,0:T(1,128)S(1)}, f32[1,128]{1,0:T(1,128)S(1)}, u32[]{:S(2)}, u32[]{:S(2)}) collective-permute-start(f32[1,128]{1,0:T(1,128)S(1)} %add.92), channel_id=1, source_target_pairs={{0,16},{8,24},{16,0},{24,8},{32,48},{40,56},{48,32},{56,40},{64,80... | collective-permute-start | bytes 1544 | tf_op jit(solution)/shard_map/ppermute | solution.py:293
  94.8 5.1 %collective-permute-start.24 = (f32[1,128]{1,0:T(1,128)S(1)}, f32[1,128]{1,0:T(1,128)S(1)}, u32[]{:S(2)}, u32[]{:S(2)}) collective-permute-start(f32[1,128]{1,0:T(1,128)S(1)} %add.92), channel_id=1, source_target_pairs={{0,1},{1,0},{2,3},{3,2},{4,5},{5,4},{6,7},{7,6},{8,9},{9,8},{10,11... | collective-permute-start | bytes 1544 | tf_op jit(solution)/shard_map/ppermute | solution.py:293
  96.9 17.2 %collective-permute-start.37 = (bf16[128,1152]{1,0:T(8,128)(2,1)S(1)}, bf16[128,1152]{1,0:T(8,128)(2,1)S(1)}, u32[]{:S(2)}, u32[]{:S(2)}) collective-permute-start(bf16[128,1152]{1,0:T(8,128)(2,1)S(1)} %fold_partner.3), channel_id=1, source_target_pairs={{0,1},{1,0},{2,3},{3,2},{4,5},{5,4},{6,7},{7,6},{8,9},{9,8},{10,11... | collective-permute-start | bytes 884744 | tf_op jit(solution)/shard_map/ppermute | solution.py:335
  99.9 5.0 %collective-permute-start.29 = (f32[1,128]{1,0:T(1,128)S(1)}, f32[1,128]{1,0:T(1,128)S(1)}, u32[]{:S(2)}, u32[]{:S(2)}) collective-permute-start(f32[1,128]{1,0:T(1,128)S(1)} %add_add_fusion.2), channel_id=1, source_target_pairs={{0,4},{1,5},{2,6},{3,7},{4,0},{5,1},{6,2},{7,3},{8,12},{9,13},{10,... | collective-permute-start | bytes 1544 | tf_op jit(solution)/shard_map/ppermute | solution.py:293
  100.1 5.8 %collective-permute-start.30 = (f32[1,128]{1,0:T(1,128)S(1)}, f32[1,128]{1,0:T(1,128)S(1)}, u32[]{:S(2)}, u32[]{:S(2)}) collective-permute-start(f32[1,128]{1,0:T(1,128)S(1)} %add_add_fusion.2), channel_id=1, source_target_pairs={{0,2},{1,3},{2,4},{3,5},{4,6},{5,7},{6,0},{7,1},{8,10},{9,11},{10,... | collective-permute-start | bytes 1544 | tf_op jit(solution)/shard_map/ppermute | solution.py:293
  104.9 3.5 %collective-permute-start.31 = (f32[1,128]{1,0:T(1,128)S(1)}, f32[1,128]{1,0:T(1,128)S(1)}, u32[]{:S(2)}, u32[]{:S(2)}) collective-permute-start(f32[1,128]{1,0:T(1,128)S(1)} %add_add_fusion.2), channel_id=1, source_target_pairs={{0,6},{1,7},{2,0},{3,1},{4,2},{5,3},{6,4},{7,5},{8,14},{9,15},{10,... | collective-permute-start | bytes 1544 | tf_op jit(solution)/shard_map/ppermute | solution.py:293
  108.9 5.3 %copy-start.1 = (f32[128,1152]{1,0:T(8,128)S(1)}, f32[128,1152]{1,0:T(8,128)}, u32[]{:S(2)}) copy-start(f32[128,1152]{1,0:T(8,128)} %get-tuple-element.82.hat_ref) | copy-start | bytes 1769476
  108.9 5.3 %copy-start.3 = (f32[128,1]{1,0:T(8,128)S(1)}, f32[128,1]{1,0:T(8,128)}, u32[]{:S(2)}) copy-start(f32[128,1]{1,0:T(8,128)} %get-tuple-element.83.norm_ref) | copy-start | bytes 1540
  108.9 7.8 %collective-permute-start.34 = (f32[1,128]{1,0:T(1,128)S(1)}, f32[1,128]{1,0:T(1,128)S(1)}, u32[]{:S(2)}, u32[]{:S(2)}) collective-permute-start(f32[1,128]{1,0:T(1,128)S(1)} %add_add_fusion.1), channel_id=1, source_target_pairs={{0,64},{8,72},{16,80},{24,88},{32,96},{40,104},{48,112},{56,120},{... | collective-permute-start | bytes 1544 | tf_op jit(solution)/shard_map/ppermute | solution.py:293
  110.6 6.1 %collective-permute-start.35 = (f32[1,128]{1,0:T(1,128)S(1)}, f32[1,128]{1,0:T(1,128)S(1)}, u32[]{:S(2)}, u32[]{:S(2)}) collective-permute-start(f32[1,128]{1,0:T(1,128)S(1)} %add_add_fusion.1), channel_id=1, source_target_pairs={{0,32},{8,40},{16,48},{24,56},{32,64},{40,72},{48,80},{56,88},{64,... | collective-permute-start | bytes 1544 | tf_op jit(solution)/shard_map/ppermute | solution.py:293
  113.2 3.5 %collective-permute-start.36 = (f32[1,128]{1,0:T(1,128)S(1)}, f32[1,128]{1,0:T(1,128)S(1)}, u32[]{:S(2)}, u32[]{:S(2)}) collective-permute-start(f32[1,128]{1,0:T(1,128)S(1)} %add_add_fusion.1), channel_id=1, source_target_pairs={{0,96},{8,104},{16,112},{24,120},{32,0},{40,8},{48,16},{56,24},{64... | collective-permute-start | bytes 1544 | tf_op jit(solution)/shard_map/ppermute | solution.py:293
  115.4 6.7 %copy-start = (f32[128,1152]{1,0:T(8,128)S(1)}, f32[128,1152]{1,0:T(8,128)}, u32[]{:S(2)}) copy-start(f32[128,1152]{1,0:T(8,128)} %get-tuple-element.84.hat_ref) | copy-start | bytes 1769476
  115.4 6.7 %copy-start.2 = (f32[128,1]{1,0:T(8,128)S(1)}, f32[128,1]{1,0:T(8,128)}, u32[]{:S(2)}) copy-start(f32[128,1]{1,0:T(8,128)} %get-tuple-element.85.norm_ref) | copy-start | bytes 1540
  115.4 6.7 %collective-permute-start.38 = (bf16[128,1152]{1,0:T(8,128)(2,1)S(1)}, bf16[128,1152]{1,0:T(8,128)(2,1)S(1)}, u32[]{:S(2)}, u32[]{:S(2)}) collective-permute-start(bf16[128,1152]{1,0:T(8,128)(2,1)S(1)} %fold_partner.2), channel_id=1, source_target_pairs={{0,16},{8,24},{16,0},{24,8},{32,48},{40,56},{48,32},{56,40},{64,80... | collective-permute-start | bytes 884744 | tf_op jit(solution)/shard_map/ppermute | solution.py:341

commit v6 on v5

--- a/solution.py
+++ b/solution.py
@@ -171,15 +171,32 @@
     return total
 
 
-def far_kernel(dims, w0, w1, r0a, r0b, r1a, r1b, out_a, out_b):
+def put_row(ref, at, row):
+    zero = jnp.zeros((16, ref.shape[1] - 384), BF)
+    for n in range(3):
+        part = row.astype(BF)
+        row = row - part.astype(F32)
+        ref[at : at + 16, 128 * n : 128 * n + 128] = jnp.broadcast_to(part.astype(F32), (16, 128)).astype(BF)
+    ref[at : at + 16, 384:] = zero
+
+
+def get_row(ref, at):
+    part = [ref[at : at + 16, 128 * n : 128 * n + 128].astype(F32)[0:1] for n in range(3)]
+    return (part[0] + part[1]) + part[2]
+
+
+def far_kernel(dims, w0, w1, r0a, r0b, r1a, r1b, *refs):
+    out_a, out_b = refs[-2:]
     total = group_pull(dims, 2, (w0, w1), ((r0a, r0b), (r1a, r1b)))
-    rows = out_a.shape[0]
-    out_a[...] = encode(total[:rows])
-    out_b[...] = encode(total[rows:])
-
-
-def near_kernel(dims, w0, w1, r0a, r0b, r1a, r1b, via_a, via_b, o1, o3, own):
-    rows = via_a.shape[0]
+    rows = total.shape[0] // 2
+    for out, half in ((out_a, total[:rows]), (out_b, total[rows:])):
+        out[:rows, :] = encode(half)
+        if len(refs) == 3:
+            put_row(out, rows, refs[0][...])
+
+
+def near_kernel(dims, w0, w1, r0a, r0b, r1a, r1b, via_a, via_b, o1, o3, own, *sides):
+    rows = own.shape[0] // 2
     for k, out in ((1, o1), (3, o3), (0, own)):
         total = group_pull(dims, k, (w0, w1), ((r0a, r0b), (r1a, r1b)))
         one, two = total[:rows], total[rows:]
@@ -187,20 +204,28 @@
             out[...] = total
             continue
         if k == 1:
-            two = two + decode(via_b[...])
+            two = two + decode(via_b[:rows, :])
         else:
-            one = one + decode(via_a[...])
+            one = one + decode(via_a[:rows, :])
         out[:rows, :] = encode(one)
-        out[rows:, :] = encode(two)
-
-
-def pulls(dims, w0, w1, rows0, rows1, name, via=()):
+        out[rows : 2 * rows, :] = encode(two)
+    if sides:
+        o1[2 * rows :, :] = via_b[rows:, :]
+        sides[0][...] = get_row(via_a, rows) + get_row(via_b, rows)
+
+
+def pulls(dims, w0, w1, rows0, rows1, name, via=(), row=()):
     rows, d = rows0[0].shape[0] // 4, rows0[0].shape[1]
     n = w0.shape[dims]
-    shapes = [sds((2 * rows, d), BF)] * 2 + [sds((2 * rows, d), F32)] if via else [sds((rows, d), BF)] * 2
+    if via:
+        more = via[0].shape[0] - rows
+        shapes = [sds((2 * rows + more, d), BF), sds((2 * rows, d), BF), sds((2 * rows, d), F32)]
+        shapes += [sds((1, 128), F32)] if more else []
+    else:
+        shapes = [sds((rows + 16 * len(row), d), BF)] * 2
     return pl.pallas_call(
         functools.partial(near_kernel if via else far_kernel, dims),
-        in_specs=[VM] * (6 + len(via)),
+        in_specs=[VM] * (6 + len(via) + len(row)),
         out_specs=[VM] * len(shapes),
         out_shape=shapes,
         compiler_params=params(),
@@ -208,7 +233,24 @@
             flops=8 * (3 if via else 1) * rows * n * d, bytes_accessed=4 * n * d, transcendentals=0
         ),
         name=name,
-    )(*here(w0, w1, *rows0, *rows1, *via))
+    )(*here(w0, w1, *rows0, *rows1, *via, *row))
+
+
+def image_partner_kernel(own, c1, c3, v, sides, out, v_out):
+    partner_kernel(own, c1, c3, out)
+    v_out[...] = (v[...] + get_row(c1, own.shape[0])) + sides[...]
+
+
+def fold_image_partner(own, codes, v, sides):
+    rows, d = own.shape[0] // 2, own.shape[1]
+    return pl.pallas_call(
+        image_partner_kernel,
+        in_specs=[VM] * 5,
+        out_specs=[VM] * 2,
+        out_shape=(sds((rows, d), BF), sds((1, 128), F32)),
+        compiler_params=small(),
+        name="fold_image_partner",
+    )(*here(own, *codes, v, sides))
 
 
 def partner_kernel(own, c1, c3, out):
@@ -317,27 +359,22 @@
     w_oth, v = score_half(0, scal, diag, images, other, (sums,))
     w_rec = send(w_oth, "img", PERM_CORE)
 
-    ia, ib = pulls(1, w_own, w_oth, own, other, "far_image")
+    ia, ib = pulls(1, w_own, w_oth, own, other, "far_image", row=(v,))
     ia, ib = send(ia, "txt", perm_x(1)), send(ib, "txt", perm_x(-1))
     ta, tb = pulls(0, w_own, w_rec, images, partner, "far_text")
-    v = after(v, ta)
     ta, tb = send(ta, "img", perm_y(1)), send(tb, "img", perm_y(-1))
+    i1, i3, i0, sides = pulls(1, w_own, w_oth, own, other, "near_image", (ia, ib))
+    i1, i3 = send(i1, "txt", perm_x(-1)), send(i3, "txt", perm_x(1))
+    t1, t3, t0 = pulls(0, after(w_own, i0), w_rec, images, partner, "near_text", (ta, tb))
+    t1, t3 = send(t1, "img", perm_y(-1)), send(t3, "img", perm_y(1))
+
+    image_code, v = fold_image_partner(i0, (i1, i3), v, sides)
+    image_code = send(image_code, "txt", PERM_ZHI)
+    image_own = fold(own_kernel, i0, (i1, i3), F32, "fold_own")
     v = exchange_sum(v, ("img",), PERM_CORE)
-    i1, i3, i0 = pulls(1, w_own, w_oth, own, other, "near_image", (ia, ib))
-    v = after(v, i0)
-    i1, i3 = send(i1, "txt", perm_x(-1)), send(i3, "txt", perm_x(1))
     both = [(n, n ^ 17) for n in range(128)]
     v = exchange_sum(v, ("img", ("img", "txt"), "txt"), PERM_ZLO, both, PERM_ZHI)
-    t1, t3, t0 = pulls(0, after(w_own, i0), w_rec, images, partner, "near_text", (ta, tb))
-    v = after(v, t0)
-    t1, t3 = send(t1, "img", perm_y(-1)), send(t3, "img", perm_y(1))
-
-    image_code = send(fold(partner_kernel, i0, (i1, i3), BF, "fold_partner"), "txt", PERM_ZHI)
-    image_own = fold(own_kernel, i0, (i1, i3), F32, "fold_own")
-    v = after(v, i1, i3)
-    v = exchange_sum(v, ("txt",) * 3, perm_x(1), perm_x(2), perm_x(-1))
     text_code = fold(partner_kernel, t0, (t1, t3), BF, "fold_partner")
-    v = after(v, text_code)
     text_code = send(text_code, "img", PERM_ZLO)
     text_own = fold(own_kernel, t0, (t1, t3), F32, "fold_own")
     v = exchange_sum(v, ("img",) * 3, perm_y(1), perm_y(2), perm_y(-1))

time: 127 us -> 133 us (1.047)
  waiting for transfers between devices: 32.7 us -> 43.8 us
  starting transfers between devices: 54.5 us -> 44.1 us
  Pallas kernels: 29.3 us -> 32.8 us
  local copies, waits for them, and re-layouts: 2.15 us -> 3.71 us
    ppermute x2, waiting for transfers between devices: 2.82 us -> 8.41 us  [local(): i1, i3 = (send(i1, 'txt', perm_x(-1)), send(i3, 'txt', perm_x(1)))]
    ppermute x1, waiting for transfers between devices: 0.01 us -> 4.62 us  [local(): image_code = send(image_code, 'txt', PERM_ZHI)]
    ppermute x10 -> x7, starting transfers between devices: 12.5 us -> 7.94 us  [exchange_sum(): got = [send(v, a, p) for a, p in zip(axis, perms)]]
    ppermute x2, waiting for transfers between devices: 0.01 us -> 4.4 us  [gather(): z3 = [send(b, axis, perm(-1)) for b, (_, axis, perm, _) in zip(z, ways)]]
    ppermute x1, waiting for transfers between devices: 2.77 us -> 0.01 us  [local(): text_code = send(text_code, 'img', PERM_ZLO)]
    ppermute x2, waiting for transfers between devices: 4.17 us -> 6.64 us  [gather(): send(b, axis, perm(-1))]
    ppermute x2, starting transfers between devices: 5.27 us -> 2.85 us  [gather(): z3 = [send(b, axis, perm(-1)) for b, (_, axis, perm, _) in zip(z, ways)]]
    ppermute x2, waiting for transfers between devices: 4.4 us -> 2.31 us  [gather(): z1 = [send(b, axis, perm(1)) for b, (_, axis, perm, _) in zip(z, ways)]]
  transfers between devices with their start and end apart: 39 -> 36, of which waited for: 18 -> 20; matrix products, arithmetic and copies ran while one was open for 2% -> 2% of each run, Pallas kernels for 16% -> 17%
where the time goes in v6:
time: 133 us; the launch traced here: 132 us
  starting transfers between devices  44.1 us (33%)
  waiting for transfers between devices  43.8 us (33%)
  Pallas kernels  32.8 us (25%)
  between operations  7.6 us (6%)
  local copies, waits for them, and re-layouts  3.71 us (3%)
    pallas_call x4, Pallas kernels, pulls(): pl.pallas_call(functools.partial(near_kernel if via else far_kernel, dims...  12.2 us
    pallas_call x2, Pallas kernels, score_half(): pl.pallas_call(lambda *refs: scores_kernel(first, *refs), in_specs=[SM, S...  10.8 us
    ppermute x2, waiting for transfers between devices, local(): i1, i3 = (send(i1, 'txt', perm_x(-1)), send(i3, 'txt', perm_x(1)))  8.41 us
    ppermute x7, starting transfers between devices, exchange_sum(): got = [send(v, a, p) for a, p in zip(axis, perms)]  7.94 us
    ppermute x7, waiting for transfers between devices, exchange_sum(): got = [send(v, a, p) for a, p in zip(axis, perms)]  7.13 us
    ppermute x2, waiting for transfers between devices, gather(): send(b, axis, perm(-1))  6.64 us
    ppermute x2, starting transfers between devices, gather(): z = [send(low, axis, pz) for low, axis, _, pz in ways]  4.98 us
    ppermute x2, starting transfers between devices, gather(): a3 = [send(low, axis, perm(-1)) for low, axis, perm, _ in ways]  4.76 us
  transfers between devices with their start and end apart: 36, of which 20 were waited for; matrix products, arithmetic and copies ran while one was open for 2% of the time, Pallas kernels for 17%

profile of v6, /device:TPU:0, one launch (start us, length us, event | category | flops | bytes accessed | tf_op | source)
XLA Modules:
  0.0 132.3 jit_solution(11655698632178742010)
XLA Ops:
  0.7 2.6 %normalize.1 = (bf16[128,1152]{1,0:T(8,128)(2,1)}, f32[128,1152]{1,0:T(8,128)}, f32[128,1]{1,0:T(8,128)}, bf16[128,1152]{1,0:T(8,128)(2,1)}, f32[128,1152]{1,0:T(8,128)}, /*index=5*/f32[128,1]{1,0:T(8,128)}) custom-call(f32[128,1152]{1,0:T(8,128)} %a_ref.1, f32[128,1152]{1,0:T(8,128)} %b_ref.1), custom_call_target="tpu_custom_call" | custom-call | tf_op jit(solution)/shard_map/normalize/pallas_call | solution.py:52
  3.3 4.0 %collective-permute-start = (bf16[128,1152]{1,0:T(8,128)(2,1)}, bf16[128,1152]{1,0:T(8,128)(2,1)S(1)}, u32[]{:S(2)}, u32[]{:S(2)}) collective-permute-start(bf16[128,1152]{1,0:T(8,128)(2,1)} %get-tuple-element.44), channel_id=1, source_target_pairs={{0,1},{1,0},{2,3},{3,2},{4,5},{5,4},{6,7},{7,6},{8,9},{9,8},{10,11... | collective-permute-start | bytes 884744 | tf_op jit(solution)/shard_map/ppermute | solution.py:319
  7.3 1.5 %collective-permute-start.2 = (bf16[128,1152]{1,0:T(8,128)(2,1)}, bf16[128,1152]{1,0:T(8,128)(2,1)S(1)}, u32[]{:S(2)}, u32[]{:S(2)}) collective-permute-start(bf16[128,1152]{1,0:T(8,128)(2,1)} %get-tuple-element.44), channel_id=1, source_target_pairs={{0,2},{1,3},{2,4},{3,5},{4,6},{5,7},{6,0},{7,1},{8,10},{9,11},{10,... | collective-permute-start | bytes 884744 | tf_op jit(solution)/shard_map/ppermute | solution.py:320
  8.8 1.0 collective-permute-start.1
  9.8 1.6 %collective-permute-start.3 = (bf16[128,1152]{1,0:T(8,128)(2,1)}, bf16[128,1152]{1,0:T(8,128)(2,1)S(1)}, u32[]{:S(2)}, u32[]{:S(2)}) collective-permute-start(bf16[128,1152]{1,0:T(8,128)(2,1)} %get-tuple-element.45), channel_id=1, source_target_pairs={{0,32},{8,40},{16,48},{24,56},{32,64},{40,72},{48,80},{56,88},{64,... | collective-permute-start | bytes 884744 | tf_op jit(solution)/shard_map/ppermute | solution.py:320
  11.4 1.7 %collective-permute-start.4 = (bf16[128,1152]{1,0:T(8,128)(2,1)}, bf16[128,1152]{1,0:T(8,128)(2,1)S(1)}, u32[]{:S(2)}, u32[]{:S(2)}) collective-permute-start(bf16[128,1152]{1,0:T(8,128)(2,1)} %get-tuple-element.44), channel_id=1, source_target_pairs={{0,6},{1,7},{2,0},{3,1},{4,2},{5,3},{6,4},{7,5},{8,14},{9,15},{10,... | collective-permute-start | bytes 884744 | tf_op jit(solution)/shard_map/ppermute | solution.py:321
  14.6 0.2 select_reduce_fusion
  14.8 0.5 collective-permute-done
  15.3 3.0 %collective-permute-start.5 = (bf16[128,1152]{1,0:T(8,128)(2,1)}, bf16[128,1152]{1,0:T(8,128)(2,1)S(1)}, u32[]{:S(2)}, u32[]{:S(2)}) collective-permute-start(bf16[128,1152]{1,0:T(8,128)(2,1)} %get-tuple-element.45), channel_id=1, source_target_pairs={{0,96},{8,104},{16,112},{24,120},{32,0},{40,8},{48,16},{56,24},{64... | collective-permute-start | bytes 884744 | tf_op jit(solution)/shard_map/ppermute | solution.py:321
  18.3 1.5 %collective-permute-start.6 = (bf16[128,1152]{1,0:T(8,128)(2,1)S(1)}, bf16[128,1152]{1,0:T(8,128)(2,1)S(1)}, u32[]{:S(2)}, u32[]{:S(2)}) collective-permute-start(bf16[128,1152]{1,0:T(8,128)(2,1)S(1)} %collective-permute-done.2), channel_id=1, source_target_pairs={{0,2},{1,3},{2,4},{3,5},{4,6},{5,7},{6,0},{7,1},{8,10},{9,11},{10,... | collective-permute-start | bytes 884744 | tf_op jit(solution)/shard_map/ppermute | solution.py:322
  19.9 1.1 constant_dynamic-update-slice_fusion.3
  21.0 0.5 collective-permute-done.1
  21.6 2.0 %collective-permute-done.5 = bf16[128,1152]{1,0:T(8,128)(2,1)S(1)} collective-permute-done((bf16[128,1152]{1,0:T(8,128)(2,1)}, bf16[128,1152]{1,0:T(8,128)(2,1)S(1)}, u32[]{:S(2)}, u32[]{:S(2)}) %collective-permute-start.5) | collective-permute-done | bytes 294944 | tf_op jit(solution)/shard_map/ppermute | solution.py:321
  23.5 3.1 %collective-permute-done.6 = bf16[128,1152]{1,0:T(8,128)(2,1)S(1)} collective-permute-done((bf16[128,1152]{1,0:T(8,128)(2,1)S(1)}, bf16[128,1152]{1,0:T(8,128)(2,1)S(1)}, u32[]{:S(2)}, u32[]{:S(2)}) %collective-permute-start.6) | collective-permute-done | bytes 294944 | tf_op jit(solution)/shard_map/ppermute | solution.py:322
  26.6 1.2 collective-permute-done.7
  27.9 1.7 %collective-permute-start.8 = (bf16[128,1152]{1,0:T(8,128)(2,1)S(1)}, bf16[128,1152]{1,0:T(8,128)(2,1)S(1)}, u32[]{:S(2)}, u32[]{:S(2)}) collective-permute-start(bf16[128,1152]{1,0:T(8,128)(2,1)S(1)} %collective-permute-done), channel_id=1, source_target_pairs={{0,6},{1,7},{2,0},{3,1},{4,2},{5,3},{6,4},{7,5},{8,14},{9,15},{10,... | collective-permute-start | bytes 884744 | tf_op jit(solution)/shard_map/ppermute | solution.py:324
  29.6 0.3 collective-permute-start.10
  29.9 1.1 collective-permute-start.9
  31.0 0.9 collective-permute-start.11
  32.2 2.4 %collective-permute-done.8 = bf16[128,1152]{1,0:T(8,128)(2,1)S(1)} collective-permute-done((bf16[128,1152]{1,0:T(8,128)(2,1)S(1)}, bf16[128,1152]{1,0:T(8,128)(2,1)S(1)}, u32[]{:S(2)}, u32[]{:S(2)}) %collective-permute-start.8) | collective-permute-done | bytes 294944 | tf_op jit(solution)/shard_map/ppermute | solution.py:324
  34.6 2.0 %collective-permute-done.9 = bf16[128,1152]{1,0:T(8,128)(2,1)S(1)} collective-permute-done((bf16[128,1152]{1,0:T(8,128)(2,1)S(1)}, bf16[128,1152]{1,0:T(8,128)(2,1)S(1)}, u32[]{:S(2)}, u32[]{:S(2)}) %collective-permute-start.9) | collective-permute-done | bytes 294944 | tf_op jit(solution)/shard_map/ppermute | solution.py:324
  36.6 0.9 collective-permute-done.10
  37.5 1.4 %collective-permute-done.11 = bf16[128,1152]{1,0:T(8,128)(2,1)S(1)} collective-permute-done((bf16[128,1152]{1,0:T(8,128)(2,1)S(1)}, bf16[128,1152]{1,0:T(8,128)(2,1)S(1)}, u32[]{:S(2)}, u32[]{:S(2)}) %collective-permute-start.11) | collective-permute-done | bytes 294944 | tf_op jit(solution)/shard_map/ppermute | solution.py:325
  38.9 3.0 %collective-permute-start.12 = (bf16[128,1152]{1,0:T(8,128)(2,1)S(1)}, bf16[128,1152]{1,0:T(8,128)(2,1)S(1)}, u32[]{:S(2)}, u32[]{:S(2)}) collective-permute-start(bf16[128,1152]{1,0:T(8,128)(2,1)S(1)} %collective-permute-done.8), channel_id=1, source_target_pairs={{0,6},{1,7},{2,0},{3,1},{4,2},{5,3},{6,4},{7,5},{8,14},{9,15},{10,... | collective-permute-start | bytes 884744 | tf_op jit(solution)/shard_map/ppermute | solution.py:327
  42.0 4.2 %collective-permute-done.12 = bf16[128,1152]{1,0:T(8,128)(2,1)S(1)} collective-permute-done((bf16[128,1152]{1,0:T(8,128)(2,1)S(1)}, bf16[128,1152]{1,0:T(8,128)(2,1)S(1)}, u32[]{:S(2)}, u32[]{:S(2)}) %collective-permute-start.12) | collective-permute-done | bytes 294944 | tf_op jit(solution)/shard_map/ppermute | solution.py:327
  46.1 2.5 %collective-permute-done.13 = bf16[128,1152]{1,0:T(8,128)(2,1)S(1)} collective-permute-done((bf16[128,1152]{1,0:T(8,128)(2,1)S(1)}, bf16[128,1152]{1,0:T(8,128)(2,1)S(1)}, u32[]{:S(2)}, u32[]{:S(2)}) %collective-permute-start.13) | collective-permute-done | bytes 294944 | tf_op jit(solution)/shard_map/ppermute | solution.py:327
  48.9 5.4 %scores.2 = (bf16[1024,1024]{1,0:T(8,128)(2,1)S(1)}, f32[24,512]{1,0:T(8,128)S(1)}) custom-call(f32[4]{0:T(128)S(1)} %pad_maximum_fusion.refs_0_, s32[8]{0:T(128)S(1)} %compare_select_fusion.6.refs_1_, bf16[512,1152]{1,0:T(8,128)(2,1)S(1)} %constant_dynamic-update-slice_fusion.refs_2_.r0a, ...), custom_call_target="tpu_custom_call" | custom-call | flops 2415919104 | bytes 4718592 | tf_op jit(solution)/shard_map/scores/pallas_call | solution.py:143
  54.4 5.4 %scores.3 = (bf16[1024,1024]{1,0:T(8,128)(2,1)S(1)}, f32[1,128]{1,0:T(1,128)S(1)}) custom-call(f32[4]{0:T(128)S(1)} %pad_maximum_fusion.refs_0_, s32[8]{0:T(128)S(1)} %compare_select_fusion.6.refs_1_, bf16[512,1152]{1,0:T(8,128)(2,1)S(1)} %constant_dynamic-update-slice_fusion.refs_2_.r0a, ...), custom_call_target="tpu_custom_call" | custom-call | flops 2415919104 | bytes 4718592 | tf_op jit(solution)/shard_map/scores/pallas_call | solution.py:143
  59.8 0.6 collective-permute-start.28
  60.4 0.4 collective-permute-start.30
  60.8 1.5 %far_image.1 = (bf16[144,1152]{1,0:T(8,128)(2,1)S(1)}, bf16[144,1152]{1,0:T(8,128)(2,1)S(1)}) custom-call(bf16[1024,1024]{1,0:T(8,128)(2,1)S(1)} %get-tuple-element.76.w0, bf16[1024,1024]{1,0:T(8,128)(2,1)S(1)} %get-tuple-element.62.w1, bf16[512,1152]{1,0:T(8,128)(2,1)S(1)} %constant_dynamic-update-slice_fusion.8.refs_4_.r0a, ...), custom_call_target="tpu_custom_call" | custom-call | flops 1207959552 | bytes 4718592 | tf_op jit(solution)/shard_map/far_image/pallas_call | solution.py:226
  62.5 3.2 %collective-permute-start.17 = (bf16[144,1152]{1,0:T(8,128)(2,1)S(1)}, bf16[144,1152]{1,0:T(8,128)(2,1)S(1)}, u32[]{:S(2)}, u32[]{:S(2)}) collective-permute-start(bf16[144,1152]{1,0:T(8,128)(2,1)S(1)} %get-tuple-element.65), channel_id=1, source_target_pairs={{0,6},{1,7},{2,0},{3,1},{4,2},{5,3},{6,4},{7,5},{8,14},{9,15},{10,... | collective-permute-start | bytes 995336 | tf_op jit(solution)/shard_map/ppermute | solution.py:363
  65.7 0.1 collective-permute-done.29.r1a
  65.8 1.7 %collective-permute-done.30.r1b = bf16[512,1152]{1,0:T(8,128)(2,1)S(1)} collective-permute-done((bf16[512,1152]{1,0:T(8,128)(2,1)S(1)}, bf16[512,1152]{1,0:T(8,128)(2,1)S(1)}, u32[]{:S(2)}, u32[]{:S(2)}) %collective-permute-start.30) | collective-permute-done | bytes 1179680 | tf_op jit(solution)/shard_map/ppermute | solution.py:344
  67.5 1.6 %far_text.1 = (bf16[128,1152]{1,0:T(8,128)(2,1)S(1)}, bf16[128,1152]{1,0:T(8,128)(2,1)S(1)}) custom-call(bf16[1024,1024]{1,0:T(8,128)(2,1)S(1)} %get-tuple-element.76.w0, bf16[1024,1024]{1,0:T(8,128)(2,1)S(1)} %collective-permute-done.28.w1, bf16[512,1152]{1,0:T(8,128)(2,1)S(1)} %constant_dynamic-update-slice_fusion.refs_2_.r0a, ...), custom_call_target="tpu_custom_call" | custom-call | flops 1207959552 | bytes 4718592 | tf_op jit(solution)/shard_map/far_text/pallas_call | solution.py:226
  69.2 3.2 %collective-permute-start.32 = (bf16[128,1152]{1,0:T(8,128)(2,1)S(1)}, bf16[128,1152]{1,0:T(8,128)(2,1)S(1)}, u32[]{:S(2)}, u32[]{:S(2)}) collective-permute-start(bf16[128,1152]{1,0:T(8,128)(2,1)S(1)} %get-tuple-element.78), channel_id=1, source_target_pairs={{0,96},{8,104},{16,112},{24,120},{32,0},{40,8},{48,16},{56,24},{64... | collective-permute-start | bytes 884744 | tf_op jit(solution)/shard_map/ppermute | solution.py:365
  72.4 1.1 collective-permute-done.16.via_a
  73.5 4.5 %near_image.1 = (bf16[272,1152]{1,0:T(8,128)(2,1)S(1)}, bf16[256,1152]{1,0:T(8,128)(2,1)S(1)}, f32[256,1152]{1,0:T(8,128)S(1)}, f32[1,128]{1,0:T(1,128)S(1)}) custom-call(bf16[1024,1024]{1,0:T(8,128)(2,1)S(1)} %get-tuple-element.76.w0, bf16[1024,1024]{1,0:T(8,128)(2,1)S(1)} %get-tuple-element.62.w1, ...), custom_call_target="tpu_custom_call" | custom-call | flops 3623878656 | bytes 4718592 | tf_op jit(solution)/shard_map/near_image/pallas_call | solution.py:226
  77.9 3.2 %collective-permute-start.18 = (bf16[272,1152]{1,0:T(8,128)(2,1)S(1)}, bf16[272,1152]{1,0:T(8,128)(2,1)S(1)}, u32[]{:S(2)}, u32[]{:S(2)}) collective-permute-start(bf16[272,1152]{1,0:T(8,128)(2,1)S(1)} %get-tuple-element.67), channel_id=1, source_target_pairs={{0,6},{1,7},{2,0},{3,1},{4,2},{5,3},{6,4},{7,5},{8,14},{9,15},{10,... | collective-permute-start | bytes 1880072 | tf_op jit(solution)/shard_map/ppermute | solution.py:367
  81.2 4.6 %near_text.1 = (bf16[256,1152]{1,0:T(8,128)(2,1)S(1)}, bf16[256,1152]{1,0:T(8,128)(2,1)S(1)}, f32[256,1152]{1,0:T(8,128)S(1)}) custom-call(bf16[1024,1024]{1,0:T(8,128)(2,1)S(1)} %get-tuple-element.76.w0, bf16[1024,1024]{1,0:T(8,128)(2,1)S(1)} %collective-permute-done.28.w1, bf16[512,1152]{1,0:T(8,128)(2,1)S(1)} %constant_dynamic-update-slice_fusion.refs_2_.r0a, ...), custom_call_target="tpu_custom_call" | custom-call | flops 3623878656 | bytes 4718592 | tf_op jit(solution)/shard_map/near_text/pallas_call | solution.py:226
  85.8 1.5 %collective-permute-start.33 = (bf16[256,1152]{1,0:T(8,128)(2,1)S(1)}, bf16[256,1152]{1,0:T(8,128)(2,1)S(1)}, u32[]{:S(2)}, u32[]{:S(2)}) collective-permute-start(bf16[256,1152]{1,0:T(8,128)(2,1)S(1)} %get-tuple-element.80), channel_id=1, source_target_pairs={{0,96},{8,104},{16,112},{24,120},{32,0},{40,8},{48,16},{56,24},{64... | collective-permute-start | bytes 1769480 | tf_op jit(solution)/shard_map/ppermute | solution.py:369
  87.2 0.6 collective-permute-start.34
  87.9 8.4 %collective-permute-done.19.c3 = bf16[256,1152]{1,0:T(8,128)(2,1)S(1)} collective-permute-done((bf16[256,1152]{1,0:T(8,128)(2,1)S(1)}, bf16[256,1152]{1,0:T(8,128)(2,1)S(1)}, u32[]{:S(2)}, u32[]{:S(2)}) %collective-permute-start.19) | collective-permute-done | bytes 589856 | tf_op jit(solution)/shard_map/ppermute | solution.py:367
  96.3 1.1 fold_image_partner.1
  97.4 1.1 collective-permute-done.20
  98.5 0.7 collective-permute-start.22
  99.2 3.3 %collective-permute-start.23 = (f32[1,128]{1,0:T(1,128)S(1)}, f32[1,128]{1,0:T(1,128)S(1)}, u32[]{:S(2)}, u32[]{:S(2)}) collective-permute-start(f32[1,128]{1,0:T(1,128)S(1)} %add.83), channel_id=1, source_target_pairs={{0,1},{1,0},{2,3},{3,2},{4,5},{5,4},{6,7},{7,6},{8,9},{9,8},{10,11... | collective-permute-start | bytes 1544 | tf_op jit(solution)/shard_map/ppermute | solution.py:335
  102.6 0.7 collective-permute-start.21
  103.2 1.0 collective-permute-done.23
  104.3 3.0 %collective-permute-done.21 = f32[1,128]{1,0:T(1,128)S(1)} collective-permute-done((f32[1,128]{1,0:T(1,128)S(1)}, f32[1,128]{1,0:T(1,128)S(1)}, u32[]{:S(2)}, u32[]{:S(2)}) %collective-permute-start.21) | collective-permute-done | bytes 544 | tf_op jit(solution)/shard_map/ppermute | solution.py:335
  107.3 0.5 collective-permute-start.25
  107.8 2.8 %collective-permute-start.26 = (f32[1,128]{1,0:T(1,128)S(1)}, f32[1,128]{1,0:T(1,128)S(1)}, u32[]{:S(2)}, u32[]{:S(2)}) collective-permute-start(f32[1,128]{1,0:T(1,128)S(1)} %add_add_fusion.1), channel_id=1, source_target_pairs={{0,96},{8,104},{16,112},{24,120},{32,0},{40,8},{48,16},{56,24},{64... | collective-permute-start | bytes 1544 | tf_op jit(solution)/shard_map/ppermute | solution.py:335
  110.6 0.3 fold_own.2.own
  110.9 0.4 collective-permute-start.27
  111.3 1.1 fold_partner.1
  112.5 1.2 collective-permute-start.35
  113.7 1.9 %collective-permute-done.24 = f32[1,128]{1,0:T(1,128)S(1)} collective-permute-done((f32[1,128]{1,0:T(1,128)S(1)}, f32[1,128]{1,0:T(1,128)S(1)}, u32[]{:S(2)}, u32[]{:S(2)}) %collective-permute-start.24) | collective-permute-done | bytes 544 | tf_op jit(solution)/shard_map/ppermute | solution.py:335
  115.6 0.6 fusion.12
  118.1 4.6 %collective-permute-done.27.code_ref = bf16[128,1152]{1,0:T(8,128)(2,1)} collective-permute-done((bf16[128,1152]{1,0:T(8,128)(2,1)}, bf16[128,1152]{1,0:T(8,128)(2,1)}, u32[]{:S(2)}, u32[]{:S(2)}) %collective-permute-start.27) | collective-permute-done | bytes 294944 | tf_op jit(solution)/shard_map/ppermute | solution.py:372
  122.7 0.8 copy-done.3
  123.6 2.1 %finish.2 = f32[128,1152]{1,0:T(8,128)} custom-call(f32[128,1152]{1,0:T(8,128)S(1)} %copy-done.1, f32[128,1]{1,0:T(8,128)S(1)} %copy-done.3, f32[128,1152]{1,0:T(8,128)S(1)} %fold_own.2.own, bf16[128,1152]{1,0:T(8,128)(2,1)} %collective-permute-done.27.code_ref), custom_call_target="tpu_custom_call" | custom-call | tf_op jit(solution)/shard_map/finish/pallas_call | solution.py:285
  125.7 0.3 fold_own.3.own
  126.1 0.7 copy-done
  126.8 2.1 %finish.3 = f32[128,1152]{1,0:T(8,128)} custom-call(f32[128,1152]{1,0:T(8,128)S(1)} %copy-done, f32[128,1]{1,0:T(8,128)S(1)} %copy-done.2, f32[128,1152]{1,0:T(8,128)S(1)} %fold_own.3.own, bf16[128,1152]{1,0:T(8,128)(2,1)} %collective-permute-done.35.code_ref), custom_call_target="tpu_custom_call" | custom-call | tf_op jit(solution)/shard_map/finish/pallas_call | solution.py:285
  (58 shorter events, 1.1 us)
Async XLA Ops:
  0.6 13.8 %copy-start.4 = (s32[8]{0:T(128)S(1)}, s32[8]{0:T(128)}, u32[]{:S(2)}) copy-start(s32[8]{0:T(128)} %constant.142.clone) | copy-start | bytes 100
  0.6 13.8 %copy-start.6 = (s32[8]{0:T(128)S(1)}, s32[8]{0:T(128)}, u32[]{:S(2)}) copy-start(s32[8]{0:T(128)} %constant.143) | copy-start | bytes 100
  0.7 13.9 %copy-start.5 = (s32[8]{0:T(128)S(1)}, s32[8]{0:T(128)}, u32[]{:S(2)}) copy-start(s32[8]{0:T(128)} %constant.141.clone) | copy-start | bytes 100
  3.3 12.0 %collective-permute-start = (bf16[128,1152]{1,0:T(8,128)(2,1)}, bf16[128,1152]{1,0:T(8,128)(2,1)S(1)}, u32[]{:S(2)}, u32[]{:S(2)}) collective-permute-start(bf16[128,1152]{1,0:T(8,128)(2,1)} %get-tuple-element.44), channel_id=1, source_target_pairs={{0,1},{1,0},{2,3},{3,2},{4,5},{5,4},{6,7},{7,6},{8,9},{9,8},{10,11... | collective-permute-start | bytes 884744 | tf_op jit(solution)/shard_map/ppermute | solution.py:319
  7.3 11.1 %collective-permute-start.2 = (bf16[128,1152]{1,0:T(8,128)(2,1)}, bf16[128,1152]{1,0:T(8,128)(2,1)S(1)}, u32[]{:S(2)}, u32[]{:S(2)}) collective-permute-start(bf16[128,1152]{1,0:T(8,128)(2,1)} %get-tuple-element.44), channel_id=1, source_target_pairs={{0,2},{1,3},{2,4},{3,5},{4,6},{5,7},{6,0},{7,1},{8,10},{9,11},{10,... | collective-permute-start | bytes 884744 | tf_op jit(solution)/shard_map/ppermute | solution.py:320
  8.8 12.8 %collective-permute-start.1 = (bf16[128,1152]{1,0:T(8,128)(2,1)}, bf16[128,1152]{1,0:T(8,128)(2,1)S(1)}, u32[]{:S(2)}, u32[]{:S(2)}) collective-permute-start(bf16[128,1152]{1,0:T(8,128)(2,1)} %get-tuple-element.45), channel_id=1, source_target_pairs={{0,16},{8,24},{16,0},{24,8},{32,48},{40,56},{48,32},{56,40},{64,80... | collective-permute-start | bytes 884744 | tf_op jit(solution)/shard_map/ppermute | solution.py:319
  9.8 10.0 %collective-permute-start.3 = (bf16[128,1152]{1,0:T(8,128)(2,1)}, bf16[128,1152]{1,0:T(8,128)(2,1)S(1)}, u32[]{:S(2)}, u32[]{:S(2)}) collective-permute-start(bf16[128,1152]{1,0:T(8,128)(2,1)} %get-tuple-element.45), channel_id=1, source_target_pairs={{0,32},{8,40},{16,48},{24,56},{32,64},{40,72},{48,80},{56,88},{64,... | collective-permute-start | bytes 884744 | tf_op jit(solution)/shard_map/ppermute | solution.py:320
  11.4 10.2 %collective-permute-start.4 = (bf16[128,1152]{1,0:T(8,128)(2,1)}, bf16[128,1152]{1,0:T(8,128)(2,1)S(1)}, u32[]{:S(2)}, u32[]{:S(2)}) collective-permute-start(bf16[128,1152]{1,0:T(8,128)(2,1)} %get-tuple-element.44), channel_id=1, source_target_pairs={{0,6},{1,7},{2,0},{3,1},{4,2},{5,3},{6,4},{7,5},{8,14},{9,15},{10,... | collective-permute-start | bytes 884744 | tf_op jit(solution)/shard_map/ppermute | solution.py:321
  15.3 8.2 %collective-permute-start.5 = (bf16[128,1152]{1,0:T(8,128)(2,1)}, bf16[128,1152]{1,0:T(8,128)(2,1)S(1)}, u32[]{:S(2)}, u32[]{:S(2)}) collective-permute-start(bf16[128,1152]{1,0:T(8,128)(2,1)} %get-tuple-element.45), channel_id=1, source_target_pairs={{0,96},{8,104},{16,112},{24,120},{32,0},{40,8},{48,16},{56,24},{64... | collective-permute-start | bytes 884744 | tf_op jit(solution)/shard_map/ppermute | solution.py:321
  18.3 8.3 %collective-permute-start.6 = (bf16[128,1152]{1,0:T(8,128)(2,1)S(1)}, bf16[128,1152]{1,0:T(8,128)(2,1)S(1)}, u32[]{:S(2)}, u32[]{:S(2)}) collective-permute-start(bf16[128,1152]{1,0:T(8,128)(2,1)S(1)} %collective-permute-done.2), channel_id=1, source_target_pairs={{0,2},{1,3},{2,4},{3,5},{4,6},{5,7},{6,0},{7,1},{8,10},{9,11},{10,... | collective-permute-start | bytes 884744 | tf_op jit(solution)/shard_map/ppermute | solution.py:322
  19.8 8.0 %collective-permute-start.7 = (bf16[128,1152]{1,0:T(8,128)(2,1)S(1)}, bf16[128,1152]{1,0:T(8,128)(2,1)S(1)}, u32[]{:S(2)}, u32[]{:S(2)}) collective-permute-start(bf16[128,1152]{1,0:T(8,128)(2,1)S(1)} %collective-permute-done.3), channel_id=1, source_target_pairs={{0,32},{8,40},{16,48},{24,56},{32,64},{40,72},{48,80},{56,88},{64,... | collective-permute-start | bytes 884744 | tf_op jit(solution)/shard_map/ppermute | solution.py:322
  27.9 6.7 %collective-permute-start.8 = (bf16[128,1152]{1,0:T(8,128)(2,1)S(1)}, bf16[128,1152]{1,0:T(8,128)(2,1)S(1)}, u32[]{:S(2)}, u32[]{:S(2)}) collective-permute-start(bf16[128,1152]{1,0:T(8,128)(2,1)S(1)} %collective-permute-done), channel_id=1, source_target_pairs={{0,6},{1,7},{2,0},{3,1},{4,2},{5,3},{6,4},{7,5},{8,14},{9,15},{10,... | collective-permute-start | bytes 884744 | tf_op jit(solution)/shard_map/ppermute | solution.py:324
  29.6 7.9 %collective-permute-start.10 = (bf16[128,1152]{1,0:T(8,128)(2,1)S(1)}, bf16[128,1152]{1,0:T(8,128)(2,1)S(1)}, u32[]{:S(2)}, u32[]{:S(2)}) collective-permute-start(bf16[128,1152]{1,0:T(8,128)(2,1)S(1)} %collective-permute-done), channel_id=1, source_target_pairs={{0,2},{1,3},{2,4},{3,5},{4,6},{5,7},{6,0},{7,1},{8,10},{9,11},{10,... | collective-permute-start | bytes 884744 | tf_op jit(solution)/shard_map/ppermute | solution.py:325
  29.9 6.7 %collective-permute-start.9 = (bf16[128,1152]{1,0:T(8,128)(2,1)S(1)}, bf16[128,1152]{1,0:T(8,128)(2,1)S(1)}, u32[]{:S(2)}, u32[]{:S(2)}) collective-permute-start(bf16[128,1152]{1,0:T(8,128)(2,1)S(1)} %collective-permute-done.1), channel_id=1, source_target_pairs={{0,96},{8,104},{16,112},{24,120},{32,0},{40,8},{48,16},{56,24},{64... | collective-permute-start | bytes 884744 | tf_op jit(solution)/shard_map/ppermute | solution.py:324
  31.0 7.9 %collective-permute-start.11 = (bf16[128,1152]{1,0:T(8,128)(2,1)S(1)}, bf16[128,1152]{1,0:T(8,128)(2,1)S(1)}, u32[]{:S(2)}, u32[]{:S(2)}) collective-permute-start(bf16[128,1152]{1,0:T(8,128)(2,1)S(1)} %collective-permute-done.1), channel_id=1, source_target_pairs={{0,32},{8,40},{16,48},{24,56},{32,64},{40,72},{48,80},{56,88},{64,... | collective-permute-start | bytes 884744 | tf_op jit(solution)/shard_map/ppermute | solution.py:325
  32.0 22.3 %collective-permute-start.14 = (bf16[512,1152]{1,0:T(8,128)(2,1)S(1)}, bf16[512,1152]{1,0:T(8,128)(2,1)S(1)}, u32[]{:S(2)}, u32[]{:S(2)}) collective-permute-start(bf16[512,1152]{1,0:T(8,128)(2,1)S(1)} %constant_dynamic-update-slice_fusion.8.refs_4_.r0a), channel_id=1, source_target_pairs={{0,8},{8,0},{16,24},{24,16},{32,40},{40,32},{48,56},{56,48},{64,72... | collective-permute-start | bytes 3538952 | tf_op jit(solution)/shard_map/ppermute | solution.py:343
  38.9 7.2 %collective-permute-start.12 = (bf16[128,1152]{1,0:T(8,128)(2,1)S(1)}, bf16[128,1152]{1,0:T(8,128)(2,1)S(1)}, u32[]{:S(2)}, u32[]{:S(2)}) collective-permute-start(bf16[128,1152]{1,0:T(8,128)(2,1)S(1)} %collective-permute-done.8), channel_id=1, source_target_pairs={{0,6},{1,7},{2,0},{3,1},{4,2},{5,3},{6,4},{7,5},{8,14},{9,15},{10,... | collective-permute-start | bytes 884744 | tf_op jit(solution)/shard_map/ppermute | solution.py:327
  41.9 6.7 %collective-permute-start.13 = (bf16[128,1152]{1,0:T(8,128)(2,1)S(1)}, bf16[128,1152]{1,0:T(8,128)(2,1)S(1)}, u32[]{:S(2)}, u32[]{:S(2)}) collective-permute-start(bf16[128,1152]{1,0:T(8,128)(2,1)S(1)} %collective-permute-done.9), channel_id=1, source_target_pairs={{0,96},{8,104},{16,112},{24,120},{32,0},{40,8},{48,16},{56,24},{64... | collective-permute-start | bytes 884744 | tf_op jit(solution)/shard_map/ppermute | solution.py:327
  48.6 5.7 %collective-permute-start.15 = (bf16[512,1152]{1,0:T(8,128)(2,1)S(1)}, bf16[512,1152]{1,0:T(8,128)(2,1)S(1)}, u32[]{:S(2)}, u32[]{:S(2)}) collective-permute-start(bf16[512,1152]{1,0:T(8,128)(2,1)S(1)} %constant_dynamic-update-slice_fusion.12.refs_5_.r0b), channel_id=1, source_target_pairs={{0,8},{8,0},{16,24},{24,16},{32,40},{40,32},{48,56},{56,48},{64,72... | collective-permute-start | bytes 3538952 | tf_op jit(solution)/shard_map/ppermute | solution.py:343
  59.8 7.7 %collective-permute-start.28 = (bf16[1024,1024]{1,0:T(8,128)(2,1)S(1)}, bf16[1024,1024]{1,0:T(8,128)(2,1)S(1)}, u32[]{:S(2)}, u32[]{:S(2)}) collective-permute-start(bf16[1024,1024]{1,0:T(8,128)(2,1)S(1)} %get-tuple-element.62.w1), channel_id=1, source_target_pairs={{0,8},{8,0},{16,24},{24,16},{32,40},{40,32},{48,56},{56,48},{64,72... | collective-permute-start | bytes 6291464 | tf_op jit(solution)/shard_map/ppermute | solution.py:360
  60.3 5.5 %collective-permute-start.29 = (bf16[512,1152]{1,0:T(8,128)(2,1)S(1)}, bf16[512,1152]{1,0:T(8,128)(2,1)S(1)}, u32[]{:S(2)}, u32[]{:S(2)}) collective-permute-start(bf16[512,1152]{1,0:T(8,128)(2,1)S(1)} %constant_dynamic-update-slice_fusion.refs_2_.r0a), channel_id=1, source_target_pairs={{0,8},{8,0},{16,24},{24,16},{32,40},{40,32},{48,56},{56,48},{64,72... | collective-permute-start | bytes 3538952 | tf_op jit(solution)/shard_map/ppermute | solution.py:344
  60.4 7.1 %collective-permute-start.30 = (bf16[512,1152]{1,0:T(8,128)(2,1)S(1)}, bf16[512,1152]{1,0:T(8,128)(2,1)S(1)}, u32[]{:S(2)}, u32[]{:S(2)}) collective-permute-start(bf16[512,1152]{1,0:T(8,128)(2,1)S(1)} %constant_dynamic-update-slice_fusion.4.refs_3_.r0b), channel_id=1, source_target_pairs={{0,8},{8,0},{16,24},{24,16},{32,40},{40,32},{48,56},{56,48},{64,72... | collective-permute-start | bytes 3538952 | tf_op jit(solution)/shard_map/ppermute | solution.py:344
  62.4 11.1 %collective-permute-start.16 = (bf16[144,1152]{1,0:T(8,128)(2,1)S(1)}, bf16[144,1152]{1,0:T(8,128)(2,1)S(1)}, u32[]{:S(2)}, u32[]{:S(2)}) collective-permute-start(bf16[144,1152]{1,0:T(8,128)(2,1)S(1)} %get-tuple-element.64), channel_id=1, source_target_pairs={{0,2},{1,3},{2,4},{3,5},{4,6},{5,7},{6,0},{7,1},{8,10},{9,11},{10,... | collective-permute-start | bytes 995336 | tf_op jit(solution)/shard_map/ppermute | solution.py:363
  62.5 11.0 %collective-permute-start.17 = (bf16[144,1152]{1,0:T(8,128)(2,1)S(1)}, bf16[144,1152]{1,0:T(8,128)(2,1)S(1)}, u32[]{:S(2)}, u32[]{:S(2)}) collective-permute-start(bf16[144,1152]{1,0:T(8,128)(2,1)S(1)} %get-tuple-element.65), channel_id=1, source_target_pairs={{0,6},{1,7},{2,0},{3,1},{4,2},{5,3},{6,4},{7,5},{8,14},{9,15},{10,... | collective-permute-start | bytes 995336 | tf_op jit(solution)/shard_map/ppermute | solution.py:363
  69.1 12.1 %collective-permute-start.31 = (bf16[128,1152]{1,0:T(8,128)(2,1)S(1)}, bf16[128,1152]{1,0:T(8,128)(2,1)S(1)}, u32[]{:S(2)}, u32[]{:S(2)}) collective-permute-start(bf16[128,1152]{1,0:T(8,128)(2,1)S(1)} %get-tuple-element.77), channel_id=1, source_target_pairs={{0,32},{8,40},{16,48},{24,56},{32,64},{40,72},{48,80},{56,88},{64,... | collective-permute-start | bytes 884744 | tf_op jit(solution)/shard_map/ppermute | solution.py:365
  69.2 12.0 %collective-permute-start.32 = (bf16[128,1152]{1,0:T(8,128)(2,1)S(1)}, bf16[128,1152]{1,0:T(8,128)(2,1)S(1)}, u32[]{:S(2)}, u32[]{:S(2)}) collective-permute-start(bf16[128,1152]{1,0:T(8,128)(2,1)S(1)} %get-tuple-element.78), channel_id=1, source_target_pairs={{0,96},{8,104},{16,112},{24,120},{32,0},{40,8},{48,16},{56,24},{64... | collective-permute-start | bytes 884744 | tf_op jit(solution)/shard_map/ppermute | solution.py:365
  77.9 18.3 %collective-permute-start.18 = (bf16[272,1152]{1,0:T(8,128)(2,1)S(1)}, bf16[272,1152]{1,0:T(8,128)(2,1)S(1)}, u32[]{:S(2)}, u32[]{:S(2)}) collective-permute-start(bf16[272,1152]{1,0:T(8,128)(2,1)S(1)} %get-tuple-element.67), channel_id=1, source_target_pairs={{0,6},{1,7},{2,0},{3,1},{4,2},{5,3},{6,4},{7,5},{8,14},{9,15},{10,... | collective-permute-start | bytes 1880072 | tf_op jit(solution)/shard_map/ppermute | solution.py:367
  81.2 15.1 %collective-permute-start.19 = (bf16[256,1152]{1,0:T(8,128)(2,1)S(1)}, bf16[256,1152]{1,0:T(8,128)(2,1)S(1)}, u32[]{:S(2)}, u32[]{:S(2)}) collective-permute-start(bf16[256,1152]{1,0:T(8,128)(2,1)S(1)} %get-tuple-element.68), channel_id=1, source_target_pairs={{0,2},{1,3},{2,4},{3,5},{4,6},{5,7},{6,0},{7,1},{8,10},{9,11},{10,... | collective-permute-start | bytes 1769480 | tf_op jit(solution)/shard_map/ppermute | solution.py:367
  85.8 25.1 %collective-permute-start.33 = (bf16[256,1152]{1,0:T(8,128)(2,1)S(1)}, bf16[256,1152]{1,0:T(8,128)(2,1)S(1)}, u32[]{:S(2)}, u32[]{:S(2)}) collective-permute-start(bf16[256,1152]{1,0:T(8,128)(2,1)S(1)} %get-tuple-element.80), channel_id=1, source_target_pairs={{0,96},{8,104},{16,112},{24,120},{32,0},{40,8},{48,16},{56,24},{64... | collective-permute-start | bytes 1769480 | tf_op jit(solution)/shard_map/ppermute | solution.py:369
  87.2 24.1 %collective-permute-start.34 = (bf16[256,1152]{1,0:T(8,128)(2,1)S(1)}, bf16[256,1152]{1,0:T(8,128)(2,1)S(1)}, u32[]{:S(2)}, u32[]{:S(2)}) collective-permute-start(bf16[256,1152]{1,0:T(8,128)(2,1)S(1)} %get-tuple-element.81), channel_id=1, source_target_pairs={{0,32},{8,40},{16,48},{24,56},{32,64},{40,72},{48,80},{56,88},{64,... | collective-permute-start | bytes 1769480 | tf_op jit(solution)/shard_map/ppermute | solution.py:369
  97.4 1.1 collective-permute-start.20
  98.5 4.7 %collective-permute-start.22 = (f32[1,128]{1,0:T(1,128)S(1)}, f32[1,128]{1,0:T(1,128)S(1)}, u32[]{:S(2)}, u32[]{:S(2)}) collective-permute-start(f32[1,128]{1,0:T(1,128)S(1)} %add.83), channel_id=1, source_target_pairs={{0,16},{8,24},{16,0},{24,8},{32,48},{40,56},{48,32},{56,40},{64,80... | collective-permute-start | bytes 1544 | tf_op jit(solution)/shard_map/ppermute | solution.py:335
  99.2 5.0 %collective-permute-start.23 = (f32[1,128]{1,0:T(1,128)S(1)}, f32[1,128]{1,0:T(1,128)S(1)}, u32[]{:S(2)}, u32[]{:S(2)}) collective-permute-start(f32[1,128]{1,0:T(1,128)S(1)} %add.83), channel_id=1, source_target_pairs={{0,1},{1,0},{2,3},{3,2},{4,5},{5,4},{6,7},{7,6},{8,9},{9,8},{10,11... | collective-permute-start | bytes 1544 | tf_op jit(solution)/shard_map/ppermute | solution.py:335
  102.6 4.8 %collective-permute-start.21 = (f32[1,128]{1,0:T(1,128)S(1)}, f32[1,128]{1,0:T(1,128)S(1)}, u32[]{:S(2)}, u32[]{:S(2)}) collective-permute-start(f32[1,128]{1,0:T(1,128)S(1)} %add.83), channel_id=1, source_target_pairs={{0,17},{1,16},{2,19},{3,18},{4,21},{5,20},{6,23},{7,22},{8,25},{9,... | collective-permute-start | bytes 1544 | tf_op jit(solution)/shard_map/ppermute | solution.py:335
  107.3 6.3 %collective-permute-start.25 = (f32[1,128]{1,0:T(1,128)S(1)}, f32[1,128]{1,0:T(1,128)S(1)}, u32[]{:S(2)}, u32[]{:S(2)}) collective-permute-start(f32[1,128]{1,0:T(1,128)S(1)} %add_add_fusion.1), channel_id=1, source_target_pairs={{0,32},{8,40},{16,48},{24,56},{32,64},{40,72},{48,80},{56,88},{64,... | collective-permute-start | bytes 1544 | tf_op jit(solution)/shard_map/ppermute | solution.py:335
  107.8 5.9 %collective-permute-start.26 = (f32[1,128]{1,0:T(1,128)S(1)}, f32[1,128]{1,0:T(1,128)S(1)}, u32[]{:S(2)}, u32[]{:S(2)}) collective-permute-start(f32[1,128]{1,0:T(1,128)S(1)} %add_add_fusion.1), channel_id=1, source_target_pairs={{0,96},{8,104},{16,112},{24,120},{32,0},{40,8},{48,16},{56,24},{64... | collective-permute-start | bytes 1544 | tf_op jit(solution)/shard_map/ppermute | solution.py:335
  110.5 5.0 %collective-permute-start.24 = (f32[1,128]{1,0:T(1,128)S(1)}, f32[1,128]{1,0:T(1,128)S(1)}, u32[]{:S(2)}, u32[]{:S(2)}) collective-permute-start(f32[1,128]{1,0:T(1,128)S(1)} %add_add_fusion.1), channel_id=1, source_target_pairs={{0,64},{8,72},{16,80},{24,88},{32,96},{40,104},{48,112},{56,120},{... | collective-permute-start | bytes 1544 | tf_op jit(solution)/shard_map/ppermute | solution.py:335
  110.9 11.8 %collective-permute-start.27 = (bf16[128,1152]{1,0:T(8,128)(2,1)}, bf16[128,1152]{1,0:T(8,128)(2,1)}, u32[]{:S(2)}, u32[]{:S(2)}) collective-permute-start(bf16[128,1152]{1,0:T(8,128)(2,1)} %get-tuple-element.73), channel_id=1, source_target_pairs={{0,1},{1,0},{2,3},{3,2},{4,5},{5,4},{6,7},{7,6},{8,9},{9,8},{10,11... | collective-permute-start | bytes 884744 | tf_op jit(solution)/shard_map/ppermute | solution.py:372
  111.3 11.4 %copy-start.1 = (f32[128,1152]{1,0:T(8,128)S(1)}, f32[128,1152]{1,0:T(8,128)}, u32[]{:S(2)}) copy-start(f32[128,1152]{1,0:T(8,128)} %get-tuple-element.71.hat_ref) | copy-start | bytes 1769476
  112.5 13.6 %collective-permute-start.35 = (bf16[128,1152]{1,0:T(8,128)(2,1)}, bf16[128,1152]{1,0:T(8,128)(2,1)}, u32[]{:S(2)}, u32[]{:S(2)}) collective-permute-start(bf16[128,1152]{1,0:T(8,128)(2,1)} %fold_partner.1), channel_id=1, source_target_pairs={{0,16},{8,24},{16,0},{24,8},{32,48},{40,56},{48,32},{56,40},{64,80... | collective-permute-start | bytes 884744 | tf_op jit(solution)/shard_map/ppermute | solution.py:378
  122.7 0.8 copy-start.3
  125.7 1.1 copy-start
  125.7 1.1 copy-start.2

commit v7 on v6

--- a/solution.py
+++ b/solution.py
@@ -375,6 +375,7 @@
     both = [(n, n ^ 17) for n in range(128)]
     v = exchange_sum(v, ("img", ("img", "txt"), "txt"), PERM_ZLO, both, PERM_ZHI)
     text_code = fold(partner_kernel, t0, (t1, t3), BF, "fold_partner")
+    v = after(v, text_code)
     text_code = send(text_code, "img", PERM_ZLO)
     text_own = fold(own_kernel, t0, (t1, t3), F32, "fold_own")
     v = exchange_sum(v, ("img",) * 3, perm_y(1), perm_y(2), perm_y(-1))

time: 133 us -> 127 us (0.955)
  Pallas kernels: 32.8 us -> 29.4 us
  local copies, waits for them, and re-layouts: 3.71 us -> 2.15 us
    ppermute x1, waiting for transfers between devices: 4.62 us -> 0.01 us  [local(): image_code = send(image_code, 'txt', PERM_ZHI)]
    ppermute x7, waiting for transfers between devices: 7.13 us -> 10.5 us  [exchange_sum(): got = [send(v, a, p) for a, p in zip(axis, perms)]]
    pallas_call x2, Pallas kernels: 4.25 us -> 2.34 us  [finish(): pl.pallas_call(finish_kernel, in_specs=[VM] * 4, out_specs=VM, out_shape=...]
    ppermute x1, starting transfers between devices: 0.45 us -> 2.12 us  [local(): image_code = send(image_code, 'txt', PERM_ZHI)]
    unnamed x24, local copies, waits for them, and re-layouts: 2.99 us -> 1.43 us
  transfers between devices with their start and end apart: 36 -> 36, of which waited for: 20 -> 21; matrix products, arithmetic and copies ran while one was open for 2% -> 2% of each run, Pallas kernels for 17% -> 16%
where the time goes in v7:
time: 127 us; the launch traced here: 126 us
  starting transfers between devices  43.4 us (34%)
  waiting for transfers between devices  43.2 us (34%)
  Pallas kernels  29.4 us (23%)
  between operations  7.68 us (6%)
  local copies, waits for them, and re-layouts  2.15 us (2%)
    pallas_call x4, Pallas kernels, pulls(): pl.pallas_call(functools.partial(near_kernel if via else far_kernel, dims...  12.2 us
    pallas_call x2, Pallas kernels, score_half(): pl.pallas_call(lambda *refs: scores_kernel(first, *refs), in_specs=[SM, S...  10.8 us
    ppermute x7, waiting for transfers between devices, exchange_sum(): got = [send(v, a, p) for a, p in zip(axis, perms)]  10.5 us
    ppermute x2, waiting for transfers between devices, local(): i1, i3 = (send(i1, 'txt', perm_x(-1)), send(i3, 'txt', perm_x(1)))  8.41 us
    ppermute x7, starting transfers between devices, exchange_sum(): got = [send(v, a, p) for a, p in zip(axis, perms)]  6.76 us
    ppermute x2, waiting for transfers between devices, gather(): send(b, axis, perm(-1))  6.64 us
    ppermute x2, starting transfers between devices, gather(): z = [send(low, axis, pz) for low, axis, _, pz in ways]  4.98 us
    ppermute x2, starting transfers between devices, gather(): a3 = [send(low, axis, perm(-1)) for low, axis, perm, _ in ways]  4.76 us
  transfers between devices with their start and end apart: 36, of which 21 were waited for; matrix products, arithmetic and copies ran while one was open for 2% of the time, Pallas kernels for 16%

profile of v7, /device:TPU:0, one launch (start us, length us, event | category | flops | bytes accessed | tf_op | source)
XLA Modules:
  0.0 126.2 jit_solution(11006376800845409379)
XLA Ops:
  0.7 2.6 %normalize.1 = (bf16[128,1152]{1,0:T(8,128)(2,1)}, f32[128,1152]{1,0:T(8,128)}, f32[128,1]{1,0:T(8,128)}, bf16[128,1152]{1,0:T(8,128)(2,1)}, f32[128,1152]{1,0:T(8,128)}, /*index=5*/f32[128,1]{1,0:T(8,128)}) custom-call(f32[128,1152]{1,0:T(8,128)} %a_ref.1, f32[128,1152]{1,0:T(8,128)} %b_ref.1), custom_call_target="tpu_custom_call" | custom-call | tf_op jit(solution)/shard_map/normalize/pallas_call | solution.py:52
  3.3 4.0 %collective-permute-start = (bf16[128,1152]{1,0:T(8,128)(2,1)}, bf16[128,1152]{1,0:T(8,128)(2,1)S(1)}, u32[]{:S(2)}, u32[]{:S(2)}) collective-permute-start(bf16[128,1152]{1,0:T(8,128)(2,1)} %get-tuple-element.45), channel_id=1, source_target_pairs={{0,1},{1,0},{2,3},{3,2},{4,5},{5,4},{6,7},{7,6},{8,9},{9,8},{10,11... | collective-permute-start | bytes 884744 | tf_op jit(solution)/shard_map/ppermute | solution.py:319
  7.3 1.5 %collective-permute-start.2 = (bf16[128,1152]{1,0:T(8,128)(2,1)}, bf16[128,1152]{1,0:T(8,128)(2,1)S(1)}, u32[]{:S(2)}, u32[]{:S(2)}) collective-permute-start(bf16[128,1152]{1,0:T(8,128)(2,1)} %get-tuple-element.45), channel_id=1, source_target_pairs={{0,2},{1,3},{2,4},{3,5},{4,6},{5,7},{6,0},{7,1},{8,10},{9,11},{10,... | collective-permute-start | bytes 884744 | tf_op jit(solution)/shard_map/ppermute | solution.py:320
  8.8 1.0 collective-permute-start.1
  9.8 1.6 %collective-permute-start.3 = (bf16[128,1152]{1,0:T(8,128)(2,1)}, bf16[128,1152]{1,0:T(8,128)(2,1)S(1)}, u32[]{:S(2)}, u32[]{:S(2)}) collective-permute-start(bf16[128,1152]{1,0:T(8,128)(2,1)} %get-tuple-element.46), channel_id=1, source_target_pairs={{0,32},{8,40},{16,48},{24,56},{32,64},{40,72},{48,80},{56,88},{64,... | collective-permute-start | bytes 884744 | tf_op jit(solution)/shard_map/ppermute | solution.py:320
  11.4 1.7 %collective-permute-start.4 = (bf16[128,1152]{1,0:T(8,128)(2,1)}, bf16[128,1152]{1,0:T(8,128)(2,1)S(1)}, u32[]{:S(2)}, u32[]{:S(2)}) collective-permute-start(bf16[128,1152]{1,0:T(8,128)(2,1)} %get-tuple-element.45), channel_id=1, source_target_pairs={{0,6},{1,7},{2,0},{3,1},{4,2},{5,3},{6,4},{7,5},{8,14},{9,15},{10,... | collective-permute-start | bytes 884744 | tf_op jit(solution)/shard_map/ppermute | solution.py:321
  14.6 0.2 select_reduce_fusion
  14.8 0.5 collective-permute-done
  15.3 3.0 %collective-permute-start.5 = (bf16[128,1152]{1,0:T(8,128)(2,1)}, bf16[128,1152]{1,0:T(8,128)(2,1)S(1)}, u32[]{:S(2)}, u32[]{:S(2)}) collective-permute-start(bf16[128,1152]{1,0:T(8,128)(2,1)} %get-tuple-element.46), channel_id=1, source_target_pairs={{0,96},{8,104},{16,112},{24,120},{32,0},{40,8},{48,16},{56,24},{64... | collective-permute-start | bytes 884744 | tf_op jit(solution)/shard_map/ppermute | solution.py:321
  18.3 1.5 %collective-permute-start.6 = (bf16[128,1152]{1,0:T(8,128)(2,1)S(1)}, bf16[128,1152]{1,0:T(8,128)(2,1)S(1)}, u32[]{:S(2)}, u32[]{:S(2)}) collective-permute-start(bf16[128,1152]{1,0:T(8,128)(2,1)S(1)} %collective-permute-done.2), channel_id=1, source_target_pairs={{0,2},{1,3},{2,4},{3,5},{4,6},{5,7},{6,0},{7,1},{8,10},{9,11},{10,... | collective-permute-start | bytes 884744 | tf_op jit(solution)/shard_map/ppermute | solution.py:322
  19.9 1.1 constant_dynamic-update-slice_fusion.3
  21.0 0.5 collective-permute-done.1
  21.6 2.0 %collective-permute-done.5 = bf16[128,1152]{1,0:T(8,128)(2,1)S(1)} collective-permute-done((bf16[128,1152]{1,0:T(8,128)(2,1)}, bf16[128,1152]{1,0:T(8,128)(2,1)S(1)}, u32[]{:S(2)}, u32[]{:S(2)}) %collective-permute-start.5) | collective-permute-done | bytes 294944 | tf_op jit(solution)/shard_map/ppermute | solution.py:321
  23.5 3.1 %collective-permute-done.6 = bf16[128,1152]{1,0:T(8,128)(2,1)S(1)} collective-permute-done((bf16[128,1152]{1,0:T(8,128)(2,1)S(1)}, bf16[128,1152]{1,0:T(8,128)(2,1)S(1)}, u32[]{:S(2)}, u32[]{:S(2)}) %collective-permute-start.6) | collective-permute-done | bytes 294944 | tf_op jit(solution)/shard_map/ppermute | solution.py:322
  26.6 1.2 collective-permute-done.7
  27.9 1.7 %collective-permute-start.8 = (bf16[128,1152]{1,0:T(8,128)(2,1)S(1)}, bf16[128,1152]{1,0:T(8,128)(2,1)S(1)}, u32[]{:S(2)}, u32[]{:S(2)}) collective-permute-start(bf16[128,1152]{1,0:T(8,128)(2,1)S(1)} %collective-permute-done), channel_id=1, source_target_pairs={{0,6},{1,7},{2,0},{3,1},{4,2},{5,3},{6,4},{7,5},{8,14},{9,15},{10,... | collective-permute-start | bytes 884744 | tf_op jit(solution)/shard_map/ppermute | solution.py:324
  29.6 0.3 collective-permute-start.10
  29.9 1.1 collective-permute-start.9
  31.0 0.9 collective-permute-start.11
  32.0 0.1 collective-permute-start.14
  32.2 2.4 %collective-permute-done.8 = bf16[128,1152]{1,0:T(8,128)(2,1)S(1)} collective-permute-done((bf16[128,1152]{1,0:T(8,128)(2,1)S(1)}, bf16[128,1152]{1,0:T(8,128)(2,1)S(1)}, u32[]{:S(2)}, u32[]{:S(2)}) %collective-permute-start.8) | collective-permute-done | bytes 294944 | tf_op jit(solution)/shard_map/ppermute | solution.py:324
  34.6 2.0 %collective-permute-done.9 = bf16[128,1152]{1,0:T(8,128)(2,1)S(1)} collective-permute-done((bf16[128,1152]{1,0:T(8,128)(2,1)S(1)}, bf16[128,1152]{1,0:T(8,128)(2,1)S(1)}, u32[]{:S(2)}, u32[]{:S(2)}) %collective-permute-start.9) | collective-permute-done | bytes 294944 | tf_op jit(solution)/shard_map/ppermute | solution.py:324
  36.6 0.9 collective-permute-done.10
  37.5 1.4 %collective-permute-done.11 = bf16[128,1152]{1,0:T(8,128)(2,1)S(1)} collective-permute-done((bf16[128,1152]{1,0:T(8,128)(2,1)S(1)}, bf16[128,1152]{1,0:T(8,128)(2,1)S(1)}, u32[]{:S(2)}, u32[]{:S(2)}) %collective-permute-start.11) | collective-permute-done | bytes 294944 | tf_op jit(solution)/shard_map/ppermute | solution.py:325
  38.9 3.0 %collective-permute-start.12 = (bf16[128,1152]{1,0:T(8,128)(2,1)S(1)}, bf16[128,1152]{1,0:T(8,128)(2,1)S(1)}, u32[]{:S(2)}, u32[]{:S(2)}) collective-permute-start(bf16[128,1152]{1,0:T(8,128)(2,1)S(1)} %collective-permute-done.8), channel_id=1, source_target_pairs={{0,6},{1,7},{2,0},{3,1},{4,2},{5,3},{6,4},{7,5},{8,14},{9,15},{10,... | collective-permute-start | bytes 884744 | tf_op jit(solution)/shard_map/ppermute | solution.py:327
  42.0 4.2 %collective-permute-done.12 = bf16[128,1152]{1,0:T(8,128)(2,1)S(1)} collective-permute-done((bf16[128,1152]{1,0:T(8,128)(2,1)S(1)}, bf16[128,1152]{1,0:T(8,128)(2,1)S(1)}, u32[]{:S(2)}, u32[]{:S(2)}) %collective-permute-start.12) | collective-permute-done | bytes 294944 | tf_op jit(solution)/shard_map/ppermute | solution.py:327
  46.1 2.5 %collective-permute-done.13 = bf16[128,1152]{1,0:T(8,128)(2,1)S(1)} collective-permute-done((bf16[128,1152]{1,0:T(8,128)(2,1)S(1)}, bf16[128,1152]{1,0:T(8,128)(2,1)S(1)}, u32[]{:S(2)}, u32[]{:S(2)}) %collective-permute-start.13) | collective-permute-done | bytes 294944 | tf_op jit(solution)/shard_map/ppermute | solution.py:327
  48.9 5.4 %scores.2 = (bf16[1024,1024]{1,0:T(8,128)(2,1)S(1)}, f32[24,512]{1,0:T(8,128)S(1)}) custom-call(f32[4]{0:T(128)S(1)} %pad_maximum_fusion.refs_0_, s32[8]{0:T(128)S(1)} %compare_select_fusion.6.refs_1_, bf16[512,1152]{1,0:T(8,128)(2,1)S(1)} %constant_dynamic-update-slice_fusion.refs_2_.r0a, ...), custom_call_target="tpu_custom_call" | custom-call | flops 2415919104 | bytes 4718592 | tf_op jit(solution)/shard_map/scores/pallas_call | solution.py:143
  54.4 5.4 %scores.3 = (bf16[1024,1024]{1,0:T(8,128)(2,1)S(1)}, f32[1,128]{1,0:T(1,128)S(1)}) custom-call(f32[4]{0:T(128)S(1)} %pad_maximum_fusion.refs_0_, s32[8]{0:T(128)S(1)} %compare_select_fusion.6.refs_1_, bf16[512,1152]{1,0:T(8,128)(2,1)S(1)} %constant_dynamic-update-slice_fusion.refs_2_.r0a, ...), custom_call_target="tpu_custom_call" | custom-call | flops 2415919104 | bytes 4718592 | tf_op jit(solution)/shard_map/scores/pallas_call | solution.py:143
  59.8 0.6 collective-permute-start.24
  60.3 0.1 collective-permute-start.25
  60.4 0.4 collective-permute-start.26
  60.8 1.5 %far_image.1 = (bf16[144,1152]{1,0:T(8,128)(2,1)S(1)}, bf16[144,1152]{1,0:T(8,128)(2,1)S(1)}) custom-call(bf16[1024,1024]{1,0:T(8,128)(2,1)S(1)} %get-tuple-element.72.w0, bf16[1024,1024]{1,0:T(8,128)(2,1)S(1)} %get-tuple-element.63.w1, bf16[512,1152]{1,0:T(8,128)(2,1)S(1)} %constant_dynamic-update-slice_fusion.8.refs_4_.r0a, ...), custom_call_target="tpu_custom_call" | custom-call | flops 1207959552 | bytes 4718592 | tf_op jit(solution)/shard_map/far_image/pallas_call | solution.py:226
  62.5 3.2 %collective-permute-start.17 = (bf16[144,1152]{1,0:T(8,128)(2,1)S(1)}, bf16[144,1152]{1,0:T(8,128)(2,1)S(1)}, u32[]{:S(2)}, u32[]{:S(2)}) collective-permute-start(bf16[144,1152]{1,0:T(8,128)(2,1)S(1)} %get-tuple-element.66), channel_id=1, source_target_pairs={{0,6},{1,7},{2,0},{3,1},{4,2},{5,3},{6,4},{7,5},{8,14},{9,15},{10,... | collective-permute-start | bytes 995336 | tf_op jit(solution)/shard_map/ppermute | solution.py:363
  65.7 0.1 collective-permute-done.25.r1a
  65.8 1.7 %collective-permute-done.26.r1b = bf16[512,1152]{1,0:T(8,128)(2,1)S(1)} collective-permute-done((bf16[512,1152]{1,0:T(8,128)(2,1)S(1)}, bf16[512,1152]{1,0:T(8,128)(2,1)S(1)}, u32[]{:S(2)}, u32[]{:S(2)}) %collective-permute-start.26) | collective-permute-done | bytes 1179680 | tf_op jit(solution)/shard_map/ppermute | solution.py:344
  67.5 1.6 %far_text.1 = (bf16[128,1152]{1,0:T(8,128)(2,1)S(1)}, bf16[128,1152]{1,0:T(8,128)(2,1)S(1)}) custom-call(bf16[1024,1024]{1,0:T(8,128)(2,1)S(1)} %get-tuple-element.72.w0, bf16[1024,1024]{1,0:T(8,128)(2,1)S(1)} %collective-permute-done.24.w1, bf16[512,1152]{1,0:T(8,128)(2,1)S(1)} %constant_dynamic-update-slice_fusion.refs_2_.r0a, ...), custom_call_target="tpu_custom_call" | custom-call | flops 1207959552 | bytes 4718592 | tf_op jit(solution)/shard_map/far_text/pallas_call | solution.py:226
  69.2 3.2 %collective-permute-start.28 = (bf16[128,1152]{1,0:T(8,128)(2,1)S(1)}, bf16[128,1152]{1,0:T(8,128)(2,1)S(1)}, u32[]{:S(2)}, u32[]{:S(2)}) collective-permute-start(bf16[128,1152]{1,0:T(8,128)(2,1)S(1)} %get-tuple-element.74), channel_id=1, source_target_pairs={{0,96},{8,104},{16,112},{24,120},{32,0},{40,8},{48,16},{56,24},{64... | collective-permute-start | bytes 884744 | tf_op jit(solution)/shard_map/ppermute | solution.py:365
  72.4 1.1 collective-permute-done.16.via_a
  73.5 4.5 %near_image.1 = (bf16[272,1152]{1,0:T(8,128)(2,1)S(1)}, bf16[256,1152]{1,0:T(8,128)(2,1)S(1)}, f32[256,1152]{1,0:T(8,128)S(1)}, f32[1,128]{1,0:T(1,128)S(1)}) custom-call(bf16[1024,1024]{1,0:T(8,128)(2,1)S(1)} %get-tuple-element.72.w0, bf16[1024,1024]{1,0:T(8,128)(2,1)S(1)} %get-tuple-element.63.w1, ...), custom_call_target="tpu_custom_call" | custom-call | flops 3623878656 | bytes 4718592 | tf_op jit(solution)/shard_map/near_image/pallas_call | solution.py:226
  77.9 3.2 %collective-permute-start.18 = (bf16[272,1152]{1,0:T(8,128)(2,1)S(1)}, bf16[272,1152]{1,0:T(8,128)(2,1)S(1)}, u32[]{:S(2)}, u32[]{:S(2)}) collective-permute-start(bf16[272,1152]{1,0:T(8,128)(2,1)S(1)} %get-tuple-element.68), channel_id=1, source_target_pairs={{0,6},{1,7},{2,0},{3,1},{4,2},{5,3},{6,4},{7,5},{8,14},{9,15},{10,... | collective-permute-start | bytes 1880072 | tf_op jit(solution)/shard_map/ppermute | solution.py:367
  81.2 4.6 %near_text.1 = (bf16[256,1152]{1,0:T(8,128)(2,1)S(1)}, bf16[256,1152]{1,0:T(8,128)(2,1)S(1)}, f32[256,1152]{1,0:T(8,128)S(1)}) custom-call(bf16[1024,1024]{1,0:T(8,128)(2,1)S(1)} %get-tuple-element.72.w0, bf16[1024,1024]{1,0:T(8,128)(2,1)S(1)} %collective-permute-done.24.w1, bf16[512,1152]{1,0:T(8,128)(2,1)S(1)} %constant_dynamic-update-slice_fusion.refs_2_.r0a, ...), custom_call_target="tpu_custom_call" | custom-call | flops 3623878656 | bytes 4718592 | tf_op jit(solution)/shard_map/near_text/pallas_call | solution.py:226
  85.8 1.5 %collective-permute-start.29 = (bf16[256,1152]{1,0:T(8,128)(2,1)S(1)}, bf16[256,1152]{1,0:T(8,128)(2,1)S(1)}, u32[]{:S(2)}, u32[]{:S(2)}) collective-permute-start(bf16[256,1152]{1,0:T(8,128)(2,1)S(1)} %get-tuple-element.76), channel_id=1, source_target_pairs={{0,96},{8,104},{16,112},{24,120},{32,0},{40,8},{48,16},{56,24},{64... | collective-permute-start | bytes 1769480 | tf_op jit(solution)/shard_map/ppermute | solution.py:369
  87.2 0.6 collective-permute-start.30
  87.9 8.4 %collective-permute-done.19.c3 = bf16[256,1152]{1,0:T(8,128)(2,1)S(1)} collective-permute-done((bf16[256,1152]{1,0:T(8,128)(2,1)S(1)}, bf16[256,1152]{1,0:T(8,128)(2,1)S(1)}, u32[]{:S(2)}, u32[]{:S(2)}) %collective-permute-start.19) | collective-permute-done | bytes 589856 | tf_op jit(solution)/shard_map/ppermute | solution.py:367
  96.3 0.4 fold_image_partner.1
  96.7 2.1 %collective-permute-start.34 = (bf16[128,1152]{1,0:T(8,128)(2,1)S(1)}, bf16[128,1152]{1,0:T(8,128)(2,1)S(1)}, u32[]{:S(2)}, u32[]{:S(2)}) collective-permute-start(bf16[128,1152]{1,0:T(8,128)(2,1)S(1)} %get-tuple-element.81), channel_id=1, source_target_pairs={{0,1},{1,0},{2,3},{3,2},{4,5},{5,4},{6,7},{7,6},{8,9},{9,8},{10,11... | collective-permute-start | bytes 884744 | tf_op jit(solution)/shard_map/ppermute | solution.py:372
  98.8 1.1 collective-permute-done.20
  99.9 1.4 %collective-permute-start.22 = (f32[1,128]{1,0:T(1,128)S(1)}, f32[1,128]{1,0:T(1,128)S(1)}, u32[]{:S(2)}, u32[]{:S(2)}) collective-permute-start(f32[1,128]{1,0:T(1,128)S(1)} %add.83), channel_id=1, source_target_pairs={{0,16},{8,24},{16,0},{24,8},{32,48},{40,56},{48,32},{56,40},{64,80... | collective-permute-start | bytes 1544 | tf_op jit(solution)/shard_map/ppermute | solution.py:335
  101.3 1.4 %collective-permute-start.23 = (f32[1,128]{1,0:T(1,128)S(1)}, f32[1,128]{1,0:T(1,128)S(1)}, u32[]{:S(2)}, u32[]{:S(2)}) collective-permute-start(f32[1,128]{1,0:T(1,128)S(1)} %add.83), channel_id=1, source_target_pairs={{0,1},{1,0},{2,3},{3,2},{4,5},{5,4},{6,7},{7,6},{8,9},{9,8},{10,11... | collective-permute-start | bytes 1544 | tf_op jit(solution)/shard_map/ppermute | solution.py:335
  102.7 2.2 %collective-permute-done.22 = f32[1,128]{1,0:T(1,128)S(1)} collective-permute-done((f32[1,128]{1,0:T(1,128)S(1)}, f32[1,128]{1,0:T(1,128)S(1)}, u32[]{:S(2)}, u32[]{:S(2)}) %collective-permute-start.22) | collective-permute-done | bytes 544 | tf_op jit(solution)/shard_map/ppermute | solution.py:335
  104.9 0.7 collective-permute-start.21
  105.5 0.8 collective-permute-done.23
  106.4 3.3 %collective-permute-done.21 = f32[1,128]{1,0:T(1,128)S(1)} collective-permute-done((f32[1,128]{1,0:T(1,128)S(1)}, f32[1,128]{1,0:T(1,128)S(1)}, u32[]{:S(2)}, u32[]{:S(2)}) %collective-permute-start.21) | collective-permute-done | bytes 544 | tf_op jit(solution)/shard_map/ppermute | solution.py:335
  109.6 0.4 fold_partner.1
  110.1 0.5 collective-permute-start.32
  110.6 2.8 %collective-permute-start.33 = (f32[1,128]{1,0:T(1,128)S(1)}, f32[1,128]{1,0:T(1,128)S(1)}, u32[]{:S(2)}, u32[]{:S(2)}) collective-permute-start(f32[1,128]{1,0:T(1,128)S(1)} %add_add_fusion.1), channel_id=1, source_target_pairs={{0,96},{8,104},{16,112},{24,120},{32,0},{40,8},{48,16},{56,24},{64... | collective-permute-start | bytes 1544 | tf_op jit(solution)/shard_map/ppermute | solution.py:335
  113.4 0.3 fold_own.2.own
  113.8 1.2 finish.2
  114.9 0.3 fold_own.3.own
  115.3 3.2 %collective-permute-done.31 = f32[1,128]{1,0:T(1,128)S(1)} collective-permute-done((f32[1,128]{1,0:T(1,128)S(1)}, f32[1,128]{1,0:T(1,128)S(1)}, u32[]{:S(2)}, u32[]{:S(2)}) %collective-permute-start.31) | collective-permute-done | bytes 544 | tf_op jit(solution)/shard_map/ppermute | solution.py:335
  118.4 0.6 fusion.12
  121.0 0.7 collective-permute-done.35.code_ref
  121.7 1.2 finish.3
  (58 shorter events, 0.9 us)
Async XLA Ops:
  0.6 13.8 %copy-start.4 = (s32[8]{0:T(128)S(1)}, s32[8]{0:T(128)}, u32[]{:S(2)}) copy-start(s32[8]{0:T(128)} %constant.142.clone) | copy-start | bytes 100
  0.6 13.8 %copy-start.6 = (s32[8]{0:T(128)S(1)}, s32[8]{0:T(128)}, u32[]{:S(2)}) copy-start(s32[8]{0:T(128)} %constant.143) | copy-start | bytes 100
  0.7 13.9 %copy-start.5 = (s32[8]{0:T(128)S(1)}, s32[8]{0:T(128)}, u32[]{:S(2)}) copy-start(s32[8]{0:T(128)} %constant.141.clone) | copy-start | bytes 100
  3.3 12.0 %collective-permute-start = (bf16[128,1152]{1,0:T(8,128)(2,1)}, bf16[128,1152]{1,0:T(8,128)(2,1)S(1)}, u32[]{:S(2)}, u32[]{:S(2)}) collective-permute-start(bf16[128,1152]{1,0:T(8,128)(2,1)} %get-tuple-element.45), channel_id=1, source_target_pairs={{0,1},{1,0},{2,3},{3,2},{4,5},{5,4},{6,7},{7,6},{8,9},{9,8},{10,11... | collective-permute-start | bytes 884744 | tf_op jit(solution)/shard_map/ppermute | solution.py:319
  7.3 11.1 %collective-permute-start.2 = (bf16[128,1152]{1,0:T(8,128)(2,1)}, bf16[128,1152]{1,0:T(8,128)(2,1)S(1)}, u32[]{:S(2)}, u32[]{:S(2)}) collective-permute-start(bf16[128,1152]{1,0:T(8,128)(2,1)} %get-tuple-element.45), channel_id=1, source_target_pairs={{0,2},{1,3},{2,4},{3,5},{4,6},{5,7},{6,0},{7,1},{8,10},{9,11},{10,... | collective-permute-start | bytes 884744 | tf_op jit(solution)/shard_map/ppermute | solution.py:320
  8.8 12.8 %collective-permute-start.1 = (bf16[128,1152]{1,0:T(8,128)(2,1)}, bf16[128,1152]{1,0:T(8,128)(2,1)S(1)}, u32[]{:S(2)}, u32[]{:S(2)}) collective-permute-start(bf16[128,1152]{1,0:T(8,128)(2,1)} %get-tuple-element.46), channel_id=1, source_target_pairs={{0,16},{8,24},{16,0},{24,8},{32,48},{40,56},{48,32},{56,40},{64,80... | collective-permute-start | bytes 884744 | tf_op jit(solution)/shard_map/ppermute | solution.py:319
  9.8 10.0 %collective-permute-start.3 = (bf16[128,1152]{1,0:T(8,128)(2,1)}, bf16[128,1152]{1,0:T(8,128)(2,1)S(1)}, u32[]{:S(2)}, u32[]{:S(2)}) collective-permute-start(bf16[128,1152]{1,0:T(8,128)(2,1)} %get-tuple-element.46), channel_id=1, source_target_pairs={{0,32},{8,40},{16,48},{24,56},{32,64},{40,72},{48,80},{56,88},{64,... | collective-permute-start | bytes 884744 | tf_op jit(solution)/shard_map/ppermute | solution.py:320
  11.4 10.2 %collective-permute-start.4 = (bf16[128,1152]{1,0:T(8,128)(2,1)}, bf16[128,1152]{1,0:T(8,128)(2,1)S(1)}, u32[]{:S(2)}, u32[]{:S(2)}) collective-permute-start(bf16[128,1152]{1,0:T(8,128)(2,1)} %get-tuple-element.45), channel_id=1, source_target_pairs={{0,6},{1,7},{2,0},{3,1},{4,2},{5,3},{6,4},{7,5},{8,14},{9,15},{10,... | collective-permute-start | bytes 884744 | tf_op jit(solution)/shard_map/ppermute | solution.py:321
  15.3 8.2 %collective-permute-start.5 = (bf16[128,1152]{1,0:T(8,128)(2,1)}, bf16[128,1152]{1,0:T(8,128)(2,1)S(1)}, u32[]{:S(2)}, u32[]{:S(2)}) collective-permute-start(bf16[128,1152]{1,0:T(8,128)(2,1)} %get-tuple-element.46), channel_id=1, source_target_pairs={{0,96},{8,104},{16,112},{24,120},{32,0},{40,8},{48,16},{56,24},{64... | collective-permute-start | bytes 884744 | tf_op jit(solution)/shard_map/ppermute | solution.py:321
  18.3 8.3 %collective-permute-start.6 = (bf16[128,1152]{1,0:T(8,128)(2,1)S(1)}, bf16[128,1152]{1,0:T(8,128)(2,1)S(1)}, u32[]{:S(2)}, u32[]{:S(2)}) collective-permute-start(bf16[128,1152]{1,0:T(8,128)(2,1)S(1)} %collective-permute-done.2), channel_id=1, source_target_pairs={{0,2},{1,3},{2,4},{3,5},{4,6},{5,7},{6,0},{7,1},{8,10},{9,11},{10,... | collective-permute-start | bytes 884744 | tf_op jit(solution)/shard_map/ppermute | solution.py:322
  19.8 8.0 %collective-permute-start.7 = (bf16[128,1152]{1,0:T(8,128)(2,1)S(1)}, bf16[128,1152]{1,0:T(8,128)(2,1)S(1)}, u32[]{:S(2)}, u32[]{:S(2)}) collective-permute-start(bf16[128,1152]{1,0:T(8,128)(2,1)S(1)} %collective-permute-done.3), channel_id=1, source_target_pairs={{0,32},{8,40},{16,48},{24,56},{32,64},{40,72},{48,80},{56,88},{64,... | collective-permute-start | bytes 884744 | tf_op jit(solution)/shard_map/ppermute | solution.py:322
  27.9 6.7 %collective-permute-start.8 = (bf16[128,1152]{1,0:T(8,128)(2,1)S(1)}, bf16[128,1152]{1,0:T(8,128)(2,1)S(1)}, u32[]{:S(2)}, u32[]{:S(2)}) collective-permute-start(bf16[128,1152]{1,0:T(8,128)(2,1)S(1)} %collective-permute-done), channel_id=1, source_target_pairs={{0,6},{1,7},{2,0},{3,1},{4,2},{5,3},{6,4},{7,5},{8,14},{9,15},{10,... | collective-permute-start | bytes 884744 | tf_op jit(solution)/shard_map/ppermute | solution.py:324
  29.6 7.9 %collective-permute-start.10 = (bf16[128,1152]{1,0:T(8,128)(2,1)S(1)}, bf16[128,1152]{1,0:T(8,128)(2,1)S(1)}, u32[]{:S(2)}, u32[]{:S(2)}) collective-permute-start(bf16[128,1152]{1,0:T(8,128)(2,1)S(1)} %collective-permute-done), channel_id=1, source_target_pairs={{0,2},{1,3},{2,4},{3,5},{4,6},{5,7},{6,0},{7,1},{8,10},{9,11},{10,... | collective-permute-start | bytes 884744 | tf_op jit(solution)/shard_map/ppermute | solution.py:325
  29.9 6.7 %collective-permute-start.9 = (bf16[128,1152]{1,0:T(8,128)(2,1)S(1)}, bf16[128,1152]{1,0:T(8,128)(2,1)S(1)}, u32[]{:S(2)}, u32[]{:S(2)}) collective-permute-start(bf16[128,1152]{1,0:T(8,128)(2,1)S(1)} %collective-permute-done.1), channel_id=1, source_target_pairs={{0,96},{8,104},{16,112},{24,120},{32,0},{40,8},{48,16},{56,24},{64... | collective-permute-start | bytes 884744 | tf_op jit(solution)/shard_map/ppermute | solution.py:324
  31.0 7.9 %collective-permute-start.11 = (bf16[128,1152]{1,0:T(8,128)(2,1)S(1)}, bf16[128,1152]{1,0:T(8,128)(2,1)S(1)}, u32[]{:S(2)}, u32[]{:S(2)}) collective-permute-start(bf16[128,1152]{1,0:T(8,128)(2,1)S(1)} %collective-permute-done.1), channel_id=1, source_target_pairs={{0,32},{8,40},{16,48},{24,56},{32,64},{40,72},{48,80},{56,88},{64,... | collective-permute-start | bytes 884744 | tf_op jit(solution)/shard_map/ppermute | solution.py:325
  32.0 22.3 %collective-permute-start.14 = (bf16[512,1152]{1,0:T(8,128)(2,1)S(1)}, bf16[512,1152]{1,0:T(8,128)(2,1)S(1)}, u32[]{:S(2)}, u32[]{:S(2)}) collective-permute-start(bf16[512,1152]{1,0:T(8,128)(2,1)S(1)} %constant_dynamic-update-slice_fusion.8.refs_4_.r0a), channel_id=1, source_target_pairs={{0,8},{8,0},{16,24},{24,16},{32,40},{40,32},{48,56},{56,48},{64,72... | collective-permute-start | bytes 3538952 | tf_op jit(solution)/shard_map/ppermute | solution.py:343
  38.9 7.2 %collective-permute-start.12 = (bf16[128,1152]{1,0:T(8,128)(2,1)S(1)}, bf16[128,1152]{1,0:T(8,128)(2,1)S(1)}, u32[]{:S(2)}, u32[]{:S(2)}) collective-permute-start(bf16[128,1152]{1,0:T(8,128)(2,1)S(1)} %collective-permute-done.8), channel_id=1, source_target_pairs={{0,6},{1,7},{2,0},{3,1},{4,2},{5,3},{6,4},{7,5},{8,14},{9,15},{10,... | collective-permute-start | bytes 884744 | tf_op jit(solution)/shard_map/ppermute | solution.py:327
  41.9 6.7 %collective-permute-start.13 = (bf16[128,1152]{1,0:T(8,128)(2,1)S(1)}, bf16[128,1152]{1,0:T(8,128)(2,1)S(1)}, u32[]{:S(2)}, u32[]{:S(2)}) collective-permute-start(bf16[128,1152]{1,0:T(8,128)(2,1)S(1)} %collective-permute-done.9), channel_id=1, source_target_pairs={{0,96},{8,104},{16,112},{24,120},{32,0},{40,8},{48,16},{56,24},{64... | collective-permute-start | bytes 884744 | tf_op jit(solution)/shard_map/ppermute | solution.py:327
  48.6 5.7 %collective-permute-start.15 = (bf16[512,1152]{1,0:T(8,128)(2,1)S(1)}, bf16[512,1152]{1,0:T(8,128)(2,1)S(1)}, u32[]{:S(2)}, u32[]{:S(2)}) collective-permute-start(bf16[512,1152]{1,0:T(8,128)(2,1)S(1)} %constant_dynamic-update-slice_fusion.12.refs_5_.r0b), channel_id=1, source_target_pairs={{0,8},{8,0},{16,24},{24,16},{32,40},{40,32},{48,56},{56,48},{64,72... | collective-permute-start | bytes 3538952 | tf_op jit(solution)/shard_map/ppermute | solution.py:343
  59.8 7.7 %collective-permute-start.24 = (bf16[1024,1024]{1,0:T(8,128)(2,1)S(1)}, bf16[1024,1024]{1,0:T(8,128)(2,1)S(1)}, u32[]{:S(2)}, u32[]{:S(2)}) collective-permute-start(bf16[1024,1024]{1,0:T(8,128)(2,1)S(1)} %get-tuple-element.63.w1), channel_id=1, source_target_pairs={{0,8},{8,0},{16,24},{24,16},{32,40},{40,32},{48,56},{56,48},{64,72... | collective-permute-start | bytes 6291464 | tf_op jit(solution)/shard_map/ppermute | solution.py:360
  60.3 5.5 %collective-permute-start.25 = (bf16[512,1152]{1,0:T(8,128)(2,1)S(1)}, bf16[512,1152]{1,0:T(8,128)(2,1)S(1)}, u32[]{:S(2)}, u32[]{:S(2)}) collective-permute-start(bf16[512,1152]{1,0:T(8,128)(2,1)S(1)} %constant_dynamic-update-slice_fusion.refs_2_.r0a), channel_id=1, source_target_pairs={{0,8},{8,0},{16,24},{24,16},{32,40},{40,32},{48,56},{56,48},{64,72... | collective-permute-start | bytes 3538952 | tf_op jit(solution)/shard_map/ppermute | solution.py:344
  60.4 7.1 %collective-permute-start.26 = (bf16[512,1152]{1,0:T(8,128)(2,1)S(1)}, bf16[512,1152]{1,0:T(8,128)(2,1)S(1)}, u32[]{:S(2)}, u32[]{:S(2)}) collective-permute-start(bf16[512,1152]{1,0:T(8,128)(2,1)S(1)} %constant_dynamic-update-slice_fusion.4.refs_3_.r0b), channel_id=1, source_target_pairs={{0,8},{8,0},{16,24},{24,16},{32,40},{40,32},{48,56},{56,48},{64,72... | collective-permute-start | bytes 3538952 | tf_op jit(solution)/shard_map/ppermute | solution.py:344
  62.4 11.1 %collective-permute-start.16 = (bf16[144,1152]{1,0:T(8,128)(2,1)S(1)}, bf16[144,1152]{1,0:T(8,128)(2,1)S(1)}, u32[]{:S(2)}, u32[]{:S(2)}) collective-permute-start(bf16[144,1152]{1,0:T(8,128)(2,1)S(1)} %get-tuple-element.65), channel_id=1, source_target_pairs={{0,2},{1,3},{2,4},{3,5},{4,6},{5,7},{6,0},{7,1},{8,10},{9,11},{10,... | collective-permute-start | bytes 995336 | tf_op jit(solution)/shard_map/ppermute | solution.py:363
  62.5 11.0 %collective-permute-start.17 = (bf16[144,1152]{1,0:T(8,128)(2,1)S(1)}, bf16[144,1152]{1,0:T(8,128)(2,1)S(1)}, u32[]{:S(2)}, u32[]{:S(2)}) collective-permute-start(bf16[144,1152]{1,0:T(8,128)(2,1)S(1)} %get-tuple-element.66), channel_id=1, source_target_pairs={{0,6},{1,7},{2,0},{3,1},{4,2},{5,3},{6,4},{7,5},{8,14},{9,15},{10,... | collective-permute-start | bytes 995336 | tf_op jit(solution)/shard_map/ppermute | solution.py:363
  69.1 12.1 %collective-permute-start.27 = (bf16[128,1152]{1,0:T(8,128)(2,1)S(1)}, bf16[128,1152]{1,0:T(8,128)(2,1)S(1)}, u32[]{:S(2)}, u32[]{:S(2)}) collective-permute-start(bf16[128,1152]{1,0:T(8,128)(2,1)S(1)} %get-tuple-element.73), channel_id=1, source_target_pairs={{0,32},{8,40},{16,48},{24,56},{32,64},{40,72},{48,80},{56,88},{64,... | collective-permute-start | bytes 884744 | tf_op jit(solution)/shard_map/ppermute | solution.py:365
  69.2 12.0 %collective-permute-start.28 = (bf16[128,1152]{1,0:T(8,128)(2,1)S(1)}, bf16[128,1152]{1,0:T(8,128)(2,1)S(1)}, u32[]{:S(2)}, u32[]{:S(2)}) collective-permute-start(bf16[128,1152]{1,0:T(8,128)(2,1)S(1)} %get-tuple-element.74), channel_id=1, source_target_pairs={{0,96},{8,104},{16,112},{24,120},{32,0},{40,8},{48,16},{56,24},{64... | collective-permute-start | bytes 884744 | tf_op jit(solution)/shard_map/ppermute | solution.py:365
  77.9 18.3 %collective-permute-start.18 = (bf16[272,1152]{1,0:T(8,128)(2,1)S(1)}, bf16[272,1152]{1,0:T(8,128)(2,1)S(1)}, u32[]{:S(2)}, u32[]{:S(2)}) collective-permute-start(bf16[272,1152]{1,0:T(8,128)(2,1)S(1)} %get-tuple-element.68), channel_id=1, source_target_pairs={{0,6},{1,7},{2,0},{3,1},{4,2},{5,3},{6,4},{7,5},{8,14},{9,15},{10,... | collective-permute-start | bytes 1880072 | tf_op jit(solution)/shard_map/ppermute | solution.py:367
  81.2 15.1 %collective-permute-start.19 = (bf16[256,1152]{1,0:T(8,128)(2,1)S(1)}, bf16[256,1152]{1,0:T(8,128)(2,1)S(1)}, u32[]{:S(2)}, u32[]{:S(2)}) collective-permute-start(bf16[256,1152]{1,0:T(8,128)(2,1)S(1)} %get-tuple-element.69), channel_id=1, source_target_pairs={{0,2},{1,3},{2,4},{3,5},{4,6},{5,7},{6,0},{7,1},{8,10},{9,11},{10,... | collective-permute-start | bytes 1769480 | tf_op jit(solution)/shard_map/ppermute | solution.py:367
  85.8 23.9 %collective-permute-start.29 = (bf16[256,1152]{1,0:T(8,128)(2,1)S(1)}, bf16[256,1152]{1,0:T(8,128)(2,1)S(1)}, u32[]{:S(2)}, u32[]{:S(2)}) collective-permute-start(bf16[256,1152]{1,0:T(8,128)(2,1)S(1)} %get-tuple-element.76), channel_id=1, source_target_pairs={{0,96},{8,104},{16,112},{24,120},{32,0},{40,8},{48,16},{56,24},{64... | collective-permute-start | bytes 1769480 | tf_op jit(solution)/shard_map/ppermute | solution.py:369
  87.2 22.4 %collective-permute-start.30 = (bf16[256,1152]{1,0:T(8,128)(2,1)S(1)}, bf16[256,1152]{1,0:T(8,128)(2,1)S(1)}, u32[]{:S(2)}, u32[]{:S(2)}) collective-permute-start(bf16[256,1152]{1,0:T(8,128)(2,1)S(1)} %get-tuple-element.77), channel_id=1, source_target_pairs={{0,32},{8,40},{16,48},{24,56},{32,64},{40,72},{48,80},{56,88},{64,... | collective-permute-start | bytes 1769480 | tf_op jit(solution)/shard_map/ppermute | solution.py:369
  96.7 17.0 %collective-permute-start.34 = (bf16[128,1152]{1,0:T(8,128)(2,1)S(1)}, bf16[128,1152]{1,0:T(8,128)(2,1)S(1)}, u32[]{:S(2)}, u32[]{:S(2)}) collective-permute-start(bf16[128,1152]{1,0:T(8,128)(2,1)S(1)} %get-tuple-element.81), channel_id=1, source_target_pairs={{0,1},{1,0},{2,3},{3,2},{4,5},{5,4},{6,7},{7,6},{8,9},{9,8},{10,11... | collective-permute-start | bytes 884744 | tf_op jit(solution)/shard_map/ppermute | solution.py:372
  98.8 1.1 collective-permute-start.20
  99.9 4.9 %collective-permute-start.22 = (f32[1,128]{1,0:T(1,128)S(1)}, f32[1,128]{1,0:T(1,128)S(1)}, u32[]{:S(2)}, u32[]{:S(2)}) collective-permute-start(f32[1,128]{1,0:T(1,128)S(1)} %add.83), channel_id=1, source_target_pairs={{0,16},{8,24},{16,0},{24,8},{32,48},{40,56},{48,32},{56,40},{64,80... | collective-permute-start | bytes 1544 | tf_op jit(solution)/shard_map/ppermute | solution.py:335
  101.3 5.0 %collective-permute-start.23 = (f32[1,128]{1,0:T(1,128)S(1)}, f32[1,128]{1,0:T(1,128)S(1)}, u32[]{:S(2)}, u32[]{:S(2)}) collective-permute-start(f32[1,128]{1,0:T(1,128)S(1)} %add.83), channel_id=1, source_target_pairs={{0,1},{1,0},{2,3},{3,2},{4,5},{5,4},{6,7},{7,6},{8,9},{9,8},{10,11... | collective-permute-start | bytes 1544 | tf_op jit(solution)/shard_map/ppermute | solution.py:335
  104.9 4.8 %collective-permute-start.21 = (f32[1,128]{1,0:T(1,128)S(1)}, f32[1,128]{1,0:T(1,128)S(1)}, u32[]{:S(2)}, u32[]{:S(2)}) collective-permute-start(f32[1,128]{1,0:T(1,128)S(1)} %add.83), channel_id=1, source_target_pairs={{0,17},{1,16},{2,19},{3,18},{4,21},{5,20},{6,23},{7,22},{8,25},{9,... | collective-permute-start | bytes 1544 | tf_op jit(solution)/shard_map/ppermute | solution.py:335
  110.1 3.7 %copy-start.1 = (f32[128,1152]{1,0:T(8,128)S(1)}, f32[128,1152]{1,0:T(8,128)}, u32[]{:S(2)}) copy-start(f32[128,1152]{1,0:T(8,128)} %get-tuple-element.79.hat_ref) | copy-start | bytes 1769476
  110.1 3.7 %copy-start.3 = (f32[128,1]{1,0:T(8,128)S(1)}, f32[128,1]{1,0:T(8,128)}, u32[]{:S(2)}) copy-start(f32[128,1]{1,0:T(8,128)} %get-tuple-element.80.norm_ref) | copy-start | bytes 1540
  110.1 5.2 %collective-permute-start.32 = (f32[1,128]{1,0:T(1,128)S(1)}, f32[1,128]{1,0:T(1,128)S(1)}, u32[]{:S(2)}, u32[]{:S(2)}) collective-permute-start(f32[1,128]{1,0:T(1,128)S(1)} %add_add_fusion.1), channel_id=1, source_target_pairs={{0,32},{8,40},{16,48},{24,56},{32,64},{40,72},{48,80},{56,88},{64,... | collective-permute-start | bytes 1544 | tf_op jit(solution)/shard_map/ppermute | solution.py:335
  110.6 4.7 %collective-permute-start.33 = (f32[1,128]{1,0:T(1,128)S(1)}, f32[1,128]{1,0:T(1,128)S(1)}, u32[]{:S(2)}, u32[]{:S(2)}) collective-permute-start(f32[1,128]{1,0:T(1,128)S(1)} %add_add_fusion.1), channel_id=1, source_target_pairs={{0,96},{8,104},{16,112},{24,120},{32,0},{40,8},{48,16},{56,24},{64... | collective-permute-start | bytes 1544 | tf_op jit(solution)/shard_map/ppermute | solution.py:335
  113.4 5.0 %collective-permute-start.31 = (f32[1,128]{1,0:T(1,128)S(1)}, f32[1,128]{1,0:T(1,128)S(1)}, u32[]{:S(2)}, u32[]{:S(2)}) collective-permute-start(f32[1,128]{1,0:T(1,128)S(1)} %add_add_fusion.1), channel_id=1, source_target_pairs={{0,64},{8,72},{16,80},{24,88},{32,96},{40,104},{48,112},{56,120},{... | collective-permute-start | bytes 1544 | tf_op jit(solution)/shard_map/ppermute | solution.py:335
  114.9 6.7 %copy-start = (f32[128,1152]{1,0:T(8,128)S(1)}, f32[128,1152]{1,0:T(8,128)}, u32[]{:S(2)}) copy-start(f32[128,1152]{1,0:T(8,128)} %get-tuple-element.82.hat_ref) | copy-start | bytes 1769476
  114.9 6.7 %copy-start.2 = (f32[128,1]{1,0:T(8,128)S(1)}, f32[128,1]{1,0:T(8,128)}, u32[]{:S(2)}) copy-start(f32[128,1]{1,0:T(8,128)} %get-tuple-element.83.norm_ref) | copy-start | bytes 1540
  114.9 6.7 %collective-permute-start.35 = (bf16[128,1152]{1,0:T(8,128)(2,1)S(1)}, bf16[128,1152]{1,0:T(8,128)(2,1)S(1)}, u32[]{:S(2)}, u32[]{:S(2)}) collective-permute-start(bf16[128,1152]{1,0:T(8,128)(2,1)S(1)} %fold_partner.1), channel_id=1, source_target_pairs={{0,16},{8,24},{16,0},{24,8},{32,48},{40,56},{48,32},{56,40},{64,80... | collective-permute-start | bytes 884744 | tf_op jit(solution)/shard_map/ppermute | solution.py:379

commit v8 on v6

--- a/solution.py
+++ b/solution.py
@@ -372,9 +372,10 @@
     image_code = send(image_code, "txt", PERM_ZHI)
     image_own = fold(own_kernel, i0, (i1, i3), F32, "fold_own")
     v = exchange_sum(v, ("img",), PERM_CORE)
+    text_code = fold(partner_kernel, t0, (t1, t3), BF, "fold_partner")
+    v = after(v, text_code)
     both = [(n, n ^ 17) for n in range(128)]
     v = exchange_sum(v, ("img", ("img", "txt"), "txt"), PERM_ZLO, both, PERM_ZHI)
-    text_code = fold(partner_kernel, t0, (t1, t3), BF, "fold_partner")
     text_code = send(text_code, "img", PERM_ZLO)
     text_own = fold(own_kernel, t0, (t1, t3), F32, "fold_own")
     v = exchange_sum(v, ("img",) * 3, perm_y(1), perm_y(2), perm_y(-1))

time: 133 us -> 129 us (0.970)
  Pallas kernels: 32.8 us -> 29.4 us
  local copies, waits for them, and re-layouts: 3.71 us -> 2.15 us
    ppermute x1, waiting for transfers between devices: 4.62 us -> 0.01 us  [local(): image_code = send(image_code, 'txt', PERM_ZHI)]
    ppermute x2, waiting for transfers between devices: 0.01 us -> 2.71 us  [local(): t1, t3 = (send(t1, 'img', perm_y(-1)), send(t3, 'img', perm_y(1)))]
    pallas_call x2, Pallas kernels: 4.25 us -> 2.34 us  [finish(): pl.pallas_call(finish_kernel, in_specs=[VM] * 4, out_specs=VM, out_shape=...]
    ppermute x1, starting transfers between devices: 0.45 us -> 2.12 us  [local(): image_code = send(image_code, 'txt', PERM_ZHI)]
    unnamed x24, local copies, waits for them, and re-layouts: 2.99 us -> 1.43 us
  transfers between devices with their start and end apart: 36 -> 36, of which waited for: 20 -> 21; matrix products, arithmetic and copies ran while one was open for 2% -> 2% of each run, Pallas kernels for 17% -> 16%
where the time goes in v8:
time: 129 us; the launch traced here: 128 us
  starting transfers between devices  44.7 us (35%)
  waiting for transfers between devices  43.7 us (34%)
  Pallas kernels  29.4 us (23%)
  between operations  7.66 us (6%)
  local copies, waits for them, and re-layouts  2.15 us (2%)
    pallas_call x4, Pallas kernels, pulls(): pl.pallas_call(functools.partial(near_kernel if via else far_kernel, dims...  12.2 us
    pallas_call x2, Pallas kernels, score_half(): pl.pallas_call(lambda *refs: scores_kernel(first, *refs), in_specs=[SM, S...  10.8 us
    ppermute x2, waiting for transfers between devices, local(): i1, i3 = (send(i1, 'txt', perm_x(-1)), send(i3, 'txt', perm_x(1)))  8.41 us
    ppermute x7, waiting for transfers between devices, exchange_sum(): got = [send(v, a, p) for a, p in zip(axis, perms)]  8.33 us
    ppermute x7, starting transfers between devices, exchange_sum(): got = [send(v, a, p) for a, p in zip(axis, perms)]  8.08 us
    ppermute x2, waiting for transfers between devices, gather(): send(b, axis, perm(-1))  6.64 us
    ppermute x2, starting transfers between devices, gather(): z = [send(low, axis, pz) for low, axis, _, pz in ways]  4.98 us
    ppermute x2, starting transfers between devices, gather(): a3 = [send(low, axis, perm(-1)) for low, axis, perm, _ in ways]  4.76 us
  transfers between devices with their start and end apart: 36, of which 21 were waited for; matrix products, arithmetic and copies ran while one was open for 2% of the time, Pallas kernels for 16%

profile of v8, /device:TPU:0, one launch (start us, length us, event | category | flops | bytes accessed | tf_op | source)
XLA Modules:
  0.0 128.0 jit_solution(10665881565744171042)
XLA Ops:
  0.7 2.6 %normalize.1 = (bf16[128,1152]{1,0:T(8,128)(2,1)}, f32[128,1152]{1,0:T(8,128)}, f32[128,1]{1,0:T(8,128)}, bf16[128,1152]{1,0:T(8,128)(2,1)}, f32[128,1152]{1,0:T(8,128)}, /*index=5*/f32[128,1]{1,0:T(8,128)}) custom-call(f32[128,1152]{1,0:T(8,128)} %a_ref.1, f32[128,1152]{1,0:T(8,128)} %b_ref.1), custom_call_target="tpu_custom_call" | custom-call | tf_op jit(solution)/shard_map/normalize/pallas_call | solution.py:52
  3.3 4.0 %collective-permute-start = (bf16[128,1152]{1,0:T(8,128)(2,1)}, bf16[128,1152]{1,0:T(8,128)(2,1)S(1)}, u32[]{:S(2)}, u32[]{:S(2)}) collective-permute-start(bf16[128,1152]{1,0:T(8,128)(2,1)} %get-tuple-element.45), channel_id=1, source_target_pairs={{0,1},{1,0},{2,3},{3,2},{4,5},{5,4},{6,7},{7,6},{8,9},{9,8},{10,11... | collective-permute-start | bytes 884744 | tf_op jit(solution)/shard_map/ppermute | solution.py:319
  7.3 1.5 %collective-permute-start.2 = (bf16[128,1152]{1,0:T(8,128)(2,1)}, bf16[128,1152]{1,0:T(8,128)(2,1)S(1)}, u32[]{:S(2)}, u32[]{:S(2)}) collective-permute-start(bf16[128,1152]{1,0:T(8,128)(2,1)} %get-tuple-element.45), channel_id=1, source_target_pairs={{0,2},{1,3},{2,4},{3,5},{4,6},{5,7},{6,0},{7,1},{8,10},{9,11},{10,... | collective-permute-start | bytes 884744 | tf_op jit(solution)/shard_map/ppermute | solution.py:320
  8.8 1.0 collective-permute-start.1
  9.8 1.6 %collective-permute-start.3 = (bf16[128,1152]{1,0:T(8,128)(2,1)}, bf16[128,1152]{1,0:T(8,128)(2,1)S(1)}, u32[]{:S(2)}, u32[]{:S(2)}) collective-permute-start(bf16[128,1152]{1,0:T(8,128)(2,1)} %get-tuple-element.46), channel_id=1, source_target_pairs={{0,32},{8,40},{16,48},{24,56},{32,64},{40,72},{48,80},{56,88},{64,... | collective-permute-start | bytes 884744 | tf_op jit(solution)/shard_map/ppermute | solution.py:320
  11.4 1.7 %collective-permute-start.4 = (bf16[128,1152]{1,0:T(8,128)(2,1)}, bf16[128,1152]{1,0:T(8,128)(2,1)S(1)}, u32[]{:S(2)}, u32[]{:S(2)}) collective-permute-start(bf16[128,1152]{1,0:T(8,128)(2,1)} %get-tuple-element.45), channel_id=1, source_target_pairs={{0,6},{1,7},{2,0},{3,1},{4,2},{5,3},{6,4},{7,5},{8,14},{9,15},{10,... | collective-permute-start | bytes 884744 | tf_op jit(solution)/shard_map/ppermute | solution.py:321
  14.6 0.2 select_reduce_fusion
  14.8 0.5 collective-permute-done
  15.3 3.0 %collective-permute-start.5 = (bf16[128,1152]{1,0:T(8,128)(2,1)}, bf16[128,1152]{1,0:T(8,128)(2,1)S(1)}, u32[]{:S(2)}, u32[]{:S(2)}) collective-permute-start(bf16[128,1152]{1,0:T(8,128)(2,1)} %get-tuple-element.46), channel_id=1, source_target_pairs={{0,96},{8,104},{16,112},{24,120},{32,0},{40,8},{48,16},{56,24},{64... | collective-permute-start | bytes 884744 | tf_op jit(solution)/shard_map/ppermute | solution.py:321
  18.3 1.5 %collective-permute-start.6 = (bf16[128,1152]{1,0:T(8,128)(2,1)S(1)}, bf16[128,1152]{1,0:T(8,128)(2,1)S(1)}, u32[]{:S(2)}, u32[]{:S(2)}) collective-permute-start(bf16[128,1152]{1,0:T(8,128)(2,1)S(1)} %collective-permute-done.2), channel_id=1, source_target_pairs={{0,2},{1,3},{2,4},{3,5},{4,6},{5,7},{6,0},{7,1},{8,10},{9,11},{10,... | collective-permute-start | bytes 884744 | tf_op jit(solution)/shard_map/ppermute | solution.py:322
  19.9 1.1 constant_dynamic-update-slice_fusion.3
  21.0 0.5 collective-permute-done.1
  21.6 2.0 %collective-permute-done.5 = bf16[128,1152]{1,0:T(8,128)(2,1)S(1)} collective-permute-done((bf16[128,1152]{1,0:T(8,128)(2,1)}, bf16[128,1152]{1,0:T(8,128)(2,1)S(1)}, u32[]{:S(2)}, u32[]{:S(2)}) %collective-permute-start.5) | collective-permute-done | bytes 294944 | tf_op jit(solution)/shard_map/ppermute | solution.py:321
  23.5 3.1 %collective-permute-done.6 = bf16[128,1152]{1,0:T(8,128)(2,1)S(1)} collective-permute-done((bf16[128,1152]{1,0:T(8,128)(2,1)S(1)}, bf16[128,1152]{1,0:T(8,128)(2,1)S(1)}, u32[]{:S(2)}, u32[]{:S(2)}) %collective-permute-start.6) | collective-permute-done | bytes 294944 | tf_op jit(solution)/shard_map/ppermute | solution.py:322
  26.6 1.2 collective-permute-done.7
  27.9 1.7 %collective-permute-start.8 = (bf16[128,1152]{1,0:T(8,128)(2,1)S(1)}, bf16[128,1152]{1,0:T(8,128)(2,1)S(1)}, u32[]{:S(2)}, u32[]{:S(2)}) collective-permute-start(bf16[128,1152]{1,0:T(8,128)(2,1)S(1)} %collective-permute-done), channel_id=1, source_target_pairs={{0,6},{1,7},{2,0},{3,1},{4,2},{5,3},{6,4},{7,5},{8,14},{9,15},{10,... | collective-permute-start | bytes 884744 | tf_op jit(solution)/shard_map/ppermute | solution.py:324
  29.6 0.3 collective-permute-start.10
  29.9 1.1 collective-permute-start.9
  31.0 0.9 collective-permute-start.11
  32.0 0.1 collective-permute-start.14
  32.2 2.4 %collective-permute-done.8 = bf16[128,1152]{1,0:T(8,128)(2,1)S(1)} collective-permute-done((bf16[128,1152]{1,0:T(8,128)(2,1)S(1)}, bf16[128,1152]{1,0:T(8,128)(2,1)S(1)}, u32[]{:S(2)}, u32[]{:S(2)}) %collective-permute-start.8) | collective-permute-done | bytes 294944 | tf_op jit(solution)/shard_map/ppermute | solution.py:324
  34.6 2.0 %collective-permute-done.9 = bf16[128,1152]{1,0:T(8,128)(2,1)S(1)} collective-permute-done((bf16[128,1152]{1,0:T(8,128)(2,1)S(1)}, bf16[128,1152]{1,0:T(8,128)(2,1)S(1)}, u32[]{:S(2)}, u32[]{:S(2)}) %collective-permute-start.9) | collective-permute-done | bytes 294944 | tf_op jit(solution)/shard_map/ppermute | solution.py:324
  36.6 0.9 collective-permute-done.10
  37.5 1.4 %collective-permute-done.11 = bf16[128,1152]{1,0:T(8,128)(2,1)S(1)} collective-permute-done((bf16[128,1152]{1,0:T(8,128)(2,1)S(1)}, bf16[128,1152]{1,0:T(8,128)(2,1)S(1)}, u32[]{:S(2)}, u32[]{:S(2)}) %collective-permute-start.11) | collective-permute-done | bytes 294944 | tf_op jit(solution)/shard_map/ppermute | solution.py:325
  38.9 3.0 %collective-permute-start.12 = (bf16[128,1152]{1,0:T(8,128)(2,1)S(1)}, bf16[128,1152]{1,0:T(8,128)(2,1)S(1)}, u32[]{:S(2)}, u32[]{:S(2)}) collective-permute-start(bf16[128,1152]{1,0:T(8,128)(2,1)S(1)} %collective-permute-done.8), channel_id=1, source_target_pairs={{0,6},{1,7},{2,0},{3,1},{4,2},{5,3},{6,4},{7,5},{8,14},{9,15},{10,... | collective-permute-start | bytes 884744 | tf_op jit(solution)/shard_map/ppermute | solution.py:327
  42.0 4.2 %collective-permute-done.12 = bf16[128,1152]{1,0:T(8,128)(2,1)S(1)} collective-permute-done((bf16[128,1152]{1,0:T(8,128)(2,1)S(1)}, bf16[128,1152]{1,0:T(8,128)(2,1)S(1)}, u32[]{:S(2)}, u32[]{:S(2)}) %collective-permute-start.12) | collective-permute-done | bytes 294944 | tf_op jit(solution)/shard_map/ppermute | solution.py:327
  46.1 2.5 %collective-permute-done.13 = bf16[128,1152]{1,0:T(8,128)(2,1)S(1)} collective-permute-done((bf16[128,1152]{1,0:T(8,128)(2,1)S(1)}, bf16[128,1152]{1,0:T(8,128)(2,1)S(1)}, u32[]{:S(2)}, u32[]{:S(2)}) %collective-permute-start.13) | collective-permute-done | bytes 294944 | tf_op jit(solution)/shard_map/ppermute | solution.py:327
  48.6 0.1 collective-permute-start.15
  48.9 5.4 %scores.2 = (bf16[1024,1024]{1,0:T(8,128)(2,1)S(1)}, f32[24,512]{1,0:T(8,128)S(1)}) custom-call(f32[4]{0:T(128)S(1)} %pad_maximum_fusion.refs_0_, s32[8]{0:T(128)S(1)} %compare_select_fusion.6.refs_1_, bf16[512,1152]{1,0:T(8,128)(2,1)S(1)} %constant_dynamic-update-slice_fusion.refs_2_.r0a, ...), custom_call_target="tpu_custom_call" | custom-call | flops 2415919104 | bytes 4718592 | tf_op jit(solution)/shard_map/scores/pallas_call | solution.py:143
  54.4 5.4 %scores.3 = (bf16[1024,1024]{1,0:T(8,128)(2,1)S(1)}, f32[1,128]{1,0:T(1,128)S(1)}) custom-call(f32[4]{0:T(128)S(1)} %pad_maximum_fusion.refs_0_, s32[8]{0:T(128)S(1)} %compare_select_fusion.6.refs_1_, bf16[512,1152]{1,0:T(8,128)(2,1)S(1)} %constant_dynamic-update-slice_fusion.refs_2_.r0a, ...), custom_call_target="tpu_custom_call" | custom-call | flops 2415919104 | bytes 4718592 | tf_op jit(solution)/shard_map/scores/pallas_call | solution.py:143
  59.8 0.6 collective-permute-start.21
  60.3 0.1 collective-permute-start.22
  60.4 0.4 collective-permute-start.23
  60.8 1.5 %far_image.1 = (bf16[144,1152]{1,0:T(8,128)(2,1)S(1)}, bf16[144,1152]{1,0:T(8,128)(2,1)S(1)}) custom-call(bf16[1024,1024]{1,0:T(8,128)(2,1)S(1)} %get-tuple-element.72.w0, bf16[1024,1024]{1,0:T(8,128)(2,1)S(1)} %get-tuple-element.63.w1, bf16[512,1152]{1,0:T(8,128)(2,1)S(1)} %constant_dynamic-update-slice_fusion.8.refs_4_.r0a, ...), custom_call_target="tpu_custom_call" | custom-call | flops 1207959552 | bytes 4718592 | tf_op jit(solution)/shard_map/far_image/pallas_call | solution.py:226
  62.5 3.2 %collective-permute-start.17 = (bf16[144,1152]{1,0:T(8,128)(2,1)S(1)}, bf16[144,1152]{1,0:T(8,128)(2,1)S(1)}, u32[]{:S(2)}, u32[]{:S(2)}) collective-permute-start(bf16[144,1152]{1,0:T(8,128)(2,1)S(1)} %get-tuple-element.66), channel_id=1, source_target_pairs={{0,6},{1,7},{2,0},{3,1},{4,2},{5,3},{6,4},{7,5},{8,14},{9,15},{10,... | collective-permute-start | bytes 995336 | tf_op jit(solution)/shard_map/ppermute | solution.py:363
  65.7 0.1 collective-permute-done.22.r1a
  65.8 1.7 %collective-permute-done.23.r1b = bf16[512,1152]{1,0:T(8,128)(2,1)S(1)} collective-permute-done((bf16[512,1152]{1,0:T(8,128)(2,1)S(1)}, bf16[512,1152]{1,0:T(8,128)(2,1)S(1)}, u32[]{:S(2)}, u32[]{:S(2)}) %collective-permute-start.23) | collective-permute-done | bytes 1179680 | tf_op jit(solution)/shard_map/ppermute | solution.py:344
  67.5 1.6 %far_text.1 = (bf16[128,1152]{1,0:T(8,128)(2,1)S(1)}, bf16[128,1152]{1,0:T(8,128)(2,1)S(1)}) custom-call(bf16[1024,1024]{1,0:T(8,128)(2,1)S(1)} %get-tuple-element.72.w0, bf16[1024,1024]{1,0:T(8,128)(2,1)S(1)} %collective-permute-done.21.w1, bf16[512,1152]{1,0:T(8,128)(2,1)S(1)} %constant_dynamic-update-slice_fusion.refs_2_.r0a, ...), custom_call_target="tpu_custom_call" | custom-call | flops 1207959552 | bytes 4718592 | tf_op jit(solution)/shard_map/far_text/pallas_call | solution.py:226
  69.2 3.2 %collective-permute-start.25 = (bf16[128,1152]{1,0:T(8,128)(2,1)S(1)}, bf16[128,1152]{1,0:T(8,128)(2,1)S(1)}, u32[]{:S(2)}, u32[]{:S(2)}) collective-permute-start(bf16[128,1152]{1,0:T(8,128)(2,1)S(1)} %get-tuple-element.74), channel_id=1, source_target_pairs={{0,96},{8,104},{16,112},{24,120},{32,0},{40,8},{48,16},{56,24},{64... | collective-permute-start | bytes 884744 | tf_op jit(solution)/shard_map/ppermute | solution.py:365
  72.4 1.1 collective-permute-done.16.via_a
  73.5 4.5 %near_image.1 = (bf16[272,1152]{1,0:T(8,128)(2,1)S(1)}, bf16[256,1152]{1,0:T(8,128)(2,1)S(1)}, f32[256,1152]{1,0:T(8,128)S(1)}, f32[1,128]{1,0:T(1,128)S(1)}) custom-call(bf16[1024,1024]{1,0:T(8,128)(2,1)S(1)} %get-tuple-element.72.w0, bf16[1024,1024]{1,0:T(8,128)(2,1)S(1)} %get-tuple-element.63.w1, ...), custom_call_target="tpu_custom_call" | custom-call | flops 3623878656 | bytes 4718592 | tf_op jit(solution)/shard_map/near_image/pallas_call | solution.py:226
  77.9 3.2 %collective-permute-start.18 = (bf16[272,1152]{1,0:T(8,128)(2,1)S(1)}, bf16[272,1152]{1,0:T(8,128)(2,1)S(1)}, u32[]{:S(2)}, u32[]{:S(2)}) collective-permute-start(bf16[272,1152]{1,0:T(8,128)(2,1)S(1)} %get-tuple-element.68), channel_id=1, source_target_pairs={{0,6},{1,7},{2,0},{3,1},{4,2},{5,3},{6,4},{7,5},{8,14},{9,15},{10,... | collective-permute-start | bytes 1880072 | tf_op jit(solution)/shard_map/ppermute | solution.py:367
  81.2 4.6 %near_text.1 = (bf16[256,1152]{1,0:T(8,128)(2,1)S(1)}, bf16[256,1152]{1,0:T(8,128)(2,1)S(1)}, f32[256,1152]{1,0:T(8,128)S(1)}) custom-call(bf16[1024,1024]{1,0:T(8,128)(2,1)S(1)} %get-tuple-element.72.w0, bf16[1024,1024]{1,0:T(8,128)(2,1)S(1)} %collective-permute-done.21.w1, bf16[512,1152]{1,0:T(8,128)(2,1)S(1)} %constant_dynamic-update-slice_fusion.refs_2_.r0a, ...), custom_call_target="tpu_custom_call" | custom-call | flops 3623878656 | bytes 4718592 | tf_op jit(solution)/shard_map/near_text/pallas_call | solution.py:226
  85.8 1.5 %collective-permute-start.26 = (bf16[256,1152]{1,0:T(8,128)(2,1)S(1)}, bf16[256,1152]{1,0:T(8,128)(2,1)S(1)}, u32[]{:S(2)}, u32[]{:S(2)}) collective-permute-start(bf16[256,1152]{1,0:T(8,128)(2,1)S(1)} %get-tuple-element.76), channel_id=1, source_target_pairs={{0,96},{8,104},{16,112},{24,120},{32,0},{40,8},{48,16},{56,24},{64... | collective-permute-start | bytes 1769480 | tf_op jit(solution)/shard_map/ppermute | solution.py:369
  87.2 0.6 collective-permute-start.27
  87.9 8.4 %collective-permute-done.19.c3 = bf16[256,1152]{1,0:T(8,128)(2,1)S(1)} collective-permute-done((bf16[256,1152]{1,0:T(8,128)(2,1)S(1)}, bf16[256,1152]{1,0:T(8,128)(2,1)S(1)}, u32[]{:S(2)}, u32[]{:S(2)}) %collective-permute-start.19) | collective-permute-done | bytes 589856 | tf_op jit(solution)/shard_map/ppermute | solution.py:367
  96.3 0.4 fold_image_partner.1
  96.7 2.1 %collective-permute-start.34 = (bf16[128,1152]{1,0:T(8,128)(2,1)S(1)}, bf16[128,1152]{1,0:T(8,128)(2,1)S(1)}, u32[]{:S(2)}, u32[]{:S(2)}) collective-permute-start(bf16[128,1152]{1,0:T(8,128)(2,1)S(1)} %get-tuple-element.81), channel_id=1, source_target_pairs={{0,1},{1,0},{2,3},{3,2},{4,5},{5,4},{6,7},{7,6},{8,9},{9,8},{10,11... | collective-permute-start | bytes 884744 | tf_op jit(solution)/shard_map/ppermute | solution.py:372
  98.8 1.1 collective-permute-done.20
  99.9 2.7 %collective-permute-done.27.c3 = bf16[256,1152]{1,0:T(8,128)(2,1)S(1)} collective-permute-done((bf16[256,1152]{1,0:T(8,128)(2,1)S(1)}, bf16[256,1152]{1,0:T(8,128)(2,1)S(1)}, u32[]{:S(2)}, u32[]{:S(2)}) %collective-permute-start.27) | collective-permute-done | bytes 589856 | tf_op jit(solution)/shard_map/ppermute | solution.py:369
  102.7 0.4 fold_partner.1
  103.1 0.7 collective-permute-start.29
  103.8 3.3 %collective-permute-start.30 = (f32[1,128]{1,0:T(1,128)S(1)}, f32[1,128]{1,0:T(1,128)S(1)}, u32[]{:S(2)}, u32[]{:S(2)}) collective-permute-start(f32[1,128]{1,0:T(1,128)S(1)} %add.83), channel_id=1, source_target_pairs={{0,1},{1,0},{2,3},{3,2},{4,5},{5,4},{6,7},{7,6},{8,9},{9,8},{10,11... | collective-permute-start | bytes 1544 | tf_op jit(solution)/shard_map/ppermute | solution.py:335
  107.1 0.7 collective-permute-start.28
  107.8 1.0 collective-permute-done.30
  108.9 3.0 %collective-permute-done.28 = f32[1,128]{1,0:T(1,128)S(1)} collective-permute-done((f32[1,128]{1,0:T(1,128)S(1)}, f32[1,128]{1,0:T(1,128)S(1)}, u32[]{:S(2)}, u32[]{:S(2)}) %collective-permute-start.28) | collective-permute-done | bytes 544 | tf_op jit(solution)/shard_map/ppermute | solution.py:335
  112.0 3.2 %collective-permute-start.33 = (f32[1,128]{1,0:T(1,128)S(1)}, f32[1,128]{1,0:T(1,128)S(1)}, u32[]{:S(2)}, u32[]{:S(2)}) collective-permute-start(f32[1,128]{1,0:T(1,128)S(1)} %add_add_fusion.1), channel_id=1, source_target_pairs={{0,96},{8,104},{16,112},{24,120},{32,0},{40,8},{48,16},{56,24},{64... | collective-permute-start | bytes 1544 | tf_op jit(solution)/shard_map/ppermute | solution.py:335
  115.2 0.3 fold_own.2.own
  115.6 1.2 finish.2
  116.8 0.3 fold_own.3.own
  117.1 3.2 %collective-permute-done.31 = f32[1,128]{1,0:T(1,128)S(1)} collective-permute-done((f32[1,128]{1,0:T(1,128)S(1)}, f32[1,128]{1,0:T(1,128)S(1)}, u32[]{:S(2)}, u32[]{:S(2)}) %collective-permute-start.31) | collective-permute-done | bytes 544 | tf_op jit(solution)/shard_map/ppermute | solution.py:335
  120.3 0.6 fusion.12
  122.8 0.7 collective-permute-done.35.code_ref
  123.5 1.2 finish.3
  (58 shorter events, 0.9 us)
Async XLA Ops:
  0.6 13.8 %copy-start.4 = (s32[8]{0:T(128)S(1)}, s32[8]{0:T(128)}, u32[]{:S(2)}) copy-start(s32[8]{0:T(128)} %constant.142.clone) | copy-start | bytes 100
  0.6 13.8 %copy-start.6 = (s32[8]{0:T(128)S(1)}, s32[8]{0:T(128)}, u32[]{:S(2)}) copy-start(s32[8]{0:T(128)} %constant.143) | copy-start | bytes 100
  0.7 13.9 %copy-start.5 = (s32[8]{0:T(128)S(1)}, s32[8]{0:T(128)}, u32[]{:S(2)}) copy-start(s32[8]{0:T(128)} %constant.141.clone) | copy-start | bytes 100
  3.3 12.0 %collective-permute-start = (bf16[128,1152]{1,0:T(8,128)(2,1)}, bf16[128,1152]{1,0:T(8,128)(2,1)S(1)}, u32[]{:S(2)}, u32[]{:S(2)}) collective-permute-start(bf16[128,1152]{1,0:T(8,128)(2,1)} %get-tuple-element.45), channel_id=1, source_target_pairs={{0,1},{1,0},{2,3},{3,2},{4,5},{5,4},{6,7},{7,6},{8,9},{9,8},{10,11... | collective-permute-start | bytes 884744 | tf_op jit(solution)/shard_map/ppermute | solution.py:319
  7.3 11.1 %collective-permute-start.2 = (bf16[128,1152]{1,0:T(8,128)(2,1)}, bf16[128,1152]{1,0:T(8,128)(2,1)S(1)}, u32[]{:S(2)}, u32[]{:S(2)}) collective-permute-start(bf16[128,1152]{1,0:T(8,128)(2,1)} %get-tuple-element.45), channel_id=1, source_target_pairs={{0,2},{1,3},{2,4},{3,5},{4,6},{5,7},{6,0},{7,1},{8,10},{9,11},{10,... | collective-permute-start | bytes 884744 | tf_op jit(solution)/shard_map/ppermute | solution.py:320
  8.8 12.8 %collective-permute-start.1 = (bf16[128,1152]{1,0:T(8,128)(2,1)}, bf16[128,1152]{1,0:T(8,128)(2,1)S(1)}, u32[]{:S(2)}, u32[]{:S(2)}) collective-permute-start(bf16[128,1152]{1,0:T(8,128)(2,1)} %get-tuple-element.46), channel_id=1, source_target_pairs={{0,16},{8,24},{16,0},{24,8},{32,48},{40,56},{48,32},{56,40},{64,80... | collective-permute-start | bytes 884744 | tf_op jit(solution)/shard_map/ppermute | solution.py:319
  9.8 10.0 %collective-permute-start.3 = (bf16[128,1152]{1,0:T(8,128)(2,1)}, bf16[128,1152]{1,0:T(8,128)(2,1)S(1)}, u32[]{:S(2)}, u32[]{:S(2)}) collective-permute-start(bf16[128,1152]{1,0:T(8,128)(2,1)} %get-tuple-element.46), channel_id=1, source_target_pairs={{0,32},{8,40},{16,48},{24,56},{32,64},{40,72},{48,80},{56,88},{64,... | collective-permute-start | bytes 884744 | tf_op jit(solution)/shard_map/ppermute | solution.py:320
  11.4 10.2 %collective-permute-start.4 = (bf16[128,1152]{1,0:T(8,128)(2,1)}, bf16[128,1152]{1,0:T(8,128)(2,1)S(1)}, u32[]{:S(2)}, u32[]{:S(2)}) collective-permute-start(bf16[128,1152]{1,0:T(8,128)(2,1)} %get-tuple-element.45), channel_id=1, source_target_pairs={{0,6},{1,7},{2,0},{3,1},{4,2},{5,3},{6,4},{7,5},{8,14},{9,15},{10,... | collective-permute-start | bytes 884744 | tf_op jit(solution)/shard_map/ppermute | solution.py:321
  15.3 8.2 %collective-permute-start.5 = (bf16[128,1152]{1,0:T(8,128)(2,1)}, bf16[128,1152]{1,0:T(8,128)(2,1)S(1)}, u32[]{:S(2)}, u32[]{:S(2)}) collective-permute-start(bf16[128,1152]{1,0:T(8,128)(2,1)} %get-tuple-element.46), channel_id=1, source_target_pairs={{0,96},{8,104},{16,112},{24,120},{32,0},{40,8},{48,16},{56,24},{64... | collective-permute-start | bytes 884744 | tf_op jit(solution)/shard_map/ppermute | solution.py:321
  18.3 8.3 %collective-permute-start.6 = (bf16[128,1152]{1,0:T(8,128)(2,1)S(1)}, bf16[128,1152]{1,0:T(8,128)(2,1)S(1)}, u32[]{:S(2)}, u32[]{:S(2)}) collective-permute-start(bf16[128,1152]{1,0:T(8,128)(2,1)S(1)} %collective-permute-done.2), channel_id=1, source_target_pairs={{0,2},{1,3},{2,4},{3,5},{4,6},{5,7},{6,0},{7,1},{8,10},{9,11},{10,... | collective-permute-start | bytes 884744 | tf_op jit(solution)/shard_map/ppermute | solution.py:322
  19.8 8.0 %collective-permute-start.7 = (bf16[128,1152]{1,0:T(8,128)(2,1)S(1)}, bf16[128,1152]{1,0:T(8,128)(2,1)S(1)}, u32[]{:S(2)}, u32[]{:S(2)}) collective-permute-start(bf16[128,1152]{1,0:T(8,128)(2,1)S(1)} %collective-permute-done.3), channel_id=1, source_target_pairs={{0,32},{8,40},{16,48},{24,56},{32,64},{40,72},{48,80},{56,88},{64,... | collective-permute-start | bytes 884744 | tf_op jit(solution)/shard_map/ppermute | solution.py:322
  27.9 6.7 %collective-permute-start.8 = (bf16[128,1152]{1,0:T(8,128)(2,1)S(1)}, bf16[128,1152]{1,0:T(8,128)(2,1)S(1)}, u32[]{:S(2)}, u32[]{:S(2)}) collective-permute-start(bf16[128,1152]{1,0:T(8,128)(2,1)S(1)} %collective-permute-done), channel_id=1, source_target_pairs={{0,6},{1,7},{2,0},{3,1},{4,2},{5,3},{6,4},{7,5},{8,14},{9,15},{10,... | collective-permute-start | bytes 884744 | tf_op jit(solution)/shard_map/ppermute | solution.py:324
  29.6 7.9 %collective-permute-start.10 = (bf16[128,1152]{1,0:T(8,128)(2,1)S(1)}, bf16[128,1152]{1,0:T(8,128)(2,1)S(1)}, u32[]{:S(2)}, u32[]{:S(2)}) collective-permute-start(bf16[128,1152]{1,0:T(8,128)(2,1)S(1)} %collective-permute-done), channel_id=1, source_target_pairs={{0,2},{1,3},{2,4},{3,5},{4,6},{5,7},{6,0},{7,1},{8,10},{9,11},{10,... | collective-permute-start | bytes 884744 | tf_op jit(solution)/shard_map/ppermute | solution.py:325
  29.9 6.7 %collective-permute-start.9 = (bf16[128,1152]{1,0:T(8,128)(2,1)S(1)}, bf16[128,1152]{1,0:T(8,128)(2,1)S(1)}, u32[]{:S(2)}, u32[]{:S(2)}) collective-permute-start(bf16[128,1152]{1,0:T(8,128)(2,1)S(1)} %collective-permute-done.1), channel_id=1, source_target_pairs={{0,96},{8,104},{16,112},{24,120},{32,0},{40,8},{48,16},{56,24},{64... | collective-permute-start | bytes 884744 | tf_op jit(solution)/shard_map/ppermute | solution.py:324
  31.0 7.9 %collective-permute-start.11 = (bf16[128,1152]{1,0:T(8,128)(2,1)S(1)}, bf16[128,1152]{1,0:T(8,128)(2,1)S(1)}, u32[]{:S(2)}, u32[]{:S(2)}) collective-permute-start(bf16[128,1152]{1,0:T(8,128)(2,1)S(1)} %collective-permute-done.1), channel_id=1, source_target_pairs={{0,32},{8,40},{16,48},{24,56},{32,64},{40,72},{48,80},{56,88},{64,... | collective-permute-start | bytes 884744 | tf_op jit(solution)/shard_map/ppermute | solution.py:325
  32.0 22.3 %collective-permute-start.14 = (bf16[512,1152]{1,0:T(8,128)(2,1)S(1)}, bf16[512,1152]{1,0:T(8,128)(2,1)S(1)}, u32[]{:S(2)}, u32[]{:S(2)}) collective-permute-start(bf16[512,1152]{1,0:T(8,128)(2,1)S(1)} %constant_dynamic-update-slice_fusion.8.refs_4_.r0a), channel_id=1, source_target_pairs={{0,8},{8,0},{16,24},{24,16},{32,40},{40,32},{48,56},{56,48},{64,72... | collective-permute-start | bytes 3538952 | tf_op jit(solution)/shard_map/ppermute | solution.py:343
  38.9 7.2 %collective-permute-start.12 = (bf16[128,1152]{1,0:T(8,128)(2,1)S(1)}, bf16[128,1152]{1,0:T(8,128)(2,1)S(1)}, u32[]{:S(2)}, u32[]{:S(2)}) collective-permute-start(bf16[128,1152]{1,0:T(8,128)(2,1)S(1)} %collective-permute-done.8), channel_id=1, source_target_pairs={{0,6},{1,7},{2,0},{3,1},{4,2},{5,3},{6,4},{7,5},{8,14},{9,15},{10,... | collective-permute-start | bytes 884744 | tf_op jit(solution)/shard_map/ppermute | solution.py:327
  41.9 6.7 %collective-permute-start.13 = (bf16[128,1152]{1,0:T(8,128)(2,1)S(1)}, bf16[128,1152]{1,0:T(8,128)(2,1)S(1)}, u32[]{:S(2)}, u32[]{:S(2)}) collective-permute-start(bf16[128,1152]{1,0:T(8,128)(2,1)S(1)} %collective-permute-done.9), channel_id=1, source_target_pairs={{0,96},{8,104},{16,112},{24,120},{32,0},{40,8},{48,16},{56,24},{64... | collective-permute-start | bytes 884744 | tf_op jit(solution)/shard_map/ppermute | solution.py:327
  48.6 5.7 %collective-permute-start.15 = (bf16[512,1152]{1,0:T(8,128)(2,1)S(1)}, bf16[512,1152]{1,0:T(8,128)(2,1)S(1)}, u32[]{:S(2)}, u32[]{:S(2)}) collective-permute-start(bf16[512,1152]{1,0:T(8,128)(2,1)S(1)} %constant_dynamic-update-slice_fusion.12.refs_5_.r0b), channel_id=1, source_target_pairs={{0,8},{8,0},{16,24},{24,16},{32,40},{40,32},{48,56},{56,48},{64,72... | collective-permute-start | bytes 3538952 | tf_op jit(solution)/shard_map/ppermute | solution.py:343
  59.8 7.7 %collective-permute-start.21 = (bf16[1024,1024]{1,0:T(8,128)(2,1)S(1)}, bf16[1024,1024]{1,0:T(8,128)(2,1)S(1)}, u32[]{:S(2)}, u32[]{:S(2)}) collective-permute-start(bf16[1024,1024]{1,0:T(8,128)(2,1)S(1)} %get-tuple-element.63.w1), channel_id=1, source_target_pairs={{0,8},{8,0},{16,24},{24,16},{32,40},{40,32},{48,56},{56,48},{64,72... | collective-permute-start | bytes 6291464 | tf_op jit(solution)/shard_map/ppermute | solution.py:360
  60.3 5.5 %collective-permute-start.22 = (bf16[512,1152]{1,0:T(8,128)(2,1)S(1)}, bf16[512,1152]{1,0:T(8,128)(2,1)S(1)}, u32[]{:S(2)}, u32[]{:S(2)}) collective-permute-start(bf16[512,1152]{1,0:T(8,128)(2,1)S(1)} %constant_dynamic-update-slice_fusion.refs_2_.r0a), channel_id=1, source_target_pairs={{0,8},{8,0},{16,24},{24,16},{32,40},{40,32},{48,56},{56,48},{64,72... | collective-permute-start | bytes 3538952 | tf_op jit(solution)/shard_map/ppermute | solution.py:344
  60.4 7.1 %collective-permute-start.23 = (bf16[512,1152]{1,0:T(8,128)(2,1)S(1)}, bf16[512,1152]{1,0:T(8,128)(2,1)S(1)}, u32[]{:S(2)}, u32[]{:S(2)}) collective-permute-start(bf16[512,1152]{1,0:T(8,128)(2,1)S(1)} %constant_dynamic-update-slice_fusion.4.refs_3_.r0b), channel_id=1, source_target_pairs={{0,8},{8,0},{16,24},{24,16},{32,40},{40,32},{48,56},{56,48},{64,72... | collective-permute-start | bytes 3538952 | tf_op jit(solution)/shard_map/ppermute | solution.py:344
  62.4 11.1 %collective-permute-start.16 = (bf16[144,1152]{1,0:T(8,128)(2,1)S(1)}, bf16[144,1152]{1,0:T(8,128)(2,1)S(1)}, u32[]{:S(2)}, u32[]{:S(2)}) collective-permute-start(bf16[144,1152]{1,0:T(8,128)(2,1)S(1)} %get-tuple-element.65), channel_id=1, source_target_pairs={{0,2},{1,3},{2,4},{3,5},{4,6},{5,7},{6,0},{7,1},{8,10},{9,11},{10,... | collective-permute-start | bytes 995336 | tf_op jit(solution)/shard_map/ppermute | solution.py:363
  62.5 11.0 %collective-permute-start.17 = (bf16[144,1152]{1,0:T(8,128)(2,1)S(1)}, bf16[144,1152]{1,0:T(8,128)(2,1)S(1)}, u32[]{:S(2)}, u32[]{:S(2)}) collective-permute-start(bf16[144,1152]{1,0:T(8,128)(2,1)S(1)} %get-tuple-element.66), channel_id=1, source_target_pairs={{0,6},{1,7},{2,0},{3,1},{4,2},{5,3},{6,4},{7,5},{8,14},{9,15},{10,... | collective-permute-start | bytes 995336 | tf_op jit(solution)/shard_map/ppermute | solution.py:363
  69.1 12.1 %collective-permute-start.24 = (bf16[128,1152]{1,0:T(8,128)(2,1)S(1)}, bf16[128,1152]{1,0:T(8,128)(2,1)S(1)}, u32[]{:S(2)}, u32[]{:S(2)}) collective-permute-start(bf16[128,1152]{1,0:T(8,128)(2,1)S(1)} %get-tuple-element.73), channel_id=1, source_target_pairs={{0,32},{8,40},{16,48},{24,56},{32,64},{40,72},{48,80},{56,88},{64,... | collective-permute-start | bytes 884744 | tf_op jit(solution)/shard_map/ppermute | solution.py:365
  69.2 12.0 %collective-permute-start.25 = (bf16[128,1152]{1,0:T(8,128)(2,1)S(1)}, bf16[128,1152]{1,0:T(8,128)(2,1)S(1)}, u32[]{:S(2)}, u32[]{:S(2)}) collective-permute-start(bf16[128,1152]{1,0:T(8,128)(2,1)S(1)} %get-tuple-element.74), channel_id=1, source_target_pairs={{0,96},{8,104},{16,112},{24,120},{32,0},{40,8},{48,16},{56,24},{64... | collective-permute-start | bytes 884744 | tf_op jit(solution)/shard_map/ppermute | solution.py:365
  77.9 18.3 %collective-permute-start.18 = (bf16[272,1152]{1,0:T(8,128)(2,1)S(1)}, bf16[272,1152]{1,0:T(8,128)(2,1)S(1)}, u32[]{:S(2)}, u32[]{:S(2)}) collective-permute-start(bf16[272,1152]{1,0:T(8,128)(2,1)S(1)} %get-tuple-element.68), channel_id=1, source_target_pairs={{0,6},{1,7},{2,0},{3,1},{4,2},{5,3},{6,4},{7,5},{8,14},{9,15},{10,... | collective-permute-start | bytes 1880072 | tf_op jit(solution)/shard_map/ppermute | solution.py:367
  81.2 15.1 %collective-permute-start.19 = (bf16[256,1152]{1,0:T(8,128)(2,1)S(1)}, bf16[256,1152]{1,0:T(8,128)(2,1)S(1)}, u32[]{:S(2)}, u32[]{:S(2)}) collective-permute-start(bf16[256,1152]{1,0:T(8,128)(2,1)S(1)} %get-tuple-element.69), channel_id=1, source_target_pairs={{0,2},{1,3},{2,4},{3,5},{4,6},{5,7},{6,0},{7,1},{8,10},{9,11},{10,... | collective-permute-start | bytes 1769480 | tf_op jit(solution)/shard_map/ppermute | solution.py:367
  85.8 14.2 %collective-permute-start.26 = (bf16[256,1152]{1,0:T(8,128)(2,1)S(1)}, bf16[256,1152]{1,0:T(8,128)(2,1)S(1)}, u32[]{:S(2)}, u32[]{:S(2)}) collective-permute-start(bf16[256,1152]{1,0:T(8,128)(2,1)S(1)} %get-tuple-element.76), channel_id=1, source_target_pairs={{0,96},{8,104},{16,112},{24,120},{32,0},{40,8},{48,16},{56,24},{64... | collective-permute-start | bytes 1769480 | tf_op jit(solution)/shard_map/ppermute | solution.py:369
  87.2 15.4 %collective-permute-start.27 = (bf16[256,1152]{1,0:T(8,128)(2,1)S(1)}, bf16[256,1152]{1,0:T(8,128)(2,1)S(1)}, u32[]{:S(2)}, u32[]{:S(2)}) collective-permute-start(bf16[256,1152]{1,0:T(8,128)(2,1)S(1)} %get-tuple-element.77), channel_id=1, source_target_pairs={{0,32},{8,40},{16,48},{24,56},{32,64},{40,72},{48,80},{56,88},{64,... | collective-permute-start | bytes 1769480 | tf_op jit(solution)/shard_map/ppermute | solution.py:369
  96.7 18.9 %collective-permute-start.34 = (bf16[128,1152]{1,0:T(8,128)(2,1)S(1)}, bf16[128,1152]{1,0:T(8,128)(2,1)S(1)}, u32[]{:S(2)}, u32[]{:S(2)}) collective-permute-start(bf16[128,1152]{1,0:T(8,128)(2,1)S(1)} %get-tuple-element.81), channel_id=1, source_target_pairs={{0,1},{1,0},{2,3},{3,2},{4,5},{5,4},{6,7},{7,6},{8,9},{9,8},{10,11... | collective-permute-start | bytes 884744 | tf_op jit(solution)/shard_map/ppermute | solution.py:372
  98.8 1.1 collective-permute-start.20
  103.1 4.8 %collective-permute-start.29 = (f32[1,128]{1,0:T(1,128)S(1)}, f32[1,128]{1,0:T(1,128)S(1)}, u32[]{:S(2)}, u32[]{:S(2)}) collective-permute-start(f32[1,128]{1,0:T(1,128)S(1)} %add.83), channel_id=1, source_target_pairs={{0,16},{8,24},{16,0},{24,8},{32,48},{40,56},{48,32},{56,40},{64,80... | collective-permute-start | bytes 1544 | tf_op jit(solution)/shard_map/ppermute | solution.py:335
  103.8 5.0 %collective-permute-start.30 = (f32[1,128]{1,0:T(1,128)S(1)}, f32[1,128]{1,0:T(1,128)S(1)}, u32[]{:S(2)}, u32[]{:S(2)}) collective-permute-start(f32[1,128]{1,0:T(1,128)S(1)} %add.83), channel_id=1, source_target_pairs={{0,1},{1,0},{2,3},{3,2},{4,5},{5,4},{6,7},{7,6},{8,9},{9,8},{10,11... | collective-permute-start | bytes 1544 | tf_op jit(solution)/shard_map/ppermute | solution.py:335
  107.1 4.8 %collective-permute-start.28 = (f32[1,128]{1,0:T(1,128)S(1)}, f32[1,128]{1,0:T(1,128)S(1)}, u32[]{:S(2)}, u32[]{:S(2)}) collective-permute-start(f32[1,128]{1,0:T(1,128)S(1)} %add.83), channel_id=1, source_target_pairs={{0,17},{1,16},{2,19},{3,18},{4,21},{5,20},{6,23},{7,22},{8,25},{9,... | collective-permute-start | bytes 1544 | tf_op jit(solution)/shard_map/ppermute | solution.py:335
  111.9 3.7 %copy-start.1 = (f32[128,1152]{1,0:T(8,128)S(1)}, f32[128,1152]{1,0:T(8,128)}, u32[]{:S(2)}) copy-start(f32[128,1152]{1,0:T(8,128)} %get-tuple-element.79.hat_ref) | copy-start | bytes 1769476
  111.9 3.7 %copy-start.3 = (f32[128,1]{1,0:T(8,128)S(1)}, f32[128,1]{1,0:T(8,128)}, u32[]{:S(2)}) copy-start(f32[128,1]{1,0:T(8,128)} %get-tuple-element.80.norm_ref) | copy-start | bytes 1540
  111.9 5.2 %collective-permute-start.32 = (f32[1,128]{1,0:T(1,128)S(1)}, f32[1,128]{1,0:T(1,128)S(1)}, u32[]{:S(2)}, u32[]{:S(2)}) collective-permute-start(f32[1,128]{1,0:T(1,128)S(1)} %add_add_fusion.1), channel_id=1, source_target_pairs={{0,32},{8,40},{16,48},{24,56},{32,64},{40,72},{48,80},{56,88},{64,... | collective-permute-start | bytes 1544 | tf_op jit(solution)/shard_map/ppermute | solution.py:335
  112.0 5.1 %collective-permute-start.33 = (f32[1,128]{1,0:T(1,128)S(1)}, f32[1,128]{1,0:T(1,128)S(1)}, u32[]{:S(2)}, u32[]{:S(2)}) collective-permute-start(f32[1,128]{1,0:T(1,128)S(1)} %add_add_fusion.1), channel_id=1, source_target_pairs={{0,96},{8,104},{16,112},{24,120},{32,0},{40,8},{48,16},{56,24},{64... | collective-permute-start | bytes 1544 | tf_op jit(solution)/shard_map/ppermute | solution.py:335
  115.2 5.0 %collective-permute-start.31 = (f32[1,128]{1,0:T(1,128)S(1)}, f32[1,128]{1,0:T(1,128)S(1)}, u32[]{:S(2)}, u32[]{:S(2)}) collective-permute-start(f32[1,128]{1,0:T(1,128)S(1)} %add_add_fusion.1), channel_id=1, source_target_pairs={{0,64},{8,72},{16,80},{24,88},{32,96},{40,104},{48,112},{56,120},{... | collective-permute-start | bytes 1544 | tf_op jit(solution)/shard_map/ppermute | solution.py:335
  116.8 6.7 %copy-start = (f32[128,1152]{1,0:T(8,128)S(1)}, f32[128,1152]{1,0:T(8,128)}, u32[]{:S(2)}) copy-start(f32[128,1152]{1,0:T(8,128)} %get-tuple-element.82.hat_ref) | copy-start | bytes 1769476
  116.8 6.7 %copy-start.2 = (f32[128,1]{1,0:T(8,128)S(1)}, f32[128,1]{1,0:T(8,128)}, u32[]{:S(2)}) copy-start(f32[128,1]{1,0:T(8,128)} %get-tuple-element.83.norm_ref) | copy-start | bytes 1540
  116.8 6.7 %collective-permute-start.35 = (bf16[128,1152]{1,0:T(8,128)(2,1)S(1)}, bf16[128,1152]{1,0:T(8,128)(2,1)S(1)}, u32[]{:S(2)}, u32[]{:S(2)}) collective-permute-start(bf16[128,1152]{1,0:T(8,128)(2,1)S(1)} %fold_partner.1), channel_id=1, source_target_pairs={{0,16},{8,24},{16,0},{24,8},{32,48},{40,56},{48,32},{56,40},{64,80... | collective-permute-start | bytes 884744 | tf_op jit(solution)/shard_map/ppermute | solution.py:379
